TPU v7x, 32 devices: a whole 2x2x4 slice. The times are simulated.
32 devices in a mesh: lat: 2 (over core), lon: 16 (over z, y, x).
Axes of the slice: x: 2, y: 2, z: 4, core: 2. Of those that a mesh axis runs over, the one named last changes fastest.
Arguments:
- forcing: bfloat16 [16, 32, 2048], P(None, 'lat', 'lon'), may hold values from -6 to 6
- hidden: bfloat16 [64, 32, 2048], P(None, 'lat', 'lon'), may hold values from -3 to 3
- cell: bfloat16 [64, 32, 2048], P(None, 'lat', 'lon'), may hold values from -6 to 6
- grad_hidden: bfloat16 [64, 32, 2048], P(None, 'lat', 'lon'), may hold values from -6 to 6
- grad_cell: bfloat16 [64, 32, 2048], P(None, 'lat', 'lon'), may hold values from -6 to 6
- wet_mask: int32 [2, 128], P('lat'), may hold values from 0 to 1
- tile_owner: int32 [2, 128], P('lat'), may hold values from 0 to 15, as said below
- w_gates: bfloat16 [256, 720], replicated, may hold values from -0.21875 to 0.21875
- b_gates: float32 [256], replicated, may hold values from -3 to 3
Outputs:
- hidden_next: bfloat16 [64, 32, 2048], P(None, 'lat', 'lon')
- cell_next: float32 [128, 64, 256], P(('lat', 'lon'))
- hidden_grad: float32 [64, 32, 2048], P(None, 'lat', 'lon')
- cell_grad: float32 [64, 32, 2048], P(None, 'lat', 'lon')
- weight_grad: float32 [256, 720], replicated
- bias_grad: float32 [256], replicated
Inputs may be any that keep to these rules, and one draw needn't show every extreme that they name: Within each group of 1 tile rows, tile_owner gives every longitude index exactly 4 wet tiles, and gives the wet tiles of one longitude block of 8 tile columns at most 1 to any one index; both bounds are reached in every draw, and some block is wet throughout. Dry tiles carry an owner too.
All inputs are finite; a program needn't handle non-finite values.
Results may differ from a plain program's by a relative error of at most 0.0033.
Values may be sent and summed in bfloat16 or wider, within the bound.
No kernel may reach another device: no remote copies, remote signals or barrier semaphores. Data moves between devices by JAX's collectives and lax.ppermute only.
A program may use at most 64 MiB of HBM per device.

v0:
```python
import math

import jax
import jax.numpy as jnp
from jax import lax
from jax.sharding import PartitionSpec as P

TILE = 16


def extended_2(cells, sides, width):
    for axis, dim in sides:
        count = lax.axis_size(axis)
        head = lax.slice_in_dim(cells, 0, width, axis=dim)
        tail = lax.slice_in_dim(cells, cells.shape[dim] - width, cells.shape[dim], axis=dim)
        cells = jnp.concatenate(
            [
                lax.ppermute(tail, axis, [(i, (i + 1) % count) for i in range(count)]),
                cells,
                lax.ppermute(head, axis, [((i + 1) % count, i) for i in range(count)]),
            ],
            axis=dim,
        )
    return cells


def last_pad(values_in, pad_front, pad_back):
    widths = [(0, 0)] * (values_in.ndim - 1) + [(pad_front, pad_back)]
    return jnp.pad(values_in, widths)


def fold_edges(values_in):
    tile_count = values_in.shape[-2]
    inner_size = values_in.shape[-1] - 2
    leading = values_in.shape[:-2]
    flat_shape = leading + (tile_count * inner_size,)
    middle = values_in[..., 1 : inner_size + 1].reshape(flat_shape)
    zeros_left = jnp.zeros(leading + (tile_count, inner_size - 1), values_in.dtype)
    left_edge = jnp.concatenate([values_in[..., 0:1], zeros_left], -1).reshape(flat_shape)
    zeros_one = jnp.zeros(leading + (tile_count, 1), values_in.dtype)
    zeros_rest = jnp.zeros(leading + (tile_count, inner_size - 2), values_in.dtype)
    right_edge = jnp.concatenate(
        [zeros_one, values_in[..., inner_size + 1 : inner_size + 2], zeros_rest], -1
    ).reshape(flat_shape)
    full_size = tile_count * inner_size + 2
    return (
        last_pad(middle, 1, 1)
        + last_pad(left_edge, 0, 2)
        + last_pad(right_edge, inner_size, 0)[..., :full_size]
    )


def lstm_terms(pre_in, pre_forget, pre_out, pre_cand, cell_in, hidden_cot, cell_cot, live_cells):
    gate_in = jax.nn.sigmoid(pre_in)
    gate_forget = jax.nn.sigmoid(pre_forget)
    gate_out = jax.nn.sigmoid(pre_out)
    candidate = jnp.tanh(pre_cand)
    cell_new = gate_forget * cell_in + gate_in * candidate
    squash = jnp.tanh(cell_new)
    hidden_new = (live_cells * gate_out * squash).astype(jnp.bfloat16)
    back_h = live_cells * hidden_cot.astype(jnp.float32)
    back_c = live_cells * cell_cot.astype(jnp.float32) + back_h * gate_out * (1.0 - squash * squash)
    cell_back = back_c * gate_forget
    delta_parts = (
        back_c * candidate * gate_in * (1.0 - gate_in),
        back_c * cell_in * gate_forget * (1.0 - gate_forget),
        back_h * squash * gate_out * (1.0 - gate_out),
        back_c * gate_in * (1.0 - candidate * candidate),
    )
    return (hidden_new, cell_new, cell_back, delta_parts)


def tile_step(slab_tiles, cell_tiles, hidden_cot, cell_cot, live_tiles, w_gates, b_gates):
    tile_count = slab_tiles.shape[0]
    channels = slab_tiles.shape[1]
    hid_count = cell_tiles.shape[1]
    side_cells = TILE
    tile_grid = slab_tiles.reshape(tile_count, channels, side_cells + 2, side_cells + 2)
    tap_list = []
    for row_off in range(3):
        for col_off in range(3):
            tap_list.append(
                tile_grid[
                    :, :, row_off : row_off + side_cells, col_off : col_off + side_cells
                ].reshape(tile_count, channels, side_cells * side_cells)
            )
    patches = jnp.concatenate(tap_list, 1)
    pre_gates = (
        jnp.einsum("gk,nkc->ngc", w_gates, patches, preferred_element_type=jnp.float32)
        + b_gates[None, :, None]
    )
    live_cells = live_tiles[:, None, None]
    hidden_new, cell_new, cell_back, delta_parts = lstm_terms(
        pre_gates[:, :hid_count],
        pre_gates[:, hid_count : 2 * hid_count],
        pre_gates[:, 2 * hid_count : 3 * hid_count],
        pre_gates[:, 3 * hid_count :],
        cell_tiles.astype(jnp.float32),
        hidden_cot,
        cell_cot,
        live_cells,
    )
    gate_delta = jnp.concatenate(delta_parts, 1).astype(jnp.bfloat16)
    weight_part = jnp.einsum("ngc,nkc->gk", gate_delta, patches, preferred_element_type=jnp.float32)
    bias_part = jnp.sum(gate_delta.astype(jnp.float32), axis=(0, 2))
    hid_weights = w_gates.reshape(w_gates.shape[0], 9, channels)[:, :, channels - hid_count :]
    spread = jnp.einsum(
        "gth,ngc->nthc", hid_weights, gate_delta, preferred_element_type=jnp.float32
    )
    grad_pad = jnp.zeros((tile_count, hid_count, side_cells + 2, side_cells + 2), jnp.float32)
    for row_off in range(3):
        for col_off in range(3):
            placed = spread[:, row_off * 3 + col_off].reshape(
                tile_count, hid_count, side_cells, side_cells
            )
            grad_pad = grad_pad + jnp.pad(
                placed, ((0, 0), (0, 0), (row_off, 2 - row_off), (col_off, 2 - col_off))
            )
    grad_pad = grad_pad.reshape(tile_count, hid_count, (side_cells + 2) * (side_cells + 2))
    return (hidden_new, cell_new, cell_back, grad_pad, weight_part, bias_part)


def outside_rows(row_total, lat_index, lat_devices):
    position = jnp.arange(row_total, dtype=jnp.int32)
    upper = (position == 0) & (lat_index == 0)
    lower = (position == row_total - 1) & (lat_index == lat_devices - 1)
    return jnp.where(upper | lower, 0.0, 1.0).astype(jnp.float32)


def cut_tiles(padded, tile_rows, tile_cols):
    channels = padded.shape[0]
    side_cells = TILE + 2
    row_pick = (
        jnp.arange(tile_rows, dtype=jnp.int32)[:, None] * TILE
        + jnp.arange(side_cells, dtype=jnp.int32)[None, :]
    ).reshape(-1)
    col_pick = (
        jnp.arange(tile_cols, dtype=jnp.int32)[:, None] * TILE
        + jnp.arange(side_cells, dtype=jnp.int32)[None, :]
    ).reshape(-1)
    strips = jnp.take(padded, row_pick, axis=1).reshape(
        channels, tile_rows, side_cells, padded.shape[2]
    )
    pieces = jnp.take(strips, col_pick, axis=3).reshape(
        channels, tile_rows, side_cells, tile_cols, side_cells
    )
    return jnp.transpose(pieces, (1, 3, 0, 2, 4)).reshape(
        tile_rows * tile_cols, channels, side_cells * side_cells
    )


def to_tiles(values_in, tile_rows, tile_cols):
    channels = values_in.shape[0]
    shaped = values_in.reshape(channels, tile_rows, TILE, tile_cols, TILE)
    return jnp.transpose(shaped, (1, 3, 0, 2, 4)).reshape(
        tile_rows * tile_cols, channels, TILE * TILE
    )


def from_tiles(tiles_in, tile_rows, tile_cols):
    channels = tiles_in.shape[1]
    shaped = tiles_in.reshape(tile_rows, tile_cols, channels, TILE, TILE)
    return jnp.transpose(shaped, (2, 0, 3, 1, 4)).reshape(
        channels, tile_rows * TILE, tile_cols * TILE
    )


def sender_plan(wet_local, dest_local, slot_count, pair_most):
    tile_count = wet_local.shape[0]
    position = jnp.arange(tile_count, dtype=jnp.int32)
    earlier = position[:, None] < position[None, :]
    same_dest = (
        (dest_local[:, None] == dest_local[None, :]) & wet_local[:, None] & wet_local[None, :]
    )
    dest_rank = jnp.sum((same_dest & earlier).astype(jnp.int32), 0)
    slot_of = dest_local * pair_most + dest_rank
    placed = wet_local[:, None] & (
        slot_of[:, None] == jnp.arange(slot_count, dtype=jnp.int32)[None, :]
    )
    source = jnp.sum(placed.astype(jnp.int32) * position[:, None], 0)
    filled = jnp.any(placed, 0)
    send_index = jnp.where(filled, source, tile_count)
    home_index = jnp.where(wet_local, slot_of, slot_count)
    return (send_index, home_index)


def receiver_plan(arrivals, pair_most, capacity):
    slot_count = arrivals.shape[0] * pair_most
    positions = jnp.arange(slot_count, dtype=jnp.int32)
    filled = positions % pair_most < jnp.repeat(arrivals, pair_most)
    slot_rank = jnp.cumsum(filled.astype(jnp.int32)) - 1
    placed = filled[None, :] & (
        slot_rank[None, :] == jnp.arange(capacity, dtype=jnp.int32)[:, None]
    )
    work_index = jnp.sum(placed.astype(jnp.int32) * positions[None, :], 1)
    back_index = jnp.where(filled, slot_rank, capacity)
    return (work_index, back_index)


def pick_rows(arrays, row_index):
    picked = []
    for member in arrays:
        extended = jnp.concatenate([member, jnp.zeros((1,) + member.shape[1:], member.dtype)], 0)
        picked.append(jnp.take(extended, row_index, axis=0))
    return tuple(picked)


def fold_grad(pad_tiles, tile_rows, tile_cols, row_keep):
    hid_count = pad_tiles.shape[1]
    side_cells = TILE + 2
    shaped = pad_tiles.reshape(tile_rows, tile_cols, hid_count, side_cells, side_cells)
    across = fold_edges(jnp.transpose(shaped, (0, 2, 3, 1, 4)))
    down_fold = fold_edges(jnp.transpose(across, (1, 3, 0, 2)))
    overhang = jnp.transpose(down_fold, (0, 2, 1)) * row_keep[None, :, None]
    received = extended_2(overhang, (("lat", 1), ("lon", 2)), 1)
    lat_size = overhang.shape[1] - 2
    lon_size = overhang.shape[2] - 2
    columns = received[:, :, 2 : lon_size + 2]
    columns = columns.at[:, :, 0].add(received[:, :, 0])
    columns = columns.at[:, :, lon_size - 1].add(received[:, :, lon_size + 3])
    result = columns[:, 2 : lat_size + 2]
    result = result.at[:, 0].add(columns[:, 0])
    result = result.at[:, lat_size - 1].add(columns[:, lat_size + 3])
    return result


def body(forcing, hidden, cell, grad_hidden, grad_cell, wet_mask, tile_owner, w_gates, b_gates):
    lat_index = lax.axis_index("lat")
    lon_index = lax.axis_index("lon")
    lat_devices = lax.axis_size("lat")
    lon_devices = lax.axis_size("lon")
    tile_rows = wet_mask.shape[0]
    tile_cols = wet_mask.shape[1] // lon_devices
    tile_count = tile_rows * tile_cols
    pair_most = max(1, tile_count // lon_devices)
    slot_count = lon_devices * pair_most
    capacity = tile_count // 2
    fields = jnp.concatenate([forcing, hidden], 0)
    padded = extended_2(fields, (("lat", 1), ("lon", 2)), 1)
    row_keep = outside_rows(padded.shape[1], lat_index, lat_devices)
    padded = padded * row_keep.astype(jnp.bfloat16)[None, :, None]
    slab_tiles = cut_tiles(padded, tile_rows, tile_cols)
    cell_tiles = to_tiles(cell, tile_rows, tile_cols)
    hidden_cot = to_tiles(grad_hidden, tile_rows, tile_cols)
    cell_cot = to_tiles(grad_cell, tile_rows, tile_cols)
    wet_local = (
        lax.dynamic_slice_in_dim(wet_mask, lon_index * tile_cols, tile_cols, 1).reshape(tile_count)
        > 0
    )
    dest_local = lax.dynamic_slice_in_dim(tile_owner, lon_index * tile_cols, tile_cols, 1).reshape(
        tile_count
    )
    send_index, home_index = sender_plan(wet_local, dest_local, slot_count, pair_most)
    owned_here = (wet_mask > 0) & (tile_owner == lon_index)
    arrivals = jnp.sum(
        owned_here.reshape(tile_rows, lon_devices, tile_cols).astype(jnp.int32), axis=(0, 2)
    )
    work_index, back_index = receiver_plan(arrivals, pair_most, capacity)
    hid_tiles, cell_new, back_tiles, pad_tiles, weight_part, bias_part = tile_step(
        slab_tiles,
        cell_tiles,
        hidden_cot,
        cell_cot,
        wet_local.astype(jnp.float32),
        w_gates,
        b_gates,
    )
    outgoing_state = pick_rows((cell_new,), send_index)[0]
    incoming_state = lax.all_to_all(outgoing_state, "lon", split_axis=0, concat_axis=0, tiled=True)
    cell_next = pick_rows((incoming_state,), work_index)[0]
    hidden_next = from_tiles(hid_tiles, tile_rows, tile_cols)
    cell_grad = from_tiles(back_tiles, tile_rows, tile_cols)
    hidden_grad = fold_grad(pad_tiles, tile_rows, tile_cols, row_keep)
    totals = lax.psum((weight_part, bias_part), ("lat", "lon"))
    scaling = 1.0 / math.sqrt(float(lat_devices * lon_devices * capacity * TILE * TILE))
    return (
        hidden_next,
        cell_next,
        hidden_grad,
        cell_grad,
        totals[0] * scaling,
        totals[1] * scaling,
    )


def solution(mesh):
    return jax.shard_map(
        body,
        mesh=mesh,
        in_specs=(
            P(None, "lat", "lon"),
            P(None, "lat", "lon"),
            P(None, "lat", "lon"),
            P(None, "lat", "lon"),
            P(None, "lat", "lon"),
            P("lat", None),
            P("lat", None),
            P(),
            P(),
        ),
        out_specs=(
            P(None, "lat", "lon"),
            P(("lat", "lon"), None, None),
            P(None, "lat", "lon"),
            P(None, "lat", "lon"),
            P(),
            P(),
        ),
        check_vma=False,
    )
```

profile of v0, /device:TPU:0, one launch (start us, length us, event | category | flops | bytes accessed | tf_op | source)
XLA Modules:
  0.0 243.5 jit_solution(237680302898935029)
XLA Ops:
  7.2 1.1 copy.77
  8.4 1.3 copy.78
  12.6 1.1 convert_bitcast_fusion
  13.7 1.1 copy.105
  14.8 1.1 convert_bitcast_fusion.1
  16.1 3.0 %collective-permute-start.2 = (bf16[80,18,1]{0,2,1:T(2,128)(2,1)S(1)}, bf16[80,18,1]{0,2,1:T(2,128)(2,1)S(1)}, u32[]{:S(2)}, u32[]{:S(2)}) collective-permute-start(bf16[80,18,1]{0,2,1:T(2,128)(2,1)S(1)} %get-tuple-element.97), channel_id=1, source_target_pairs={{0,1},{1,2},{2,3},{3,4},{4,5},{5,6},{6,7},{7,8},{8,9},{9,10},{10,1... | collective-permute-start | bytes 8648 | tf_op jit(solution)/shard_map/ppermute | solution.py:18
  19.1 4.2 %collective-permute-start.3 = (bf16[80,18,1]{0,2,1:T(2,128)(2,1)S(1)}, bf16[80,18,1]{0,2,1:T(2,128)(2,1)S(1)}, u32[]{:S(2)}, u32[]{:S(2)}) collective-permute-start(bf16[80,18,1]{0,2,1:T(2,128)(2,1)S(1)} %get-tuple-element.98), channel_id=1, source_target_pairs={{1,0},{2,1},{3,2},{4,3},{5,4},{6,5},{7,6},{8,7},{9,8},{10,9},{11,1... | collective-permute-start | bytes 8648 | tf_op jit(solution)/shard_map/ppermute | solution.py:20
  23.4 1.1 copy.100
  24.5 1.5 copy.101
  26.0 2.3 copy.109
  28.3 1.5 copy.110
  29.8 1.1 copy.106
  30.9 2.3 copy.107
  33.8 0.7 gather_fusion
  34.8 0.8 gather_fusion.1
  35.8 2.0 fusion.35
  37.8 0.8 copy.89
  38.6 1.2 copy.98
  39.8 1.9 copy.88
  41.7 2.0 copy.97
  43.7 1.9 copy.87
  45.5 2.0 copy.96
  47.5 1.9 copy.86
  49.4 2.0 copy.95
  51.3 1.9 copy.85
  53.2 2.0 copy.94
  55.2 0.8 copy.84
  56.0 2.0 copy.93
  58.0 0.9 copy.92
  58.9 0.9 copy.91
  60.2 0.7 copy-done.17
  60.9 1.1 constant_dynamic-update-slice_fusion.6
  61.9 1.0 constant_dynamic-update-slice_fusion.5
  63.2 0.8 copy-done.21
  63.9 1.0 add_bitcast_fusion
  65.0 1.4 fusion.29
  66.5 1.5 multiply_convert_fusion.3
  67.9 1.8 convolution_bitcast_fusion.1
  69.8 0.8 convolution_bitcast_fusion
  70.6 1.9 fusion.32
  72.8 1.4 copy.120
  74.2 2.4 copy.119
  76.6 2.3 copy.118
  78.9 2.4 copy.117
  81.3 2.3 copy.116
  83.6 2.4 copy.115
  86.0 2.4 copy.114
  88.3 1.3 copy.113
  89.7 4.6 %add_bitcast_fusion.1 = f32[1,64,18,8,18]{1,4,2,3,0:T(8,128)S(1)} fusion(f32[8,64,16,16]{1,3,2,0:T(8,128)S(1)} %bitcast.122, f32[8,64,16,16]{1,3,2,0:T(8,128)} %bitcast.123, f32[8,64,16,16]{1,3,2,0:T(8,128)} %bitcast.124, f32[8,64,16,16]{1,3,2,0:T(8,128)} %bitcast.125, f32[8,64,16,16]{1,3,2,0:T(8,128)} %bitcast.126, f32[8,64,16,16]{1,3,2,0:T(8,128)} %bitcast.127, ...), kind=kLoop, calls=%fused_computation.8 | loop fusion | flops 1327104 | bytes 5382144 | tf_op jit(solution)/shard_map/transpose | solution.py:212
  95.4 1.6 slice_bitcast_fusion
  97.7 1.1 broadcast_select_fusion
  98.9 4.5 %all-to-all-start = ((f32[16,64,256]{2,1,0:T(8,128)}), f32[16,64,256]{2,1,0:T(8,128)}, u32[]{:S(2)}, u32[]{:S(2)}) async-start(f32[16,64,256]{2,1,0:T(8,128)} %broadcast_select_fusion), calls=%async_computation | async-start | bytes 2097152 | tf_op jit(solution)/shard_map/all_to_all | solution.py:269
  103.8 0.7 fusion.34
  105.2 47.1 %psum.15 = f32[256]{0:T(256)S(1)} all-reduce(f32[256]{0:T(256)S(1)} %convert_reduce_fusion), channel_id=1, replica_groups=mesh['lat'=2,'lon'=16] {'lat','lon'}, use_global_device_ids=true, to_apply=%region_8.9 | all-reduce | flops 256 | bytes 2048 | tf_op jit(solution)/shard_map/psum | solution.py:274
  152.9 1.2 copy.102
  154.2 1.0 copy.126
  155.6 1.1 copy.128
  156.8 4.1 %collective-permute-start.7 = (f32[64,20,1]{0,2,1:T(1,128)S(1)}, f32[64,20,1]{0,2,1:T(1,128)S(1)}, u32[]{:S(2)}, u32[]{:S(2)}) collective-permute-start(f32[64,20,1]{0,2,1:T(1,128)S(1)} %get-tuple-element.91), channel_id=1, source_target_pairs={{1,0},{2,1},{3,2},{4,3},{5,4},{6,5},{7,6},{8,7},{9,8},{10,9},{11,1... | collective-permute-start | bytes 15368 | tf_op jit(solution)/shard_map/ppermute | solution.py:20
  161.1 7.0 %collective-permute-done.6 = f32[64,20,1]{0,2,1:T(1,128)S(1)} collective-permute-done((f32[64,20,1]{0,2,1:T(1,128)S(1)}, f32[64,20,1]{0,2,1:T(1,128)S(1)}, u32[]{:S(2)}, u32[]{:S(2)}) %collective-permute-start.6) | collective-permute-done | bytes 5152 | tf_op jit(solution)/shard_map/ppermute | solution.py:18
  168.5 1.1 copy.127
  169.6 62.3 %all-reduce.19.cloned.1.call-done = f32[256,720]{0,1:T(8,128)} async-done(((f32[256,720]{0,1:T(8,128)}), f32[256,720]{0,1:T(8,128)}) %all-reduce.19.cloned.1.call-update) | async-done | bytes 737296 | tf_op jit(solution)/shard_map/psum | solution.py:274
  231.9 2.0 broadcast_multiply_fusion
  233.9 1.3 concatenate.50
  235.8 0.8 broadcast_select_fusion.1
  (147 shorter events, 10.0 us)
Async XLA Ops:
  7.2 3.2 %copy-start.25 = (s32[1,128]{1,0:T(1,128)S(1)}, s32[1,128]{1,0:T(1,128)}, u32[]{:S(2)}) copy-start(s32[1,128]{1,0:T(1,128)} %param.23) | copy-start | bytes 1540
  7.2 3.2 %copy-start.24 = (s32[1,128]{1,0:T(1,128)S(1)}, s32[1,128]{1,0:T(1,128)}, u32[]{:S(2)}) copy-start(s32[1,128]{1,0:T(1,128)} %param.22) | copy-start | bytes 1540
  7.2 4.6 %copy-start.18 = (bf16[64,16,128]{2,1,0:T(8,128)(2,1)S(1)}, bf16[64,16,128]{2,1,0:T(8,128)(2,1)}, u32[]{:S(2)}) copy-start(bf16[64,16,128]{2,1,0:T(8,128)(2,1)} %param.19) | copy-start | bytes 786436
  7.2 224.7 %all-reduce.19.cloned.1.call-start = ((), (), s32[]{:S(2)}) async-start(), calls=%async_computation.1 | async-start | bytes 1474560 | tf_op jit(solution)/shard_map/psum | solution.py:274
  9.7 2.6 %copy-start.19 = (bf16[64,16,128]{2,1,0:T(8,128)(2,1)S(1)}, bf16[64,16,128]{2,1,0:T(8,128)(2,1)}, u32[]{:S(2)}) copy-start(bf16[64,16,128]{2,1,0:T(8,128)(2,1)} %param.20) | copy-start | bytes 786436
  9.8 6.2 %collective-permute-start = (bf16[80,1,128]{0,2,1:T(8,128)(2,1)S(1)}, bf16[80,1,128]{0,2,1:T(8,128)(2,1)S(1)}, u32[]{:S(2)}, u32[]{:S(2)}) collective-permute-start(bf16[80,1,128]{0,2,1:T(8,128)(2,1)S(1)} %get-tuple-element.99), channel_id=1, source_target_pairs={{0,16},{16,0},{1,17},{17,1},{2,18},{18,2},{3,19},{19,3},{4,20},{20... | collective-permute-start | bytes 61448 | tf_op jit(solution)/shard_map/ppermute | solution.py:18
  10.3 5.7 %collective-permute-start.1 = (bf16[80,1,128]{0,2,1:T(8,128)(2,1)S(1)}, bf16[80,1,128]{0,2,1:T(8,128)(2,1)S(1)}, u32[]{:S(2)}, u32[]{:S(2)}) collective-permute-start(bf16[80,1,128]{0,2,1:T(8,128)(2,1)S(1)} %get-tuple-element.100), channel_id=1, source_target_pairs={{16,0},{0,16},{17,1},{1,17},{18,2},{2,18},{19,3},{3,19},{20,4},{4,... | collective-permute-start | bytes 61448 | tf_op jit(solution)/shard_map/ppermute | solution.py:20
  12.1 1.6 copy-start.20
  16.1 17.2 %collective-permute-start.2 = (bf16[80,18,1]{0,2,1:T(2,128)(2,1)S(1)}, bf16[80,18,1]{0,2,1:T(2,128)(2,1)S(1)}, u32[]{:S(2)}, u32[]{:S(2)}) collective-permute-start(bf16[80,18,1]{0,2,1:T(2,128)(2,1)S(1)} %get-tuple-element.97), channel_id=1, source_target_pairs={{0,1},{1,2},{2,3},{3,4},{4,5},{5,6},{6,7},{7,8},{8,9},{9,10},{10,1... | collective-permute-start | bytes 8648 | tf_op jit(solution)/shard_map/ppermute | solution.py:18
  19.1 14.2 %collective-permute-start.3 = (bf16[80,18,1]{0,2,1:T(2,128)(2,1)S(1)}, bf16[80,18,1]{0,2,1:T(2,128)(2,1)S(1)}, u32[]{:S(2)}, u32[]{:S(2)}) collective-permute-start(bf16[80,18,1]{0,2,1:T(2,128)(2,1)S(1)} %get-tuple-element.98), channel_id=1, source_target_pairs={{1,0},{2,1},{3,2},{4,3},{5,4},{6,5},{7,6},{8,7},{9,8},{10,9},{11,1... | collective-permute-start | bytes 8648 | tf_op jit(solution)/shard_map/ppermute | solution.py:20
  59.9 1.0 copy-start.17
  59.9 3.0 %copy-start.16 = (bf16[8,80,256]{2,1,0:T(8,128)(2,1)S(1)}, bf16[8,80,256]{2,1,0:T(8,128)(2,1)}, u32[]{:S(2)}) copy-start(bf16[8,80,256]{2,1,0:T(8,128)(2,1)} %copy.94) | copy-start | bytes 983044
  60.1 2.9 %copy-start.15 = (bf16[8,80,256]{2,1,0:T(8,128)(2,1)S(1)}, bf16[8,80,256]{2,1,0:T(8,128)(2,1)}, u32[]{:S(2)}) copy-start(bf16[8,80,256]{2,1,0:T(8,128)(2,1)} %copy.95) | copy-start | bytes 983044
  60.8 2.2 copy-start.14
  60.9 2.2 copy-start.13
  62.9 1.0 copy-start.21
  63.0 1.0 copy-start.26
  63.9 1.0 copy-start.12
  67.9 1.9 copy-start.3
  67.9 1.9 copy-start.5
  67.9 1.9 copy-start.7
  67.9 1.9 copy-start.9
  67.9 1.9 copy-start.22
  89.7 4.6 %copy-start.23 = (pred[16]{0:T(512)(128)(4,1)S(1)}, pred[16]{0:T(512)(128)(4,1)}, u32[]{:S(2)}) copy-start(pred[16]{0:T(512)(128)(4,1)} %constant.225.clone.1) | copy-start | bytes 52
  95.4 1.7 copy-start
  97.7 5.6 %slice-start = ((f32[64,130,1,18]{0,1,3,2:T(8,128)}), f32[64,130,1,1]{0,1,3,2:T(8,128)S(1)}, s32[]{:S(2)}) async-start(f32[64,130,1,18]{0,1,3,2:T(8,128)} %copy-done), calls=%async_computation.2 | async-start | bytes 139264 | tf_op jit(solution)/shard_map/slice | solution.py:43
  98.9 4.6 %copy-start.1 = (f32[64,130,16]{0,1,2:T(8,128)S(1)}, f32[64,130,16]{0,1,2:T(8,128)}, u32[]{:S(2)}) copy-start(f32[64,130,16]{0,1,2:T(8,128)} %get-tuple-element.95) | copy-start | bytes 1597444
  98.9 4.6 %copy-start.2 = (f32[64,130,16]{0,1,2:T(8,128)S(1)}, f32[64,130,16]{0,1,2:T(8,128)}, u32[]{:S(2)}) copy-start(f32[64,130,16]{0,1,2:T(8,128)} %get-tuple-element.96) | copy-start | bytes 1597444
  98.9 135.0 %all-to-all-start = ((f32[16,64,256]{2,1,0:T(8,128)}), f32[16,64,256]{2,1,0:T(8,128)}, u32[]{:S(2)}, u32[]{:S(2)}) async-start(f32[16,64,256]{2,1,0:T(8,128)} %broadcast_select_fusion), calls=%async_computation | async-start | bytes 2097152 | tf_op jit(solution)/shard_map/all_to_all | solution.py:269
  103.5 1.4 copy-start.4
  103.5 1.4 copy-start.6
  103.6 1.4 copy-start.8
  103.6 1.4 copy-start.10
  104.4 52.3 %collective-permute-start.4 = (f32[64,1,130]{0,2,1:T(8,128)}, f32[64,1,130]{0,2,1:T(8,128)S(1)}, u32[]{:S(2)}, u32[]{:S(2)}) collective-permute-start(f32[64,1,130]{0,2,1:T(8,128)} %get-tuple-element.93), channel_id=1, source_target_pairs={{0,16},{16,0},{1,17},{17,1},{2,18},{18,2},{3,19},{19,3},{4,20},{20... | collective-permute-start | bytes 99848 | tf_op jit(solution)/shard_map/ppermute | solution.py:18
  104.4 50.7 %copy-start.11 = (f32[8,64,256]{2,1,0:T(8,128)S(1)}, f32[8,64,256]{2,1,0:T(8,128)}, u32[]{:S(2)}) copy-start(f32[8,64,256]{2,1,0:T(8,128)} %get-tuple-element.66) | copy-start | bytes 1572868
  104.4 52.3 %collective-permute-start.5 = (f32[64,1,130]{0,2,1:T(8,128)}, f32[64,1,130]{0,2,1:T(8,128)S(1)}, u32[]{:S(2)}, u32[]{:S(2)}) collective-permute-start(f32[64,1,130]{0,2,1:T(8,128)} %get-tuple-element.94), channel_id=1, source_target_pairs={{16,0},{0,16},{17,1},{1,17},{18,2},{2,18},{19,3},{3,19},{20,4},{4,... | collective-permute-start | bytes 99848 | tf_op jit(solution)/shard_map/ppermute | solution.py:20
  156.8 11.5 %collective-permute-start.7 = (f32[64,20,1]{0,2,1:T(1,128)S(1)}, f32[64,20,1]{0,2,1:T(1,128)S(1)}, u32[]{:S(2)}, u32[]{:S(2)}) collective-permute-start(f32[64,20,1]{0,2,1:T(1,128)S(1)} %get-tuple-element.91), channel_id=1, source_target_pairs={{1,0},{2,1},{3,2},{4,3},{5,4},{6,5},{7,6},{8,7},{9,8},{10,9},{11,1... | collective-permute-start | bytes 15368 | tf_op jit(solution)/shard_map/ppermute | solution.py:20
  160.9 7.3 %collective-permute-start.6 = (f32[64,20,1]{0,2,1:T(1,128)S(1)}, f32[64,20,1]{0,2,1:T(1,128)S(1)}, u32[]{:S(2)}, u32[]{:S(2)}) collective-permute-start(f32[64,20,1]{0,2,1:T(1,128)S(1)} %get-tuple-element.92), channel_id=1, source_target_pairs={{0,1},{1,2},{2,3},{3,4},{4,5},{5,6},{6,7},{7,8},{8,9},{9,10},{10,1... | collective-permute-start | bytes 15368 | tf_op jit(solution)/shard_map/ppermute | solution.py:18
Sparse Core Ops, SparseCore 0:
  97.2 134.5 all-reduce.18
where the time goes:
time: 245 us; the launch traced here: 243 us
  local copies, waits for them, and re-layouts  72.1 us (29%)
  waiting for transfers between devices  69.3 us (28%)
  blocking collectives  47.1 us (19%)
  other arithmetic  19.6 us (8%)
  starting transfers between devices  16.9 us (7%)
  between operations  14.8 us (6%)
  matrix products  3.66 us (1%)
    psum x1, waiting for transfers between devices, body(): totals = lax.psum((weight_part, bias_part), ('lat', 'lon'))  62.3 us
    psum x1, blocking collectives, body(): totals = lax.psum((weight_part, bias_part), ('lat', 'lon'))  47.1 us
    slice x10, local copies, waits for them, and re-layouts, tile_step(): spread[:, row_off * 3 + col_off]  19 us
    reshape x9, local copies, waits for them, and re-layouts, tile_step(): tap_list.append(tile_grid[:, :, row_off:row_off + side_cells, col_off:col...  13.1 us
    unnamed x70, local copies, waits for them, and re-layouts  11.3 us
    slice x10, local copies, waits for them, and re-layouts, tile_step(): tile_grid[:, :, row_off:row_off + side_cells, col_off:col_off + side_cells]  11.2 us
    ppermute x4, starting transfers between devices, extended_2(): lax.ppermute(head, axis, [((i + 1) % count, i) for i in range(count)])  8.91 us
    ppermute x4, waiting for transfers between devices, extended_2(): lax.ppermute(tail, axis, [(i, (i + 1) % count) for i in range(count)])  7.03 us
  transfers between devices with their start and end apart: 10, of which 2 were waited for; matrix products, arithmetic and copies ran while one was open for 11% of the time, Pallas kernels for 0%

commit v1 on v0

v1 whole, which is shorter than its diff:
```python
import math

import jax
import jax.numpy as jnp
from jax import lax
from jax.experimental import pallas as pl
from jax.experimental.pallas import tpu as pltpu
from jax.sharding import PartitionSpec as P

TILE = 16
F32 = jnp.float32
BF16 = jnp.bfloat16
LIMIT = 48 * 1024 * 1024
SMEM = pl.BlockSpec(memory_space=pltpu.SMEM)
VMEM = pl.BlockSpec(memory_space=pltpu.VMEM)


def call(kernel, outs, operands, scalars=0, scratch=(), flops=0, moved=0):
    return pl.pallas_call(
        kernel,
        out_shape=outs,
        in_specs=[SMEM] * scalars + [VMEM] * (len(operands) - scalars),
        out_specs=jax.tree.map(lambda _: VMEM, outs),
        scratch_shapes=list(scratch),
        compiler_params=pltpu.CompilerParams(vmem_limit_bytes=LIMIT),
        cost_estimate=pl.CostEstimate(flops=flops, bytes_accessed=moved, transcendentals=0),
    )(*operands)


def lane_index(shape):
    return lax.broadcasted_iota(jnp.int32, shape, 1)


def sigmoid(values):
    return 0.5 * jnp.tanh(0.5 * values) + 0.5


def edges_kernel(place_ref, forcing_ref, hidden_ref, flat_ref, *rest):
    row_refs, (left_ref, right_ref, wide_ref) = rest[:-3], rest[-3:]
    inp, rows, width = forcing_ref.shape
    channels = inp + hidden_ref.shape[0]
    wide_ref[: inp * rows] = forcing_ref[...].astype(F32).reshape(inp * rows, width)
    wide_ref[inp * rows :] = hidden_ref[...].astype(F32).reshape((channels - inp) * rows, width)
    lane = lane_index((channels, width))
    left = jnp.zeros((channels, width), F32)
    right = jnp.zeros((channels, width), F32)
    ends = []
    for row in range(rows):
        slab = wide_ref[pl.ds(row, channels, stride=rows), :]
        flat_ref[:, row * width : (row + 1) * width] = slab.astype(BF16)
        left = jnp.where(lane == row, slab[:, :1], left)
        right = jnp.where(lane == row, slab[:, width - 1 :], right)
        if row in (0, rows - 1):
            ends.append(slab)
    left_ref[...] = left.astype(BF16)
    right_ref[...] = right.astype(BF16)
    if len(row_refs) == 1:
        row_refs[0][...] = jnp.where(place_ref[0] == 0, ends[-1], ends[0]).astype(BF16)
    else:
        row_refs[0][...] = ends[0].astype(BF16)
        row_refs[1][...] = ends[-1].astype(BF16)


def flatten_kernel(cell_ref, hcot_ref, ccot_ref, w_ref, cell_out, hcot_out, ccot_out, wt_ref, wide_ref):
    hid, rows, width = cell_ref.shape
    for source, target in ((cell_ref, cell_out), (hcot_ref, hcot_out), (ccot_ref, ccot_out)):
        wide_ref[...] = source[...].astype(F32).reshape(hid * rows, width)
        for row in range(rows):
            target[:, row * width : (row + 1) * width] = wide_ref[
                pl.ds(row, hid, stride=rows), :
            ].astype(BF16)
    wt_ref[...] = w_ref[...].astype(F32).T.astype(BF16)


def step_kernel(
    place_ref,
    wet_ref,
    owner_ref,
    flat_ref,
    up_ref,
    down_ref,
    up_left_ref,
    up_right_ref,
    down_left_ref,
    down_right_ref,
    left_ref,
    right_ref,
    cell_ref,
    hcot_ref,
    ccot_ref,
    w_ref,
    b_ref,
    hidden_next_ref,
    cell_grad_ref,
    send_ref,
    weight_ref,
    delta_ref,
    taps_ref,
    wide_ref,
    tiles_ref,
):
    channels = flat_ref.shape[0]
    hid = cell_ref.shape[0]
    gates = w_ref.shape[0]
    width = up_ref.shape[1]
    rows = flat_ref.shape[1] // width
    tile_cols = width // TILE
    span = 3 * channels
    first_tile = place_ref[1] * tile_cols
    lane = lane_index((channels, width))

    def put(row, slab, before, after):
        lanes = slice(row * width, (row + 1) * width)
        shifted = jnp.where(lane == 0, before, pltpu.roll(slab, 1, 1))
        taps_ref[0:channels, lanes] = shifted.astype(BF16)
        taps_ref[channels : 2 * channels, lanes] = slab.astype(BF16)
        shifted = jnp.where(lane == width - 1, after, pltpu.roll(slab, width - 1, 1))
        taps_ref[2 * channels : span, lanes] = shifted.astype(BF16)

    for row, flag, refs in (
        (0, place_ref[2], (up_ref, up_left_ref, up_right_ref)),
        (rows + 1, place_ref[3], (down_ref, down_left_ref, down_right_ref)),
    ):
        slab, before, after = [
            jnp.where(flag == 1, ref[...].astype(F32), 0.0) for ref in refs
        ]
        put(row, slab, before[:, width - 1 :], after[:, :1])
    left = left_ref[...].astype(F32)
    right = right_ref[...].astype(F32)
    for row in range(rows):
        slab = flat_ref[:, row * width : (row + 1) * width].astype(F32)
        put(row + 1, slab, left[:, row : row + 1], right[:, row : row + 1])
    extra = taps_ref.shape[0] - span
    ones = lax.broadcasted_iota(jnp.int32, (extra, taps_ref.shape[1]), 0) == 0
    taps_ref[span:] = jnp.where(ones, 1.0, 0.0).astype(BF16)

    live = jnp.zeros((1, width), F32)
    live_lane = lane_index((1, width)) // TILE
    for tile in range(tile_cols):
        wet = (wet_ref[0, first_tile + tile] > 0).astype(F32)
        live = jnp.where(live_lane == tile, wet, live)
    step = 2 if rows % 2 == 0 else 1
    chunk = step * width
    live = jnp.concatenate([live] * step, 1)
    blank = jnp.zeros((gates, 2 * width), BF16)
    delta_ref[:, : 2 * width] = blank
    delta_ref[:, (rows + 2) * width :] = blank
    bias = b_ref[...]
    group = 128 // TILE
    states = []
    for start in range(0, rows, step):
        pre = bias
        for row_off in range(3):
            low = (start + row_off) * width
            pre = pre + jnp.dot(
                w_ref[:, row_off * span : (row_off + 1) * span],
                taps_ref[:span, low : low + chunk],
                preferred_element_type=F32,
            )
        gate_in = sigmoid(pre[:hid])
        gate_forget = sigmoid(pre[hid : 2 * hid])
        gate_out = sigmoid(pre[2 * hid : 3 * hid])
        candidate = jnp.tanh(pre[3 * hid :])
        lanes = slice(start * width, start * width + chunk)
        cell_in = cell_ref[:, lanes].astype(F32)
        cell_new = gate_forget * cell_in + gate_in * candidate
        squash = jnp.tanh(cell_new)
        hidden_new = live * gate_out * squash
        back_h = live * hcot_ref[:, lanes].astype(F32)
        back_c = live * ccot_ref[:, lanes].astype(F32) + back_h * gate_out * (1.0 - squash * squash)
        cell_back = back_c * gate_forget
        carried = back_c * gate_in
        terms = (
            carried * candidate * (1.0 - gate_in),
            cell_back * cell_in * (1.0 - gate_forget),
            back_h * squash * gate_out * (1.0 - gate_out),
            carried * (1.0 - candidate * candidate),
        )
        low = (start + 2) * width
        for index, term in enumerate(terms):
            delta_ref[index * hid : (index + 1) * hid, low : low + chunk] = term.astype(BF16)
        for part in range(step):
            piece = slice(part * width, (part + 1) * width)
            wide_ref[pl.ds(start + part, hid, stride=rows), :] = hidden_new[:, piece]
            cell_grad_ref[pl.ds(start + part, hid, stride=rows), :] = cell_back[:, piece]
            states.append(cell_new[:, piece])
        if len(states) == group:
            block_of = lane_index((hid, width)) // TILE
            half = (start + step) // group - 1
            stride = group // 2
            while stride:
                upper = (block_of & stride) != 0
                mixed = list(states)
                for low_index in range(group):
                    if low_index & stride == 0:
                        first, second = states[low_index], states[low_index + stride]
                        mixed[low_index] = jnp.where(
                            upper, pltpu.roll(second, stride * TILE, 1), first
                        )
                        mixed[low_index + stride] = jnp.where(
                            upper, second, pltpu.roll(first, width - stride * TILE, 1)
                        )
                states = mixed
                stride //= 2
            for tile in range(tile_cols):
                tiles_ref[tile, :, half * 128 : (half + 1) * 128] = states[tile].astype(BF16)
            states = []
    hidden_next_ref[...] = wide_ref[...].reshape(hid, rows, width).astype(BF16)
    send_ref[...] = jnp.zeros(send_ref.shape, BF16)
    for tile in range(tile_cols):

        @pl.when(wet_ref[0, first_tile + tile] > 0)
        def _():
            send_ref[owner_ref[0, first_tile + tile]] = tiles_ref[tile]

    delta = delta_ref[:, 2 * width : (rows + 2) * width]
    lane_out = lane_index((gates, taps_ref.shape[0]))
    for row_off in range(3):
        part = lax.dot_general(
            delta,
            taps_ref[:, row_off * width : (row_off + rows) * width],
            (((1,), (1,)), ((), ())),
            preferred_element_type=F32,
        )
        if row_off == 1:
            rest = part - part.astype(BF16).astype(F32)
            part = jnp.where(lane_out == span, rest, part)
        base = row_off * taps_ref.shape[0]
        weight_ref[:, base : base + taps_ref.shape[0]] = part.astype(BF16)


def spread_kernel(place_ref, delta_ref, wt_ref, grad_ref, *rest):
    row_refs, (left_ref, right_ref, side_ref) = rest[:-3], rest[-3:]
    hid = grad_ref.shape[0]
    width = left_ref.shape[1]
    rows = grad_ref.shape[1] // width
    channels = wt_ref.shape[0] // 9
    total = [None] * 3
    for col_off in range(3):
        for row_off in range(3):
            first = (row_off * 3 + col_off + 1) * channels - hid
            low = (2 - row_off) * width
            term = jnp.dot(
                wt_ref[first : first + hid],
                delta_ref[:, low : low + (rows + 2) * width],
                preferred_element_type=F32,
            )
            total[col_off] = term if row_off == 0 else total[col_off] + term
        side_ref[col_off] = total[col_off]
    lane = lane_index((hid, width))
    left = jnp.zeros((hid, width), F32)
    right = jnp.zeros((hid, width), F32)
    ends = []
    for row in range(rows + 2):
        lanes = slice(row * width, (row + 1) * width)
        before = side_ref[0, :, lanes]
        after = side_ref[2, :, lanes]
        slab = (
            side_ref[1, :, lanes]
            + jnp.where(lane == width - 1, 0.0, pltpu.roll(before, width - 1, 1))
            + jnp.where(lane == 0, 0.0, pltpu.roll(after, 1, 1))
        )
        if row in (0, rows + 1):
            corners = jnp.where(lane == 0, before[:, :1], 0.0)
            corners = jnp.where(lane == width - 1, after[:, width - 1 :], corners)
            ends.append((slab, corners))
        else:
            grad_ref[:, (row - 1) * width : row * width] = slab
            left = jnp.where(lane == row - 1, before[:, :1], left)
            right = jnp.where(lane == row - 1, after[:, width - 1 :], right)
    left_ref[...] = left.astype(BF16)
    right_ref[...] = right.astype(BF16)
    if len(row_refs) == 2:
        for index in range(2):
            row_refs[index][...] = jnp.where(
                place_ref[0] == 0, ends[1][index], ends[0][index]
            ).astype(BF16)
    else:
        for end in range(2):
            for index in range(2):
                row_refs[2 * end + index][...] = ends[end][index].astype(BF16)


def fold_kernel(
    place_ref,
    grad_ref,
    up_ref,
    down_ref,
    up_left_ref,
    up_right_ref,
    down_left_ref,
    down_right_ref,
    left_ref,
    right_ref,
    out_ref,
):
    hid = grad_ref.shape[0]
    width = up_ref.shape[1]
    rows = grad_ref.shape[1] // width
    lane = lane_index((hid, width))
    left = left_ref[...].astype(F32)
    right = right_ref[...].astype(F32)
    ends = {}
    for row, flag, refs in (
        (0, place_ref[2], (up_ref, up_left_ref, up_right_ref)),
        (rows - 1, place_ref[3], (down_ref, down_left_ref, down_right_ref)),
    ):
        slab, before, after = [ref[...].astype(F32) for ref in refs]
        slab = slab + jnp.where(lane == 0, before[:, width - 1 :], 0.0)
        slab = slab + jnp.where(lane == width - 1, after[:, :1], 0.0)
        ends[row] = jnp.where(flag == 1, slab, 0.0)
    for row in range(rows):
        slab = grad_ref[:, row * width : (row + 1) * width]
        slab = slab + jnp.where(lane == 0, left[:, row : row + 1], 0.0)
        slab = slab + jnp.where(lane == width - 1, right[:, row : row + 1], 0.0)
        if row in ends:
            slab = slab + ends[row]
        out_ref[pl.ds(row, hid, stride=rows), :] = slab


def sum_kernel(parts_ref, out_ref):
    total = parts_ref[0].astype(F32)
    for index in range(1, parts_ref.shape[0]):
        total = total + parts_ref[index].astype(F32)
    out_ref[...] = total


def share_kernel(scaling, span, *refs):
    total = refs[0][...]
    for ref in refs[1:-1]:
        total = total + ref[...]
    total = total * scaling
    out_ref = refs[-1]
    third = total.shape[1] // 3
    lane = lane_index(total.shape)
    whole = total + pltpu.roll(total, 2 * third, 1)
    total = jnp.where(lane == span, whole, total)
    rest = whole - whole.astype(BF16).astype(F32)
    total = jnp.where(lane == third + span, pltpu.roll(rest, third, 1), total)
    for index in range(out_ref.shape[0]):
        out_ref[index] = total.astype(BF16)


def weights_kernel(span, parts_ref, weight_ref, bias_ref):
    third = parts_ref.shape[1] // 3
    for index in range(3):
        weight_ref[:, index * span : (index + 1) * span] = parts_ref[
            :, index * third : index * third + span
        ].astype(F32)
    first = span // 128 * 128
    both = parts_ref[:, first : first + 128].astype(F32)
    both = both + parts_ref[:, third + first : third + first + 128].astype(F32)
    bias_ref[...] = both.T[span - first : span - first + 1, :]


def tiles_kernel(work_ref, arrived_ref, out_ref):
    for index in range(out_ref.shape[0]):
        out_ref[index] = arrived_ref[work_ref[index]].astype(F32)


def moved(values, lat_step, lon_step, lat_devices, lon_devices):
    pairs = []
    for lat in range(lat_devices):
        for lon in range(lon_devices):
            to_lat = lat + lat_step
            if lat_step and lat_devices == 2:
                to_lat = 1 - lat
            if 0 <= to_lat < lat_devices:
                to = to_lat * lon_devices + (lon + lon_step) % lon_devices
                pairs.append((lat * lon_devices + lon, to))
    return lax.ppermute(values, ("lat", "lon"), pairs)


def exchange(ends, corners, left, right, lat_devices, lon_devices):
    def go(values, lat_step, lon_step):
        return moved(values, lat_step, lon_step, lat_devices, lon_devices)

    from_left, from_right = go(right, 0, 1), go(left, 0, -1)
    if lat_devices == 2:
        row = go(ends[0], 1, 0)
        row_left, row_right = go(corners[0], 1, 1), go(corners[0], 1, -1)
        return (row, row, row_left, row_right, row_left, row_right, from_left, from_right)
    return (
        go(ends[1], 1, 0),
        go(ends[0], -1, 0),
        go(corners[1], 1, 1),
        go(corners[1], 1, -1),
        go(corners[0], -1, 1),
        go(corners[0], -1, -1),
        from_left,
        from_right,
    )


def body(forcing, hidden, cell, grad_hidden, grad_cell, wet_mask, tile_owner, w_gates, b_gates):
    lat_index = lax.axis_index("lat")
    lon_index = lax.axis_index("lon")
    lat_devices = lax.axis_size("lat")
    lon_devices = lax.axis_size("lon")
    inp, rows, width = forcing.shape
    hid = hidden.shape[0]
    channels = inp + hid
    gates = w_gates.shape[0]
    span = 3 * channels
    third = (span + 128) // 128 * 128
    cells = rows * width
    tile_cols = width // TILE
    capacity = tile_cols // 2
    place = jnp.stack(
        [
            lat_index,
            lon_index,
            (lat_index > 0).astype(jnp.int32),
            (lat_index < lat_devices - 1).astype(jnp.int32),
        ]
    ).astype(jnp.int32)

    def shaped(*shape, dtype=BF16):
        return jax.ShapeDtypeStruct(shape, dtype)

    end_count = 1 if lat_devices == 2 else 2
    edges = call(
        edges_kernel,
        (shaped(channels, cells),) + (shaped(channels, width),) * (end_count + 2),
        (place, forcing, hidden),
        scalars=1,
        scratch=[pltpu.VMEM((channels * rows, width), F32)],
        moved=4 * channels * cells,
    )
    flat, ends, (left, right) = edges[0], edges[1:-2], edges[-2:]
    halo = exchange(ends, ends, left, right, lat_devices, lon_devices)
    cell_flat, hcot_flat, ccot_flat, w_turned = call(
        flatten_kernel,
        (shaped(hid, cells),) * 3 + (shaped(w_gates.shape[1], gates),),
        (cell, grad_hidden, grad_cell, w_gates),
        scratch=[pltpu.VMEM((hid * rows, width), F32)],
        moved=12 * hid * cells,
    )
    hidden_next, cell_grad, outgoing, weight_part, delta = call(
        step_kernel,
        (
            shaped(hid, rows, width),
            shaped(hid * rows, width, dtype=F32),
            shaped(lon_devices, hid, TILE * TILE),
            shaped(gates, 3 * third),
            shaped(gates, (rows + 4) * width),
        ),
        (place, wet_mask, tile_owner, flat, *halo)
        + (cell_flat, hcot_flat, ccot_flat, w_gates, b_gates.reshape(gates, 1)),
        scalars=3,
        scratch=[
            pltpu.VMEM((third, (rows + 2) * width), BF16),
            pltpu.VMEM((hid * rows, width), F32),
            pltpu.VMEM((tile_cols, hid, TILE * TILE), BF16),
        ],
        flops=4 * gates * 3 * span * cells,
        moved=16 * hid * cells,
    )
    share = gates // lon_devices
    parts = lax.all_to_all(
        weight_part.reshape(lon_devices, share, 3 * third), "lon", 0, 0, tiled=True
    )
    incoming = lax.all_to_all(outgoing, "lon", 0, 0, tiled=True)
    grad_parts = call(
        spread_kernel,
        (shaped(hid, cells, dtype=F32),) + (shaped(hid, width),) * (2 * end_count + 2),
        (place, delta, w_turned),
        scalars=1,
        scratch=[pltpu.VMEM((3, hid, (rows + 2) * width), F32)],
        flops=2 * gates * 9 * hid * cells,
        moved=8 * gates * cells,
    )
    grad_flat, grad_ends, grad_sides = grad_parts[0], grad_parts[1:-2], grad_parts[-2:]
    grad_halo = exchange(
        grad_ends[0::2], grad_ends[1::2], *grad_sides, lat_devices, lon_devices
    )
    hidden_grad = call(
        fold_kernel,
        shaped(hid * rows, width, dtype=F32),
        (place, grad_flat, *grad_halo),
        scalars=1,
        moved=8 * hid * cells,
    )
    summed = call(
        sum_kernel,
        shaped(share, 3 * third, dtype=F32),
        (parts,),
        moved=2 * gates * 3 * third,
    )
    scaling = 1.0 / math.sqrt(float(lat_devices * lon_devices * capacity * TILE * TILE))
    around = [summed]
    for _ in range(lat_devices - 1):
        pairs = [(i, (i + 1) % lat_devices) for i in range(lat_devices)]
        around.append(lax.ppermute(around[-1], "lat", pairs))
    shares = call(
        lambda *refs: share_kernel(scaling, span, *refs),
        shaped(lon_devices, share, 3 * third),
        tuple(around),
        moved=2 * gates * 3 * third,
    )
    gathered = lax.all_to_all(shares, "lon", 0, 0, tiled=True)
    weight_grad, bias_grad = call(
        lambda *refs: weights_kernel(span, *refs),
        (shaped(gates, 3 * span, dtype=F32), shaped(1, gates, dtype=F32)),
        (gathered.reshape(gates, 3 * third),),
        moved=6 * gates * 3 * third,
    )
    owned = (wet_mask > 0) & (tile_owner == lon_index)
    arrived = jnp.any(owned.reshape(lon_devices, tile_cols), 1)
    order = jnp.arange(lon_devices, dtype=jnp.int32)
    rank = jnp.sum((arrived[:, None] & (order[:, None] < order[None, :])).astype(jnp.int32), 0)
    placed = arrived[None, :] & (rank[None, :] == jnp.arange(capacity, dtype=jnp.int32)[:, None])
    work = jnp.sum(jnp.where(placed, order[None, :], 0), 1)
    cell_next = call(
        tiles_kernel,
        shaped(capacity, hid, TILE * TILE, dtype=F32),
        (work, incoming),
        scalars=1,
        moved=2 * lon_devices * hid * TILE * TILE,
    )
    return (
        hidden_next,
        cell_next,
        hidden_grad.reshape(hid, rows, width),
        cell_grad.reshape(hid, rows, width),
        weight_grad,
        bias_grad.reshape(gates),
    )


def solution(mesh):
    return jax.shard_map(
        body,
        mesh=mesh,
        in_specs=(
            P(None, "lat", "lon"),
            P(None, "lat", "lon"),
            P(None, "lat", "lon"),
            P(None, "lat", "lon"),
            P(None, "lat", "lon"),
            P("lat", None),
            P("lat", None),
            P(),
            P(),
        ),
        out_specs=(
            P(None, "lat", "lon"),
            P(("lat", "lon"), None, None),
            P(None, "lat", "lon"),
            P(None, "lat", "lon"),
            P(),
            P(),
        ),
        check_vma=False,
    )
```

time: 245 us -> 83.8 us (0.34)
  local copies, waits for them, and re-layouts: 72.1 us -> 4.99 us
  waiting for transfers between devices: 69.3 us -> 18.1 us
  blocking collectives: 47.1 us -> 16.8 us
  other arithmetic: 19.6 us -> 0.43 us
  Pallas kernels: 0 us -> 14.1 us
  between operations: 14.8 us -> 0.79 us
  starting transfers between devices: 16.9 us -> 28.1 us
  matrix products: 3.66 us -> 0 us
    psum x1 -> x0, waiting for transfers between devices: 62.3 us -> none  [body(): totals = lax.psum((weight_part, bias_part), ('lat', 'lon'))]
    psum x1 -> x0, blocking collectives: 47.1 us -> none  [body(): totals = lax.psum((weight_part, bias_part), ('lat', 'lon'))]
    slice x26 -> x0, local copies, waits for them, and re-layouts: 31.3 us -> none  [the longest x10 19 us: tile_step(): spread[:, row_off * 3 + col_off]]
    all_to_all x0 -> x1, blocking collectives: none -> 16.8 us  [body(): lax.all_to_all(weight_part.reshape(lon_devices, share, 3 * third), 'lon',...]
    pallas_call x0 -> x9, Pallas kernels: none -> 14.1 us  [call(): pl.pallas_call(kernel, out_shape=outs, in_specs=[SMEM] * scalars + [VMEM]...]
    all_to_all x1 -> x2, waiting for transfers between devices: 0.01 us -> 12.5 us  [the longest x1 12.5 us: body(): incoming = lax.all_to_all(outgoing, 'lon', 0, 0, tiled=True)]
    reshape x10 -> x2, local copies, waits for them, and re-layouts: 13.1 us -> 0.9 us  [the longest x1 0.8 us: body(): b_gates.reshape(gates, 1)]
    convert_element_type x9 -> x0, local copies, waits for them, and re-layouts: 11.3 us -> none  [the longest x2 3.83 us: lstm_terms(): back_h = live_cells * hidden_cot.astype(jnp.float32)]
  transfers between devices with their start and end apart: 10 -> 13, of which waited for: 2 -> 4; matrix products, arithmetic and copies ran while one was open for 11% -> 3% of each run, Pallas kernels for 0% -> 9%
where the time goes in v1:
time: 83.8 us; the launch traced here: 83.4 us
  starting transfers between devices  28.1 us (34%)
  waiting for transfers between devices  18.1 us (22%)
  blocking collectives  16.8 us (20%)
  Pallas kernels  14.1 us (17%)
  local copies, waits for them, and re-layouts  4.99 us (6%)
    ppermute x10, starting transfers between devices, moved(): return lax.ppermute(values, ('lat', 'lon'), pairs)  20.4 us
    all_to_all x1, blocking collectives, body(): lax.all_to_all(weight_part.reshape(lon_devices, share, 3 * third), 'lon',...  16.8 us
    pallas_call x9, Pallas kernels, call(): pl.pallas_call(kernel, out_shape=outs, in_specs=[SMEM] * scalars + [VMEM]...  14.1 us
    all_to_all x1, waiting for transfers between devices, body(): incoming = lax.all_to_all(outgoing, 'lon', 0, 0, tiled=True)  12.5 us
    ppermute x10, waiting for transfers between devices, moved(): return lax.ppermute(values, ('lat', 'lon'), pairs)  4.41 us
    unnamed x16, local copies, waits for them, and re-layouts  4.09 us
    all_to_all x1, starting transfers between devices, body(): gathered = lax.all_to_all(shares, 'lon', 0, 0, tiled=True)  3.89 us
    all_to_all x1, starting transfers between devices, body(): incoming = lax.all_to_all(outgoing, 'lon', 0, 0, tiled=True)  3.73 us
  transfers between devices with their start and end apart: 13, of which 4 were waited for; matrix products, arithmetic and copies ran while one was open for 3% of the time, Pallas kernels for 9%

profile of v1, /device:TPU:0, one launch (start us, length us, event | category | flops | bytes accessed | tf_op | source)
XLA Modules:
  0.0 83.4 jit_solution(16883020145315535701)
XLA Ops:
  0.6 0.0 copy-start.6
  0.6 0.0 copy-start.5
  0.7 0.1 pad_add_fusion.place_ref
  0.7 0.0 copy-start
  0.7 0.9 %copy-done = bf16[64,16,128]{2,1,0:T(8,128)(2,1)S(1)} copy-done((bf16[64,16,128]{2,1,0:T(8,128)(2,1)S(1)}, bf16[64,16,128]{2,1,0:T(8,128)(2,1)}, u32[]{:S(2)}) %copy-start) | copy-done | bytes 262168
  1.7 0.0 copy-start.4
  1.7 0.8 %copy-done.4 = bf16[16,16,128]{2,1,0:T(8,128)(2,1)S(1)} copy-done((bf16[16,16,128]{2,1,0:T(8,128)(2,1)S(1)}, bf16[16,16,128]{2,1,0:T(8,128)(2,1)}, u32[]{:S(2)}) %copy-start.4) | copy-done | bytes 65560
  2.5 0.0 copy-start.1
  2.5 0.0 copy-start.2
  2.5 0.0 copy-start.3
  2.5 1.0 %shard_map.136 = (bf16[80,2048]{1,0:T(8,128)(2,1)S(1)}, bf16[80,128]{1,0:T(8,128)(2,1)S(1)}, bf16[80,128]{1,0:T(8,128)(2,1)S(1)}, bf16[80,128]{1,0:T(8,128)(2,1)S(1)}) custom-call(s32[4]{0:T(128)S(1)} %pad_add_fusion.place_ref, bf16[16,16,128]{2,1,0:T(8,128)(2,1)S(1)} %copy-done.4, bf16[64,16,128]{2,1,0:T(8,128)(2,1)S(1)} %copy-done), custom_call_target="tpu_custom_call" | custom-call | bytes 655360 | tf_op jit(solution)/shard_map/pallas_call | solution.py:19
  3.5 3.0 %collective-permute-start.3 = (bf16[80,128]{1,0:T(8,128)(2,1)S(1)}, bf16[80,128]{1,0:T(8,128)(2,1)S(1)}, u32[]{:S(2)}, u32[]{:S(2)}) collective-permute-start(bf16[80,128]{1,0:T(8,128)(2,1)S(1)} %get-tuple-element.28), channel_id=1, source_target_pairs={{0,1},{1,2},{2,3},{3,4},{4,5},{5,6},{6,7},{7,8},{8,9},{9,10},{10,1... | collective-permute-start | bytes 61448 | tf_op jit(solution)/shard_map/ppermute | solution.py:371
  6.5 4.1 %collective-permute-start.4 = (bf16[80,128]{1,0:T(8,128)(2,1)S(1)}, bf16[80,128]{1,0:T(8,128)(2,1)S(1)}, u32[]{:S(2)}, u32[]{:S(2)}) collective-permute-start(bf16[80,128]{1,0:T(8,128)(2,1)S(1)} %get-tuple-element.29), channel_id=1, source_target_pairs={{0,15},{1,0},{2,1},{3,2},{4,3},{5,4},{6,5},{7,6},{8,7},{9,8},{10,9... | collective-permute-start | bytes 61448 | tf_op jit(solution)/shard_map/ppermute | solution.py:371
  10.5 0.8 %collective-permute-start.2 = (bf16[80,128]{1,0:T(8,128)(2,1)S(1)}, bf16[80,128]{1,0:T(8,128)(2,1)S(1)}, u32[]{:S(2)}, u32[]{:S(2)}) collective-permute-start(bf16[80,128]{1,0:T(8,128)(2,1)S(1)} %get-tuple-element.27), channel_id=1, source_target_pairs={{0,31},{1,16},{2,17},{3,18},{4,19},{5,20},{6,21},{7,22},{8,23},{9,... | collective-permute-start | bytes 61448 | tf_op jit(solution)/shard_map/ppermute | solution.py:371
  11.4 0.9 %collective-permute-start.1 = (bf16[80,128]{1,0:T(8,128)(2,1)S(1)}, bf16[80,128]{1,0:T(8,128)(2,1)S(1)}, u32[]{:S(2)}, u32[]{:S(2)}) collective-permute-start(bf16[80,128]{1,0:T(8,128)(2,1)S(1)} %get-tuple-element.27), channel_id=1, source_target_pairs={{0,17},{1,18},{2,19},{3,20},{4,21},{5,22},{6,23},{7,24},{8,25},{9,... | collective-permute-start | bytes 61448 | tf_op jit(solution)/shard_map/ppermute | solution.py:371
  12.3 0.3 collective-permute-start
  12.6 0.8 copy.24.b_ref
  13.4 1.2 %copy.22.w_ref = bf16[256,720]{1,0:T(8,128)(2,1)S(1)} copy(bf16[256,720]{0,1:T(8,128)(2,1)} %param.16) | data formatting | bytes 737280 | tf_op args[7]
  14.6 0.0 copy-done.1
  14.6 0.0 copy-done.2
  14.6 0.0 copy-done.3
  14.6 0.7 shard_map.137
  15.4 0.0 collective-permute-done.3.left_ref
  15.4 0.0 collective-permute-done.4.right_ref
  15.4 0.0 collective-permute-done.2.up_right_ref.down_right_ref
  15.4 2.8 %collective-permute-done.1.up_left_ref.down_left_ref = bf16[80,128]{1,0:T(8,128)(2,1)S(1)} collective-permute-done((bf16[80,128]{1,0:T(8,128)(2,1)S(1)}, bf16[80,128]{1,0:T(8,128)(2,1)S(1)}, u32[]{:S(2)}, u32[]{:S(2)}) %collective-permute-start.1) | collective-permute-done | bytes 20512 | tf_op jit(solution)/shard_map/ppermute | solution.py:371
  18.2 0.0 collective-permute-done.up_ref.down_ref
  18.2 0.0 copy-done.6
  18.2 0.0 copy-done.5
  18.2 5.3 %shard_map.138 = (bf16[64,16,128]{2,1,0:T(8,128)(2,1)}, f32[1024,128]{1,0:T(8,128)}, bf16[16,64,256]{2,1,0:T(8,128)(2,1)}, bf16[256,768]{1,0:T(8,128)(2,1)S(1)}, bf16[256,2560]{1,0:T(8,128)(2,1)S(1)}) custom-call(s32[4]{0:T(128)S(1)} %pad_add_fusion.place_ref, s32[1,128]{1,0:T(1,128)S(1)} %copy-done.5, s32[1,128]{1,0:T(1,128)S(1)} %copy-done.6, ...), custom_call_target="tpu_custom_call" | custom-call | flops 1509949440 | bytes 2097152 | tf_op jit(solution)/shard_map/pallas_call | solution.py:19
  23.5 16.8 %all_to_all.15.parts_ref = bf16[16,16,768]{2,1,0:T(8,128)(2,1)S(1)} all-to-all(bf16[16,16,768]{2,1,0:T(8,128)(2,1)S(1)} %bitcast.11), channel_id=1, replica_groups=mesh['lat'=2,'lon'=16] {'lon'}, dimensions={0} | all-to-all | bytes 786432 | tf_op jit(solution)/shard_map/all_to_all | solution.py:460
  40.3 3.7 %all-to-all-start = ((bf16[16,64,256]{2,1,0:T(8,128)(2,1)}), bf16[16,64,256]{2,1,0:T(8,128)(2,1)S(1)}, u32[]{:S(2)}, u32[]{:S(2)}) async-start(bf16[16,64,256]{2,1,0:T(8,128)(2,1)} %get-tuple-element.34), calls=%async_computation | async-start | bytes 1048576 | tf_op jit(solution)/shard_map/all_to_all | solution.py:463
  44.0 0.1 shard_map.142.refs_0_
  44.1 0.1 collective-permute-start.10
  44.1 1.2 %collective-permute-done.10.refs_1_ = f32[16,768]{1,0:T(8,128)S(1)} collective-permute-done((f32[16,768]{1,0:T(8,128)S(1)}, f32[16,768]{1,0:T(8,128)S(1)}, u32[]{:S(2)}, u32[]{:S(2)}) %collective-permute-start.10) | collective-permute-done | bytes 49184 | tf_op jit(solution)/shard_map/ppermute | solution.py:494
  45.4 0.8 shard_map.143
  46.1 12.5 %all-to-all-done.arrived_ref = bf16[16,64,256]{2,1,0:T(8,128)(2,1)S(1)} async-done(((bf16[16,64,256]{2,1,0:T(8,128)(2,1)}), bf16[16,64,256]{2,1,0:T(8,128)(2,1)S(1)}, u32[]{:S(2)}, u32[]{:S(2)}) %all-to-all-start) | async-done | bytes 524320 | tf_op jit(solution)/shard_map/all_to_all | solution.py:463
  58.6 3.9 %all-to-all-start.2 = ((bf16[16,16,768]{2,1,0:T(8,128)(2,1)}), bf16[16,16,768]{2,1,0:T(8,128)(2,1)S(1)}, u32[]{:S(2)}, u32[]{:S(2)}) async-start(bf16[16,16,768]{2,1,0:T(8,128)(2,1)} %shard_map.143), calls=%async_computation.2 | async-start | bytes 786432 | tf_op jit(solution)/shard_map/all_to_all | solution.py:501
  62.5 0.1 reshape.37
  62.6 0.1 reduce_or.9
  62.7 0.1 convert_reduce_fusion
  62.8 2.6 %shard_map.140 = (f32[64,2048]{1,0:T(8,128)S(1)}, bf16[64,128]{1,0:T(8,128)(2,1)S(1)}, bf16[64,128]{1,0:T(8,128)(2,1)S(1)}, bf16[64,128]{1,0:T(8,128)(2,1)S(1)}, bf16[64,128]{1,0:T(8,128)(2,1)S(1)}) custom-call(s32[4]{0:T(128)S(1)} %pad_add_fusion.place_ref, bf16[256,2560]{1,0:T(8,128)(2,1)S(1)} %get-tuple-element.35.delta_ref, ...), custom_call_target="tpu_custom_call" | custom-call | flops 603979776 | bytes 4194304 | tf_op jit(solution)/shard_map/pallas_call | solution.py:19
  65.5 3.7 %collective-permute-start.7 = (bf16[64,128]{1,0:T(8,128)(2,1)S(1)}, bf16[64,128]{1,0:T(8,128)(2,1)S(1)}, u32[]{:S(2)}, u32[]{:S(2)}) collective-permute-start(bf16[64,128]{1,0:T(8,128)(2,1)S(1)} %get-tuple-element.39), channel_id=1, source_target_pairs={{0,31},{1,16},{2,17},{3,18},{4,19},{5,20},{6,21},{7,22},{8,23},{9,... | collective-permute-start | bytes 49160 | tf_op jit(solution)/shard_map/ppermute | solution.py:371
  69.1 0.0 collective-permute-start.6
  69.1 2.0 %collective-permute-start.5 = (bf16[64,128]{1,0:T(8,128)(2,1)S(1)}, bf16[64,128]{1,0:T(8,128)(2,1)S(1)}, u32[]{:S(2)}, u32[]{:S(2)}) collective-permute-start(bf16[64,128]{1,0:T(8,128)(2,1)S(1)} %get-tuple-element.38), channel_id=1, source_target_pairs={{0,16},{1,17},{2,18},{3,19},{4,20},{5,21},{6,22},{7,23},{8,24},{9,... | collective-permute-start | bytes 49160 | tf_op jit(solution)/shard_map/ppermute | solution.py:371
  71.2 0.0 collective-permute-start.8
  71.2 5.6 %collective-permute-start.9 = (bf16[64,128]{1,0:T(8,128)(2,1)S(1)}, bf16[64,128]{1,0:T(8,128)(2,1)S(1)}, u32[]{:S(2)}, u32[]{:S(2)}) collective-permute-start(bf16[64,128]{1,0:T(8,128)(2,1)S(1)} %get-tuple-element.41), channel_id=1, source_target_pairs={{0,15},{1,0},{2,1},{3,2},{4,3},{5,4},{6,5},{7,6},{8,7},{9,8},{10,9... | collective-permute-start | bytes 49160 | tf_op jit(solution)/shard_map/ppermute | solution.py:371
  76.8 0.1 select_reduce_fusion.work_ref
  76.9 0.0 collective-permute-done.5.up_ref.down_ref
  76.9 1.6 %collective-permute-done.8.left_ref = bf16[64,128]{1,0:T(8,128)(2,1)S(1)} collective-permute-done((bf16[64,128]{1,0:T(8,128)(2,1)S(1)}, bf16[64,128]{1,0:T(8,128)(2,1)S(1)}, u32[]{:S(2)}, u32[]{:S(2)}) %collective-permute-start.8) | collective-permute-done | bytes 16416 | tf_op jit(solution)/shard_map/ppermute | solution.py:371
  78.5 0.0 collective-permute-done.9.right_ref
  78.5 0.0 collective-permute-done.7.up_right_ref.down_right_ref
  78.5 0.0 collective-permute-done.6.up_left_ref.down_left_ref
  78.5 1.7 %shard_map.141 = f32[1024,128]{1,0:T(8,128)} custom-call(s32[4]{0:T(128)S(1)} %pad_add_fusion.place_ref, f32[64,2048]{1,0:T(8,128)S(1)} %get-tuple-element.37.grad_ref, bf16[64,128]{1,0:T(8,128)(2,1)S(1)} %collective-permute-done.5.up_ref.down_ref, bf16[64,128]{1,0:T(8,128)(2,1)S(1)} %collective-permute-done.5.up_ref.down_ref, ...), custom_call_target="tpu_custom_call" | custom-call | bytes 1048576 | tf_op jit(solution)/shard_map/pallas_call | solution.py:19
  80.2 1.3 %shard_map.139 = f32[4,64,256]{2,1,0:T(8,128)} custom-call(s32[4]{0:T(128)S(1)} %select_reduce_fusion.work_ref, bf16[16,64,256]{2,1,0:T(8,128)(2,1)S(1)} %all-to-all-done.arrived_ref), custom_call_target="tpu_custom_call" | custom-call | bytes 524288 | tf_op jit(solution)/shard_map/pallas_call | solution.py:19
  81.5 0.0 all-to-all-done.2
  81.5 0.8 shard_map.144
  82.2 1.1 %copy.25 = f32[256,720]{0,1:T(8,128)} copy(f32[256,720]{1,0:T(8,128)S(1)} %get-tuple-element.62) | data formatting | bytes 1474560
  (1 shorter events, 0.0 us)
Async XLA Ops:
  0.6 17.6 %copy-start.6 = (s32[1,128]{1,0:T(1,128)S(1)}, s32[1,128]{1,0:T(1,128)}, u32[]{:S(2)}) copy-start(s32[1,128]{1,0:T(1,128)} %owner_ref.1) | copy-start | bytes 1540
  0.6 17.6 %copy-start.5 = (s32[1,128]{1,0:T(1,128)S(1)}, s32[1,128]{1,0:T(1,128)}, u32[]{:S(2)}) copy-start(s32[1,128]{1,0:T(1,128)} %wet_ref.1) | copy-start | bytes 1540
  0.7 1.0 %copy-start = (bf16[64,16,128]{2,1,0:T(8,128)(2,1)S(1)}, bf16[64,16,128]{2,1,0:T(8,128)(2,1)}, u32[]{:S(2)}) copy-start(bf16[64,16,128]{2,1,0:T(8,128)(2,1)} %hidden_ref.1) | copy-start | bytes 786436
  1.7 0.8 %copy-start.4 = (bf16[16,16,128]{2,1,0:T(8,128)(2,1)S(1)}, bf16[16,16,128]{2,1,0:T(8,128)(2,1)}, u32[]{:S(2)}) copy-start(bf16[16,16,128]{2,1,0:T(8,128)(2,1)} %forcing_ref.1) | copy-start | bytes 196612
  2.5 12.1 %copy-start.1 = (bf16[64,16,128]{2,1,0:T(8,128)(2,1)S(1)}, bf16[64,16,128]{2,1,0:T(8,128)(2,1)}, u32[]{:S(2)}) copy-start(bf16[64,16,128]{2,1,0:T(8,128)(2,1)} %cell_ref.1) | copy-start | bytes 786436
  2.5 12.1 %copy-start.2 = (bf16[64,16,128]{2,1,0:T(8,128)(2,1)S(1)}, bf16[64,16,128]{2,1,0:T(8,128)(2,1)}, u32[]{:S(2)}) copy-start(bf16[64,16,128]{2,1,0:T(8,128)(2,1)} %hcot_ref.1) | copy-start | bytes 786436
  2.5 12.1 %copy-start.3 = (bf16[64,16,128]{2,1,0:T(8,128)(2,1)S(1)}, bf16[64,16,128]{2,1,0:T(8,128)(2,1)}, u32[]{:S(2)}) copy-start(bf16[64,16,128]{2,1,0:T(8,128)(2,1)} %ccot_ref.1) | copy-start | bytes 786436
  3.5 11.9 %collective-permute-start.3 = (bf16[80,128]{1,0:T(8,128)(2,1)S(1)}, bf16[80,128]{1,0:T(8,128)(2,1)S(1)}, u32[]{:S(2)}, u32[]{:S(2)}) collective-permute-start(bf16[80,128]{1,0:T(8,128)(2,1)S(1)} %get-tuple-element.28), channel_id=1, source_target_pairs={{0,1},{1,2},{2,3},{3,4},{4,5},{5,6},{6,7},{7,8},{8,9},{9,10},{10,1... | collective-permute-start | bytes 61448 | tf_op jit(solution)/shard_map/ppermute | solution.py:371
  6.5 8.9 %collective-permute-start.4 = (bf16[80,128]{1,0:T(8,128)(2,1)S(1)}, bf16[80,128]{1,0:T(8,128)(2,1)S(1)}, u32[]{:S(2)}, u32[]{:S(2)}) collective-permute-start(bf16[80,128]{1,0:T(8,128)(2,1)S(1)} %get-tuple-element.29), channel_id=1, source_target_pairs={{0,15},{1,0},{2,1},{3,2},{4,3},{5,4},{6,5},{7,6},{8,7},{9,8},{10,9... | collective-permute-start | bytes 61448 | tf_op jit(solution)/shard_map/ppermute | solution.py:371
  10.5 4.8 %collective-permute-start.2 = (bf16[80,128]{1,0:T(8,128)(2,1)S(1)}, bf16[80,128]{1,0:T(8,128)(2,1)S(1)}, u32[]{:S(2)}, u32[]{:S(2)}) collective-permute-start(bf16[80,128]{1,0:T(8,128)(2,1)S(1)} %get-tuple-element.27), channel_id=1, source_target_pairs={{0,31},{1,16},{2,17},{3,18},{4,19},{5,20},{6,21},{7,22},{8,23},{9,... | collective-permute-start | bytes 61448 | tf_op jit(solution)/shard_map/ppermute | solution.py:371
  11.4 6.8 %collective-permute-start.1 = (bf16[80,128]{1,0:T(8,128)(2,1)S(1)}, bf16[80,128]{1,0:T(8,128)(2,1)S(1)}, u32[]{:S(2)}, u32[]{:S(2)}) collective-permute-start(bf16[80,128]{1,0:T(8,128)(2,1)S(1)} %get-tuple-element.27), channel_id=1, source_target_pairs={{0,17},{1,18},{2,19},{3,20},{4,21},{5,22},{6,23},{7,24},{8,25},{9,... | collective-permute-start | bytes 61448 | tf_op jit(solution)/shard_map/ppermute | solution.py:371
  12.3 5.9 %collective-permute-start = (bf16[80,128]{1,0:T(8,128)(2,1)S(1)}, bf16[80,128]{1,0:T(8,128)(2,1)S(1)}, u32[]{:S(2)}, u32[]{:S(2)}) collective-permute-start(bf16[80,128]{1,0:T(8,128)(2,1)S(1)} %get-tuple-element.27), channel_id=1, source_target_pairs={{0,16},{1,17},{2,18},{3,19},{4,20},{5,21},{6,22},{7,23},{8,24},{9,... | collective-permute-start | bytes 61448 | tf_op jit(solution)/shard_map/ppermute | solution.py:371
  40.3 18.3 %all-to-all-start = ((bf16[16,64,256]{2,1,0:T(8,128)(2,1)}), bf16[16,64,256]{2,1,0:T(8,128)(2,1)S(1)}, u32[]{:S(2)}, u32[]{:S(2)}) async-start(bf16[16,64,256]{2,1,0:T(8,128)(2,1)} %get-tuple-element.34), calls=%async_computation | async-start | bytes 1048576 | tf_op jit(solution)/shard_map/all_to_all | solution.py:463
  44.1 1.3 %collective-permute-start.10 = (f32[16,768]{1,0:T(8,128)S(1)}, f32[16,768]{1,0:T(8,128)S(1)}, u32[]{:S(2)}, u32[]{:S(2)}) collective-permute-start(f32[16,768]{1,0:T(8,128)S(1)} %shard_map.142.refs_0_), channel_id=1, source_target_pairs={{0,16},{16,0},{1,17},{17,1},{2,18},{18,2},{3,19},{19,3},{4,20},{20... | collective-permute-start | bytes 147464 | tf_op jit(solution)/shard_map/ppermute | solution.py:494
  58.6 22.9 %all-to-all-start.2 = ((bf16[16,16,768]{2,1,0:T(8,128)(2,1)}), bf16[16,16,768]{2,1,0:T(8,128)(2,1)S(1)}, u32[]{:S(2)}, u32[]{:S(2)}) async-start(bf16[16,16,768]{2,1,0:T(8,128)(2,1)} %shard_map.143), calls=%async_computation.2 | async-start | bytes 786432 | tf_op jit(solution)/shard_map/all_to_all | solution.py:501
  65.5 13.0 %collective-permute-start.7 = (bf16[64,128]{1,0:T(8,128)(2,1)S(1)}, bf16[64,128]{1,0:T(8,128)(2,1)S(1)}, u32[]{:S(2)}, u32[]{:S(2)}) collective-permute-start(bf16[64,128]{1,0:T(8,128)(2,1)S(1)} %get-tuple-element.39), channel_id=1, source_target_pairs={{0,31},{1,16},{2,17},{3,18},{4,19},{5,20},{6,21},{7,22},{8,23},{9,... | collective-permute-start | bytes 49160 | tf_op jit(solution)/shard_map/ppermute | solution.py:371
  69.1 9.4 %collective-permute-start.6 = (bf16[64,128]{1,0:T(8,128)(2,1)S(1)}, bf16[64,128]{1,0:T(8,128)(2,1)S(1)}, u32[]{:S(2)}, u32[]{:S(2)}) collective-permute-start(bf16[64,128]{1,0:T(8,128)(2,1)S(1)} %get-tuple-element.39), channel_id=1, source_target_pairs={{0,17},{1,18},{2,19},{3,20},{4,21},{5,22},{6,23},{7,24},{8,25},{9,... | collective-permute-start | bytes 49160 | tf_op jit(solution)/shard_map/ppermute | solution.py:371
  69.1 7.8 %collective-permute-start.5 = (bf16[64,128]{1,0:T(8,128)(2,1)S(1)}, bf16[64,128]{1,0:T(8,128)(2,1)S(1)}, u32[]{:S(2)}, u32[]{:S(2)}) collective-permute-start(bf16[64,128]{1,0:T(8,128)(2,1)S(1)} %get-tuple-element.38), channel_id=1, source_target_pairs={{0,16},{1,17},{2,18},{3,19},{4,20},{5,21},{6,22},{7,23},{8,24},{9,... | collective-permute-start | bytes 49160 | tf_op jit(solution)/shard_map/ppermute | solution.py:371
  71.2 7.3 %collective-permute-start.8 = (bf16[64,128]{1,0:T(8,128)(2,1)S(1)}, bf16[64,128]{1,0:T(8,128)(2,1)S(1)}, u32[]{:S(2)}, u32[]{:S(2)}) collective-permute-start(bf16[64,128]{1,0:T(8,128)(2,1)S(1)} %get-tuple-element.40), channel_id=1, source_target_pairs={{0,1},{1,2},{2,3},{3,4},{4,5},{5,6},{6,7},{7,8},{8,9},{9,10},{10,1... | collective-permute-start | bytes 49160 | tf_op jit(solution)/shard_map/ppermute | solution.py:371
  71.2 7.3 %collective-permute-start.9 = (bf16[64,128]{1,0:T(8,128)(2,1)S(1)}, bf16[64,128]{1,0:T(8,128)(2,1)S(1)}, u32[]{:S(2)}, u32[]{:S(2)}) collective-permute-start(bf16[64,128]{1,0:T(8,128)(2,1)S(1)} %get-tuple-element.41), channel_id=1, source_target_pairs={{0,15},{1,0},{2,1},{3,2},{4,3},{5,4},{6,5},{7,6},{8,7},{9,8},{10,9... | collective-permute-start | bytes 49160 | tf_op jit(solution)/shard_map/ppermute | solution.py:371

commit v2 on v1

--- a/solution.py
+++ b/solution.py
@@ -15,16 +15,23 @@
 VMEM = pl.BlockSpec(memory_space=pltpu.VMEM)
 
 
-def call(kernel, outs, operands, scalars=0, scratch=(), flops=0, moved=0):
+def call(kernel, outs, operands, scalars=0, scratch=(), flops=0, moved=0, after=()):
+    count = len(operands)
+
+    def run(*refs):
+        kernel(*refs[:count], *refs[count + len(after) :])
+
     return pl.pallas_call(
-        kernel,
+        run,
         out_shape=outs,
-        in_specs=[SMEM] * scalars + [VMEM] * (len(operands) - scalars),
+        in_specs=[SMEM] * scalars
+        + [VMEM] * (count - scalars)
+        + [pl.BlockSpec(memory_space=pl.ANY)] * len(after),
         out_specs=jax.tree.map(lambda _: VMEM, outs),
         scratch_shapes=list(scratch),
         compiler_params=pltpu.CompilerParams(vmem_limit_bytes=LIMIT),
         cost_estimate=pl.CostEstimate(flops=flops, bytes_accessed=moved, transcendentals=0),
-    )(*operands)
+    )(*operands, *after)
 
 
 def lane_index(shape):
@@ -61,15 +68,26 @@
         row_refs[1][...] = ends[-1].astype(BF16)
 
 
-def flatten_kernel(cell_ref, hcot_ref, ccot_ref, w_ref, cell_out, hcot_out, ccot_out, wt_ref, wide_ref):
+def flatten_kernel(
+    cell_ref, hcot_ref, ccot_ref, wt_ref, b_ref, cell_out, hcot_out, ccot_out, w_ref, bias_ref, wide_ref
+):
     hid, rows, width = cell_ref.shape
+    gates = wt_ref.shape[1]
+    span = wt_ref.shape[0] // 3
+    third = w_ref.shape[1] // 3
     for source, target in ((cell_ref, cell_out), (hcot_ref, hcot_out), (ccot_ref, ccot_out)):
         wide_ref[...] = source[...].astype(F32).reshape(hid * rows, width)
         for row in range(rows):
             target[:, row * width : (row + 1) * width] = wide_ref[
                 pl.ds(row, hid, stride=rows), :
             ].astype(BF16)
-    wt_ref[...] = w_ref[...].astype(F32).T.astype(BF16)
+    blank = jnp.zeros((third - span, gates), F32)
+    for index in range(3):
+        block = wt_ref[index * span : (index + 1) * span].astype(F32)
+        w_ref[:, index * third : (index + 1) * third] = (
+            jnp.concatenate([block, blank], 0).T.astype(BF16)
+        )
+    bias_ref[...] = jnp.broadcast_to(b_ref[...], (bias_ref.shape[1], gates)).T
 
 
 def step_kernel(
@@ -92,13 +110,10 @@
     b_ref,
     hidden_next_ref,
     cell_grad_ref,
-    send_ref,
-    weight_ref,
-    delta_ref,
-    taps_ref,
-    wide_ref,
     tiles_ref,
+    *rest,
 ):
+    weight_refs, (delta_ref, taps_ref, wide_ref) = rest[:-3], rest[-3:]
     channels = flat_ref.shape[0]
     hid = cell_ref.shape[0]
     gates = w_ref.shape[0]
@@ -142,10 +157,11 @@
     step = 2 if rows % 2 == 0 else 1
     chunk = step * width
     live = jnp.concatenate([live] * step, 1)
+    third = w_ref.shape[1] // 3
     blank = jnp.zeros((gates, 2 * width), BF16)
     delta_ref[:, : 2 * width] = blank
     delta_ref[:, (rows + 2) * width :] = blank
-    bias = b_ref[...]
+    bias = jnp.concatenate([b_ref[...]] * step, 1)
     group = 128 // TILE
     states = []
     for start in range(0, rows, step):
@@ -153,8 +169,8 @@
         for row_off in range(3):
             low = (start + row_off) * width
             pre = pre + jnp.dot(
-                w_ref[:, row_off * span : (row_off + 1) * span],
-                taps_ref[:span, low : low + chunk],
+                w_ref[:, row_off * third : (row_off + 1) * third],
+                taps_ref[:, low : low + chunk],
                 preferred_element_type=F32,
             )
         gate_in = sigmoid(pre[:hid])
@@ -206,27 +222,21 @@
                 tiles_ref[tile, :, half * 128 : (half + 1) * 128] = states[tile].astype(BF16)
             states = []
     hidden_next_ref[...] = wide_ref[...].reshape(hid, rows, width).astype(BF16)
-    send_ref[...] = jnp.zeros(send_ref.shape, BF16)
-    for tile in range(tile_cols):
-
-        @pl.when(wet_ref[0, first_tile + tile] > 0)
-        def _():
-            send_ref[owner_ref[0, first_tile + tile]] = tiles_ref[tile]
-
     delta = delta_ref[:, 2 * width : (rows + 2) * width]
-    lane_out = lane_index((gates, taps_ref.shape[0]))
     for row_off in range(3):
         part = lax.dot_general(
+            taps_ref[:, row_off * width : (row_off + rows) * width],
             delta,
-            taps_ref[:, row_off * width : (row_off + rows) * width],
             (((1,), (1,)), ((), ())),
             preferred_element_type=F32,
         )
-        if row_off == 1:
-            rest = part - part.astype(BF16).astype(F32)
-            part = jnp.where(lane_out == span, rest, part)
-        base = row_off * taps_ref.shape[0]
-        weight_ref[:, base : base + taps_ref.shape[0]] = part.astype(BF16)
+        place = slice(row_off * third, (row_off + 1) * third)
+        if len(weight_refs) == 1:
+            weight_refs[0][place] = part
+        else:
+            low, high = part[:, : gates // 2], part[:, gates // 2 :]
+            weight_refs[0][place] = jnp.where(place_ref[0] == 0, low, high)
+            weight_refs[1][place] = jnp.where(place_ref[0] == 0, high, low)
 
 
 def spread_kernel(place_ref, delta_ref, wt_ref, grad_ref, *rest):
@@ -318,44 +328,81 @@
         out_ref[pl.ds(row, hid, stride=rows), :] = slab
 
 
-def sum_kernel(parts_ref, out_ref):
-    total = parts_ref[0].astype(F32)
-    for index in range(1, parts_ref.shape[0]):
-        total = total + parts_ref[index].astype(F32)
-    out_ref[...] = total
-
-
-def share_kernel(scaling, span, *refs):
+def split_bias(block, row):
+    index = lax.broadcasted_iota(jnp.int32, block.shape, 0)
+    rest = pltpu.roll(block - block.astype(BF16).astype(F32), 1, 0)
+    return jnp.where(index == row + 1, rest, block)
+
+
+def pack_kernel(span, place_ref, wet_ref, owner_ref, tiles_ref, *refs):
+    out_ref = refs[-1]
+    tile_cols, hid, cells = tiles_ref.shape
+    lanes = out_ref.shape[2]
+    pieces = cells // 128
+    state_rows = hid * pieces * 128 // lanes
+    slots = out_ref.shape[0]
+    third = refs[0].shape[0] // 3
+    out_ref[:, :state_rows] = jnp.zeros((slots, state_rows, lanes), BF16)
+    for tile in range(tile_cols):
+        index = place_ref[1] * tile_cols + tile
+
+        @pl.when(wet_ref[0, index] > 0)
+        def _():
+            for piece in range(cells // lanes):
+                out_ref[owner_ref[0, index], piece * hid : (piece + 1) * hid] = tiles_ref[
+                    tile, :, piece * lanes : (piece + 1) * lanes
+                ]
+
     total = refs[0][...]
     for ref in refs[1:-1]:
         total = total + ref[...]
-    total = total * scaling
-    out_ref = refs[-1]
-    third = total.shape[1] // 3
-    lane = lane_index(total.shape)
-    whole = total + pltpu.roll(total, 2 * third, 1)
-    total = jnp.where(lane == span, whole, total)
-    rest = whole - whole.astype(BF16).astype(F32)
-    total = jnp.where(lane == third + span, pltpu.roll(rest, third, 1), total)
+    total = jnp.concatenate([split_bias(total[:third], span), total[third:]], 0)
+    share = total.shape[0] // slots
+    for slot in range(slots):
+        out_ref[slot, state_rows:] = total[slot * share : (slot + 1) * share].astype(BF16)
+
+
+def sum_kernel(scaling, state_rows, parts_ref, out_ref):
+    total = parts_ref[0, state_rows:].astype(F32)
+    for index in range(1, parts_ref.shape[0]):
+        total = total + parts_ref[index, state_rows:].astype(F32)
+    out_ref[...] = total * scaling
+
+
+def share_kernel(span, place_ref, *refs):
+    *parts, out_ref = refs
+    lanes = parts[0].shape[1]
+    share = out_ref.shape[1]
+    row = span % share
+    for side in range(len(parts)):
+        total = parts[0][...]
+        if len(parts) == 2:
+            total = jnp.where(place_ref[0] == side, total, parts[1][...])
+        index = lax.broadcasted_iota(jnp.int32, total.shape, 0)
+        whole = jnp.where(index == row, total + pltpu.roll(total, share - 1, 0), total)
+        total = jnp.where(place_ref[1] == span // share, split_bias(whole, row), total)
+        total = total.astype(BF16)
+        for slot in range(out_ref.shape[0]):
+            out_ref[slot, :, side * lanes : (side + 1) * lanes] = total
+
+
+def weights_kernel(span, parts_ref, weight_ref, bias_ref):
+    third = parts_ref.shape[0] // 3
+    for index in range(3):
+        low = index * third
+        weight_ref[index * span : (index + 1) * span] = parts_ref[low : low + span].astype(F32)
+    pair = parts_ref[span:third].astype(F32)
+    bias_ref[...] = pair[0:1] + pair[1:2]
+
+
+def tiles_kernel(work_ref, arrived_ref, out_ref):
+    hid, cells = out_ref.shape[1:]
+    lanes = arrived_ref.shape[2]
     for index in range(out_ref.shape[0]):
-        out_ref[index] = total.astype(BF16)
-
-
-def weights_kernel(span, parts_ref, weight_ref, bias_ref):
-    third = parts_ref.shape[1] // 3
-    for index in range(3):
-        weight_ref[:, index * span : (index + 1) * span] = parts_ref[
-            :, index * third : index * third + span
-        ].astype(F32)
-    first = span // 128 * 128
-    both = parts_ref[:, first : first + 128].astype(F32)
-    both = both + parts_ref[:, third + first : third + first + 128].astype(F32)
-    bias_ref[...] = both.T[span - first : span - first + 1, :]
-
-
-def tiles_kernel(work_ref, arrived_ref, out_ref):
-    for index in range(out_ref.shape[0]):
-        out_ref[index] = arrived_ref[work_ref[index]].astype(F32)
+        for piece in range(cells // lanes):
+            out_ref[index, :, piece * lanes : (piece + 1) * lanes] = arrived_ref[
+                work_ref[index], piece * hid : (piece + 1) * hid
+            ].astype(F32)
 
 
 def moved(values, lat_step, lon_step, lat_devices, lon_devices):
@@ -429,81 +476,67 @@
     )
     flat, ends, (left, right) = edges[0], edges[1:-2], edges[-2:]
     halo = exchange(ends, ends, left, right, lat_devices, lon_devices)
-    cell_flat, hcot_flat, ccot_flat, w_turned = call(
+    w_turned = w_gates.T
+    cell_flat, hcot_flat, ccot_flat, w_rows, bias = call(
         flatten_kernel,
-        (shaped(hid, cells),) * 3 + (shaped(w_gates.shape[1], gates),),
-        (cell, grad_hidden, grad_cell, w_gates),
+        (shaped(hid, cells),) * 3
+        + (shaped(gates, 3 * third), shaped(gates, width, dtype=F32)),
+        (cell, grad_hidden, grad_cell, w_turned, b_gates.reshape(1, gates)),
         scratch=[pltpu.VMEM((hid * rows, width), F32)],
         moved=12 * hid * cells,
     )
-    hidden_next, cell_grad, outgoing, weight_part, delta = call(
+    halves = 2 if lat_devices == 2 else 1
+    lanes = gates // halves
+    hidden_next, cell_grad, tiles, *weight_parts, delta = call(
         step_kernel,
         (
             shaped(hid, rows, width),
             shaped(hid * rows, width, dtype=F32),
-            shaped(lon_devices, hid, TILE * TILE),
-            shaped(gates, 3 * third),
-            shaped(gates, (rows + 4) * width),
-        ),
+            shaped(tile_cols, hid, TILE * TILE),
+        )
+        + (shaped(3 * third, lanes, dtype=F32),) * halves
+        + (shaped(gates, (rows + 4) * width),),
         (place, wet_mask, tile_owner, flat, *halo)
-        + (cell_flat, hcot_flat, ccot_flat, w_gates, b_gates.reshape(gates, 1)),
+        + (cell_flat, hcot_flat, ccot_flat, w_rows, bias),
         scalars=3,
         scratch=[
             pltpu.VMEM((third, (rows + 2) * width), BF16),
             pltpu.VMEM((hid * rows, width), F32),
-            pltpu.VMEM((tile_cols, hid, TILE * TILE), BF16),
         ],
         flops=4 * gates * 3 * span * cells,
         moved=16 * hid * cells,
     )
-    share = gates // lon_devices
-    parts = lax.all_to_all(
-        weight_part.reshape(lon_devices, share, 3 * third), "lon", 0, 0, tiled=True
+    swap = [(0, 1), (1, 0)]
+    if halves == 2:
+        weight_parts = (weight_parts[0], lax.ppermute(weight_parts[1], "lat", swap))
+    else:
+        weight_parts = (lax.psum(weight_parts[0], "lat"),)
+    state_rows = hid * TILE * TILE // lanes
+    share = 3 * third // lon_devices
+    outgoing = call(
+        lambda *refs: pack_kernel(span, *refs),
+        shaped(lon_devices, state_rows + share, lanes),
+        (place, wet_mask, tile_owner, tiles, *weight_parts),
+        scalars=3,
+        moved=4 * lon_devices * hid * TILE * TILE,
     )
     incoming = lax.all_to_all(outgoing, "lon", 0, 0, tiled=True)
-    grad_parts = call(
-        spread_kernel,
-        (shaped(hid, cells, dtype=F32),) + (shaped(hid, width),) * (2 * end_count + 2),
-        (place, delta, w_turned),
+    scaling = 1.0 / math.sqrt(float(lat_devices * lon_devices * capacity * TILE * TILE))
+    summed = call(
+        lambda *refs: sum_kernel(scaling, state_rows, *refs),
+        shaped(share, lanes, dtype=F32),
+        (incoming,),
+        moved=2 * gates * 3 * third,
+    )
+    around = (summed,)
+    if halves == 2:
+        around += (lax.ppermute(summed, "lat", swap),)
+    shares = call(
+        lambda *refs: share_kernel(span, *refs),
+        shaped(lon_devices, share, gates),
+        (place, *around),
         scalars=1,
-        scratch=[pltpu.VMEM((3, hid, (rows + 2) * width), F32)],
-        flops=2 * gates * 9 * hid * cells,
-        moved=8 * gates * cells,
-    )
-    grad_flat, grad_ends, grad_sides = grad_parts[0], grad_parts[1:-2], grad_parts[-2:]
-    grad_halo = exchange(
-        grad_ends[0::2], grad_ends[1::2], *grad_sides, lat_devices, lon_devices
-    )
-    hidden_grad = call(
-        fold_kernel,
-        shaped(hid * rows, width, dtype=F32),
-        (place, grad_flat, *grad_halo),
-        scalars=1,
-        moved=8 * hid * cells,
-    )
-    summed = call(
-        sum_kernel,
-        shaped(share, 3 * third, dtype=F32),
-        (parts,),
         moved=2 * gates * 3 * third,
-    )
-    scaling = 1.0 / math.sqrt(float(lat_devices * lon_devices * capacity * TILE * TILE))
-    around = [summed]
-    for _ in range(lat_devices - 1):
-        pairs = [(i, (i + 1) % lat_devices) for i in range(lat_devices)]
-        around.append(lax.ppermute(around[-1], "lat", pairs))
-    shares = call(
-        lambda *refs: share_kernel(scaling, span, *refs),
-        shaped(lon_devices, share, 3 * third),
-        tuple(around),
-        moved=2 * gates * 3 * third,
-    )
-    gathered = lax.all_to_all(shares, "lon", 0, 0, tiled=True)
-    weight_grad, bias_grad = call(
-        lambda *refs: weights_kernel(span, *refs),
-        (shaped(gates, 3 * span, dtype=F32), shaped(1, gates, dtype=F32)),
-        (gathered.reshape(gates, 3 * third),),
-        moved=6 * gates * 3 * third,
     )
     owned = (wet_mask > 0) & (tile_owner == lon_index)
     arrived = jnp.any(owned.reshape(lon_devices, tile_cols), 1)
@@ -517,13 +550,42 @@
         (work, incoming),
         scalars=1,
         moved=2 * lon_devices * hid * TILE * TILE,
+        after=(shares,),
+    )
+    grad_parts = call(
+        spread_kernel,
+        (shaped(hid, cells, dtype=F32),) + (shaped(hid, width),) * (2 * end_count + 2),
+        (place, delta, w_turned),
+        scalars=1,
+        scratch=[pltpu.VMEM((3, hid, (rows + 2) * width), F32)],
+        flops=2 * gates * 9 * hid * cells,
+        moved=8 * gates * cells,
+        after=(shares,),
+    )
+    grad_flat, grad_ends, grad_sides = grad_parts[0], grad_parts[1:-2], grad_parts[-2:]
+    grad_halo = exchange(
+        grad_ends[0::2], grad_ends[1::2], *grad_sides, lat_devices, lon_devices
+    )
+    hidden_grad = call(
+        fold_kernel,
+        shaped(hid * rows, width, dtype=F32),
+        (place, grad_flat, *grad_halo),
+        scalars=1,
+        moved=8 * hid * cells,
+    )
+    gathered = lax.all_to_all(shares, "lon", 0, 0, tiled=True)
+    weight_grad, bias_grad = call(
+        lambda *refs: weights_kernel(span, *refs),
+        (shaped(3 * span, gates, dtype=F32), shaped(1, gates, dtype=F32)),
+        (gathered.reshape(3 * third, gates),),
+        moved=6 * gates * 3 * third,
     )
     return (
         hidden_next,
         cell_next,
         hidden_grad.reshape(hid, rows, width),
         cell_grad.reshape(hid, rows, width),
-        weight_grad,
+        weight_grad.T,
         bias_grad.reshape(gates),
     )
 

time: 83.8 us -> 76.5 us (0.913)
  waiting for transfers between devices: 18.1 us -> 3.15 us
  blocking collectives: 16.8 us -> 26 us
  starting transfers between devices: 28.1 us -> 25.3 us
  local copies, waits for them, and re-layouts: 4.99 us -> 6.41 us
    all_to_all x1 -> x0, waiting for transfers between devices: 12.5 us -> none  [body(): incoming = lax.all_to_all(outgoing, 'lon', 0, 0, tiled=True)]
    all_to_all x1, blocking collectives: 16.8 us -> 26 us  [body(): incoming = lax.all_to_all(outgoing, 'lon', 0, 0, tiled=True)]
    ppermute x10, waiting for transfers between devices: 4.41 us -> 0.62 us  [moved(): return lax.ppermute(values, ('lat', 'lon'), pairs)]
    all_to_all x1 -> x0, starting transfers between devices: 3.73 us -> none  [body(): incoming = lax.all_to_all(outgoing, 'lon', 0, 0, tiled=True)]
    unnamed x16 -> x20, local copies, waits for them, and re-layouts: 4.09 us -> 6.32 us
    ppermute x1 -> x2, waiting for transfers between devices: 1.22 us -> 2.53 us  [the longest x1 1.35 us: body(): weight_parts = (weight_parts[0], lax.ppermute(weight_parts[1], 'lat', swap))]
    ppermute x1 -> x2, starting transfers between devices: 0.07 us -> 1.31 us  [the longest x1 1.24 us: body(): weight_parts = (weight_parts[0], lax.ppermute(weight_parts[1], 'lat', swap))]
    pallas_call x9 -> x10, Pallas kernels: 14.1 us -> 14 us  [call(): pl.pallas_call(run, out_shape=outs, in_specs=[SMEM] * scalars + [VMEM] *...]
  transfers between devices with their start and end apart: 13 -> 13, of which waited for: 4 -> 4; matrix products, arithmetic and copies ran while one was open for 3% -> 1% of each run, Pallas kernels for 9% -> 8%
where the time goes in v2:
time: 76.5 us; the launch traced here: 76.1 us
  blocking collectives  26 us (34%)
  starting transfers between devices  25.3 us (33%)
  Pallas kernels  14 us (18%)
  local copies, waits for them, and re-layouts  6.41 us (8%)
  waiting for transfers between devices  3.15 us (4%)
    all_to_all x1, blocking collectives, body(): incoming = lax.all_to_all(outgoing, 'lon', 0, 0, tiled=True)  26 us
    ppermute x10, starting transfers between devices, moved(): return lax.ppermute(values, ('lat', 'lon'), pairs)  20.4 us
    pallas_call x10, Pallas kernels, call(): pl.pallas_call(run, out_shape=outs, in_specs=[SMEM] * scalars + [VMEM] *...  14 us
    unnamed x20, local copies, waits for them, and re-layouts  6.32 us
    all_to_all x1, starting transfers between devices, body(): gathered = lax.all_to_all(shares, 'lon', 0, 0, tiled=True)  3.55 us
  transfers between devices with their start and end apart: 13, of which 4 were waited for; matrix products, arithmetic and copies ran while one was open for 1% of the time, Pallas kernels for 8%

profile of v2, /device:TPU:0, one launch (start us, length us, event | category | flops | bytes accessed | tf_op | source)
XLA Modules:
  0.0 76.1 jit_solution(851970632814776939)
XLA Ops:
  0.6 0.0 copy-start.8
  0.6 0.0 copy-start.7
  0.7 0.1 pad_add_fusion.refs_0_
  0.7 0.0 copy-start.2
  0.7 0.9 %copy-done.2 = bf16[64,16,128]{2,1,0:T(8,128)(2,1)S(1)} copy-done((bf16[64,16,128]{2,1,0:T(8,128)(2,1)S(1)}, bf16[64,16,128]{2,1,0:T(8,128)(2,1)}, u32[]{:S(2)}) %copy-start.2) | copy-done | bytes 262168
  1.7 0.0 copy-start.6
  1.7 0.8 %copy-done.6 = bf16[16,16,128]{2,1,0:T(8,128)(2,1)S(1)} copy-done((bf16[16,16,128]{2,1,0:T(8,128)(2,1)S(1)}, bf16[16,16,128]{2,1,0:T(8,128)(2,1)}, u32[]{:S(2)}) %copy-start.6) | copy-done | bytes 65560
  2.5 1.0 %shard_map.136 = (bf16[80,2048]{1,0:T(8,128)(2,1)S(1)}, bf16[80,128]{1,0:T(8,128)(2,1)S(1)}, bf16[80,128]{1,0:T(8,128)(2,1)S(1)}, bf16[80,128]{1,0:T(8,128)(2,1)S(1)}) custom-call(s32[4]{0:T(128)S(1)} %pad_add_fusion.refs_0_, bf16[16,16,128]{2,1,0:T(8,128)(2,1)S(1)} %copy-done.6, bf16[64,16,128]{2,1,0:T(8,128)(2,1)S(1)} %copy-done.2), custom_call_target="tpu_custom_call" | custom-call | bytes 655360 | tf_op jit(solution)/shard_map/pallas_call | solution.py:24
  3.5 3.0 %collective-permute-start.3 = (bf16[80,128]{1,0:T(8,128)(2,1)S(1)}, bf16[80,128]{1,0:T(8,128)(2,1)S(1)}, u32[]{:S(2)}, u32[]{:S(2)}) collective-permute-start(bf16[80,128]{1,0:T(8,128)(2,1)S(1)} %get-tuple-element.30), channel_id=1, source_target_pairs={{0,1},{1,2},{2,3},{3,4},{4,5},{5,6},{6,7},{7,8},{8,9},{9,10},{10,1... | collective-permute-start | bytes 61448 | tf_op jit(solution)/shard_map/ppermute | solution.py:418
  6.5 4.1 %collective-permute-start.4 = (bf16[80,128]{1,0:T(8,128)(2,1)S(1)}, bf16[80,128]{1,0:T(8,128)(2,1)S(1)}, u32[]{:S(2)}, u32[]{:S(2)}) collective-permute-start(bf16[80,128]{1,0:T(8,128)(2,1)S(1)} %get-tuple-element.31), channel_id=1, source_target_pairs={{0,15},{1,0},{2,1},{3,2},{4,3},{5,4},{6,5},{7,6},{8,7},{9,8},{10,9... | collective-permute-start | bytes 61448 | tf_op jit(solution)/shard_map/ppermute | solution.py:418
  10.5 0.8 %collective-permute-start.2 = (bf16[80,128]{1,0:T(8,128)(2,1)S(1)}, bf16[80,128]{1,0:T(8,128)(2,1)S(1)}, u32[]{:S(2)}, u32[]{:S(2)}) collective-permute-start(bf16[80,128]{1,0:T(8,128)(2,1)S(1)} %get-tuple-element.29), channel_id=1, source_target_pairs={{0,31},{1,16},{2,17},{3,18},{4,19},{5,20},{6,21},{7,22},{8,23},{9,... | collective-permute-start | bytes 61448 | tf_op jit(solution)/shard_map/ppermute | solution.py:418
  11.4 0.9 %collective-permute-start.1 = (bf16[80,128]{1,0:T(8,128)(2,1)S(1)}, bf16[80,128]{1,0:T(8,128)(2,1)S(1)}, u32[]{:S(2)}, u32[]{:S(2)}) collective-permute-start(bf16[80,128]{1,0:T(8,128)(2,1)S(1)} %get-tuple-element.29), channel_id=1, source_target_pairs={{0,17},{1,18},{2,19},{3,20},{4,21},{5,22},{6,23},{7,24},{8,25},{9,... | collective-permute-start | bytes 61448 | tf_op jit(solution)/shard_map/ppermute | solution.py:418
  12.3 0.3 collective-permute-start
  12.6 0.0 copy-start
  12.6 1.0 %copy-done = bf16[256,720]{0,1:T(8,128)(2,1)S(1)} copy-done((bf16[256,720]{0,1:T(8,128)(2,1)S(1)}, bf16[256,720]{0,1:T(8,128)(2,1)}, u32[]{:S(2)}) %copy-start) | copy-done | bytes 368664
  13.6 0.0 copy-start.3
  13.6 0.9 %copy-done.3 = bf16[64,16,128]{2,1,0:T(8,128)(2,1)S(1)} copy-done((bf16[64,16,128]{2,1,0:T(8,128)(2,1)S(1)}, bf16[64,16,128]{2,1,0:T(8,128)(2,1)}, u32[]{:S(2)}) %copy-start.3) | copy-done | bytes 262168
  14.6 0.0 copy-start.4
  14.6 0.9 %copy-done.4 = bf16[64,16,128]{2,1,0:T(8,128)(2,1)S(1)} copy-done((bf16[64,16,128]{2,1,0:T(8,128)(2,1)S(1)}, bf16[64,16,128]{2,1,0:T(8,128)(2,1)}, u32[]{:S(2)}) %copy-start.4) | copy-done | bytes 262168
  15.5 0.0 copy-start.5
  15.5 0.9 %copy-done.5 = bf16[64,16,128]{2,1,0:T(8,128)(2,1)S(1)} copy-done((bf16[64,16,128]{2,1,0:T(8,128)(2,1)S(1)}, bf16[64,16,128]{2,1,0:T(8,128)(2,1)}, u32[]{:S(2)}) %copy-start.5) | copy-done | bytes 262168
  16.5 0.0 copy-start.9
  16.5 0.7 copy-done.9
  17.1 0.7 shard_map.137
  17.9 0.0 collective-permute-done.3.refs_10_
  17.9 0.0 collective-permute-done.4.refs_11_
  17.9 0.0 collective-permute-done.2.refs_7_.refs_9_
  17.9 0.3 collective-permute-done.1.refs_6_.refs_8_
  18.2 0.0 collective-permute-done.refs_4_.refs_5_
  18.2 0.0 copy-done.8
  18.2 0.0 copy-done.7
  18.2 3.7 %shard_map.138 = (bf16[64,16,128]{2,1,0:T(8,128)(2,1)}, f32[1024,128]{1,0:T(8,128)}, bf16[8,64,256]{2,1,0:T(8,128)(2,1)S(1)}, f32[768,128]{1,0:T(8,128)S(1)}, f3...) custom-call(s32[4]{0:T(128)S(1)} %pad_add_fusion.refs_0_, s32[1,128]{1,0:T(1,128)S(1)} %copy-done.7, ...), custom_call_target="tpu_custom_call" | custom-call | flops 1509949440 | bytes 2097152 | tf_op jit(solution)/shard_map/pallas_call | solution.py:24
  21.9 1.2 %collective-permute-start.5 = (f32[768,128]{1,0:T(8,128)S(1)}, f32[768,128]{1,0:T(8,128)S(1)}, u32[]{:S(2)}, u32[]{:S(2)}) collective-permute-start(f32[768,128]{1,0:T(8,128)S(1)} %get-tuple-element.40), channel_id=1, source_target_pairs={{0,16},{16,0},{1,17},{17,1},{2,18},{18,2},{3,19},{19,3},{4,20},{20... | collective-permute-start | bytes 1179656 | tf_op jit(solution)/shard_map/ppermute | solution.py:511
  23.1 1.3 %collective-permute-done.5.refs_5_ = f32[768,128]{1,0:T(8,128)S(1)} collective-permute-done((f32[768,128]{1,0:T(8,128)S(1)}, f32[768,128]{1,0:T(8,128)S(1)}, u32[]{:S(2)}, u32[]{:S(2)}) %collective-permute-start.5) | collective-permute-done | bytes 393248 | tf_op jit(solution)/shard_map/ppermute | solution.py:511
  24.5 0.7 shard_map.139
  25.2 26.0 %all_to_all.10.refs_0_.refs_1_ = bf16[16,176,128]{2,1,0:T(8,128)(2,1)S(1)} all-to-all(bf16[16,176,128]{2,1,0:T(8,128)(2,1)S(1)} %shard_map.139), channel_id=1, replica_groups=mesh['lat'=2,'lon'=16] {'lon'}, dimensions={0} | all-to-all | bytes 1441792 | tf_op jit(solution)/shard_map/all_to_all | solution.py:523
  51.2 0.0 copy-start.1
  51.3 0.1 collective-permute-start.6
  51.3 1.2 %collective-permute-done.6.refs_2_ = f32[48,128]{1,0:T(8,128)S(1)} collective-permute-done((f32[48,128]{1,0:T(8,128)S(1)}, f32[48,128]{1,0:T(8,128)S(1)}, u32[]{:S(2)}, u32[]{:S(2)}) %collective-permute-start.6) | collective-permute-done | bytes 24608 | tf_op jit(solution)/shard_map/ppermute | solution.py:533
  52.5 1.3 %shard_map.141.refs_2_.refs_3_ = bf16[16,48,256]{2,1,0:T(8,128)(2,1)} custom-call(s32[4]{0:T(128)S(1)} %pad_add_fusion.refs_0_, f32[48,128]{1,0:T(8,128)S(1)} %shard_map.140.refs_1_, f32[48,128]{1,0:T(8,128)S(1)} %collective-permute-done.6.refs_2_), custom_call_target="tpu_custom_call" | custom-call | bytes 393216 | tf_op jit(solution)/shard_map/pallas_call | solution.py:24
  53.9 3.6 %all-to-all-start.1 = ((bf16[16,48,256]{2,1,0:T(8,128)(2,1)}), bf16[16,48,256]{2,1,0:T(8,128)(2,1)S(1)}, u32[]{:S(2)}, u32[]{:S(2)}) async-start(bf16[16,48,256]{2,1,0:T(8,128)(2,1)} %shard_map.141.refs_2_.refs_3_), calls=%async_computation.1 | async-start | bytes 786432 | tf_op jit(solution)/shard_map/all_to_all | solution.py:576
  57.5 0.1 reshape.34
  57.5 0.1 reduce_or.9
  57.7 0.1 convert_reduce_fusion
  57.8 0.0 copy-done.1
  57.8 2.6 %shard_map.143 = (f32[64,2048]{1,0:T(8,128)S(1)}, bf16[64,128]{1,0:T(8,128)(2,1)S(1)}, bf16[64,128]{1,0:T(8,128)(2,1)S(1)}, bf16[64,128]{1,0:T(8,128)(2,1)S(1)}, bf16[64,128]{1,0:T(8,128)(2,1)S(1)}) custom-call(s32[4]{0:T(128)S(1)} %pad_add_fusion.refs_0_, bf16[256,2560]{1,0:T(8,128)(2,1)S(1)} %get-tuple-element.41.refs_1_, bf16[720,256]{1,0:T(8,128)(2,1)S(1)} %bitcast.13, ...), custom_call_target="tpu_custom_call" | custom-call | flops 603979776 | bytes 4194304 | tf_op jit(solution)/shard_map/pallas_call | solution.py:24
  60.4 5.0 %collective-permute-start.9 = (bf16[64,128]{1,0:T(8,128)(2,1)S(1)}, bf16[64,128]{1,0:T(8,128)(2,1)S(1)}, u32[]{:S(2)}, u32[]{:S(2)}) collective-permute-start(bf16[64,128]{1,0:T(8,128)(2,1)S(1)} %get-tuple-element.44), channel_id=1, source_target_pairs={{0,31},{1,16},{2,17},{3,18},{4,19},{5,20},{6,21},{7,22},{8,23},{9,... | collective-permute-start | bytes 49160 | tf_op jit(solution)/shard_map/ppermute | solution.py:418
  65.5 0.0 collective-permute-start.8
  65.5 0.6 collective-permute-start.7
  66.1 0.0 collective-permute-start.10
  66.1 5.6 %collective-permute-start.11 = (bf16[64,128]{1,0:T(8,128)(2,1)S(1)}, bf16[64,128]{1,0:T(8,128)(2,1)S(1)}, u32[]{:S(2)}, u32[]{:S(2)}) collective-permute-start(bf16[64,128]{1,0:T(8,128)(2,1)S(1)} %get-tuple-element.46), channel_id=1, source_target_pairs={{0,15},{1,0},{2,1},{3,2},{4,3},{5,4},{6,5},{7,6},{8,7},{9,8},{10,9... | collective-permute-start | bytes 49160 | tf_op jit(solution)/shard_map/ppermute | solution.py:418
  71.7 0.1 select_reduce_fusion.refs_0_
  71.8 1.3 %shard_map.142 = f32[4,64,256]{2,1,0:T(8,128)} custom-call(s32[4]{0:T(128)S(1)} %select_reduce_fusion.refs_0_, bf16[16,176,128]{2,1,0:T(8,128)(2,1)S(1)} %all_to_all.10.refs_0_.refs_1_, bf16[16,48,256]{2,1,0:T(8,128)(2,1)} %shard_map.141.refs_2_.refs_3_), custom_call_target="tpu_custom_call" | custom-call | bytes 524288 | tf_op jit(solution)/shard_map/pallas_call | solution.py:24
  73.1 0.0 collective-permute-done.7.refs_2_.refs_3_
  73.1 0.3 collective-permute-done.10.refs_8_
  73.4 0.0 collective-permute-done.11.refs_9_
  73.4 0.0 collective-permute-done.9.refs_5_.refs_7_
  73.4 0.0 collective-permute-done.8.refs_4_.refs_6_
  73.4 1.7 %shard_map.144 = f32[1024,128]{1,0:T(8,128)} custom-call(s32[4]{0:T(128)S(1)} %pad_add_fusion.refs_0_, f32[64,2048]{1,0:T(8,128)S(1)} %get-tuple-element.42.refs_1_, bf16[64,128]{1,0:T(8,128)(2,1)S(1)} %collective-permute-done.7.refs_2_.refs_3_, bf16[64,128]{1,0:T(8,128)(2,1)S(1)} %collective-permute-done.7.refs_2_.refs_3_, ...), custom_call_target="tpu_custom_call" | custom-call | bytes 1048576 | tf_op jit(solution)/shard_map/pallas_call | solution.py:24
  75.1 0.0 all-to-all-done.1
  75.1 0.9 %shard_map.145 = (f32[720,256]{1,0:T(8,128)}, f32[1,256]{1,0:T(1,128)}) custom-call(bf16[768,256]{1,0:T(8,128)(2,1)S(1)} %bitcast.11), custom_call_target="tpu_custom_call" | custom-call | bytes 1179648 | tf_op jit(solution)/shard_map/pallas_call | solution.py:24
  (2 shorter events, 0.1 us)
Async XLA Ops:
  0.6 17.6 %copy-start.8 = (s32[1,128]{1,0:T(1,128)S(1)}, s32[1,128]{1,0:T(1,128)}, u32[]{:S(2)}) copy-start(s32[1,128]{1,0:T(1,128)} %refs_2_.7) | copy-start | bytes 1540
  0.6 17.6 %copy-start.7 = (s32[1,128]{1,0:T(1,128)S(1)}, s32[1,128]{1,0:T(1,128)}, u32[]{:S(2)}) copy-start(s32[1,128]{1,0:T(1,128)} %refs_1_.7) | copy-start | bytes 1540
  0.7 1.0 %copy-start.2 = (bf16[64,16,128]{2,1,0:T(8,128)(2,1)S(1)}, bf16[64,16,128]{2,1,0:T(8,128)(2,1)}, u32[]{:S(2)}) copy-start(bf16[64,16,128]{2,1,0:T(8,128)(2,1)} %refs_2_.4) | copy-start | bytes 786436
  1.7 0.8 %copy-start.6 = (bf16[16,16,128]{2,1,0:T(8,128)(2,1)S(1)}, bf16[16,16,128]{2,1,0:T(8,128)(2,1)}, u32[]{:S(2)}) copy-start(bf16[16,16,128]{2,1,0:T(8,128)(2,1)} %refs_1_.4) | copy-start | bytes 196612
  3.5 14.4 %collective-permute-start.3 = (bf16[80,128]{1,0:T(8,128)(2,1)S(1)}, bf16[80,128]{1,0:T(8,128)(2,1)S(1)}, u32[]{:S(2)}, u32[]{:S(2)}) collective-permute-start(bf16[80,128]{1,0:T(8,128)(2,1)S(1)} %get-tuple-element.30), channel_id=1, source_target_pairs={{0,1},{1,2},{2,3},{3,4},{4,5},{5,6},{6,7},{7,8},{8,9},{9,10},{10,1... | collective-permute-start | bytes 61448 | tf_op jit(solution)/shard_map/ppermute | solution.py:418
  6.5 11.4 %collective-permute-start.4 = (bf16[80,128]{1,0:T(8,128)(2,1)S(1)}, bf16[80,128]{1,0:T(8,128)(2,1)S(1)}, u32[]{:S(2)}, u32[]{:S(2)}) collective-permute-start(bf16[80,128]{1,0:T(8,128)(2,1)S(1)} %get-tuple-element.31), channel_id=1, source_target_pairs={{0,15},{1,0},{2,1},{3,2},{4,3},{5,4},{6,5},{7,6},{8,7},{9,8},{10,9... | collective-permute-start | bytes 61448 | tf_op jit(solution)/shard_map/ppermute | solution.py:418
  10.5 7.4 %collective-permute-start.2 = (bf16[80,128]{1,0:T(8,128)(2,1)S(1)}, bf16[80,128]{1,0:T(8,128)(2,1)S(1)}, u32[]{:S(2)}, u32[]{:S(2)}) collective-permute-start(bf16[80,128]{1,0:T(8,128)(2,1)S(1)} %get-tuple-element.29), channel_id=1, source_target_pairs={{0,31},{1,16},{2,17},{3,18},{4,19},{5,20},{6,21},{7,22},{8,23},{9,... | collective-permute-start | bytes 61448 | tf_op jit(solution)/shard_map/ppermute | solution.py:418
  11.4 6.8 %collective-permute-start.1 = (bf16[80,128]{1,0:T(8,128)(2,1)S(1)}, bf16[80,128]{1,0:T(8,128)(2,1)S(1)}, u32[]{:S(2)}, u32[]{:S(2)}) collective-permute-start(bf16[80,128]{1,0:T(8,128)(2,1)S(1)} %get-tuple-element.29), channel_id=1, source_target_pairs={{0,17},{1,18},{2,19},{3,20},{4,21},{5,22},{6,23},{7,24},{8,25},{9,... | collective-permute-start | bytes 61448 | tf_op jit(solution)/shard_map/ppermute | solution.py:418
  12.3 5.9 %collective-permute-start = (bf16[80,128]{1,0:T(8,128)(2,1)S(1)}, bf16[80,128]{1,0:T(8,128)(2,1)S(1)}, u32[]{:S(2)}, u32[]{:S(2)}) collective-permute-start(bf16[80,128]{1,0:T(8,128)(2,1)S(1)} %get-tuple-element.29), channel_id=1, source_target_pairs={{0,16},{1,17},{2,18},{3,19},{4,20},{5,21},{6,22},{7,23},{8,24},{9,... | collective-permute-start | bytes 61448 | tf_op jit(solution)/shard_map/ppermute | solution.py:418
  12.6 1.0 %copy-start = (bf16[256,720]{0,1:T(8,128)(2,1)S(1)}, bf16[256,720]{0,1:T(8,128)(2,1)}, u32[]{:S(2)}) copy-start(bf16[256,720]{0,1:T(8,128)(2,1)} %param.16) | copy-start | bytes 1105924
  13.6 0.9 %copy-start.3 = (bf16[64,16,128]{2,1,0:T(8,128)(2,1)S(1)}, bf16[64,16,128]{2,1,0:T(8,128)(2,1)}, u32[]{:S(2)}) copy-start(bf16[64,16,128]{2,1,0:T(8,128)(2,1)} %refs_0_.1) | copy-start | bytes 786436
  14.6 0.9 %copy-start.4 = (bf16[64,16,128]{2,1,0:T(8,128)(2,1)S(1)}, bf16[64,16,128]{2,1,0:T(8,128)(2,1)}, u32[]{:S(2)}) copy-start(bf16[64,16,128]{2,1,0:T(8,128)(2,1)} %refs_1_.5) | copy-start | bytes 786436
  15.5 0.9 %copy-start.5 = (bf16[64,16,128]{2,1,0:T(8,128)(2,1)S(1)}, bf16[64,16,128]{2,1,0:T(8,128)(2,1)}, u32[]{:S(2)}) copy-start(bf16[64,16,128]{2,1,0:T(8,128)(2,1)} %refs_2_.5) | copy-start | bytes 786436
  16.5 0.7 copy-start.9
  21.9 2.6 %collective-permute-start.5 = (f32[768,128]{1,0:T(8,128)S(1)}, f32[768,128]{1,0:T(8,128)S(1)}, u32[]{:S(2)}, u32[]{:S(2)}) collective-permute-start(f32[768,128]{1,0:T(8,128)S(1)} %get-tuple-element.40), channel_id=1, source_target_pairs={{0,16},{16,0},{1,17},{17,1},{2,18},{18,2},{3,19},{19,3},{4,20},{20... | collective-permute-start | bytes 1179656 | tf_op jit(solution)/shard_map/ppermute | solution.py:511
  51.2 6.5 %copy-start.1 = (bf16[256,720]{0,1:T(8,128)(2,1)S(1)}, bf16[256,720]{0,1:T(8,128)(2,1)}, u32[]{:S(2)}) copy-start(bf16[256,720]{0,1:T(8,128)(2,1)} %param.16) | copy-start | bytes 1105924
  51.3 1.3 %collective-permute-start.6 = (f32[48,128]{1,0:T(8,128)S(1)}, f32[48,128]{1,0:T(8,128)S(1)}, u32[]{:S(2)}, u32[]{:S(2)}) collective-permute-start(f32[48,128]{1,0:T(8,128)S(1)} %shard_map.140.refs_1_), channel_id=1, source_target_pairs={{0,16},{16,0},{1,17},{17,1},{2,18},{18,2},{3,19},{19,3},{4,20},{20... | collective-permute-start | bytes 73736 | tf_op jit(solution)/shard_map/ppermute | solution.py:533
  53.9 21.3 %all-to-all-start.1 = ((bf16[16,48,256]{2,1,0:T(8,128)(2,1)}), bf16[16,48,256]{2,1,0:T(8,128)(2,1)S(1)}, u32[]{:S(2)}, u32[]{:S(2)}) async-start(bf16[16,48,256]{2,1,0:T(8,128)(2,1)} %shard_map.141.refs_2_.refs_3_), calls=%async_computation.1 | async-start | bytes 786432 | tf_op jit(solution)/shard_map/all_to_all | solution.py:576
  60.4 13.0 %collective-permute-start.9 = (bf16[64,128]{1,0:T(8,128)(2,1)S(1)}, bf16[64,128]{1,0:T(8,128)(2,1)S(1)}, u32[]{:S(2)}, u32[]{:S(2)}) collective-permute-start(bf16[64,128]{1,0:T(8,128)(2,1)S(1)} %get-tuple-element.44), channel_id=1, source_target_pairs={{0,31},{1,16},{2,17},{3,18},{4,19},{5,20},{6,21},{7,22},{8,23},{9,... | collective-permute-start | bytes 49160 | tf_op jit(solution)/shard_map/ppermute | solution.py:418
  65.5 8.0 %collective-permute-start.8 = (bf16[64,128]{1,0:T(8,128)(2,1)S(1)}, bf16[64,128]{1,0:T(8,128)(2,1)S(1)}, u32[]{:S(2)}, u32[]{:S(2)}) collective-permute-start(bf16[64,128]{1,0:T(8,128)(2,1)S(1)} %get-tuple-element.44), channel_id=1, source_target_pairs={{0,17},{1,18},{2,19},{3,20},{4,21},{5,22},{6,23},{7,24},{8,25},{9,... | collective-permute-start | bytes 49160 | tf_op jit(solution)/shard_map/ppermute | solution.py:418
  65.5 7.6 %collective-permute-start.7 = (bf16[64,128]{1,0:T(8,128)(2,1)S(1)}, bf16[64,128]{1,0:T(8,128)(2,1)S(1)}, u32[]{:S(2)}, u32[]{:S(2)}) collective-permute-start(bf16[64,128]{1,0:T(8,128)(2,1)S(1)} %get-tuple-element.43), channel_id=1, source_target_pairs={{0,16},{1,17},{2,18},{3,19},{4,20},{5,21},{6,22},{7,23},{8,24},{9,... | collective-permute-start | bytes 49160 | tf_op jit(solution)/shard_map/ppermute | solution.py:418
  66.1 7.3 %collective-permute-start.10 = (bf16[64,128]{1,0:T(8,128)(2,1)S(1)}, bf16[64,128]{1,0:T(8,128)(2,1)S(1)}, u32[]{:S(2)}, u32[]{:S(2)}) collective-permute-start(bf16[64,128]{1,0:T(8,128)(2,1)S(1)} %get-tuple-element.45), channel_id=1, source_target_pairs={{0,1},{1,2},{2,3},{3,4},{4,5},{5,6},{6,7},{7,8},{8,9},{9,10},{10,1... | collective-permute-start | bytes 49160 | tf_op jit(solution)/shard_map/ppermute | solution.py:418
  66.1 7.3 %collective-permute-start.11 = (bf16[64,128]{1,0:T(8,128)(2,1)S(1)}, bf16[64,128]{1,0:T(8,128)(2,1)S(1)}, u32[]{:S(2)}, u32[]{:S(2)}) collective-permute-start(bf16[64,128]{1,0:T(8,128)(2,1)S(1)} %get-tuple-element.46), channel_id=1, source_target_pairs={{0,15},{1,0},{2,1},{3,2},{4,3},{5,4},{6,5},{7,6},{8,7},{9,8},{10,9... | collective-permute-start | bytes 49160 | tf_op jit(solution)/shard_map/ppermute | solution.py:418

commit v3 on v2

--- a/solution.py
+++ b/solution.py
@@ -15,20 +15,43 @@
 VMEM = pl.BlockSpec(memory_space=pltpu.VMEM)
 
 
-def call(kernel, outs, operands, scalars=0, scratch=(), flops=0, moved=0, after=()):
+def call(kernel, outs, operands, scalars=0, scratch=(), flops=0, moved=0, after=(), fetched=0):
     count = len(operands)
+    kept = count - fetched
+    total = count + len(after)
 
     def run(*refs):
-        kernel(*refs[:count], *refs[count + len(after) :])
+        if not fetched:
+            kernel(*refs[:count], *refs[total:])
+            return
+        *rest, semaphores = refs[total:]
+        buffers = rest[len(rest) - fetched :]
+        copies = [
+            pltpu.make_async_copy(source, target, semaphores.at[index])
+            for index, (source, target) in enumerate(zip(refs[kept:count], buffers))
+        ]
+        for copy in copies:
+            copy.start()
+        waits = [copy.wait for copy in copies]
+        kernel(waits, *refs[:kept], *buffers, *rest[: len(rest) - fetched])
+
+    scratch = list(scratch)
+    operands = list(operands)
+    for index in range(kept, count):
+        operands[index] = pltpu.with_memory_space_constraint(operands[index], pltpu.HBM)
+    if fetched:
+        scratch += [pltpu.VMEM(leaf.shape, leaf.dtype) for leaf in operands[kept:]]
+        scratch.append(pltpu.SemaphoreType.DMA((fetched,)))
 
     return pl.pallas_call(
         run,
         out_shape=outs,
         in_specs=[SMEM] * scalars
-        + [VMEM] * (count - scalars)
-        + [pl.BlockSpec(memory_space=pl.ANY)] * len(after),
+        + [VMEM] * (kept - scalars)
+        + [pl.BlockSpec(memory_space=pltpu.HBM)] * fetched
+        + [VMEM] * len(after),
         out_specs=jax.tree.map(lambda _: VMEM, outs),
-        scratch_shapes=list(scratch),
+        scratch_shapes=scratch,
         compiler_params=pltpu.CompilerParams(vmem_limit_bytes=LIMIT),
         cost_estimate=pl.CostEstimate(flops=flops, bytes_accessed=moved, transcendentals=0),
     )(*operands, *after)
@@ -42,10 +65,12 @@
     return 0.5 * jnp.tanh(0.5 * values) + 0.5
 
 
-def edges_kernel(place_ref, forcing_ref, hidden_ref, flat_ref, *rest):
+def edges_kernel(waits, place_ref, forcing_ref, hidden_ref, flat_ref, *rest):
     row_refs, (left_ref, right_ref, wide_ref) = rest[:-3], rest[-3:]
     inp, rows, width = forcing_ref.shape
     channels = inp + hidden_ref.shape[0]
+    for wait in waits:
+        wait()
     wide_ref[: inp * rows] = forcing_ref[...].astype(F32).reshape(inp * rows, width)
     wide_ref[inp * rows :] = hidden_ref[...].astype(F32).reshape((channels - inp) * rows, width)
     lane = lane_index((channels, width))
@@ -69,25 +94,41 @@
 
 
 def flatten_kernel(
-    cell_ref, hcot_ref, ccot_ref, wt_ref, b_ref, cell_out, hcot_out, ccot_out, w_ref, bias_ref, wide_ref
+    waits,
+    b_ref,
+    wt_ref,
+    cell_ref,
+    hcot_ref,
+    ccot_ref,
+    cell_out,
+    hcot_out,
+    ccot_out,
+    w_ref,
+    bias_ref,
+    wide_ref,
 ):
     hid, rows, width = cell_ref.shape
     gates = wt_ref.shape[1]
     span = wt_ref.shape[0] // 3
     third = w_ref.shape[1] // 3
-    for source, target in ((cell_ref, cell_out), (hcot_ref, hcot_out), (ccot_ref, ccot_out)):
-        wide_ref[...] = source[...].astype(F32).reshape(hid * rows, width)
-        for row in range(rows):
-            target[:, row * width : (row + 1) * width] = wide_ref[
-                pl.ds(row, hid, stride=rows), :
-            ].astype(BF16)
+    waits[0]()
+    bias_ref[...] = jnp.broadcast_to(b_ref[...], (bias_ref.shape[1], gates)).T
+    waits[1]()
     blank = jnp.zeros((third - span, gates), F32)
     for index in range(3):
         block = wt_ref[index * span : (index + 1) * span].astype(F32)
         w_ref[:, index * third : (index + 1) * third] = (
             jnp.concatenate([block, blank], 0).T.astype(BF16)
         )
-    bias_ref[...] = jnp.broadcast_to(b_ref[...], (bias_ref.shape[1], gates)).T
+    for wait, source, target in zip(
+        waits[2:], (cell_ref, hcot_ref, ccot_ref), (cell_out, hcot_out, ccot_out)
+    ):
+        wait()
+        wide_ref[...] = source[...].astype(F32).reshape(hid * rows, width)
+        for row in range(rows):
+            target[:, row * width : (row + 1) * width] = wide_ref[
+                pl.ds(row, hid, stride=rows), :
+            ].astype(BF16)
 
 
 def step_kernel(
@@ -303,7 +344,9 @@
     left_ref,
     right_ref,
     out_ref,
+    token_ref,
 ):
+    token_ref[...] = jnp.zeros(token_ref.shape, F32)
     hid = grad_ref.shape[0]
     width = up_ref.shape[1]
     rows = grad_ref.shape[1] // width
@@ -335,7 +378,8 @@
 
 
 def pack_kernel(span, place_ref, wet_ref, owner_ref, tiles_ref, *refs):
-    out_ref = refs[-1]
+    out_ref, token_ref = refs[-2:]
+    token_ref[...] = jnp.zeros(token_ref.shape, F32)
     tile_cols, hid, cells = tiles_ref.shape
     lanes = out_ref.shape[2]
     pieces = cells // 128
@@ -354,7 +398,7 @@
                 ]
 
     total = refs[0][...]
-    for ref in refs[1:-1]:
+    for ref in refs[1:-2]:
         total = total + ref[...]
     total = jnp.concatenate([split_bias(total[:third], span), total[third:]], 0)
     share = total.shape[0] // slots
@@ -362,37 +406,36 @@
         out_ref[slot, state_rows:] = total[slot * share : (slot + 1) * share].astype(BF16)
 
 
-def sum_kernel(scaling, state_rows, parts_ref, out_ref):
+def sum_kernel(scaling, span, state_rows, place_ref, parts_ref, out_ref):
     total = parts_ref[0, state_rows:].astype(F32)
     for index in range(1, parts_ref.shape[0]):
         total = total + parts_ref[index, state_rows:].astype(F32)
-    out_ref[...] = total * scaling
-
-
-def share_kernel(span, place_ref, *refs):
-    *parts, out_ref = refs
-    lanes = parts[0].shape[1]
-    share = out_ref.shape[1]
+    total = total * scaling
+    share = total.shape[0]
     row = span % share
+    index = lax.broadcasted_iota(jnp.int32, total.shape, 0)
+    whole = jnp.where(index == row, total + pltpu.roll(total, share - 1, 0), total)
+    total = jnp.where(place_ref[1] == span // share, split_bias(whole, row), total)
+    for index in range(out_ref.shape[0]):
+        out_ref[index] = total.astype(BF16)
+
+
+def weights_kernel(span, place_ref, *refs):
+    *parts, weight_ref, bias_ref = refs
+    third = parts[0].shape[0] // 3
+    half = parts[0].shape[1]
     for side in range(len(parts)):
-        total = parts[0][...]
-        if len(parts) == 2:
-            total = jnp.where(place_ref[0] == side, total, parts[1][...])
-        index = lax.broadcasted_iota(jnp.int32, total.shape, 0)
-        whole = jnp.where(index == row, total + pltpu.roll(total, share - 1, 0), total)
-        total = jnp.where(place_ref[1] == span // share, split_bias(whole, row), total)
-        total = total.astype(BF16)
-        for slot in range(out_ref.shape[0]):
-            out_ref[slot, :, side * lanes : (side + 1) * lanes] = total
-
-
-def weights_kernel(span, parts_ref, weight_ref, bias_ref):
-    third = parts_ref.shape[0] // 3
-    for index in range(3):
-        low = index * third
-        weight_ref[index * span : (index + 1) * span] = parts_ref[low : low + span].astype(F32)
-    pair = parts_ref[span:third].astype(F32)
-    bias_ref[...] = pair[0:1] + pair[1:2]
+        if len(parts) == 1:
+            pick = parts[0][...]
+        else:
+            pick = jnp.where(place_ref[0] == side, parts[0][...], parts[1][...])
+        pick = pick.astype(F32)
+        lanes = slice(side * half, (side + 1) * half)
+        for index in range(3):
+            weight_ref[index * span : (index + 1) * span, lanes] = pick[
+                index * third : index * third + span
+            ]
+        bias_ref[:, lanes] = pick[span : span + 1] + pick[span + 1 : span + 2]
 
 
 def tiles_kernel(work_ref, arrived_ref, out_ref):
@@ -473,6 +516,7 @@
         scalars=1,
         scratch=[pltpu.VMEM((channels * rows, width), F32)],
         moved=4 * channels * cells,
+        fetched=2,
     )
     flat, ends, (left, right) = edges[0], edges[1:-2], edges[-2:]
     halo = exchange(ends, ends, left, right, lat_devices, lon_devices)
@@ -481,9 +525,10 @@
         flatten_kernel,
         (shaped(hid, cells),) * 3
         + (shaped(gates, 3 * third), shaped(gates, width, dtype=F32)),
-        (cell, grad_hidden, grad_cell, w_turned, b_gates.reshape(1, gates)),
+        (b_gates.reshape(1, gates), w_turned, cell, grad_hidden, grad_cell),
         scratch=[pltpu.VMEM((hid * rows, width), F32)],
         moved=12 * hid * cells,
+        fetched=5,
     )
     halves = 2 if lat_devices == 2 else 1
     lanes = gates // halves
@@ -513,30 +558,43 @@
         weight_parts = (lax.psum(weight_parts[0], "lat"),)
     state_rows = hid * TILE * TILE // lanes
     share = 3 * third // lon_devices
-    outgoing = call(
+    outgoing, packed = call(
         lambda *refs: pack_kernel(span, *refs),
-        shaped(lon_devices, state_rows + share, lanes),
+        (shaped(lon_devices, state_rows + share, lanes), shaped(8, 128, dtype=F32)),
         (place, wet_mask, tile_owner, tiles, *weight_parts),
         scalars=3,
         moved=4 * lon_devices * hid * TILE * TILE,
     )
     incoming = lax.all_to_all(outgoing, "lon", 0, 0, tiled=True)
+    grad_parts = call(
+        spread_kernel,
+        (shaped(hid, cells, dtype=F32),) + (shaped(hid, width),) * (2 * end_count + 2),
+        (place, delta, w_turned),
+        scalars=1,
+        scratch=[pltpu.VMEM((3, hid, (rows + 2) * width), F32)],
+        flops=2 * gates * 9 * hid * cells,
+        moved=8 * gates * cells,
+        after=(packed,),
+    )
+    grad_flat, grad_ends, grad_sides = grad_parts[0], grad_parts[1:-2], grad_parts[-2:]
+    grad_halo = exchange(
+        grad_ends[0::2], grad_ends[1::2], *grad_sides, lat_devices, lon_devices
+    )
+    hidden_grad, folded = call(
+        fold_kernel,
+        (shaped(hid * rows, width, dtype=F32), shaped(8, 128, dtype=F32)),
+        (place, grad_flat, *grad_halo),
+        scalars=1,
+        moved=8 * hid * cells,
+    )
     scaling = 1.0 / math.sqrt(float(lat_devices * lon_devices * capacity * TILE * TILE))
-    summed = call(
-        lambda *refs: sum_kernel(scaling, state_rows, *refs),
-        shaped(share, lanes, dtype=F32),
-        (incoming,),
-        moved=2 * gates * 3 * third,
-    )
-    around = (summed,)
-    if halves == 2:
-        around += (lax.ppermute(summed, "lat", swap),)
     shares = call(
-        lambda *refs: share_kernel(span, *refs),
-        shaped(lon_devices, share, gates),
-        (place, *around),
+        lambda *refs: sum_kernel(scaling, span, state_rows, *refs),
+        shaped(lon_devices, share, lanes),
+        (place, incoming),
         scalars=1,
         moved=2 * gates * 3 * third,
+        after=(folded,),
     )
     owned = (wet_mask > 0) & (tile_owner == lon_index)
     arrived = jnp.any(owned.reshape(lon_devices, tile_cols), 1)
@@ -550,34 +608,16 @@
         (work, incoming),
         scalars=1,
         moved=2 * lon_devices * hid * TILE * TILE,
-        after=(shares,),
-    )
-    grad_parts = call(
-        spread_kernel,
-        (shaped(hid, cells, dtype=F32),) + (shaped(hid, width),) * (2 * end_count + 2),
-        (place, delta, w_turned),
-        scalars=1,
-        scratch=[pltpu.VMEM((3, hid, (rows + 2) * width), F32)],
-        flops=2 * gates * 9 * hid * cells,
-        moved=8 * gates * cells,
-        after=(shares,),
-    )
-    grad_flat, grad_ends, grad_sides = grad_parts[0], grad_parts[1:-2], grad_parts[-2:]
-    grad_halo = exchange(
-        grad_ends[0::2], grad_ends[1::2], *grad_sides, lat_devices, lon_devices
-    )
-    hidden_grad = call(
-        fold_kernel,
-        shaped(hid * rows, width, dtype=F32),
-        (place, grad_flat, *grad_halo),
-        scalars=1,
-        moved=8 * hid * cells,
-    )
-    gathered = lax.all_to_all(shares, "lon", 0, 0, tiled=True)
+    )
+    gathered = lax.all_to_all(shares, "lon", 0, 0, tiled=True).reshape(3 * third, lanes)
+    gathered = (gathered,)
+    if halves == 2:
+        gathered += (lax.ppermute(gathered[0], "lat", swap),)
     weight_grad, bias_grad = call(
         lambda *refs: weights_kernel(span, *refs),
         (shaped(3 * span, gates, dtype=F32), shaped(1, gates, dtype=F32)),
-        (gathered.reshape(3 * third, gates),),
+        (place, *gathered),
+        scalars=1,
         moved=6 * gates * 3 * third,
     )
     return (

time: 76.5 us -> 67.9 us (0.89)
  blocking collectives: 26 us -> 0 us
  waiting for transfers between devices: 3.15 us -> 22.3 us
  local copies, waits for them, and re-layouts: 6.41 us -> 0.1 us
  Pallas kernels: 14 us -> 17.4 us
  starting transfers between devices: 25.3 us -> 26.4 us
    all_to_all x1 -> x0, blocking collectives: 26 us -> none  [body(): incoming = lax.all_to_all(outgoing, 'lon', 0, 0, tiled=True)]
    ppermute x10, waiting for transfers between devices: 0.62 us -> 12.2 us  [moved(): return lax.ppermute(values, ('lat', 'lon'), pairs)]
    all_to_all x1 -> x2, waiting for transfers between devices: 0.01 us -> 8.67 us  [the longest x1 8.67 us: body(): lax.all_to_all(shares, 'lon', 0, 0, tiled=True).reshape(3 * third, lanes)]
    unnamed x20 -> x6, local copies, waits for them, and re-layouts: 6.32 us -> 0.01 us
    all_to_all x1 -> x2, starting transfers between devices: 3.55 us -> 8.28 us  [the longest x1 4.67 us: body(): lax.all_to_all(shares, 'lon', 0, 0, tiled=True).reshape(3 * third, lanes)]
    ppermute x10, starting transfers between devices: 20.4 us -> 16.9 us  [moved(): return lax.ppermute(values, ('lat', 'lon'), pairs)]
    pallas_call x10 -> x9, Pallas kernels: 14 us -> 17.4 us  [call(): pl.pallas_call(run, out_shape=outs, in_specs=[SMEM] * scalars + [VMEM] *...]
    ppermute x1, waiting for transfers between devices: 1.18 us -> 0.01 us  [body(): gathered += (lax.ppermute(gathered[0], 'lat', swap),)]
  transfers between devices with their start and end apart: 13 -> 14, of which waited for: 4 -> 4; matrix products, arithmetic and copies ran while one was open for 1% -> 1% of each run, Pallas kernels for 8% -> 11%
where the time goes in v3:
time: 67.9 us; the launch traced here: 67.4 us
  starting transfers between devices  26.4 us (39%)
  waiting for transfers between devices  22.3 us (33%)
  Pallas kernels  17.4 us (26%)
  between operations  0.76 us (1%)
    pallas_call x9, Pallas kernels, call(): pl.pallas_call(run, out_shape=outs, in_specs=[SMEM] * scalars + [VMEM] *...  17.4 us
    ppermute x10, starting transfers between devices, moved(): return lax.ppermute(values, ('lat', 'lon'), pairs)  16.9 us
    ppermute x10, waiting for transfers between devices, moved(): return lax.ppermute(values, ('lat', 'lon'), pairs)  12.2 us
    all_to_all x1, waiting for transfers between devices, body(): lax.all_to_all(shares, 'lon', 0, 0, tiled=True).reshape(3 * third, lanes)  8.67 us
    all_to_all x1, starting transfers between devices, body(): lax.all_to_all(shares, 'lon', 0, 0, tiled=True).reshape(3 * third, lanes)  4.67 us
    all_to_all x1, starting transfers between devices, body(): incoming = lax.all_to_all(outgoing, 'lon', 0, 0, tiled=True)  3.6 us
  transfers between devices with their start and end apart: 14, of which 4 were waited for; matrix products, arithmetic and copies ran while one was open for 1% of the time, Pallas kernels for 11%

profile of v3, /device:TPU:0, one launch (start us, length us, event | category | flops | bytes accessed | tf_op | source)
XLA Modules:
  0.0 67.4 jit_solution(13009475788290354795)
XLA Ops:
  0.6 0.0 copy-start.2
  0.6 0.0 copy-start.1
  0.7 0.1 pad_add_fusion.refs_0_
  0.7 1.9 %shard_map.136 = (bf16[80,2048]{1,0:T(8,128)(2,1)S(1)}, bf16[80,128]{1,0:T(8,128)(2,1)S(1)}, bf16[80,128]{1,0:T(8,128)(2,1)S(1)}, bf16[80,128]{1,0:T(8,128)(2,1)S(1)}) custom-call(s32[4]{0:T(128)S(1)} %pad_add_fusion.refs_0_, bf16[16,16,128]{2,1,0:T(8,128)(2,1)} %refs_1_.3, bf16[64,16,128]{2,1,0:T(8,128)(2,1)} %refs_2_.4), custom_call_target="tpu_custom_call" | custom-call | bytes 655360 | tf_op jit(solution)/shard_map/pallas_call | solution.py:46
  2.7 3.0 %collective-permute-start.3 = (bf16[80,128]{1,0:T(8,128)(2,1)S(1)}, bf16[80,128]{1,0:T(8,128)(2,1)S(1)}, u32[]{:S(2)}, u32[]{:S(2)}) collective-permute-start(bf16[80,128]{1,0:T(8,128)(2,1)S(1)} %get-tuple-element.34), channel_id=1, source_target_pairs={{0,1},{1,2},{2,3},{3,4},{4,5},{5,6},{6,7},{7,8},{8,9},{9,10},{10,1... | collective-permute-start | bytes 61448 | tf_op jit(solution)/shard_map/ppermute | solution.py:461
  5.7 4.1 %collective-permute-start.4 = (bf16[80,128]{1,0:T(8,128)(2,1)S(1)}, bf16[80,128]{1,0:T(8,128)(2,1)S(1)}, u32[]{:S(2)}, u32[]{:S(2)}) collective-permute-start(bf16[80,128]{1,0:T(8,128)(2,1)S(1)} %get-tuple-element.35), channel_id=1, source_target_pairs={{0,15},{1,0},{2,1},{3,2},{4,3},{5,4},{6,5},{7,6},{8,7},{9,8},{10,9... | collective-permute-start | bytes 61448 | tf_op jit(solution)/shard_map/ppermute | solution.py:461
  9.7 0.8 %collective-permute-start.2 = (bf16[80,128]{1,0:T(8,128)(2,1)S(1)}, bf16[80,128]{1,0:T(8,128)(2,1)S(1)}, u32[]{:S(2)}, u32[]{:S(2)}) collective-permute-start(bf16[80,128]{1,0:T(8,128)(2,1)S(1)} %get-tuple-element.33), channel_id=1, source_target_pairs={{0,31},{1,16},{2,17},{3,18},{4,19},{5,20},{6,21},{7,22},{8,23},{9,... | collective-permute-start | bytes 61448 | tf_op jit(solution)/shard_map/ppermute | solution.py:461
  10.6 0.9 %collective-permute-start.1 = (bf16[80,128]{1,0:T(8,128)(2,1)S(1)}, bf16[80,128]{1,0:T(8,128)(2,1)S(1)}, u32[]{:S(2)}, u32[]{:S(2)}) collective-permute-start(bf16[80,128]{1,0:T(8,128)(2,1)S(1)} %get-tuple-element.33), channel_id=1, source_target_pairs={{0,17},{1,18},{2,19},{3,20},{4,21},{5,22},{6,23},{7,24},{8,25},{9,... | collective-permute-start | bytes 61448 | tf_op jit(solution)/shard_map/ppermute | solution.py:461
  11.5 0.3 collective-permute-start
  11.8 1.8 %shard_map.137 = (bf16[64,2048]{1,0:T(8,128)(2,1)S(1)}, bf16[64,2048]{1,0:T(8,128)(2,1)S(1)}, bf16[64,2048]{1,0:T(8,128)(2,1)S(1)}, bf16[256,768]{1,0:T(8,128)(2,1)S(1)}, f32[256,128]{1,0:T(8,128)S(1)}) custom-call(f32[1,256]{1,0:T(1,128)} %bitcast.15, bf16[720,256]{1,0:T(8,128)(2,1)} %bitcast.13, bf16[64,16,128]{2,1,0:T(8,128)(2,1)} %refs_2_.5, ...), custom_call_target="tpu_custom_call" | custom-call | bytes 1572864 | tf_op jit(solution)/shard_map/pallas_call | solution.py:46
  13.7 0.0 collective-permute-done.3.refs_10_
  13.7 0.0 collective-permute-done.4.refs_11_
  13.7 0.0 collective-permute-done.2.refs_7_.refs_9_
  13.7 3.7 %collective-permute-done.1.refs_6_.refs_8_ = bf16[80,128]{1,0:T(8,128)(2,1)S(1)} collective-permute-done((bf16[80,128]{1,0:T(8,128)(2,1)S(1)}, bf16[80,128]{1,0:T(8,128)(2,1)S(1)}, u32[]{:S(2)}, u32[]{:S(2)}) %collective-permute-start.1) | collective-permute-done | bytes 20512 | tf_op jit(solution)/shard_map/ppermute | solution.py:461
  17.4 0.0 collective-permute-done.refs_4_.refs_5_
  17.4 0.0 copy-done.2
  17.4 0.0 copy-done.1
  17.4 3.7 %shard_map.138 = (bf16[64,16,128]{2,1,0:T(8,128)(2,1)}, f32[1024,128]{1,0:T(8,128)}, bf16[8,64,256]{2,1,0:T(8,128)(2,1)S(1)}, f32[768,128]{1,0:T(8,128)S(1)}, f3...) custom-call(s32[4]{0:T(128)S(1)} %pad_add_fusion.refs_0_, s32[1,128]{1,0:T(1,128)S(1)} %copy-done.1, ...), custom_call_target="tpu_custom_call" | custom-call | flops 1509949440 | bytes 2097152 | tf_op jit(solution)/shard_map/pallas_call | solution.py:46
  21.1 0.0 copy-start
  21.1 1.2 %collective-permute-start.5 = (f32[768,128]{1,0:T(8,128)S(1)}, f32[768,128]{1,0:T(8,128)S(1)}, u32[]{:S(2)}, u32[]{:S(2)}) collective-permute-start(f32[768,128]{1,0:T(8,128)S(1)} %get-tuple-element.44), channel_id=1, source_target_pairs={{0,16},{16,0},{1,17},{17,1},{2,18},{18,2},{3,19},{19,3},{4,20},{20... | collective-permute-start | bytes 1179656 | tf_op jit(solution)/shard_map/ppermute | solution.py:556
  22.3 1.3 %collective-permute-done.5.refs_5_ = f32[768,128]{1,0:T(8,128)S(1)} collective-permute-done((f32[768,128]{1,0:T(8,128)S(1)}, f32[768,128]{1,0:T(8,128)S(1)}, u32[]{:S(2)}, u32[]{:S(2)}) %collective-permute-start.5) | collective-permute-done | bytes 393248 | tf_op jit(solution)/shard_map/ppermute | solution.py:556
  23.6 1.6 %shard_map.139 = (bf16[16,176,128]{2,1,0:T(8,128)(2,1)}, f32[8,128]{1,0:T(8,128)S(1)}) custom-call(s32[4]{0:T(128)S(1)} %pad_add_fusion.refs_0_, s32[1,128]{1,0:T(1,128)S(1)} %copy-done.1, s32[1,128]{1,0:T(1,128)S(1)} %copy-done.2, bf16[8,64,256]{2,1,0:T(8,128)(2,1)S(1)} %get-tuple-element.42.refs_3_, f32[768,128]{1,0:T(8,128)S(1)} %get-tuple-element.43.refs_4_, ...), custom_call_target="tpu_custom_call" | custom-call | bytes 1048576 | tf_op jit(solution)/shard_map/pallas_call | solution.py:46
  25.3 3.6 %all-to-all-start = ((bf16[16,176,128]{2,1,0:T(8,128)(2,1)}), bf16[16,176,128]{2,1,0:T(8,128)(2,1)S(1)}, u32[]{:S(2)}, u32[]{:S(2)}) async-start(bf16[16,176,128]{2,1,0:T(8,128)(2,1)} %get-tuple-element.45), calls=%async_computation | async-start | bytes 1441792 | tf_op jit(solution)/shard_map/all_to_all | solution.py:568
  28.9 0.0 copy-done
  28.9 2.6 %shard_map.141 = (f32[64,2048]{1,0:T(8,128)S(1)}, bf16[64,128]{1,0:T(8,128)(2,1)S(1)}, bf16[64,128]{1,0:T(8,128)(2,1)S(1)}, bf16[64,128]{1,0:T(8,128)(2,1)S(1)}, bf16[64,128]{1,0:T(8,128)(2,1)S(1)}) custom-call(s32[4]{0:T(128)S(1)} %pad_add_fusion.refs_0_, bf16[256,2560]{1,0:T(8,128)(2,1)S(1)} %get-tuple-element.46.refs_1_, bf16[720,256]{1,0:T(8,128)(2,1)S(1)} %bitcast.14, ...), custom_call_target="tpu_custom_call" | custom-call | flops 603979776 | bytes 4194304 | tf_op jit(solution)/shard_map/pallas_call | solution.py:46
  31.5 0.4 collective-permute-start.6
  32.0 1.5 %collective-permute-start.9 = (bf16[64,128]{1,0:T(8,128)(2,1)S(1)}, bf16[64,128]{1,0:T(8,128)(2,1)S(1)}, u32[]{:S(2)}, u32[]{:S(2)}) collective-permute-start(bf16[64,128]{1,0:T(8,128)(2,1)S(1)} %get-tuple-element.51), channel_id=1, source_target_pairs={{0,1},{1,2},{2,3},{3,4},{4,5},{5,6},{6,7},{7,8},{8,9},{9,10},{10,1... | collective-permute-start | bytes 49160 | tf_op jit(solution)/shard_map/ppermute | solution.py:461
  33.5 4.1 %collective-permute-start.10 = (bf16[64,128]{1,0:T(8,128)(2,1)S(1)}, bf16[64,128]{1,0:T(8,128)(2,1)S(1)}, u32[]{:S(2)}, u32[]{:S(2)}) collective-permute-start(bf16[64,128]{1,0:T(8,128)(2,1)S(1)} %get-tuple-element.52), channel_id=1, source_target_pairs={{0,15},{1,0},{2,1},{3,2},{4,3},{5,4},{6,5},{7,6},{8,7},{9,8},{10,9... | collective-permute-start | bytes 49160 | tf_op jit(solution)/shard_map/ppermute | solution.py:461
  37.6 1.1 %collective-permute-start.8 = (bf16[64,128]{1,0:T(8,128)(2,1)S(1)}, bf16[64,128]{1,0:T(8,128)(2,1)S(1)}, u32[]{:S(2)}, u32[]{:S(2)}) collective-permute-start(bf16[64,128]{1,0:T(8,128)(2,1)S(1)} %get-tuple-element.50), channel_id=1, source_target_pairs={{0,31},{1,16},{2,17},{3,18},{4,19},{5,20},{6,21},{7,22},{8,23},{9,... | collective-permute-start | bytes 49160 | tf_op jit(solution)/shard_map/ppermute | solution.py:461
  38.7 0.6 collective-permute-start.7
  39.3 0.0 collective-permute-done.6.refs_2_.refs_3_
  39.3 8.5 %collective-permute-done.9.refs_8_ = bf16[64,128]{1,0:T(8,128)(2,1)S(1)} collective-permute-done((bf16[64,128]{1,0:T(8,128)(2,1)S(1)}, bf16[64,128]{1,0:T(8,128)(2,1)S(1)}, u32[]{:S(2)}, u32[]{:S(2)}) %collective-permute-start.9) | collective-permute-done | bytes 16416 | tf_op jit(solution)/shard_map/ppermute | solution.py:461
  47.9 0.0 collective-permute-done.10.refs_9_
  47.9 0.0 collective-permute-done.8.refs_5_.refs_7_
  47.9 0.0 collective-permute-done.7.refs_4_.refs_6_
  47.9 1.7 %shard_map.142 = (f32[1024,128]{1,0:T(8,128)}, f32[8,128]{1,0:T(8,128)S(1)}) custom-call(s32[4]{0:T(128)S(1)} %pad_add_fusion.refs_0_, f32[64,2048]{1,0:T(8,128)S(1)} %get-tuple-element.48.refs_1_, bf16[64,128]{1,0:T(8,128)(2,1)S(1)} %collective-permute-done.6.refs_2_.refs_3_, bf16[64,128]{1,0:T(8,128)(2,1)S(1)} %collective-permute-done.6.refs_2_.refs_3_, ...), custom_call_target="tpu_custom_call" | custom-call | bytes 1048576 | tf_op jit(solution)/shard_map/pallas_call | solution.py:46
  49.6 0.0 all-to-all-done.refs_1_
  49.6 1.3 %shard_map.143 = bf16[16,48,128]{2,1,0:T(8,128)(2,1)} custom-call(s32[4]{0:T(128)S(1)} %pad_add_fusion.refs_0_, bf16[16,176,128]{2,1,0:T(8,128)(2,1)S(1)} %all-to-all-done.refs_1_, f32[8,128]{1,0:T(8,128)S(1)} %get-tuple-element.55.refs_2_), custom_call_target="tpu_custom_call" | custom-call | bytes 393216 | tf_op jit(solution)/shard_map/pallas_call | solution.py:46
  50.9 4.7 %all-to-all-start.1 = ((bf16[16,48,128]{2,1,0:T(8,128)(2,1)}), bf16[16,48,128]{2,1,0:T(8,128)(2,1)S(1)}, u32[]{:S(2)}, u32[]{:S(2)}) async-start(bf16[16,48,128]{2,1,0:T(8,128)(2,1)} %shard_map.143), calls=%async_computation.1 | async-start | bytes 393216 | tf_op jit(solution)/shard_map/all_to_all | solution.py:612
  55.6 0.1 reshape.34
  55.7 0.1 reduce_or.9
  55.8 8.7 %all-to-all-done.1 = bf16[16,48,128]{2,1,0:T(8,128)(2,1)S(1)} async-done(((bf16[16,48,128]{2,1,0:T(8,128)(2,1)}), bf16[16,48,128]{2,1,0:T(8,128)(2,1)S(1)}, u32[]{:S(2)}, u32[]{:S(2)}) %all-to-all-start.1) | async-done | bytes 196640 | tf_op jit(solution)/shard_map/all_to_all | solution.py:612
  64.4 0.0 collective-permute-start.11
  64.4 0.1 convert_reduce_fusion
  64.5 0.1 select_reduce_fusion.refs_0_
  64.7 1.3 %shard_map.140 = f32[4,64,256]{2,1,0:T(8,128)} custom-call(s32[4]{0:T(128)S(1)} %select_reduce_fusion.refs_0_, bf16[16,176,128]{2,1,0:T(8,128)(2,1)S(1)} %all-to-all-done.refs_1_), custom_call_target="tpu_custom_call" | custom-call | bytes 524288 | tf_op jit(solution)/shard_map/pallas_call | solution.py:46
  65.9 0.0 collective-permute-done.11.refs_2_
  65.9 1.5 %shard_map.144 = (f32[720,256]{1,0:T(8,128)}, f32[1,256]{1,0:T(1,128)}) custom-call(s32[4]{0:T(128)S(1)} %pad_add_fusion.refs_0_, bf16[768,128]{1,0:T(8,128)(2,1)S(1)} %bitcast.12, bf16[768,128]{1,0:T(8,128)(2,1)S(1)} %collective-permute-done.11.refs_2_), custom_call_target="tpu_custom_call" | custom-call | bytes 1179648 | tf_op jit(solution)/shard_map/pallas_call | solution.py:46
  (1 shorter events, 0.0 us)
Async XLA Ops:
  0.6 16.8 %copy-start.2 = (s32[1,128]{1,0:T(1,128)S(1)}, s32[1,128]{1,0:T(1,128)}, u32[]{:S(2)}) copy-start(s32[1,128]{1,0:T(1,128)} %refs_2_.7) | copy-start | bytes 1540
  0.6 16.7 %copy-start.1 = (s32[1,128]{1,0:T(1,128)S(1)}, s32[1,128]{1,0:T(1,128)}, u32[]{:S(2)}) copy-start(s32[1,128]{1,0:T(1,128)} %refs_1_.5) | copy-start | bytes 1540
  2.7 11.0 %collective-permute-start.3 = (bf16[80,128]{1,0:T(8,128)(2,1)S(1)}, bf16[80,128]{1,0:T(8,128)(2,1)S(1)}, u32[]{:S(2)}, u32[]{:S(2)}) collective-permute-start(bf16[80,128]{1,0:T(8,128)(2,1)S(1)} %get-tuple-element.34), channel_id=1, source_target_pairs={{0,1},{1,2},{2,3},{3,4},{4,5},{5,6},{6,7},{7,8},{8,9},{9,10},{10,1... | collective-permute-start | bytes 61448 | tf_op jit(solution)/shard_map/ppermute | solution.py:461
  5.7 8.0 %collective-permute-start.4 = (bf16[80,128]{1,0:T(8,128)(2,1)S(1)}, bf16[80,128]{1,0:T(8,128)(2,1)S(1)}, u32[]{:S(2)}, u32[]{:S(2)}) collective-permute-start(bf16[80,128]{1,0:T(8,128)(2,1)S(1)} %get-tuple-element.35), channel_id=1, source_target_pairs={{0,15},{1,0},{2,1},{3,2},{4,3},{5,4},{6,5},{7,6},{8,7},{9,8},{10,9... | collective-permute-start | bytes 61448 | tf_op jit(solution)/shard_map/ppermute | solution.py:461
  9.7 4.0 %collective-permute-start.2 = (bf16[80,128]{1,0:T(8,128)(2,1)S(1)}, bf16[80,128]{1,0:T(8,128)(2,1)S(1)}, u32[]{:S(2)}, u32[]{:S(2)}) collective-permute-start(bf16[80,128]{1,0:T(8,128)(2,1)S(1)} %get-tuple-element.33), channel_id=1, source_target_pairs={{0,31},{1,16},{2,17},{3,18},{4,19},{5,20},{6,21},{7,22},{8,23},{9,... | collective-permute-start | bytes 61448 | tf_op jit(solution)/shard_map/ppermute | solution.py:461
  10.6 6.8 %collective-permute-start.1 = (bf16[80,128]{1,0:T(8,128)(2,1)S(1)}, bf16[80,128]{1,0:T(8,128)(2,1)S(1)}, u32[]{:S(2)}, u32[]{:S(2)}) collective-permute-start(bf16[80,128]{1,0:T(8,128)(2,1)S(1)} %get-tuple-element.33), channel_id=1, source_target_pairs={{0,17},{1,18},{2,19},{3,20},{4,21},{5,22},{6,23},{7,24},{8,25},{9,... | collective-permute-start | bytes 61448 | tf_op jit(solution)/shard_map/ppermute | solution.py:461
  11.5 5.9 %collective-permute-start = (bf16[80,128]{1,0:T(8,128)(2,1)S(1)}, bf16[80,128]{1,0:T(8,128)(2,1)S(1)}, u32[]{:S(2)}, u32[]{:S(2)}) collective-permute-start(bf16[80,128]{1,0:T(8,128)(2,1)S(1)} %get-tuple-element.33), channel_id=1, source_target_pairs={{0,16},{1,17},{2,18},{3,19},{4,20},{5,21},{6,22},{7,23},{8,24},{9,... | collective-permute-start | bytes 61448 | tf_op jit(solution)/shard_map/ppermute | solution.py:461
  21.1 7.8 %copy-start = (bf16[256,720]{0,1:T(8,128)(2,1)S(1)}, bf16[256,720]{0,1:T(8,128)(2,1)}, u32[]{:S(2)}) copy-start(bf16[256,720]{0,1:T(8,128)(2,1)} %param.16) | copy-start | bytes 1105924
  21.1 2.6 %collective-permute-start.5 = (f32[768,128]{1,0:T(8,128)S(1)}, f32[768,128]{1,0:T(8,128)S(1)}, u32[]{:S(2)}, u32[]{:S(2)}) collective-permute-start(f32[768,128]{1,0:T(8,128)S(1)} %get-tuple-element.44), channel_id=1, source_target_pairs={{0,16},{16,0},{1,17},{17,1},{2,18},{18,2},{3,19},{19,3},{4,20},{20... | collective-permute-start | bytes 1179656 | tf_op jit(solution)/shard_map/ppermute | solution.py:556
  25.3 24.3 %all-to-all-start = ((bf16[16,176,128]{2,1,0:T(8,128)(2,1)}), bf16[16,176,128]{2,1,0:T(8,128)(2,1)S(1)}, u32[]{:S(2)}, u32[]{:S(2)}) async-start(bf16[16,176,128]{2,1,0:T(8,128)(2,1)} %get-tuple-element.45), calls=%async_computation | async-start | bytes 1441792 | tf_op jit(solution)/shard_map/all_to_all | solution.py:568
  31.5 7.8 %collective-permute-start.6 = (bf16[64,128]{1,0:T(8,128)(2,1)S(1)}, bf16[64,128]{1,0:T(8,128)(2,1)S(1)}, u32[]{:S(2)}, u32[]{:S(2)}) collective-permute-start(bf16[64,128]{1,0:T(8,128)(2,1)S(1)} %get-tuple-element.49), channel_id=1, source_target_pairs={{0,16},{1,17},{2,18},{3,19},{4,20},{5,21},{6,22},{7,23},{8,24},{9,... | collective-permute-start | bytes 49160 | tf_op jit(solution)/shard_map/ppermute | solution.py:461
  32.0 15.9 %collective-permute-start.9 = (bf16[64,128]{1,0:T(8,128)(2,1)S(1)}, bf16[64,128]{1,0:T(8,128)(2,1)S(1)}, u32[]{:S(2)}, u32[]{:S(2)}) collective-permute-start(bf16[64,128]{1,0:T(8,128)(2,1)S(1)} %get-tuple-element.51), channel_id=1, source_target_pairs={{0,1},{1,2},{2,3},{3,4},{4,5},{5,6},{6,7},{7,8},{8,9},{9,10},{10,1... | collective-permute-start | bytes 49160 | tf_op jit(solution)/shard_map/ppermute | solution.py:461
  33.5 14.4 %collective-permute-start.10 = (bf16[64,128]{1,0:T(8,128)(2,1)S(1)}, bf16[64,128]{1,0:T(8,128)(2,1)S(1)}, u32[]{:S(2)}, u32[]{:S(2)}) collective-permute-start(bf16[64,128]{1,0:T(8,128)(2,1)S(1)} %get-tuple-element.52), channel_id=1, source_target_pairs={{0,15},{1,0},{2,1},{3,2},{4,3},{5,4},{6,5},{7,6},{8,7},{9,8},{10,9... | collective-permute-start | bytes 49160 | tf_op jit(solution)/shard_map/ppermute | solution.py:461
  37.6 10.3 %collective-permute-start.8 = (bf16[64,128]{1,0:T(8,128)(2,1)S(1)}, bf16[64,128]{1,0:T(8,128)(2,1)S(1)}, u32[]{:S(2)}, u32[]{:S(2)}) collective-permute-start(bf16[64,128]{1,0:T(8,128)(2,1)S(1)} %get-tuple-element.50), channel_id=1, source_target_pairs={{0,31},{1,16},{2,17},{3,18},{4,19},{5,20},{6,21},{7,22},{8,23},{9,... | collective-permute-start | bytes 49160 | tf_op jit(solution)/shard_map/ppermute | solution.py:461
  38.7 9.2 %collective-permute-start.7 = (bf16[64,128]{1,0:T(8,128)(2,1)S(1)}, bf16[64,128]{1,0:T(8,128)(2,1)S(1)}, u32[]{:S(2)}, u32[]{:S(2)}) collective-permute-start(bf16[64,128]{1,0:T(8,128)(2,1)S(1)} %get-tuple-element.50), channel_id=1, source_target_pairs={{0,17},{1,18},{2,19},{3,20},{4,21},{5,22},{6,23},{7,24},{8,25},{9,... | collective-permute-start | bytes 49160 | tf_op jit(solution)/shard_map/ppermute | solution.py:461
  50.9 13.6 %all-to-all-start.1 = ((bf16[16,48,128]{2,1,0:T(8,128)(2,1)}), bf16[16,48,128]{2,1,0:T(8,128)(2,1)S(1)}, u32[]{:S(2)}, u32[]{:S(2)}) async-start(bf16[16,48,128]{2,1,0:T(8,128)(2,1)} %shard_map.143), calls=%async_computation.1 | async-start | bytes 393216 | tf_op jit(solution)/shard_map/all_to_all | solution.py:612
  64.4 1.5 %collective-permute-start.11 = (bf16[768,128]{1,0:T(8,128)(2,1)S(1)}, bf16[768,128]{1,0:T(8,128)(2,1)S(1)}, u32[]{:S(2)}, u32[]{:S(2)}) collective-permute-start(bf16[768,128]{1,0:T(8,128)(2,1)S(1)} %bitcast.11), channel_id=1, source_target_pairs={{0,16},{16,0},{1,17},{17,1},{2,18},{18,2},{3,19},{19,3},{4,20},{20... | collective-permute-start | bytes 589832 | tf_op jit(solution)/shard_map/ppermute | solution.py:615

commit v4 on v3

--- a/solution.py
+++ b/solution.py
@@ -131,6 +131,18 @@
             ].astype(BF16)
 
 
+def corners_kernel(rows, up_ref, down_ref, left_ref, right_ref, left_out, right_out):
+    lane = lane_index(left_ref.shape)
+    width = up_ref.shape[1]
+    up = up_ref[...].astype(F32)
+    down = down_ref[...].astype(F32)
+    for column, source, target in ((0, left_ref, left_out), (width - 1, right_ref, right_out)):
+        values = source[...].astype(F32)
+        values = jnp.where(lane == rows, up[:, column : column + 1], values)
+        values = jnp.where(lane == rows + 1, down[:, column : column + 1], values)
+        target[...] = values.astype(BF16)
+
+
 def step_kernel(
     place_ref,
     wet_ref,
@@ -138,10 +150,6 @@
     flat_ref,
     up_ref,
     down_ref,
-    up_left_ref,
-    up_right_ref,
-    down_left_ref,
-    down_right_ref,
     left_ref,
     right_ref,
     cell_ref,
@@ -173,16 +181,15 @@
         shifted = jnp.where(lane == width - 1, after, pltpu.roll(slab, width - 1, 1))
         taps_ref[2 * channels : span, lanes] = shifted.astype(BF16)
 
-    for row, flag, refs in (
-        (0, place_ref[2], (up_ref, up_left_ref, up_right_ref)),
-        (rows + 1, place_ref[3], (down_ref, down_left_ref, down_right_ref)),
-    ):
-        slab, before, after = [
-            jnp.where(flag == 1, ref[...].astype(F32), 0.0) for ref in refs
-        ]
-        put(row, slab, before[:, width - 1 :], after[:, :1])
     left = left_ref[...].astype(F32)
     right = right_ref[...].astype(F32)
+    for end, flag, ref in ((0, place_ref[2], up_ref), (1, place_ref[3], down_ref)):
+        corner = slice(rows + end, rows + end + 1)
+        slab, before, after = [
+            jnp.where(flag == 1, values, 0.0)
+            for values in (ref[...].astype(F32), left[:, corner], right[:, corner])
+        ]
+        put(end * (rows + 1), slab, before, after)
     for row in range(rows):
         slab = flat_ref[:, row * width : (row + 1) * width].astype(F32)
         put(row + 1, slab, left[:, row : row + 1], right[:, row : row + 1])
@@ -344,9 +351,7 @@
     left_ref,
     right_ref,
     out_ref,
-    token_ref,
 ):
-    token_ref[...] = jnp.zeros(token_ref.shape, F32)
     hid = grad_ref.shape[0]
     width = up_ref.shape[1]
     rows = grad_ref.shape[1] // width
@@ -519,7 +524,23 @@
         fetched=2,
     )
     flat, ends, (left, right) = edges[0], edges[1:-2], edges[-2:]
-    halo = exchange(ends, ends, left, right, lat_devices, lon_devices)
+    if lat_devices == 2:
+        up = down = moved(ends[0], 1, 0, lat_devices, lon_devices)
+    else:
+        up = moved(ends[1], 1, 0, lat_devices, lon_devices)
+        down = moved(ends[0], -1, 0, lat_devices, lon_devices)
+    left, right = call(
+        lambda *refs: corners_kernel(rows, *refs),
+        (shaped(channels, width),) * 2,
+        (up, down, left, right),
+        moved=8 * channels * width,
+    )
+    halo = (
+        up,
+        down,
+        moved(right, 0, 1, lat_devices, lon_devices),
+        moved(left, 0, -1, lat_devices, lon_devices),
+    )
     w_turned = w_gates.T
     cell_flat, hcot_flat, ccot_flat, w_rows, bias = call(
         flatten_kernel,
@@ -580,9 +601,9 @@
     grad_halo = exchange(
         grad_ends[0::2], grad_ends[1::2], *grad_sides, lat_devices, lon_devices
     )
-    hidden_grad, folded = call(
+    hidden_grad = call(
         fold_kernel,
-        (shaped(hid * rows, width, dtype=F32), shaped(8, 128, dtype=F32)),
+        shaped(hid * rows, width, dtype=F32),
         (place, grad_flat, *grad_halo),
         scalars=1,
         moved=8 * hid * cells,
@@ -594,7 +615,7 @@
         (place, incoming),
         scalars=1,
         moved=2 * gates * 3 * third,
-        after=(folded,),
+        after=grad_halo,
     )
     owned = (wet_mask > 0) & (tile_owner == lon_index)
     arrived = jnp.any(owned.reshape(lon_devices, tile_cols), 1)

time: 67.9 us -> 65.6 us (0.966)
  waiting for transfers between devices: 22.3 us -> 19.8 us
    all_to_all x1, starting transfers between devices: 3.6 us -> 6.86 us  [body(): incoming = lax.all_to_all(outgoing, 'lon', 0, 0, tiled=True)]
    ppermute x10 -> x8, waiting for transfers between devices: 12.2 us -> 9.03 us  [moved(): return lax.ppermute(values, ('lat', 'lon'), pairs)]
    ppermute x10 -> x8, starting transfers between devices: 16.9 us -> 15 us  [moved(): return lax.ppermute(values, ('lat', 'lon'), pairs)]
    ppermute x1, starting transfers between devices: 1.24 us -> 0.01 us  [body(): weight_parts = (weight_parts[0], lax.ppermute(weight_parts[1], 'lat', swap))]
    all_to_all x1, waiting for transfers between devices: 0.01 us -> 1.19 us  [body(): incoming = lax.all_to_all(outgoing, 'lon', 0, 0, tiled=True)]
    all_to_all x1, waiting for transfers between devices: 8.67 us -> 7.84 us  [body(): lax.all_to_all(shares, 'lon', 0, 0, tiled=True).reshape(3 * third, lanes)]
    pallas_call x9 -> x10, Pallas kernels: 17.4 us -> 17.6 us  [call(): pl.pallas_call(run, out_shape=outs, in_specs=[SMEM] * scalars + [VMEM] *...]
  transfers between devices with their start and end apart: 14 -> 12, of which waited for: 4 -> 5; matrix products, arithmetic and copies ran while one was open for 1% -> 1% of each run, Pallas kernels for 11% -> 11%
where the time goes in v4:
time: 65.6 us; the launch traced here: 65.2 us
  starting transfers between devices  26.5 us (40%)
  waiting for transfers between devices  19.8 us (30%)
  Pallas kernels  17.6 us (27%)
  between operations  0.77 us (1%)
    pallas_call x10, Pallas kernels, call(): pl.pallas_call(run, out_shape=outs, in_specs=[SMEM] * scalars + [VMEM] *...  17.6 us
    ppermute x8, starting transfers between devices, moved(): return lax.ppermute(values, ('lat', 'lon'), pairs)  15 us
    ppermute x8, waiting for transfers between devices, moved(): return lax.ppermute(values, ('lat', 'lon'), pairs)  9.03 us
    all_to_all x1, waiting for transfers between devices, body(): lax.all_to_all(shares, 'lon', 0, 0, tiled=True).reshape(3 * third, lanes)  7.84 us
    all_to_all x1, starting transfers between devices, body(): incoming = lax.all_to_all(outgoing, 'lon', 0, 0, tiled=True)  6.86 us
    all_to_all x1, starting transfers between devices, body(): lax.all_to_all(shares, 'lon', 0, 0, tiled=True).reshape(3 * third, lanes)  4.67 us
    ppermute x1, waiting for transfers between devices, body(): weight_parts = (weight_parts[0], lax.ppermute(weight_parts[1], 'lat', swap))  1.72 us
  transfers between devices with their start and end apart: 12, of which 5 were waited for; matrix products, arithmetic and copies ran while one was open for 1% of the time, Pallas kernels for 11%

profile of v4, /device:TPU:0, one launch (start us, length us, event | category | flops | bytes accessed | tf_op | source)
XLA Modules:
  0.0 65.2 jit_solution(8274159776254833985)
XLA Ops:
  0.6 0.0 copy-start.2
  0.6 0.0 copy-start.1
  0.7 0.1 pad_add_fusion.refs_0_
  0.7 1.9 %shard_map.136 = (bf16[80,2048]{1,0:T(8,128)(2,1)S(1)}, bf16[80,128]{1,0:T(8,128)(2,1)S(1)}, bf16[80,128]{1,0:T(8,128)(2,1)S(1)}, bf16[80,128]{1,0:T(8,128)(2,1)S(1)}) custom-call(s32[4]{0:T(128)S(1)} %pad_add_fusion.refs_0_, bf16[16,16,128]{2,1,0:T(8,128)(2,1)} %refs_1_.3, bf16[64,16,128]{2,1,0:T(8,128)(2,1)} %refs_2_.4), custom_call_target="tpu_custom_call" | custom-call | bytes 655360 | tf_op jit(solution)/shard_map/pallas_call | solution.py:46
  2.7 0.5 collective-permute-start
  3.2 0.8 %collective-permute-done.refs_0_.refs_1_.refs_4_.refs_5_ = bf16[80,128]{1,0:T(8,128)(2,1)S(1)} collective-permute-done((bf16[80,128]{1,0:T(8,128)(2,1)S(1)}, bf16[80,128]{1,0:T(8,128)(2,1)S(1)}, u32[]{:S(2)}, u32[]{:S(2)}) %collective-permute-start) | collective-permute-done | bytes 20512 | tf_op jit(solution)/shard_map/ppermute | solution.py:466
  4.0 0.1 shard_map.137
  4.1 2.9 %collective-permute-start.1 = (bf16[80,128]{1,0:T(8,128)(2,1)S(1)}, bf16[80,128]{1,0:T(8,128)(2,1)S(1)}, u32[]{:S(2)}, u32[]{:S(2)}) collective-permute-start(bf16[80,128]{1,0:T(8,128)(2,1)S(1)} %get-tuple-element.36), channel_id=1, source_target_pairs={{0,1},{1,2},{2,3},{3,4},{4,5},{5,6},{6,7},{7,8},{8,9},{9,10},{10,1... | collective-permute-start | bytes 61448 | tf_op jit(solution)/shard_map/ppermute | solution.py:466
  7.0 4.1 %collective-permute-start.2 = (bf16[80,128]{1,0:T(8,128)(2,1)S(1)}, bf16[80,128]{1,0:T(8,128)(2,1)S(1)}, u32[]{:S(2)}, u32[]{:S(2)}) collective-permute-start(bf16[80,128]{1,0:T(8,128)(2,1)S(1)} %get-tuple-element.37), channel_id=1, source_target_pairs={{0,15},{1,0},{2,1},{3,2},{4,3},{5,4},{6,5},{7,6},{8,7},{9,8},{10,9... | collective-permute-start | bytes 61448 | tf_op jit(solution)/shard_map/ppermute | solution.py:466
  11.1 1.8 %shard_map.138 = (bf16[64,2048]{1,0:T(8,128)(2,1)S(1)}, bf16[64,2048]{1,0:T(8,128)(2,1)S(1)}, bf16[64,2048]{1,0:T(8,128)(2,1)S(1)}, bf16[256,768]{1,0:T(8,128)(2,1)S(1)}, f32[256,128]{1,0:T(8,128)S(1)}) custom-call(f32[1,256]{1,0:T(1,128)} %bitcast.16, bf16[720,256]{1,0:T(8,128)(2,1)} %bitcast.13, bf16[64,16,128]{2,1,0:T(8,128)(2,1)} %refs_2_.5, ...), custom_call_target="tpu_custom_call" | custom-call | bytes 1572864 | tf_op jit(solution)/shard_map/pallas_call | solution.py:46
  12.9 0.0 collective-permute-done.1.refs_6_
  13.0 0.0 collective-permute-done.2.refs_7_
  13.0 0.0 copy-done.2
  13.0 0.0 copy-done.1
  13.0 3.7 %shard_map.139 = (bf16[64,16,128]{2,1,0:T(8,128)(2,1)}, f32[1024,128]{1,0:T(8,128)}, bf16[8,64,256]{2,1,0:T(8,128)(2,1)S(1)}, f32[768,128]{1,0:T(8,128)S(1)}, f3...) custom-call(s32[4]{0:T(128)S(1)} %pad_add_fusion.refs_0_, s32[1,128]{1,0:T(1,128)S(1)} %copy-done.1, ...), custom_call_target="tpu_custom_call" | custom-call | flops 1509949440 | bytes 2097152 | tf_op jit(solution)/shard_map/pallas_call | solution.py:46
  16.7 0.0 copy-start
  16.7 0.0 collective-permute-start.3
  16.7 1.7 %collective-permute-done.3.refs_5_ = f32[768,128]{1,0:T(8,128)S(1)} collective-permute-done((f32[768,128]{1,0:T(8,128)S(1)}, f32[768,128]{1,0:T(8,128)S(1)}, u32[]{:S(2)}, u32[]{:S(2)}) %collective-permute-start.3) | collective-permute-done | bytes 393248 | tf_op jit(solution)/shard_map/ppermute | solution.py:577
  18.4 1.7 %shard_map.140 = (bf16[16,176,128]{2,1,0:T(8,128)(2,1)}, f32[8,128]{1,0:T(8,128)S(1)}) custom-call(s32[4]{0:T(128)S(1)} %pad_add_fusion.refs_0_, s32[1,128]{1,0:T(1,128)S(1)} %copy-done.1, s32[1,128]{1,0:T(1,128)S(1)} %copy-done.2, bf16[8,64,256]{2,1,0:T(8,128)(2,1)S(1)} %get-tuple-element.44.refs_3_, f32[768,128]{1,0:T(8,128)S(1)} %get-tuple-element.45.refs_4_, ...), custom_call_target="tpu_custom_call" | custom-call | bytes 1048576 | tf_op jit(solution)/shard_map/pallas_call | solution.py:46
  20.1 6.9 %all-to-all-start = ((bf16[16,176,128]{2,1,0:T(8,128)(2,1)}), bf16[16,176,128]{2,1,0:T(8,128)(2,1)S(1)}, u32[]{:S(2)}, u32[]{:S(2)}) async-start(bf16[16,176,128]{2,1,0:T(8,128)(2,1)} %get-tuple-element.47), calls=%async_computation | async-start | bytes 1441792 | tf_op jit(solution)/shard_map/all_to_all | solution.py:589
  27.0 0.0 copy-done
  27.0 2.6 %shard_map.142 = (f32[64,2048]{1,0:T(8,128)S(1)}, bf16[64,128]{1,0:T(8,128)(2,1)S(1)}, bf16[64,128]{1,0:T(8,128)(2,1)S(1)}, bf16[64,128]{1,0:T(8,128)(2,1)S(1)}, bf16[64,128]{1,0:T(8,128)(2,1)S(1)}) custom-call(s32[4]{0:T(128)S(1)} %pad_add_fusion.refs_0_, bf16[256,2560]{1,0:T(8,128)(2,1)S(1)} %get-tuple-element.48.refs_1_, bf16[720,256]{1,0:T(8,128)(2,1)S(1)} %bitcast.14, ...), custom_call_target="tpu_custom_call" | custom-call | flops 603979776 | bytes 4194304 | tf_op jit(solution)/shard_map/pallas_call | solution.py:46
  29.6 0.1 collective-permute-start.4
  29.7 2.0 %collective-permute-start.7 = (bf16[64,128]{1,0:T(8,128)(2,1)S(1)}, bf16[64,128]{1,0:T(8,128)(2,1)S(1)}, u32[]{:S(2)}, u32[]{:S(2)}) collective-permute-start(bf16[64,128]{1,0:T(8,128)(2,1)S(1)} %get-tuple-element.53), channel_id=1, source_target_pairs={{0,1},{1,2},{2,3},{3,4},{4,5},{5,6},{6,7},{7,8},{8,9},{9,10},{10,1... | collective-permute-start | bytes 49160 | tf_op jit(solution)/shard_map/ppermute | solution.py:466
  31.7 3.7 %collective-permute-start.8 = (bf16[64,128]{1,0:T(8,128)(2,1)S(1)}, bf16[64,128]{1,0:T(8,128)(2,1)S(1)}, u32[]{:S(2)}, u32[]{:S(2)}) collective-permute-start(bf16[64,128]{1,0:T(8,128)(2,1)S(1)} %get-tuple-element.54), channel_id=1, source_target_pairs={{0,15},{1,0},{2,1},{3,2},{4,3},{5,4},{6,5},{7,6},{8,7},{9,8},{10,9... | collective-permute-start | bytes 49160 | tf_op jit(solution)/shard_map/ppermute | solution.py:466
  35.4 1.4 %collective-permute-start.6 = (bf16[64,128]{1,0:T(8,128)(2,1)S(1)}, bf16[64,128]{1,0:T(8,128)(2,1)S(1)}, u32[]{:S(2)}, u32[]{:S(2)}) collective-permute-start(bf16[64,128]{1,0:T(8,128)(2,1)S(1)} %get-tuple-element.52), channel_id=1, source_target_pairs={{0,31},{1,16},{2,17},{3,18},{4,19},{5,20},{6,21},{7,22},{8,23},{9,... | collective-permute-start | bytes 49160 | tf_op jit(solution)/shard_map/ppermute | solution.py:466
  36.8 0.3 collective-permute-start.5
  37.1 0.0 collective-permute-done.4.refs_2_.refs_3_
  37.1 8.2 %collective-permute-done.7.refs_8_ = bf16[64,128]{1,0:T(8,128)(2,1)S(1)} collective-permute-done((bf16[64,128]{1,0:T(8,128)(2,1)S(1)}, bf16[64,128]{1,0:T(8,128)(2,1)S(1)}, u32[]{:S(2)}, u32[]{:S(2)}) %collective-permute-start.7) | collective-permute-done | bytes 16416 | tf_op jit(solution)/shard_map/ppermute | solution.py:466
  45.3 0.0 collective-permute-done.8.refs_9_
  45.3 0.0 collective-permute-done.6.refs_5_.refs_7_
  45.3 0.0 collective-permute-done.5.refs_4_.refs_6_
  45.3 1.2 %all-to-all-done.refs_1_ = bf16[16,176,128]{2,1,0:T(8,128)(2,1)S(1)} async-done(((bf16[16,176,128]{2,1,0:T(8,128)(2,1)}), bf16[16,176,128]{2,1,0:T(8,128)(2,1)S(1)}, u32[]{:S(2)}, u32[]{:S(2)}) %all-to-all-start) | async-done | bytes 720928 | tf_op jit(solution)/shard_map/all_to_all | solution.py:589
  46.5 1.3 %shard_map.144 = bf16[16,48,128]{2,1,0:T(8,128)(2,1)} custom-call(s32[4]{0:T(128)S(1)} %pad_add_fusion.refs_0_, bf16[16,176,128]{2,1,0:T(8,128)(2,1)S(1)} %all-to-all-done.refs_1_, bf16[64,128]{1,0:T(8,128)(2,1)S(1)} %collective-permute-done.4.refs_2_.refs_3_, bf16[64,128]{1,0:T(8,128)(2,1)S(1)} %collective-permute-done.4.refs_2_.refs_3_, ...), custom_call_target="tpu_custom_call" | custom-call | bytes 393216 | tf_op jit(solution)/shard_map/pallas_call | solution.py:46
  47.8 4.7 %all-to-all-start.1 = ((bf16[16,48,128]{2,1,0:T(8,128)(2,1)}), bf16[16,48,128]{2,1,0:T(8,128)(2,1)S(1)}, u32[]{:S(2)}, u32[]{:S(2)}) async-start(bf16[16,48,128]{2,1,0:T(8,128)(2,1)} %shard_map.144), calls=%async_computation.1 | async-start | bytes 393216 | tf_op jit(solution)/shard_map/all_to_all | solution.py:633
  52.5 0.1 reshape.34
  52.6 0.1 reduce_or.9
  52.7 7.8 %all-to-all-done.1 = bf16[16,48,128]{2,1,0:T(8,128)(2,1)S(1)} async-done(((bf16[16,48,128]{2,1,0:T(8,128)(2,1)}), bf16[16,48,128]{2,1,0:T(8,128)(2,1)S(1)}, u32[]{:S(2)}, u32[]{:S(2)}) %all-to-all-start.1) | async-done | bytes 196640 | tf_op jit(solution)/shard_map/all_to_all | solution.py:633
  60.5 0.0 collective-permute-start.9
  60.5 0.1 convert_reduce_fusion
  60.6 0.1 select_reduce_fusion.refs_0_
  60.8 1.7 %shard_map.143 = f32[1024,128]{1,0:T(8,128)} custom-call(s32[4]{0:T(128)S(1)} %pad_add_fusion.refs_0_, f32[64,2048]{1,0:T(8,128)S(1)} %get-tuple-element.50.refs_1_, bf16[64,128]{1,0:T(8,128)(2,1)S(1)} %collective-permute-done.4.refs_2_.refs_3_, bf16[64,128]{1,0:T(8,128)(2,1)S(1)} %collective-permute-done.4.refs_2_.refs_3_, ...), custom_call_target="tpu_custom_call" | custom-call | bytes 1048576 | tf_op jit(solution)/shard_map/pallas_call | solution.py:46
  62.5 1.3 %shard_map.141 = f32[4,64,256]{2,1,0:T(8,128)} custom-call(s32[4]{0:T(128)S(1)} %select_reduce_fusion.refs_0_, bf16[16,176,128]{2,1,0:T(8,128)(2,1)S(1)} %all-to-all-done.refs_1_), custom_call_target="tpu_custom_call" | custom-call | bytes 524288 | tf_op jit(solution)/shard_map/pallas_call | solution.py:46
  63.7 0.0 collective-permute-done.9.refs_2_
  63.7 1.5 %shard_map.145 = (f32[720,256]{1,0:T(8,128)}, f32[1,256]{1,0:T(1,128)}) custom-call(s32[4]{0:T(128)S(1)} %pad_add_fusion.refs_0_, bf16[768,128]{1,0:T(8,128)(2,1)S(1)} %bitcast.12, bf16[768,128]{1,0:T(8,128)(2,1)S(1)} %collective-permute-done.9.refs_2_), custom_call_target="tpu_custom_call" | custom-call | bytes 1179648 | tf_op jit(solution)/shard_map/pallas_call | solution.py:46
  (1 shorter events, 0.0 us)
Async XLA Ops:
  0.6 12.3 %copy-start.2 = (s32[1,128]{1,0:T(1,128)S(1)}, s32[1,128]{1,0:T(1,128)}, u32[]{:S(2)}) copy-start(s32[1,128]{1,0:T(1,128)} %refs_2_.7) | copy-start | bytes 1540
  0.6 12.3 %copy-start.1 = (s32[1,128]{1,0:T(1,128)S(1)}, s32[1,128]{1,0:T(1,128)}, u32[]{:S(2)}) copy-start(s32[1,128]{1,0:T(1,128)} %refs_1_.5) | copy-start | bytes 1540
  2.7 1.4 %collective-permute-start = (bf16[80,128]{1,0:T(8,128)(2,1)S(1)}, bf16[80,128]{1,0:T(8,128)(2,1)S(1)}, u32[]{:S(2)}, u32[]{:S(2)}) collective-permute-start(bf16[80,128]{1,0:T(8,128)(2,1)S(1)} %get-tuple-element.33), channel_id=1, source_target_pairs={{0,16},{1,17},{2,18},{3,19},{4,20},{5,21},{6,22},{7,23},{8,24},{9,... | collective-permute-start | bytes 61448 | tf_op jit(solution)/shard_map/ppermute | solution.py:466
  4.1 8.8 %collective-permute-start.1 = (bf16[80,128]{1,0:T(8,128)(2,1)S(1)}, bf16[80,128]{1,0:T(8,128)(2,1)S(1)}, u32[]{:S(2)}, u32[]{:S(2)}) collective-permute-start(bf16[80,128]{1,0:T(8,128)(2,1)S(1)} %get-tuple-element.36), channel_id=1, source_target_pairs={{0,1},{1,2},{2,3},{3,4},{4,5},{5,6},{6,7},{7,8},{8,9},{9,10},{10,1... | collective-permute-start | bytes 61448 | tf_op jit(solution)/shard_map/ppermute | solution.py:466
  7.0 5.9 %collective-permute-start.2 = (bf16[80,128]{1,0:T(8,128)(2,1)S(1)}, bf16[80,128]{1,0:T(8,128)(2,1)S(1)}, u32[]{:S(2)}, u32[]{:S(2)}) collective-permute-start(bf16[80,128]{1,0:T(8,128)(2,1)S(1)} %get-tuple-element.37), channel_id=1, source_target_pairs={{0,15},{1,0},{2,1},{3,2},{4,3},{5,4},{6,5},{7,6},{8,7},{9,8},{10,9... | collective-permute-start | bytes 61448 | tf_op jit(solution)/shard_map/ppermute | solution.py:466
  16.7 10.3 %copy-start = (bf16[256,720]{0,1:T(8,128)(2,1)S(1)}, bf16[256,720]{0,1:T(8,128)(2,1)}, u32[]{:S(2)}) copy-start(bf16[256,720]{0,1:T(8,128)(2,1)} %param.16) | copy-start | bytes 1105924
  16.7 1.7 %collective-permute-start.3 = (f32[768,128]{1,0:T(8,128)S(1)}, f32[768,128]{1,0:T(8,128)S(1)}, u32[]{:S(2)}, u32[]{:S(2)}) collective-permute-start(f32[768,128]{1,0:T(8,128)S(1)} %get-tuple-element.46), channel_id=1, source_target_pairs={{0,16},{16,0},{1,17},{17,1},{2,18},{18,2},{3,19},{19,3},{4,20},{20... | collective-permute-start | bytes 1179656 | tf_op jit(solution)/shard_map/ppermute | solution.py:577
  20.1 26.4 %all-to-all-start = ((bf16[16,176,128]{2,1,0:T(8,128)(2,1)}), bf16[16,176,128]{2,1,0:T(8,128)(2,1)S(1)}, u32[]{:S(2)}, u32[]{:S(2)}) async-start(bf16[16,176,128]{2,1,0:T(8,128)(2,1)} %get-tuple-element.47), calls=%async_computation | async-start | bytes 1441792 | tf_op jit(solution)/shard_map/all_to_all | solution.py:589
  29.6 7.5 %collective-permute-start.4 = (bf16[64,128]{1,0:T(8,128)(2,1)S(1)}, bf16[64,128]{1,0:T(8,128)(2,1)S(1)}, u32[]{:S(2)}, u32[]{:S(2)}) collective-permute-start(bf16[64,128]{1,0:T(8,128)(2,1)S(1)} %get-tuple-element.51), channel_id=1, source_target_pairs={{0,16},{1,17},{2,18},{3,19},{4,20},{5,21},{6,22},{7,23},{8,24},{9,... | collective-permute-start | bytes 49160 | tf_op jit(solution)/shard_map/ppermute | solution.py:466
  29.7 15.6 %collective-permute-start.7 = (bf16[64,128]{1,0:T(8,128)(2,1)S(1)}, bf16[64,128]{1,0:T(8,128)(2,1)S(1)}, u32[]{:S(2)}, u32[]{:S(2)}) collective-permute-start(bf16[64,128]{1,0:T(8,128)(2,1)S(1)} %get-tuple-element.53), channel_id=1, source_target_pairs={{0,1},{1,2},{2,3},{3,4},{4,5},{5,6},{6,7},{7,8},{8,9},{9,10},{10,1... | collective-permute-start | bytes 49160 | tf_op jit(solution)/shard_map/ppermute | solution.py:466
  31.7 13.6 %collective-permute-start.8 = (bf16[64,128]{1,0:T(8,128)(2,1)S(1)}, bf16[64,128]{1,0:T(8,128)(2,1)S(1)}, u32[]{:S(2)}, u32[]{:S(2)}) collective-permute-start(bf16[64,128]{1,0:T(8,128)(2,1)S(1)} %get-tuple-element.54), channel_id=1, source_target_pairs={{0,15},{1,0},{2,1},{3,2},{4,3},{5,4},{6,5},{7,6},{8,7},{9,8},{10,9... | collective-permute-start | bytes 49160 | tf_op jit(solution)/shard_map/ppermute | solution.py:466
  35.4 9.9 %collective-permute-start.6 = (bf16[64,128]{1,0:T(8,128)(2,1)S(1)}, bf16[64,128]{1,0:T(8,128)(2,1)S(1)}, u32[]{:S(2)}, u32[]{:S(2)}) collective-permute-start(bf16[64,128]{1,0:T(8,128)(2,1)S(1)} %get-tuple-element.52), channel_id=1, source_target_pairs={{0,31},{1,16},{2,17},{3,18},{4,19},{5,20},{6,21},{7,22},{8,23},{9,... | collective-permute-start | bytes 49160 | tf_op jit(solution)/shard_map/ppermute | solution.py:466
  36.8 8.5 %collective-permute-start.5 = (bf16[64,128]{1,0:T(8,128)(2,1)S(1)}, bf16[64,128]{1,0:T(8,128)(2,1)S(1)}, u32[]{:S(2)}, u32[]{:S(2)}) collective-permute-start(bf16[64,128]{1,0:T(8,128)(2,1)S(1)} %get-tuple-element.52), channel_id=1, source_target_pairs={{0,17},{1,18},{2,19},{3,20},{4,21},{5,22},{6,23},{7,24},{8,25},{9,... | collective-permute-start | bytes 49160 | tf_op jit(solution)/shard_map/ppermute | solution.py:466
  47.8 12.8 %all-to-all-start.1 = ((bf16[16,48,128]{2,1,0:T(8,128)(2,1)}), bf16[16,48,128]{2,1,0:T(8,128)(2,1)S(1)}, u32[]{:S(2)}, u32[]{:S(2)}) async-start(bf16[16,48,128]{2,1,0:T(8,128)(2,1)} %shard_map.144), calls=%async_computation.1 | async-start | bytes 393216 | tf_op jit(solution)/shard_map/all_to_all | solution.py:633
  60.5 3.2 %collective-permute-start.9 = (bf16[768,128]{1,0:T(8,128)(2,1)S(1)}, bf16[768,128]{1,0:T(8,128)(2,1)S(1)}, u32[]{:S(2)}, u32[]{:S(2)}) collective-permute-start(bf16[768,128]{1,0:T(8,128)(2,1)S(1)} %bitcast.11), channel_id=1, source_target_pairs={{0,16},{16,0},{1,17},{17,1},{2,18},{18,2},{3,19},{19,3},{4,20},{20... | collective-permute-start | bytes 589832 | tf_op jit(solution)/shard_map/ppermute | solution.py:636

commit v5 on v4

--- a/solution.py
+++ b/solution.py
@@ -157,12 +157,12 @@
     ccot_ref,
     w_ref,
     b_ref,
-    hidden_next_ref,
-    cell_grad_ref,
+    hidden_new_ref,
+    cell_back_ref,
     tiles_ref,
     *rest,
 ):
-    weight_refs, (delta_ref, taps_ref, wide_ref) = rest[:-3], rest[-3:]
+    weight_refs, (delta_ref, taps_ref) = rest[:-2], rest[-2:]
     channels = flat_ref.shape[0]
     hid = cell_ref.shape[0]
     gates = w_ref.shape[0]
@@ -243,10 +243,10 @@
         low = (start + 2) * width
         for index, term in enumerate(terms):
             delta_ref[index * hid : (index + 1) * hid, low : low + chunk] = term.astype(BF16)
+        hidden_new_ref[:, lanes] = hidden_new.astype(BF16)
+        cell_back_ref[:, lanes] = cell_back
         for part in range(step):
             piece = slice(part * width, (part + 1) * width)
-            wide_ref[pl.ds(start + part, hid, stride=rows), :] = hidden_new[:, piece]
-            cell_grad_ref[pl.ds(start + part, hid, stride=rows), :] = cell_back[:, piece]
             states.append(cell_new[:, piece])
         if len(states) == group:
             block_of = lane_index((hid, width)) // TILE
@@ -269,7 +269,6 @@
             for tile in range(tile_cols):
                 tiles_ref[tile, :, half * 128 : (half + 1) * 128] = states[tile].astype(BF16)
             states = []
-    hidden_next_ref[...] = wide_ref[...].reshape(hid, rows, width).astype(BF16)
     delta = delta_ref[:, 2 * width : (rows + 2) * width]
     for row_off in range(3):
         part = lax.dot_general(
@@ -339,8 +338,12 @@
                 row_refs[2 * end + index][...] = ends[end][index].astype(BF16)
 
 
-def fold_kernel(
+def finish_kernel(
     place_ref,
+    work_ref,
+    hidden_new_ref,
+    cell_back_ref,
+    arrived_ref,
     grad_ref,
     up_ref,
     down_ref,
@@ -350,7 +353,11 @@
     down_right_ref,
     left_ref,
     right_ref,
-    out_ref,
+    hidden_next_ref,
+    cell_grad_ref,
+    cell_next_ref,
+    hidden_grad_ref,
+    wide_ref,
 ):
     hid = grad_ref.shape[0]
     width = up_ref.shape[1]
@@ -368,12 +375,22 @@
         slab = slab + jnp.where(lane == width - 1, after[:, :1], 0.0)
         ends[row] = jnp.where(flag == 1, slab, 0.0)
     for row in range(rows):
-        slab = grad_ref[:, row * width : (row + 1) * width]
+        lanes = slice(row * width, (row + 1) * width)
+        slab = grad_ref[:, lanes]
         slab = slab + jnp.where(lane == 0, left[:, row : row + 1], 0.0)
         slab = slab + jnp.where(lane == width - 1, right[:, row : row + 1], 0.0)
         if row in ends:
             slab = slab + ends[row]
-        out_ref[pl.ds(row, hid, stride=rows), :] = slab
+        hidden_grad_ref[pl.ds(row, hid, stride=rows), :] = slab
+        cell_grad_ref[pl.ds(row, hid, stride=rows), :] = cell_back_ref[:, lanes]
+        wide_ref[pl.ds(row, hid, stride=rows), :] = hidden_new_ref[:, lanes].astype(F32)
+    hidden_next_ref[...] = wide_ref[...].reshape(hid, rows, width).astype(BF16)
+    pieces = arrived_ref.shape[2]
+    for index in range(cell_next_ref.shape[0]):
+        for piece in range(cell_next_ref.shape[2] // pieces):
+            cell_next_ref[index, :, piece * pieces : (piece + 1) * pieces] = arrived_ref[
+                work_ref[index], piece * hid : (piece + 1) * hid
+            ].astype(F32)
 
 
 def split_bias(block, row):
@@ -382,16 +399,10 @@
     return jnp.where(index == row + 1, rest, block)
 
 
-def pack_kernel(span, place_ref, wet_ref, owner_ref, tiles_ref, *refs):
-    out_ref, token_ref = refs[-2:]
-    token_ref[...] = jnp.zeros(token_ref.shape, F32)
+def slots_kernel(place_ref, wet_ref, owner_ref, tiles_ref, out_ref):
     tile_cols, hid, cells = tiles_ref.shape
-    lanes = out_ref.shape[2]
-    pieces = cells // 128
-    state_rows = hid * pieces * 128 // lanes
-    slots = out_ref.shape[0]
-    third = refs[0].shape[0] // 3
-    out_ref[:, :state_rows] = jnp.zeros((slots, state_rows, lanes), BF16)
+    slots, _, lanes = out_ref.shape
+    out_ref[...] = jnp.zeros(out_ref.shape, BF16)
     for tile in range(tile_cols):
         index = place_ref[1] * tile_cols + tile
 
@@ -402,16 +413,26 @@
                     tile, :, piece * lanes : (piece + 1) * lanes
                 ]
 
+
+def pack_kernel(span, count, *refs):
+    slots_ref, out_ref, token_ref, share_ref, semaphore = refs[count:]
+    token_ref[...] = jnp.zeros(token_ref.shape, F32)
+    slots, share, _ = share_ref.shape
+    third = refs[0].shape[0] // 3
     total = refs[0][...]
-    for ref in refs[1:-2]:
+    for ref in refs[1:count]:
         total = total + ref[...]
     total = jnp.concatenate([split_bias(total[:third], span), total[third:]], 0)
-    share = total.shape[0] // slots
     for slot in range(slots):
-        out_ref[slot, state_rows:] = total[slot * share : (slot + 1) * share].astype(BF16)
-
-
-def sum_kernel(scaling, span, state_rows, place_ref, parts_ref, out_ref):
+        share_ref[slot] = total[slot * share : (slot + 1) * share].astype(BF16)
+    state_rows = out_ref.shape[1] - share
+    copy = pltpu.make_async_copy(share_ref, out_ref.at[:, pl.ds(state_rows, share)], semaphore)
+    copy.start()
+    copy.wait()
+
+
+def sum_kernel(scaling, span, state_rows, place_ref, parts_ref, out_ref, token_ref):
+    token_ref[...] = jnp.zeros(token_ref.shape, F32)
     total = parts_ref[0, state_rows:].astype(F32)
     for index in range(1, parts_ref.shape[0]):
         total = total + parts_ref[index, state_rows:].astype(F32)
@@ -441,16 +462,6 @@
                 index * third : index * third + span
             ]
         bias_ref[:, lanes] = pick[span : span + 1] + pick[span + 1 : span + 2]
-
-
-def tiles_kernel(work_ref, arrived_ref, out_ref):
-    hid, cells = out_ref.shape[1:]
-    lanes = arrived_ref.shape[2]
-    for index in range(out_ref.shape[0]):
-        for piece in range(cells // lanes):
-            out_ref[index, :, piece * lanes : (piece + 1) * lanes] = arrived_ref[
-                work_ref[index], piece * hid : (piece + 1) * hid
-            ].astype(F32)
 
 
 def moved(values, lat_step, lon_step, lat_devices, lon_devices):
@@ -553,11 +564,11 @@
     )
     halves = 2 if lat_devices == 2 else 1
     lanes = gates // halves
-    hidden_next, cell_grad, tiles, *weight_parts, delta = call(
+    hidden_new, cell_back, tiles, *weight_parts, delta = call(
         step_kernel,
         (
-            shaped(hid, rows, width),
-            shaped(hid * rows, width, dtype=F32),
+            shaped(hid, cells),
+            shaped(hid, cells, dtype=F32),
             shaped(tile_cols, hid, TILE * TILE),
         )
         + (shaped(3 * third, lanes, dtype=F32),) * halves
@@ -565,10 +576,7 @@
         (place, wet_mask, tile_owner, flat, *halo)
         + (cell_flat, hcot_flat, ccot_flat, w_rows, bias),
         scalars=3,
-        scratch=[
-            pltpu.VMEM((third, (rows + 2) * width), BF16),
-            pltpu.VMEM((hid * rows, width), F32),
-        ],
+        scratch=[pltpu.VMEM((third, (rows + 2) * width), BF16)],
         flops=4 * gates * 3 * span * cells,
         moved=16 * hid * cells,
     )
@@ -579,13 +587,30 @@
         weight_parts = (lax.psum(weight_parts[0], "lat"),)
     state_rows = hid * TILE * TILE // lanes
     share = 3 * third // lon_devices
-    outgoing, packed = call(
-        lambda *refs: pack_kernel(span, *refs),
-        (shaped(lon_devices, state_rows + share, lanes), shaped(8, 128, dtype=F32)),
-        (place, wet_mask, tile_owner, tiles, *weight_parts),
+    slots = call(
+        slots_kernel,
+        shaped(lon_devices, state_rows + share, lanes),
+        (place, wet_mask, tile_owner, tiles),
         scalars=3,
         moved=4 * lon_devices * hid * TILE * TILE,
     )
+    anywhere = pl.BlockSpec(memory_space=pl.ANY)
+    count = len(weight_parts)
+    outgoing, packed = pl.pallas_call(
+        lambda *refs: pack_kernel(span, count, *refs),
+        out_shape=(shaped(*slots.shape), shaped(8, 128, dtype=F32)),
+        in_specs=[VMEM] * count + [anywhere],
+        out_specs=(anywhere, VMEM),
+        scratch_shapes=[
+            pltpu.VMEM((lon_devices, share, lanes), BF16),
+            pltpu.SemaphoreType.DMA(()),
+        ],
+        input_output_aliases={count: 0},
+        compiler_params=pltpu.CompilerParams(vmem_limit_bytes=LIMIT),
+        cost_estimate=pl.CostEstimate(
+            flops=0, bytes_accessed=8 * gates * 3 * third, transcendentals=0
+        ),
+    )(*weight_parts, slots)
     incoming = lax.all_to_all(outgoing, "lon", 0, 0, tiled=True)
     grad_parts = call(
         spread_kernel,
@@ -601,17 +626,10 @@
     grad_halo = exchange(
         grad_ends[0::2], grad_ends[1::2], *grad_sides, lat_devices, lon_devices
     )
-    hidden_grad = call(
-        fold_kernel,
-        shaped(hid * rows, width, dtype=F32),
-        (place, grad_flat, *grad_halo),
-        scalars=1,
-        moved=8 * hid * cells,
-    )
     scaling = 1.0 / math.sqrt(float(lat_devices * lon_devices * capacity * TILE * TILE))
-    shares = call(
+    shares, shared = call(
         lambda *refs: sum_kernel(scaling, span, state_rows, *refs),
-        shaped(lon_devices, share, lanes),
+        (shaped(lon_devices, share, lanes), shaped(8, 128, dtype=F32)),
         (place, incoming),
         scalars=1,
         moved=2 * gates * 3 * third,
@@ -623,14 +641,23 @@
     rank = jnp.sum((arrived[:, None] & (order[:, None] < order[None, :])).astype(jnp.int32), 0)
     placed = arrived[None, :] & (rank[None, :] == jnp.arange(capacity, dtype=jnp.int32)[:, None])
     work = jnp.sum(jnp.where(placed, order[None, :], 0), 1)
-    cell_next = call(
-        tiles_kernel,
-        shaped(capacity, hid, TILE * TILE, dtype=F32),
-        (work, incoming),
-        scalars=1,
-        moved=2 * lon_devices * hid * TILE * TILE,
+    finished = call(
+        finish_kernel,
+        (
+            shaped(hid, rows, width),
+            shaped(hid * rows, width, dtype=F32),
+            shaped(capacity, hid, TILE * TILE, dtype=F32),
+            shaped(hid * rows, width, dtype=F32),
+        ),
+        (place, work, hidden_new, cell_back, incoming, grad_flat, *grad_halo),
+        scalars=2,
+        scratch=[pltpu.VMEM((hid * rows, width), F32)],
+        moved=32 * hid * cells,
+        after=(shared,),
     )
     gathered = lax.all_to_all(shares, "lon", 0, 0, tiled=True).reshape(3 * third, lanes)
+    gathered, finished = lax.optimization_barrier((gathered, finished))
+    hidden_next, cell_grad, cell_next, hidden_grad = finished
     gathered = (gathered,)
     if halves == 2:
         gathered += (lax.ppermute(gathered[0], "lat", swap),)

time: 65.6 us -> 62.7 us (0.956)
  waiting for transfers between devices: 19.8 us -> 15.9 us
  local copies, waits for them, and re-layouts: 0.1 us -> 1.42 us
    all_to_all x1, waiting for transfers between devices: 7.84 us -> 5.31 us  [body(): lax.all_to_all(shares, 'lon', 0, 0, tiled=True).reshape(3 * third, lanes)]
    ppermute x1, waiting for transfers between devices: 1.72 us -> 0.12 us  [body(): weight_parts = (weight_parts[0], lax.ppermute(weight_parts[1], 'lat', swap))]
    ppermute x1, waiting for transfers between devices: 0.01 us -> 1.44 us  [body(): gathered += (lax.ppermute(gathered[0], 'lat', swap),)]
    pallas_call x10 -> x9, Pallas kernels: 17.6 us -> 16.3 us  [call(): pl.pallas_call(run, out_shape=outs, in_specs=[SMEM] * scalars + [VMEM] *...]
    unnamed x6 -> x10, local copies, waits for them, and re-layouts: 0.01 us -> 1.33 us
    ppermute x8, waiting for transfers between devices: 9.03 us -> 7.98 us  [moved(): return lax.ppermute(values, ('lat', 'lon'), pairs)]
    pallas_call x0 -> x1, Pallas kernels: none -> 0.72 us  [body(): pl.pallas_call(lambda *refs: pack_kernel(span, count, *refs), out_shape=(...]
  transfers between devices with their start and end apart: 12 -> 12, of which waited for: 5 -> 6; matrix products, arithmetic and copies ran while one was open for 1% -> 1% of each run, Pallas kernels for 11% -> 13%
where the time goes in v5:
time: 62.7 us; the launch traced here: 62.4 us
  starting transfers between devices  26.8 us (43%)
  Pallas kernels  17 us (27%)
  waiting for transfers between devices  15.9 us (25%)
  local copies, waits for them, and re-layouts  1.42 us (2%)
  between operations  0.82 us (1%)
    pallas_call x9, Pallas kernels, call(): pl.pallas_call(run, out_shape=outs, in_specs=[SMEM] * scalars + [VMEM] *...  16.3 us
    ppermute x8, starting transfers between devices, moved(): return lax.ppermute(values, ('lat', 'lon'), pairs)  15 us
    ppermute x8, waiting for transfers between devices, moved(): return lax.ppermute(values, ('lat', 'lon'), pairs)  7.98 us
    all_to_all x1, starting transfers between devices, body(): incoming = lax.all_to_all(outgoing, 'lon', 0, 0, tiled=True)  6.89 us
    all_to_all x1, waiting for transfers between devices, body(): lax.all_to_all(shares, 'lon', 0, 0, tiled=True).reshape(3 * third, lanes)  5.31 us
    all_to_all x1, starting transfers between devices, body(): lax.all_to_all(shares, 'lon', 0, 0, tiled=True).reshape(3 * third, lanes)  4.84 us
    ppermute x1, waiting for transfers between devices, body(): gathered += (lax.ppermute(gathered[0], 'lat', swap),)  1.44 us
    unnamed x10, local copies, waits for them, and re-layouts  1.33 us
  transfers between devices with their start and end apart: 12, of which 6 were waited for; matrix products, arithmetic and copies ran while one was open for 1% of the time, Pallas kernels for 13%

profile of v5, /device:TPU:0, one launch (start us, length us, event | category | flops | bytes accessed | tf_op | source)
XLA Modules:
  0.0 62.4 jit_solution(4553980350156747136)
XLA Ops:
  0.6 0.0 copy-start.1
  0.6 0.0 copy-start.2
  0.7 0.1 pad_add_fusion.refs_0_
  0.7 1.9 %shard_map.136 = (bf16[80,2048]{1,0:T(8,128)(2,1)S(1)}, bf16[80,128]{1,0:T(8,128)(2,1)S(1)}, bf16[80,128]{1,0:T(8,128)(2,1)S(1)}, bf16[80,128]{1,0:T(8,128)(2,1)S(1)}) custom-call(s32[4]{0:T(128)S(1)} %pad_add_fusion.refs_0_, bf16[16,16,128]{2,1,0:T(8,128)(2,1)} %refs_1_.3, bf16[64,16,128]{2,1,0:T(8,128)(2,1)} %refs_2_.4), custom_call_target="tpu_custom_call" | custom-call | bytes 655360 | tf_op jit(solution)/shard_map/pallas_call | solution.py:46
  2.7 0.5 collective-permute-start
  3.2 0.8 %collective-permute-done.refs_0_.refs_1_.refs_4_.refs_5_ = bf16[80,128]{1,0:T(8,128)(2,1)S(1)} collective-permute-done((bf16[80,128]{1,0:T(8,128)(2,1)S(1)}, bf16[80,128]{1,0:T(8,128)(2,1)S(1)}, u32[]{:S(2)}, u32[]{:S(2)}) %collective-permute-start) | collective-permute-done | bytes 20512 | tf_op jit(solution)/shard_map/ppermute | solution.py:477
  4.0 0.1 shard_map.137
  4.1 2.9 %collective-permute-start.1 = (bf16[80,128]{1,0:T(8,128)(2,1)S(1)}, bf16[80,128]{1,0:T(8,128)(2,1)S(1)}, u32[]{:S(2)}, u32[]{:S(2)}) collective-permute-start(bf16[80,128]{1,0:T(8,128)(2,1)S(1)} %get-tuple-element.47), channel_id=1, source_target_pairs={{0,1},{1,2},{2,3},{3,4},{4,5},{5,6},{6,7},{7,8},{8,9},{9,10},{10,1... | collective-permute-start | bytes 61448 | tf_op jit(solution)/shard_map/ppermute | solution.py:477
  7.0 4.1 %collective-permute-start.2 = (bf16[80,128]{1,0:T(8,128)(2,1)S(1)}, bf16[80,128]{1,0:T(8,128)(2,1)S(1)}, u32[]{:S(2)}, u32[]{:S(2)}) collective-permute-start(bf16[80,128]{1,0:T(8,128)(2,1)S(1)} %get-tuple-element.48), channel_id=1, source_target_pairs={{0,15},{1,0},{2,1},{3,2},{4,3},{5,4},{6,5},{7,6},{8,7},{9,8},{10,9... | collective-permute-start | bytes 61448 | tf_op jit(solution)/shard_map/ppermute | solution.py:477
  11.1 1.8 %shard_map.138 = (bf16[64,2048]{1,0:T(8,128)(2,1)S(1)}, bf16[64,2048]{1,0:T(8,128)(2,1)S(1)}, bf16[64,2048]{1,0:T(8,128)(2,1)S(1)}, bf16[256,768]{1,0:T(8,128)(2,1)S(1)}, f32[256,128]{1,0:T(8,128)S(1)}) custom-call(f32[1,256]{1,0:T(1,128)} %bitcast.15, bf16[720,256]{1,0:T(8,128)(2,1)} %bitcast.13, bf16[64,16,128]{2,1,0:T(8,128)(2,1)} %refs_2_.5, ...), custom_call_target="tpu_custom_call" | custom-call | bytes 1572864 | tf_op jit(solution)/shard_map/pallas_call | solution.py:46
  12.9 0.0 collective-permute-done.1.refs_6_
  13.0 0.0 collective-permute-done.2.refs_7_
  13.0 0.0 copy-done.1
  13.0 0.0 copy-done.2
  13.0 3.1 %shard_map.139 = (bf16[64,2048]{1,0:T(8,128)(2,1)S(1)}, f32[64,2048]{1,0:T(8,128)S(1)}, bf16[8,64,256]{2,1,0:T(8,128)(2,1)S(1)}, f32[768,128]{1,0:T(8,128)S(1)},...) custom-call(s32[4]{0:T(128)S(1)} %pad_add_fusion.refs_0_, s32[1,128]{1,0:T(1,128)S(1)} %copy-done.2, ...), custom_call_target="tpu_custom_call" | custom-call | flops 1509949440 | bytes 2097152 | tf_op jit(solution)/shard_map/pallas_call | solution.py:46
  16.1 0.0 copy-start.3
  16.1 0.1 collective-permute-start.3
  16.2 1.6 %shard_map.140.refs_2_ = bf16[16,176,128]{2,1,0:T(8,128)(2,1)} custom-call(s32[4]{0:T(128)S(1)} %pad_add_fusion.refs_0_, s32[1,128]{1,0:T(1,128)S(1)} %copy-done.2, s32[1,128]{1,0:T(1,128)S(1)} %copy-done.1, bf16[8,64,256]{2,1,0:T(8,128)(2,1)S(1)} %get-tuple-element.56.refs_3_), custom_call_target="tpu_custom_call" | custom-call | bytes 1048576 | tf_op jit(solution)/shard_map/pallas_call | solution.py:46
  17.8 0.1 collective-permute-done.3.refs_1_
  17.9 0.0 copy-start
  17.9 0.7 %shard_map.141 = (bf16[16,176,128]{2,1,0:T(8,128)(2,1)}, f32[8,128]{1,0:T(8,128)S(1)}) custom-call(f32[768,128]{1,0:T(8,128)S(1)} %get-tuple-element.54.refs_0_, f32[768,128]{1,0:T(8,128)S(1)} %collective-permute-done.3.refs_1_, bf16[16,176,128]{2,1,0:T(8,128)(2,1)} %shard_map.140.refs_2_), custom_call_target="tpu_custom_call", output_to_operand_aliasing={{0}: (2, {})} | custom-call | bytes 1572864 | tf_op jit(solution)/shard_map/pallas_call | solution.py:599
  18.7 0.0 copy-done.3
  18.7 6.9 %all-to-all-start = ((bf16[16,176,128]{2,1,0:T(8,128)(2,1)}), bf16[16,176,128]{2,1,0:T(8,128)(2,1)S(1)}, u32[]{:S(2)}, u32[]{:S(2)}) async-start(bf16[16,176,128]{2,1,0:T(8,128)(2,1)} %get-tuple-element.57), calls=%async_computation | async-start | bytes 1441792 | tf_op jit(solution)/shard_map/all_to_all | solution.py:614
  25.6 0.0 copy-done
  25.6 0.0 copy-start.4
  25.6 1.3 %copy-done.4 = bf16[256,2560]{1,0:T(8,128)(2,1)S(1)} copy-done((bf16[256,2560]{1,0:T(8,128)(2,1)S(1)}, bf16[256,2560]{1,0:T(8,128)(2,1)}, u32[]{:S(2)}) %copy-start.4) | copy-done | bytes 1310744
  26.9 2.6 %shard_map.142 = (f32[64,2048]{1,0:T(8,128)S(1)}, bf16[64,128]{1,0:T(8,128)(2,1)S(1)}, bf16[64,128]{1,0:T(8,128)(2,1)S(1)}, bf16[64,128]{1,0:T(8,128)(2,1)S(1)}, bf16[64,128]{1,0:T(8,128)(2,1)S(1)}) custom-call(s32[4]{0:T(128)S(1)} %pad_add_fusion.refs_0_, bf16[256,2560]{1,0:T(8,128)(2,1)S(1)} %copy-done.4, bf16[720,256]{1,0:T(8,128)(2,1)S(1)} %bitcast.14, ...), custom_call_target="tpu_custom_call" | custom-call | flops 603979776 | bytes 4194304 | tf_op jit(solution)/shard_map/pallas_call | solution.py:46
  29.5 0.1 collective-permute-start.4
  29.7 1.9 %collective-permute-start.7 = (bf16[64,128]{1,0:T(8,128)(2,1)S(1)}, bf16[64,128]{1,0:T(8,128)(2,1)S(1)}, u32[]{:S(2)}, u32[]{:S(2)}) collective-permute-start(bf16[64,128]{1,0:T(8,128)(2,1)S(1)} %get-tuple-element.62), channel_id=1, source_target_pairs={{0,1},{1,2},{2,3},{3,4},{4,5},{5,6},{6,7},{7,8},{8,9},{9,10},{10,1... | collective-permute-start | bytes 49160 | tf_op jit(solution)/shard_map/ppermute | solution.py:477
  31.6 3.7 %collective-permute-start.8 = (bf16[64,128]{1,0:T(8,128)(2,1)S(1)}, bf16[64,128]{1,0:T(8,128)(2,1)S(1)}, u32[]{:S(2)}, u32[]{:S(2)}) collective-permute-start(bf16[64,128]{1,0:T(8,128)(2,1)S(1)} %get-tuple-element.63), channel_id=1, source_target_pairs={{0,15},{1,0},{2,1},{3,2},{4,3},{5,4},{6,5},{7,6},{8,7},{9,8},{10,9... | collective-permute-start | bytes 49160 | tf_op jit(solution)/shard_map/ppermute | solution.py:477
  35.3 1.4 %collective-permute-start.6 = (bf16[64,128]{1,0:T(8,128)(2,1)S(1)}, bf16[64,128]{1,0:T(8,128)(2,1)S(1)}, u32[]{:S(2)}, u32[]{:S(2)}) collective-permute-start(bf16[64,128]{1,0:T(8,128)(2,1)S(1)} %get-tuple-element.61), channel_id=1, source_target_pairs={{0,31},{1,16},{2,17},{3,18},{4,19},{5,20},{6,21},{7,22},{8,23},{9,... | collective-permute-start | bytes 49160 | tf_op jit(solution)/shard_map/ppermute | solution.py:477
  36.7 0.3 collective-permute-start.5
  37.0 0.0 collective-permute-done.4.refs_2_.refs_3_.refs_6_.refs_7_
  37.0 7.1 %collective-permute-done.7.refs_8_.refs_12_ = bf16[64,128]{1,0:T(8,128)(2,1)S(1)} collective-permute-done((bf16[64,128]{1,0:T(8,128)(2,1)S(1)}, bf16[64,128]{1,0:T(8,128)(2,1)S(1)}, u32[]{:S(2)}, u32[]{:S(2)}) %collective-permute-start.7) | collective-permute-done | bytes 16416 | tf_op jit(solution)/shard_map/ppermute | solution.py:477
  44.2 0.0 collective-permute-done.8.refs_9_.refs_13_
  44.2 0.0 collective-permute-done.6.refs_5_.refs_7_.refs_9_.refs_11_
  44.2 0.0 collective-permute-done.5.refs_4_.refs_6_.refs_8_.refs_10_
  44.2 1.0 %all-to-all-done.refs_1_.refs_4_ = bf16[16,176,128]{2,1,0:T(8,128)(2,1)S(1)} async-done(((bf16[16,176,128]{2,1,0:T(8,128)(2,1)}), bf16[16,176,128]{2,1,0:T(8,128)(2,1)S(1)}, u32[]{:S(2)}, u32[]{:S(2)}) %all-to-all-start) | async-done | bytes 720928 | tf_op jit(solution)/shard_map/all_to_all | solution.py:614
  45.2 1.3 %shard_map.143 = (bf16[16,48,128]{2,1,0:T(8,128)(2,1)}, f32[8,128]{1,0:T(8,128)S(1)}) custom-call(s32[4]{0:T(128)S(1)} %pad_add_fusion.refs_0_, bf16[16,176,128]{2,1,0:T(8,128)(2,1)S(1)} %all-to-all-done.refs_1_.refs_4_, bf16[64,128]{1,0:T(8,128)(2,1)S(1)} %collective-permute-done.4.refs_2_.refs_3_.refs_6_.refs_7_, ...), custom_call_target="tpu_custom_call" | custom-call | bytes 393216 | tf_op jit(solution)/shard_map/pallas_call | solution.py:46
  46.5 4.8 %all-to-all-start.1 = ((bf16[16,48,128]{2,1,0:T(8,128)(2,1)}), bf16[16,48,128]{2,1,0:T(8,128)(2,1)S(1)}, u32[]{:S(2)}, u32[]{:S(2)}) async-start(bf16[16,48,128]{2,1,0:T(8,128)(2,1)} %get-tuple-element.64), calls=%async_computation.1 | async-start | bytes 393216 | tf_op jit(solution)/shard_map/all_to_all | solution.py:658
  51.3 0.1 reshape.35
  51.4 0.1 reduce_or.9
  51.6 0.1 convert_reduce_fusion
  51.6 0.1 select_reduce_fusion.refs_1_
  51.8 2.3 %shard_map.144 = (bf16[64,16,128]{2,1,0:T(8,128)(2,1)}, f32[1024,128]{1,0:T(8,128)}, f32[4,64,256]{2,1,0:T(8,128)}, f32[1024,128]{1,0:T(8,128)}) custom-call(s32[4]{0:T(128)S(1)} %pad_add_fusion.refs_0_, s32[4]{0:T(128)S(1)} %select_reduce_fusion.refs_1_, bf16[64,2048]{1,0:T(8,128)(2,1)S(1)} %get-tuple-element.65.refs_2_, ...), custom_call_target="tpu_custom_call" | custom-call | bytes 4194304 | tf_op jit(solution)/shard_map/pallas_call | solution.py:46
  54.1 5.3 %all-to-all-done.1 = bf16[16,48,128]{2,1,0:T(8,128)(2,1)S(1)} async-done(((bf16[16,48,128]{2,1,0:T(8,128)(2,1)}), bf16[16,48,128]{2,1,0:T(8,128)(2,1)S(1)}, u32[]{:S(2)}, u32[]{:S(2)}) %all-to-all-start.1) | async-done | bytes 196640 | tf_op jit(solution)/shard_map/all_to_all | solution.py:658
  59.4 0.0 collective-permute-start.9
  59.4 1.4 %collective-permute-done.9.refs_2_ = bf16[768,128]{1,0:T(8,128)(2,1)S(1)} collective-permute-done((bf16[768,128]{1,0:T(8,128)(2,1)S(1)}, bf16[768,128]{1,0:T(8,128)(2,1)S(1)}, u32[]{:S(2)}, u32[]{:S(2)}) %collective-permute-start.9) | collective-permute-done | bytes 196640 | tf_op jit(solution)/shard_map/ppermute | solution.py:663
  60.8 1.5 %shard_map.145 = (f32[720,256]{1,0:T(8,128)}, f32[1,256]{1,0:T(1,128)}) custom-call(s32[4]{0:T(128)S(1)} %pad_add_fusion.refs_0_, bf16[768,128]{1,0:T(8,128)(2,1)S(1)} %bitcast.12, bf16[768,128]{1,0:T(8,128)(2,1)S(1)} %collective-permute-done.9.refs_2_), custom_call_target="tpu_custom_call" | custom-call | bytes 1179648 | tf_op jit(solution)/shard_map/pallas_call | solution.py:46
  (1 shorter events, 0.0 us)
Async XLA Ops:
  0.6 12.3 %copy-start.1 = (s32[1,128]{1,0:T(1,128)S(1)}, s32[1,128]{1,0:T(1,128)}, u32[]{:S(2)}) copy-start(s32[1,128]{1,0:T(1,128)} %refs_2_.7) | copy-start | bytes 1540
  0.6 12.3 %copy-start.2 = (s32[1,128]{1,0:T(1,128)S(1)}, s32[1,128]{1,0:T(1,128)}, u32[]{:S(2)}) copy-start(s32[1,128]{1,0:T(1,128)} %refs_1_.5) | copy-start | bytes 1540
  2.7 1.4 %collective-permute-start = (bf16[80,128]{1,0:T(8,128)(2,1)S(1)}, bf16[80,128]{1,0:T(8,128)(2,1)S(1)}, u32[]{:S(2)}, u32[]{:S(2)}) collective-permute-start(bf16[80,128]{1,0:T(8,128)(2,1)S(1)} %get-tuple-element.44), channel_id=1, source_target_pairs={{0,16},{1,17},{2,18},{3,19},{4,20},{5,21},{6,22},{7,23},{8,24},{9,... | collective-permute-start | bytes 61448 | tf_op jit(solution)/shard_map/ppermute | solution.py:477
  4.1 8.8 %collective-permute-start.1 = (bf16[80,128]{1,0:T(8,128)(2,1)S(1)}, bf16[80,128]{1,0:T(8,128)(2,1)S(1)}, u32[]{:S(2)}, u32[]{:S(2)}) collective-permute-start(bf16[80,128]{1,0:T(8,128)(2,1)S(1)} %get-tuple-element.47), channel_id=1, source_target_pairs={{0,1},{1,2},{2,3},{3,4},{4,5},{5,6},{6,7},{7,8},{8,9},{9,10},{10,1... | collective-permute-start | bytes 61448 | tf_op jit(solution)/shard_map/ppermute | solution.py:477
  7.0 5.9 %collective-permute-start.2 = (bf16[80,128]{1,0:T(8,128)(2,1)S(1)}, bf16[80,128]{1,0:T(8,128)(2,1)S(1)}, u32[]{:S(2)}, u32[]{:S(2)}) collective-permute-start(bf16[80,128]{1,0:T(8,128)(2,1)S(1)} %get-tuple-element.48), channel_id=1, source_target_pairs={{0,15},{1,0},{2,1},{3,2},{4,3},{5,4},{6,5},{7,6},{8,7},{9,8},{10,9... | collective-permute-start | bytes 61448 | tf_op jit(solution)/shard_map/ppermute | solution.py:477
  16.1 2.5 %copy-start.3 = (bf16[256,2560]{1,0:T(8,128)(2,1)}, bf16[256,2560]{1,0:T(8,128)(2,1)S(1)}, u32[]{:S(2)}) copy-start(bf16[256,2560]{1,0:T(8,128)(2,1)S(1)} %get-tuple-element.58.refs_1_) | copy-start | bytes 3932164
  16.1 1.8 %collective-permute-start.3 = (f32[768,128]{1,0:T(8,128)S(1)}, f32[768,128]{1,0:T(8,128)S(1)}, u32[]{:S(2)}, u32[]{:S(2)}) collective-permute-start(f32[768,128]{1,0:T(8,128)S(1)} %get-tuple-element.55), channel_id=1, source_target_pairs={{0,16},{16,0},{1,17},{17,1},{2,18},{18,2},{3,19},{19,3},{4,20},{20... | collective-permute-start | bytes 1179656 | tf_op jit(solution)/shard_map/ppermute | solution.py:585
  17.9 7.6 %copy-start = (bf16[256,720]{0,1:T(8,128)(2,1)S(1)}, bf16[256,720]{0,1:T(8,128)(2,1)}, u32[]{:S(2)}) copy-start(bf16[256,720]{0,1:T(8,128)(2,1)} %param.16) | copy-start | bytes 1105924
  18.7 26.5 %all-to-all-start = ((bf16[16,176,128]{2,1,0:T(8,128)(2,1)}), bf16[16,176,128]{2,1,0:T(8,128)(2,1)S(1)}, u32[]{:S(2)}, u32[]{:S(2)}) async-start(bf16[16,176,128]{2,1,0:T(8,128)(2,1)} %get-tuple-element.57), calls=%async_computation | async-start | bytes 1441792 | tf_op jit(solution)/shard_map/all_to_all | solution.py:614
  25.6 1.3 %copy-start.4 = (bf16[256,2560]{1,0:T(8,128)(2,1)S(1)}, bf16[256,2560]{1,0:T(8,128)(2,1)}, u32[]{:S(2)}) copy-start(bf16[256,2560]{1,0:T(8,128)(2,1)} %copy-done.3) | copy-start | bytes 3932164
  29.5 7.5 %collective-permute-start.4 = (bf16[64,128]{1,0:T(8,128)(2,1)S(1)}, bf16[64,128]{1,0:T(8,128)(2,1)S(1)}, u32[]{:S(2)}, u32[]{:S(2)}) collective-permute-start(bf16[64,128]{1,0:T(8,128)(2,1)S(1)} %get-tuple-element.60), channel_id=1, source_target_pairs={{0,16},{1,17},{2,18},{3,19},{4,20},{5,21},{6,22},{7,23},{8,24},{9,... | collective-permute-start | bytes 49160 | tf_op jit(solution)/shard_map/ppermute | solution.py:477
  29.7 14.5 %collective-permute-start.7 = (bf16[64,128]{1,0:T(8,128)(2,1)S(1)}, bf16[64,128]{1,0:T(8,128)(2,1)S(1)}, u32[]{:S(2)}, u32[]{:S(2)}) collective-permute-start(bf16[64,128]{1,0:T(8,128)(2,1)S(1)} %get-tuple-element.62), channel_id=1, source_target_pairs={{0,1},{1,2},{2,3},{3,4},{4,5},{5,6},{6,7},{7,8},{8,9},{9,10},{10,1... | collective-permute-start | bytes 49160 | tf_op jit(solution)/shard_map/ppermute | solution.py:477
  31.6 12.6 %collective-permute-start.8 = (bf16[64,128]{1,0:T(8,128)(2,1)S(1)}, bf16[64,128]{1,0:T(8,128)(2,1)S(1)}, u32[]{:S(2)}, u32[]{:S(2)}) collective-permute-start(bf16[64,128]{1,0:T(8,128)(2,1)S(1)} %get-tuple-element.63), channel_id=1, source_target_pairs={{0,15},{1,0},{2,1},{3,2},{4,3},{5,4},{6,5},{7,6},{8,7},{9,8},{10,9... | collective-permute-start | bytes 49160 | tf_op jit(solution)/shard_map/ppermute | solution.py:477
  35.3 8.9 %collective-permute-start.6 = (bf16[64,128]{1,0:T(8,128)(2,1)S(1)}, bf16[64,128]{1,0:T(8,128)(2,1)S(1)}, u32[]{:S(2)}, u32[]{:S(2)}) collective-permute-start(bf16[64,128]{1,0:T(8,128)(2,1)S(1)} %get-tuple-element.61), channel_id=1, source_target_pairs={{0,31},{1,16},{2,17},{3,18},{4,19},{5,20},{6,21},{7,22},{8,23},{9,... | collective-permute-start | bytes 49160 | tf_op jit(solution)/shard_map/ppermute | solution.py:477
  36.7 7.5 %collective-permute-start.5 = (bf16[64,128]{1,0:T(8,128)(2,1)S(1)}, bf16[64,128]{1,0:T(8,128)(2,1)S(1)}, u32[]{:S(2)}, u32[]{:S(2)}) collective-permute-start(bf16[64,128]{1,0:T(8,128)(2,1)S(1)} %get-tuple-element.61), channel_id=1, source_target_pairs={{0,17},{1,18},{2,19},{3,20},{4,21},{5,22},{6,23},{7,24},{8,25},{9,... | collective-permute-start | bytes 49160 | tf_op jit(solution)/shard_map/ppermute | solution.py:477
  46.5 12.9 %all-to-all-start.1 = ((bf16[16,48,128]{2,1,0:T(8,128)(2,1)}), bf16[16,48,128]{2,1,0:T(8,128)(2,1)S(1)}, u32[]{:S(2)}, u32[]{:S(2)}) async-start(bf16[16,48,128]{2,1,0:T(8,128)(2,1)} %get-tuple-element.64), calls=%async_computation.1 | async-start | bytes 393216 | tf_op jit(solution)/shard_map/all_to_all | solution.py:658
  59.4 1.4 %collective-permute-start.9 = (bf16[768,128]{1,0:T(8,128)(2,1)S(1)}, bf16[768,128]{1,0:T(8,128)(2,1)S(1)}, u32[]{:S(2)}, u32[]{:S(2)}) collective-permute-start(bf16[768,128]{1,0:T(8,128)(2,1)S(1)} %bitcast.11), channel_id=1, source_target_pairs={{0,16},{16,0},{1,17},{17,1},{2,18},{18,2},{3,19},{19,3},{4,20},{20... | collective-permute-start | bytes 589832 | tf_op jit(solution)/shard_map/ppermute | solution.py:663

commit v6 on v5

--- a/solution.py
+++ b/solution.py
@@ -10,7 +10,7 @@
 TILE = 16
 F32 = jnp.float32
 BF16 = jnp.bfloat16
-LIMIT = 48 * 1024 * 1024
+LIMIT = 24 * 1024 * 1024
 SMEM = pl.BlockSpec(memory_space=pltpu.SMEM)
 VMEM = pl.BlockSpec(memory_space=pltpu.VMEM)
 
@@ -65,7 +65,7 @@
     return 0.5 * jnp.tanh(0.5 * values) + 0.5
 
 
-def edges_kernel(waits, place_ref, forcing_ref, hidden_ref, flat_ref, *rest):
+def edges_kernel(waits, place_ref, forcing_ref, hidden_ref, *rest):
     row_refs, (left_ref, right_ref, wide_ref) = rest[:-3], rest[-3:]
     inp, rows, width = forcing_ref.shape
     channels = inp + hidden_ref.shape[0]
@@ -79,7 +79,6 @@
     ends = []
     for row in range(rows):
         slab = wide_ref[pl.ds(row, channels, stride=rows), :]
-        flat_ref[:, row * width : (row + 1) * width] = slab.astype(BF16)
         left = jnp.where(lane == row, slab[:, :1], left)
         right = jnp.where(lane == row, slab[:, width - 1 :], right)
         if row in (0, rows - 1):
@@ -93,35 +92,86 @@
         row_refs[1][...] = ends[-1].astype(BF16)
 
 
-def flatten_kernel(
+def middle_kernel(
     waits,
+    place_ref,
+    up_ref,
+    down_ref,
     b_ref,
     wt_ref,
+    forcing_ref,
+    hidden_ref,
     cell_ref,
     hcot_ref,
     ccot_ref,
     cell_out,
     hcot_out,
     ccot_out,
+    taps_ref,
+    pre_ref,
+    sides_ref,
     w_ref,
-    bias_ref,
+    fields_ref,
     wide_ref,
 ):
     hid, rows, width = cell_ref.shape
     gates = wt_ref.shape[1]
     span = wt_ref.shape[0] // 3
     third = w_ref.shape[1] // 3
-    waits[0]()
-    bias_ref[...] = jnp.broadcast_to(b_ref[...], (bias_ref.shape[1], gates)).T
-    waits[1]()
+    inp = forcing_ref.shape[0]
+    channels = inp + hid
+    wait_b, wait_w, wait_forcing, wait_hidden, *wait_cells = waits
+    wait_b()
+    bias = jnp.broadcast_to(b_ref[...], (width, gates)).T
+    wait_w()
     blank = jnp.zeros((third - span, gates), F32)
+
+    def turned(blocks):
+        blocks = [block.astype(F32) for block in blocks]
+        return jnp.concatenate(blocks + [blank], 0).T.astype(BF16)
+
     for index in range(3):
-        block = wt_ref[index * span : (index + 1) * span].astype(F32)
-        w_ref[:, index * third : (index + 1) * third] = (
-            jnp.concatenate([block, blank], 0).T.astype(BF16)
+        w_ref[:, index * third : (index + 1) * third] = turned(
+            [wt_ref[index * span : (index + 1) * span]]
         )
+    for side, tap in enumerate((0, 2)):
+        starts = [index * span + tap * channels for index in range(3)]
+        sides_ref[side] = turned([wt_ref[first : first + channels] for first in starts])
+    wait_forcing()
+    fields_ref[: inp * rows] = forcing_ref[...].astype(F32).reshape(inp * rows, width)
+    wait_hidden()
+    fields_ref[inp * rows :] = hidden_ref[...].astype(F32).reshape(hid * rows, width)
+    lane = lane_index((channels, width))
+
+    def put(row, slab):
+        lanes = slice(row * width, (row + 1) * width)
+        shifted = jnp.where(lane == 0, 0.0, pltpu.roll(slab, 1, 1))
+        taps_ref[0:channels, lanes] = shifted.astype(BF16)
+        taps_ref[channels : 2 * channels, lanes] = slab.astype(BF16)
+        shifted = jnp.where(lane == width - 1, 0.0, pltpu.roll(slab, width - 1, 1))
+        taps_ref[2 * channels : span, lanes] = shifted.astype(BF16)
+
+    put(0, jnp.where(place_ref[2] == 1, up_ref[...].astype(F32), 0.0))
+    put(rows + 1, jnp.where(place_ref[3] == 1, down_ref[...].astype(F32), 0.0))
+    for row in range(rows):
+        put(row + 1, fields_ref[pl.ds(row, channels, stride=rows), :])
+    ones = lax.broadcasted_iota(jnp.int32, (third - span, taps_ref.shape[1]), 0) == 0
+    taps_ref[span:] = jnp.where(ones, 1.0, 0.0).astype(BF16)
+    step = 2 if rows % 2 == 0 else 1
+    chunk = step * width
+    bias = jnp.concatenate([bias] * step, 1)
+    for start in range(0, rows, step):
+        pre = bias
+        for row_off in range(3):
+            low = (start + row_off) * width
+            pre = pre + jnp.dot(
+                w_ref[:, row_off * third : (row_off + 1) * third],
+                taps_ref[:, low : low + chunk],
+                preferred_element_type=F32,
+            )
+        pre_ref[:, start * width : start * width + chunk] = pre
     for wait, source, target in zip(
-        waits[2:], (cell_ref, hcot_ref, ccot_ref), (cell_out, hcot_out, ccot_out)
+        wait_cells, (cell_ref, hcot_ref, ccot_ref), (cell_out, hcot_out, ccot_out)
     ):
         wait()
         wide_ref[...] = source[...].astype(F32).reshape(hid * rows, width)
@@ -146,56 +196,54 @@
 def step_kernel(
     place_ref,
     wet_ref,
-    owner_ref,
-    flat_ref,
-    up_ref,
-    down_ref,
     left_ref,
     right_ref,
     cell_ref,
     hcot_ref,
     ccot_ref,
-    w_ref,
-    b_ref,
+    early_ref,
+    pre_ref,
+    sides_ref,
     hidden_new_ref,
     cell_back_ref,
     tiles_ref,
     *rest,
 ):
     weight_refs, (delta_ref, taps_ref) = rest[:-2], rest[-2:]
-    channels = flat_ref.shape[0]
+    channels, width = left_ref.shape
     hid = cell_ref.shape[0]
-    gates = w_ref.shape[0]
-    width = up_ref.shape[1]
-    rows = flat_ref.shape[1] // width
+    gates = pre_ref.shape[0]
+    rows = pre_ref.shape[1] // width
     tile_cols = width // TILE
     span = 3 * channels
+    third = early_ref.shape[0]
     first_tile = place_ref[1] * tile_cols
     lane = lane_index((channels, width))
-
-    def put(row, slab, before, after):
-        lanes = slice(row * width, (row + 1) * width)
-        shifted = jnp.where(lane == 0, before, pltpu.roll(slab, 1, 1))
-        taps_ref[0:channels, lanes] = shifted.astype(BF16)
-        taps_ref[channels : 2 * channels, lanes] = slab.astype(BF16)
-        shifted = jnp.where(lane == width - 1, after, pltpu.roll(slab, width - 1, 1))
-        taps_ref[2 * channels : span, lanes] = shifted.astype(BF16)
-
-    left = left_ref[...].astype(F32)
-    right = right_ref[...].astype(F32)
-    for end, flag, ref in ((0, place_ref[2], up_ref), (1, place_ref[3], down_ref)):
-        corner = slice(rows + end, rows + end + 1)
-        slab, before, after = [
-            jnp.where(flag == 1, values, 0.0)
-            for values in (ref[...].astype(F32), left[:, corner], right[:, corner])
-        ]
-        put(end * (rows + 1), slab, before, after)
-    for row in range(rows):
-        slab = flat_ref[:, row * width : (row + 1) * width].astype(F32)
-        put(row + 1, slab, left[:, row : row + 1], right[:, row : row + 1])
-    extra = taps_ref.shape[0] - span
-    ones = lax.broadcasted_iota(jnp.int32, (extra, taps_ref.shape[1]), 0) == 0
-    taps_ref[span:] = jnp.where(ones, 1.0, 0.0).astype(BF16)
+    taps_ref[...] = early_ref[...]
+    fixes = []
+    for side, ref in enumerate((left_ref, right_ref)):
+        halo = ref[...].astype(F32)
+        above = jnp.where(place_ref[2] == 1, halo[:, rows : rows + 1], 0.0)
+        below = jnp.where(place_ref[3] == 1, halo[:, rows + 1 : rows + 2], 0.0)
+        column = jnp.where(lane == 0, above, pltpu.roll(halo, 1, 1))
+        column = jnp.where(lane == rows + 1, below, column)
+        place = slice(2 * side * channels, (2 * side + 1) * channels)
+        edge = side * (width - 1)
+        for row in range(rows + 2):
+            lanes = slice(row * width, (row + 1) * width)
+            slab = early_ref[place, lanes].astype(F32)
+            slab = jnp.where(lane == edge, column[:, row : row + 1], slab)
+            taps_ref[place, lanes] = slab.astype(BF16)
+        parts = [column] + [pltpu.roll(column, width - row_off, 1) for row_off in (1, 2)]
+        parts.append(jnp.zeros((third - span, width), F32))
+        fixes.append(
+            jnp.dot(
+                sides_ref[side],
+                jnp.concatenate(parts, 0).astype(BF16),
+                preferred_element_type=F32,
+            )
+        )
+    gate_lane = lane_index((gates, width))
 
     live = jnp.zeros((1, width), F32)
     live_lane = lane_index((1, width)) // TILE
@@ -205,22 +253,19 @@
     step = 2 if rows % 2 == 0 else 1
     chunk = step * width
     live = jnp.concatenate([live] * step, 1)
-    third = w_ref.shape[1] // 3
     blank = jnp.zeros((gates, 2 * width), BF16)
     delta_ref[:, : 2 * width] = blank
     delta_ref[:, (rows + 2) * width :] = blank
-    bias = jnp.concatenate([b_ref[...]] * step, 1)
     group = 128 // TILE
     states = []
     for start in range(0, rows, step):
-        pre = bias
-        for row_off in range(3):
-            low = (start + row_off) * width
-            pre = pre + jnp.dot(
-                w_ref[:, row_off * third : (row_off + 1) * third],
-                taps_ref[:, low : low + chunk],
-                preferred_element_type=F32,
-            )
+        pre = []
+        for row in range(start, start + step):
+            part = pre_ref[:, row * width : (row + 1) * width]
+            part = part + jnp.where(gate_lane == 0, fixes[0][:, row : row + 1], 0.0)
+            part = part + jnp.where(gate_lane == width - 1, fixes[1][:, row : row + 1], 0.0)
+            pre.append(part)
+        pre = jnp.concatenate(pre, 1)
         gate_in = sigmoid(pre[:hid])
         gate_forget = sigmoid(pre[hid : 2 * hid])
         gate_out = sigmoid(pre[2 * hid : 3 * hid])
@@ -527,14 +572,14 @@
     end_count = 1 if lat_devices == 2 else 2
     edges = call(
         edges_kernel,
-        (shaped(channels, cells),) + (shaped(channels, width),) * (end_count + 2),
+        (shaped(channels, width),) * (end_count + 2),
         (place, forcing, hidden),
         scalars=1,
         scratch=[pltpu.VMEM((channels * rows, width), F32)],
         moved=4 * channels * cells,
         fetched=2,
     )
-    flat, ends, (left, right) = edges[0], edges[1:-2], edges[-2:]
+    ends, (left, right) = edges[:-2], edges[-2:]
     if lat_devices == 2:
         up = down = moved(ends[0], 1, 0, lat_devices, lon_devices)
     else:
@@ -547,20 +592,29 @@
         moved=8 * channels * width,
     )
     halo = (
-        up,
-        down,
         moved(right, 0, 1, lat_devices, lon_devices),
         moved(left, 0, -1, lat_devices, lon_devices),
     )
     w_turned = w_gates.T
-    cell_flat, hcot_flat, ccot_flat, w_rows, bias = call(
-        flatten_kernel,
+    early = call(
+        middle_kernel,
         (shaped(hid, cells),) * 3
-        + (shaped(gates, 3 * third), shaped(gates, width, dtype=F32)),
-        (b_gates.reshape(1, gates), w_turned, cell, grad_hidden, grad_cell),
-        scratch=[pltpu.VMEM((hid * rows, width), F32)],
+        + (
+            shaped(third, (rows + 2) * width),
+            shaped(gates, cells, dtype=F32),
+            shaped(2, gates, third),
+        ),
+        (place, up, down)
+        + (b_gates.reshape(1, gates), w_turned, forcing, hidden, cell, grad_hidden, grad_cell),
+        scalars=1,
+        scratch=[
+            pltpu.VMEM((gates, 3 * third), BF16),
+            pltpu.VMEM((channels * rows, width), F32),
+            pltpu.VMEM((hid * rows, width), F32),
+        ],
+        flops=2 * gates * 3 * span * cells,
         moved=12 * hid * cells,
-        fetched=5,
+        fetched=7,
     )
     halves = 2 if lat_devices == 2 else 1
     lanes = gates // halves
@@ -573,11 +627,10 @@
         )
         + (shaped(3 * third, lanes, dtype=F32),) * halves
         + (shaped(gates, (rows + 4) * width),),
-        (place, wet_mask, tile_owner, flat, *halo)
-        + (cell_flat, hcot_flat, ccot_flat, w_rows, bias),
-        scalars=3,
+        (place, wet_mask, *halo, *early),
+        scalars=2,
         scratch=[pltpu.VMEM((third, (rows + 2) * width), BF16)],
-        flops=4 * gates * 3 * span * cells,
+        flops=2 * gates * 3 * span * cells,
         moved=16 * hid * cells,
     )
     swap = [(0, 1), (1, 0)]

time: 62.7 us -> 63.5 us (1.013)
  Pallas kernels: 17 us -> 19.6 us
  starting transfers between devices: 26.8 us -> 25.1 us
    pallas_call x9, Pallas kernels: 16.3 us -> 18.9 us  [call(): pl.pallas_call(run, out_shape=outs, in_specs=[SMEM] * scalars + [VMEM] *...]
    all_to_all x1, starting transfers between devices: 6.89 us -> 5.02 us  [body(): incoming = lax.all_to_all(outgoing, 'lon', 0, 0, tiled=True)]
  transfers between devices with their start and end apart: 12 -> 12, of which waited for: 6 -> 6; matrix products, arithmetic and copies ran while one was open for 1% -> 1% of each run, Pallas kernels for 13% -> 16%
where the time goes in v6:
time: 63.5 us; the launch traced here: 63.1 us
  starting transfers between devices  25.1 us (40%)
  Pallas kernels  19.6 us (31%)
  waiting for transfers between devices  15.8 us (25%)
  local copies, waits for them, and re-layouts  1.42 us (2%)
  between operations  0.81 us (1%)
    pallas_call x9, Pallas kernels, call(): pl.pallas_call(run, out_shape=outs, in_specs=[SMEM] * scalars + [VMEM] *...  18.9 us
    ppermute x8, starting transfers between devices, moved(): return lax.ppermute(values, ('lat', 'lon'), pairs)  15.1 us
    ppermute x8, waiting for transfers between devices, moved(): return lax.ppermute(values, ('lat', 'lon'), pairs)  7.97 us
    all_to_all x1, waiting for transfers between devices, body(): lax.all_to_all(shares, 'lon', 0, 0, tiled=True).reshape(3 * third, lanes)  5.31 us
    all_to_all x1, starting transfers between devices, body(): incoming = lax.all_to_all(outgoing, 'lon', 0, 0, tiled=True)  5.02 us
    all_to_all x1, starting transfers between devices, body(): lax.all_to_all(shares, 'lon', 0, 0, tiled=True).reshape(3 * third, lanes)  4.94 us
    ppermute x1, waiting for transfers between devices, body(): gathered += (lax.ppermute(gathered[0], 'lat', swap),)  1.44 us
    unnamed x10, local copies, waits for them, and re-layouts  1.33 us
  transfers between devices with their start and end apart: 12, of which 6 were waited for; matrix products, arithmetic and copies ran while one was open for 1% of the time, Pallas kernels for 16%

profile of v6, /device:TPU:0, one launch (start us, length us, event | category | flops | bytes accessed | tf_op | source)
XLA Modules:
  0.0 63.1 jit_solution(13057384861050987253)
XLA Ops:
  0.6 0.1 pad_add_fusion.refs_0_
  0.7 1.9 %shard_map.136 = (bf16[80,128]{1,0:T(8,128)(2,1)S(1)}, bf16[80,128]{1,0:T(8,128)(2,1)S(1)}, bf16[80,128]{1,0:T(8,128)(2,1)S(1)}) custom-call(s32[4]{0:T(128)S(1)} %pad_add_fusion.refs_0_, bf16[16,16,128]{2,1,0:T(8,128)(2,1)} %refs_5_.1, bf16[64,16,128]{2,1,0:T(8,128)(2,1)} %refs_6_.1), custom_call_target="tpu_custom_call" | custom-call | bytes 655360 | tf_op jit(solution)/shard_map/pallas_call | solution.py:46
  2.6 0.5 collective-permute-start
  3.2 0.8 %collective-permute-done.refs_0_.refs_1_.refs_2_ = bf16[80,128]{1,0:T(8,128)(2,1)S(1)} collective-permute-done((bf16[80,128]{1,0:T(8,128)(2,1)S(1)}, bf16[80,128]{1,0:T(8,128)(2,1)S(1)}, u32[]{:S(2)}, u32[]{:S(2)}) %collective-permute-start) | collective-permute-done | bytes 20512 | tf_op jit(solution)/shard_map/ppermute | solution.py:522
  4.0 0.1 shard_map.137
  4.1 2.9 %collective-permute-start.1 = (bf16[80,128]{1,0:T(8,128)(2,1)S(1)}, bf16[80,128]{1,0:T(8,128)(2,1)S(1)}, u32[]{:S(2)}, u32[]{:S(2)}) collective-permute-start(bf16[80,128]{1,0:T(8,128)(2,1)S(1)} %get-tuple-element.46), channel_id=1, source_target_pairs={{0,1},{1,2},{2,3},{3,4},{4,5},{5,6},{6,7},{7,8},{8,9},{9,10},{10,1... | collective-permute-start | bytes 61448 | tf_op jit(solution)/shard_map/ppermute | solution.py:522
  7.0 4.1 %collective-permute-start.2 = (bf16[80,128]{1,0:T(8,128)(2,1)S(1)}, bf16[80,128]{1,0:T(8,128)(2,1)S(1)}, u32[]{:S(2)}, u32[]{:S(2)}) collective-permute-start(bf16[80,128]{1,0:T(8,128)(2,1)S(1)} %get-tuple-element.47), channel_id=1, source_target_pairs={{0,15},{1,0},{2,1},{3,2},{4,3},{5,4},{6,5},{7,6},{8,7},{9,8},{10,9... | collective-permute-start | bytes 61448 | tf_op jit(solution)/shard_map/ppermute | solution.py:522
  11.0 0.0 copy-start
  11.0 3.7 %shard_map.138 = (bf16[64,2048]{1,0:T(8,128)(2,1)S(1)}, bf16[64,2048]{1,0:T(8,128)(2,1)S(1)}, bf16[64,2048]{1,0:T(8,128)(2,1)S(1)}, bf16[256,2304]{1,0:T(8,128)(...) custom-call(s32[4]{0:T(128)S(1)} %pad_add_fusion.refs_0_, ...), custom_call_target="tpu_custom_call" | custom-call | flops 754974720 | bytes 1572864 | tf_op jit(solution)/shard_map/pallas_call | solution.py:46
  14.8 0.0 collective-permute-done.1.refs_2_
  14.8 0.0 collective-permute-done.2.refs_3_
  14.8 0.0 copy-done
  14.8 0.0 copy-start.1
  14.8 3.9 %shard_map.139 = (bf16[64,2048]{1,0:T(8,128)(2,1)S(1)}, f32[64,2048]{1,0:T(8,128)S(1)}, bf16[8,64,256]{2,1,0:T(8,128)(2,1)S(1)}, f32[768,128]{1,0:T(8,128)S(1)},...) custom-call(s32[4]{0:T(128)S(1)} %pad_add_fusion.refs_0_, s32[1,128]{1,0:T(1,128)S(1)} %copy-done, ...), custom_call_target="tpu_custom_call" | custom-call | flops 754974720 | bytes 2097152 | tf_op jit(solution)/shard_map/pallas_call | solution.py:46
  18.7 0.0 copy-start.2
  18.7 0.1 collective-permute-start.3
  18.8 0.0 copy-done.1
  18.8 1.6 %shard_map.140.refs_2_ = bf16[16,176,128]{2,1,0:T(8,128)(2,1)} custom-call(s32[4]{0:T(128)S(1)} %pad_add_fusion.refs_0_, s32[1,128]{1,0:T(1,128)S(1)} %copy-done, s32[1,128]{1,0:T(1,128)S(1)} %copy-done.1, bf16[8,64,256]{2,1,0:T(8,128)(2,1)S(1)} %get-tuple-element.56.refs_3_), custom_call_target="tpu_custom_call" | custom-call | bytes 1048576 | tf_op jit(solution)/shard_map/pallas_call | solution.py:46
  20.4 0.1 collective-permute-done.3.refs_1_
  20.5 0.0 copy-start.4
  20.5 0.8 %shard_map.141 = (bf16[16,176,128]{2,1,0:T(8,128)(2,1)}, f32[8,128]{1,0:T(8,128)S(1)}) custom-call(f32[768,128]{1,0:T(8,128)S(1)} %get-tuple-element.54.refs_0_, f32[768,128]{1,0:T(8,128)S(1)} %collective-permute-done.3.refs_1_, bf16[16,176,128]{2,1,0:T(8,128)(2,1)} %shard_map.140.refs_2_), custom_call_target="tpu_custom_call", output_to_operand_aliasing={{0}: (2, {})} | custom-call | bytes 1572864 | tf_op jit(solution)/shard_map/pallas_call | solution.py:652
  21.2 0.0 copy-done.2
  21.2 5.0 %all-to-all-start = ((bf16[16,176,128]{2,1,0:T(8,128)(2,1)}), bf16[16,176,128]{2,1,0:T(8,128)(2,1)S(1)}, u32[]{:S(2)}, u32[]{:S(2)}) async-start(bf16[16,176,128]{2,1,0:T(8,128)(2,1)} %get-tuple-element.57), calls=%async_computation | async-start | bytes 1441792 | tf_op jit(solution)/shard_map/all_to_all | solution.py:667
  26.3 0.0 copy-done.4
  26.3 0.0 copy-start.3
  26.3 1.3 %copy-done.3 = bf16[256,2560]{1,0:T(8,128)(2,1)S(1)} copy-done((bf16[256,2560]{1,0:T(8,128)(2,1)S(1)}, bf16[256,2560]{1,0:T(8,128)(2,1)}, u32[]{:S(2)}) %copy-start.3) | copy-done | bytes 1310744
  27.6 2.6 %shard_map.142 = (f32[64,2048]{1,0:T(8,128)S(1)}, bf16[64,128]{1,0:T(8,128)(2,1)S(1)}, bf16[64,128]{1,0:T(8,128)(2,1)S(1)}, bf16[64,128]{1,0:T(8,128)(2,1)S(1)}, bf16[64,128]{1,0:T(8,128)(2,1)S(1)}) custom-call(s32[4]{0:T(128)S(1)} %pad_add_fusion.refs_0_, bf16[256,2560]{1,0:T(8,128)(2,1)S(1)} %copy-done.3, bf16[720,256]{1,0:T(8,128)(2,1)S(1)} %bitcast.14, ...), custom_call_target="tpu_custom_call" | custom-call | flops 603979776 | bytes 4194304 | tf_op jit(solution)/shard_map/pallas_call | solution.py:46
  30.2 0.2 collective-permute-start.4
  30.5 1.8 %collective-permute-start.7 = (bf16[64,128]{1,0:T(8,128)(2,1)S(1)}, bf16[64,128]{1,0:T(8,128)(2,1)S(1)}, u32[]{:S(2)}, u32[]{:S(2)}) collective-permute-start(bf16[64,128]{1,0:T(8,128)(2,1)S(1)} %get-tuple-element.62), channel_id=1, source_target_pairs={{0,1},{1,2},{2,3},{3,4},{4,5},{5,6},{6,7},{7,8},{8,9},{9,10},{10,1... | collective-permute-start | bytes 49160 | tf_op jit(solution)/shard_map/ppermute | solution.py:522
  32.3 3.8 %collective-permute-start.8 = (bf16[64,128]{1,0:T(8,128)(2,1)S(1)}, bf16[64,128]{1,0:T(8,128)(2,1)S(1)}, u32[]{:S(2)}, u32[]{:S(2)}) collective-permute-start(bf16[64,128]{1,0:T(8,128)(2,1)S(1)} %get-tuple-element.63), channel_id=1, source_target_pairs={{0,15},{1,0},{2,1},{3,2},{4,3},{5,4},{6,5},{7,6},{8,7},{9,8},{10,9... | collective-permute-start | bytes 49160 | tf_op jit(solution)/shard_map/ppermute | solution.py:522
  36.1 1.3 %collective-permute-start.6 = (bf16[64,128]{1,0:T(8,128)(2,1)S(1)}, bf16[64,128]{1,0:T(8,128)(2,1)S(1)}, u32[]{:S(2)}, u32[]{:S(2)}) collective-permute-start(bf16[64,128]{1,0:T(8,128)(2,1)S(1)} %get-tuple-element.61), channel_id=1, source_target_pairs={{0,31},{1,16},{2,17},{3,18},{4,19},{5,20},{6,21},{7,22},{8,23},{9,... | collective-permute-start | bytes 49160 | tf_op jit(solution)/shard_map/ppermute | solution.py:522
  37.4 0.4 collective-permute-start.5
  37.8 0.0 collective-permute-done.4.refs_2_.refs_3_.refs_6_.refs_7_
  37.8 7.1 %collective-permute-done.7.refs_8_.refs_12_ = bf16[64,128]{1,0:T(8,128)(2,1)S(1)} collective-permute-done((bf16[64,128]{1,0:T(8,128)(2,1)S(1)}, bf16[64,128]{1,0:T(8,128)(2,1)S(1)}, u32[]{:S(2)}, u32[]{:S(2)}) %collective-permute-start.7) | collective-permute-done | bytes 16416 | tf_op jit(solution)/shard_map/ppermute | solution.py:522
  44.9 0.0 collective-permute-done.8.refs_9_.refs_13_
  44.9 0.0 collective-permute-done.6.refs_5_.refs_7_.refs_9_.refs_11_
  44.9 0.0 collective-permute-done.5.refs_4_.refs_6_.refs_8_.refs_10_
  44.9 1.0 %all-to-all-done.refs_1_.refs_4_ = bf16[16,176,128]{2,1,0:T(8,128)(2,1)S(1)} async-done(((bf16[16,176,128]{2,1,0:T(8,128)(2,1)}), bf16[16,176,128]{2,1,0:T(8,128)(2,1)S(1)}, u32[]{:S(2)}, u32[]{:S(2)}) %all-to-all-start) | async-done | bytes 720928 | tf_op jit(solution)/shard_map/all_to_all | solution.py:667
  45.9 1.3 %shard_map.143 = (bf16[16,48,128]{2,1,0:T(8,128)(2,1)}, f32[8,128]{1,0:T(8,128)S(1)}) custom-call(s32[4]{0:T(128)S(1)} %pad_add_fusion.refs_0_, bf16[16,176,128]{2,1,0:T(8,128)(2,1)S(1)} %all-to-all-done.refs_1_.refs_4_, bf16[64,128]{1,0:T(8,128)(2,1)S(1)} %collective-permute-done.4.refs_2_.refs_3_.refs_6_.refs_7_, ...), custom_call_target="tpu_custom_call" | custom-call | bytes 393216 | tf_op jit(solution)/shard_map/pallas_call | solution.py:46
  47.2 4.9 %all-to-all-start.1 = ((bf16[16,48,128]{2,1,0:T(8,128)(2,1)}), bf16[16,48,128]{2,1,0:T(8,128)(2,1)S(1)}, u32[]{:S(2)}, u32[]{:S(2)}) async-start(bf16[16,48,128]{2,1,0:T(8,128)(2,1)} %get-tuple-element.64), calls=%async_computation.1 | async-start | bytes 393216 | tf_op jit(solution)/shard_map/all_to_all | solution.py:711
  52.1 0.1 reshape.35
  52.2 0.1 reduce_or.9
  52.4 0.1 convert_reduce_fusion
  52.4 0.1 select_reduce_fusion.refs_1_
  52.6 2.3 %shard_map.144 = (bf16[64,16,128]{2,1,0:T(8,128)(2,1)}, f32[1024,128]{1,0:T(8,128)}, f32[4,64,256]{2,1,0:T(8,128)}, f32[1024,128]{1,0:T(8,128)}) custom-call(s32[4]{0:T(128)S(1)} %pad_add_fusion.refs_0_, s32[4]{0:T(128)S(1)} %select_reduce_fusion.refs_1_, bf16[64,2048]{1,0:T(8,128)(2,1)S(1)} %get-tuple-element.65.refs_2_, ...), custom_call_target="tpu_custom_call" | custom-call | bytes 4194304 | tf_op jit(solution)/shard_map/pallas_call | solution.py:46
  54.9 5.3 %all-to-all-done.1 = bf16[16,48,128]{2,1,0:T(8,128)(2,1)S(1)} async-done(((bf16[16,48,128]{2,1,0:T(8,128)(2,1)}), bf16[16,48,128]{2,1,0:T(8,128)(2,1)S(1)}, u32[]{:S(2)}, u32[]{:S(2)}) %all-to-all-start.1) | async-done | bytes 196640 | tf_op jit(solution)/shard_map/all_to_all | solution.py:711
  60.2 0.0 collective-permute-start.9
  60.2 1.4 %collective-permute-done.9.refs_2_ = bf16[768,128]{1,0:T(8,128)(2,1)S(1)} collective-permute-done((bf16[768,128]{1,0:T(8,128)(2,1)S(1)}, bf16[768,128]{1,0:T(8,128)(2,1)S(1)}, u32[]{:S(2)}, u32[]{:S(2)}) %collective-permute-start.9) | collective-permute-done | bytes 196640 | tf_op jit(solution)/shard_map/ppermute | solution.py:716
  61.6 1.5 %shard_map.145 = (f32[720,256]{1,0:T(8,128)}, f32[1,256]{1,0:T(1,128)}) custom-call(s32[4]{0:T(128)S(1)} %pad_add_fusion.refs_0_, bf16[768,128]{1,0:T(8,128)(2,1)S(1)} %bitcast.12, bf16[768,128]{1,0:T(8,128)(2,1)S(1)} %collective-permute-done.9.refs_2_), custom_call_target="tpu_custom_call" | custom-call | bytes 1179648 | tf_op jit(solution)/shard_map/pallas_call | solution.py:46
  (1 shorter events, 0.0 us)
Async XLA Ops:
  2.6 1.4 %collective-permute-start = (bf16[80,128]{1,0:T(8,128)(2,1)S(1)}, bf16[80,128]{1,0:T(8,128)(2,1)S(1)}, u32[]{:S(2)}, u32[]{:S(2)}) collective-permute-start(bf16[80,128]{1,0:T(8,128)(2,1)S(1)} %get-tuple-element.43), channel_id=1, source_target_pairs={{0,16},{1,17},{2,18},{3,19},{4,20},{5,21},{6,22},{7,23},{8,24},{9,... | collective-permute-start | bytes 61448 | tf_op jit(solution)/shard_map/ppermute | solution.py:522
  4.1 10.7 %collective-permute-start.1 = (bf16[80,128]{1,0:T(8,128)(2,1)S(1)}, bf16[80,128]{1,0:T(8,128)(2,1)S(1)}, u32[]{:S(2)}, u32[]{:S(2)}) collective-permute-start(bf16[80,128]{1,0:T(8,128)(2,1)S(1)} %get-tuple-element.46), channel_id=1, source_target_pairs={{0,1},{1,2},{2,3},{3,4},{4,5},{5,6},{6,7},{7,8},{8,9},{9,10},{10,1... | collective-permute-start | bytes 61448 | tf_op jit(solution)/shard_map/ppermute | solution.py:522
  7.0 7.8 %collective-permute-start.2 = (bf16[80,128]{1,0:T(8,128)(2,1)S(1)}, bf16[80,128]{1,0:T(8,128)(2,1)S(1)}, u32[]{:S(2)}, u32[]{:S(2)}) collective-permute-start(bf16[80,128]{1,0:T(8,128)(2,1)S(1)} %get-tuple-element.47), channel_id=1, source_target_pairs={{0,15},{1,0},{2,1},{3,2},{4,3},{5,4},{6,5},{7,6},{8,7},{9,8},{10,9... | collective-permute-start | bytes 61448 | tf_op jit(solution)/shard_map/ppermute | solution.py:522
  11.0 3.7 %copy-start = (s32[1,128]{1,0:T(1,128)S(1)}, s32[1,128]{1,0:T(1,128)}, u32[]{:S(2)}) copy-start(s32[1,128]{1,0:T(1,128)} %refs_1_.5) | copy-start | bytes 1540
  14.8 4.0 %copy-start.1 = (s32[1,128]{1,0:T(1,128)S(1)}, s32[1,128]{1,0:T(1,128)}, u32[]{:S(2)}) copy-start(s32[1,128]{1,0:T(1,128)} %refs_2_.3) | copy-start | bytes 1540
  18.7 2.6 %copy-start.2 = (bf16[256,2560]{1,0:T(8,128)(2,1)}, bf16[256,2560]{1,0:T(8,128)(2,1)S(1)}, u32[]{:S(2)}) copy-start(bf16[256,2560]{1,0:T(8,128)(2,1)S(1)} %get-tuple-element.58.refs_1_) | copy-start | bytes 3932164
  18.7 1.8 %collective-permute-start.3 = (f32[768,128]{1,0:T(8,128)S(1)}, f32[768,128]{1,0:T(8,128)S(1)}, u32[]{:S(2)}, u32[]{:S(2)}) collective-permute-start(f32[768,128]{1,0:T(8,128)S(1)} %get-tuple-element.55), channel_id=1, source_target_pairs={{0,16},{16,0},{1,17},{17,1},{2,18},{18,2},{3,19},{19,3},{4,20},{20... | collective-permute-start | bytes 1179656 | tf_op jit(solution)/shard_map/ppermute | solution.py:638
  20.5 5.8 %copy-start.4 = (bf16[256,720]{0,1:T(8,128)(2,1)S(1)}, bf16[256,720]{0,1:T(8,128)(2,1)}, u32[]{:S(2)}) copy-start(bf16[256,720]{0,1:T(8,128)(2,1)} %param.16) | copy-start | bytes 1105924
  21.2 24.7 %all-to-all-start = ((bf16[16,176,128]{2,1,0:T(8,128)(2,1)}), bf16[16,176,128]{2,1,0:T(8,128)(2,1)S(1)}, u32[]{:S(2)}, u32[]{:S(2)}) async-start(bf16[16,176,128]{2,1,0:T(8,128)(2,1)} %get-tuple-element.57), calls=%async_computation | async-start | bytes 1441792 | tf_op jit(solution)/shard_map/all_to_all | solution.py:667
  26.3 1.3 %copy-start.3 = (bf16[256,2560]{1,0:T(8,128)(2,1)S(1)}, bf16[256,2560]{1,0:T(8,128)(2,1)}, u32[]{:S(2)}) copy-start(bf16[256,2560]{1,0:T(8,128)(2,1)} %copy-done.2) | copy-start | bytes 3932164
  30.2 7.6 %collective-permute-start.4 = (bf16[64,128]{1,0:T(8,128)(2,1)S(1)}, bf16[64,128]{1,0:T(8,128)(2,1)S(1)}, u32[]{:S(2)}, u32[]{:S(2)}) collective-permute-start(bf16[64,128]{1,0:T(8,128)(2,1)S(1)} %get-tuple-element.60), channel_id=1, source_target_pairs={{0,16},{1,17},{2,18},{3,19},{4,20},{5,21},{6,22},{7,23},{8,24},{9,... | collective-permute-start | bytes 49160 | tf_op jit(solution)/shard_map/ppermute | solution.py:522
  30.5 14.5 %collective-permute-start.7 = (bf16[64,128]{1,0:T(8,128)(2,1)S(1)}, bf16[64,128]{1,0:T(8,128)(2,1)S(1)}, u32[]{:S(2)}, u32[]{:S(2)}) collective-permute-start(bf16[64,128]{1,0:T(8,128)(2,1)S(1)} %get-tuple-element.62), channel_id=1, source_target_pairs={{0,1},{1,2},{2,3},{3,4},{4,5},{5,6},{6,7},{7,8},{8,9},{9,10},{10,1... | collective-permute-start | bytes 49160 | tf_op jit(solution)/shard_map/ppermute | solution.py:522
  32.3 12.7 %collective-permute-start.8 = (bf16[64,128]{1,0:T(8,128)(2,1)S(1)}, bf16[64,128]{1,0:T(8,128)(2,1)S(1)}, u32[]{:S(2)}, u32[]{:S(2)}) collective-permute-start(bf16[64,128]{1,0:T(8,128)(2,1)S(1)} %get-tuple-element.63), channel_id=1, source_target_pairs={{0,15},{1,0},{2,1},{3,2},{4,3},{5,4},{6,5},{7,6},{8,7},{9,8},{10,9... | collective-permute-start | bytes 49160 | tf_op jit(solution)/shard_map/ppermute | solution.py:522
  36.1 8.9 %collective-permute-start.6 = (bf16[64,128]{1,0:T(8,128)(2,1)S(1)}, bf16[64,128]{1,0:T(8,128)(2,1)S(1)}, u32[]{:S(2)}, u32[]{:S(2)}) collective-permute-start(bf16[64,128]{1,0:T(8,128)(2,1)S(1)} %get-tuple-element.61), channel_id=1, source_target_pairs={{0,31},{1,16},{2,17},{3,18},{4,19},{5,20},{6,21},{7,22},{8,23},{9,... | collective-permute-start | bytes 49160 | tf_op jit(solution)/shard_map/ppermute | solution.py:522
  37.4 7.5 %collective-permute-start.5 = (bf16[64,128]{1,0:T(8,128)(2,1)S(1)}, bf16[64,128]{1,0:T(8,128)(2,1)S(1)}, u32[]{:S(2)}, u32[]{:S(2)}) collective-permute-start(bf16[64,128]{1,0:T(8,128)(2,1)S(1)} %get-tuple-element.61), channel_id=1, source_target_pairs={{0,17},{1,18},{2,19},{3,20},{4,21},{5,22},{6,23},{7,24},{8,25},{9,... | collective-permute-start | bytes 49160 | tf_op jit(solution)/shard_map/ppermute | solution.py:522
  47.2 13.0 %all-to-all-start.1 = ((bf16[16,48,128]{2,1,0:T(8,128)(2,1)}), bf16[16,48,128]{2,1,0:T(8,128)(2,1)S(1)}, u32[]{:S(2)}, u32[]{:S(2)}) async-start(bf16[16,48,128]{2,1,0:T(8,128)(2,1)} %get-tuple-element.64), calls=%async_computation.1 | async-start | bytes 393216 | tf_op jit(solution)/shard_map/all_to_all | solution.py:711
  60.2 1.4 %collective-permute-start.9 = (bf16[768,128]{1,0:T(8,128)(2,1)S(1)}, bf16[768,128]{1,0:T(8,128)(2,1)S(1)}, u32[]{:S(2)}, u32[]{:S(2)}) collective-permute-start(bf16[768,128]{1,0:T(8,128)(2,1)S(1)} %bitcast.11), channel_id=1, source_target_pairs={{0,16},{16,0},{1,17},{17,1},{2,18},{18,2},{3,19},{19,3},{4,20},{20... | collective-permute-start | bytes 589832 | tf_op jit(solution)/shard_map/ppermute | solution.py:716

commit v7 on v5

--- a/solution.py
+++ b/solution.py
@@ -65,32 +65,34 @@
     return 0.5 * jnp.tanh(0.5 * values) + 0.5
 
 
-def edges_kernel(waits, place_ref, forcing_ref, hidden_ref, flat_ref, *rest):
-    row_refs, (left_ref, right_ref, wide_ref) = rest[:-3], rest[-3:]
+def edges_kernel(waits, place_ref, forcing_ref, hidden_ref, wide_ref, *row_refs):
     inp, rows, width = forcing_ref.shape
     channels = inp + hidden_ref.shape[0]
     for wait in waits:
         wait()
     wide_ref[: inp * rows] = forcing_ref[...].astype(F32).reshape(inp * rows, width)
     wide_ref[inp * rows :] = hidden_ref[...].astype(F32).reshape((channels - inp) * rows, width)
+    ends = [wide_ref[pl.ds(row, channels, stride=rows), :] for row in (0, rows - 1)]
+    if len(row_refs) == 1:
+        row_refs[0][...] = jnp.where(place_ref[0] == 0, ends[1], ends[0]).astype(BF16)
+    else:
+        for ref, end in zip(row_refs, ends):
+            ref[...] = end.astype(BF16)
+
+
+def columns_kernel(wide_ref, flat_ref, left_ref, right_ref):
+    channels, width = left_ref.shape
+    rows = wide_ref.shape[0] // channels
     lane = lane_index((channels, width))
     left = jnp.zeros((channels, width), F32)
     right = jnp.zeros((channels, width), F32)
-    ends = []
     for row in range(rows):
         slab = wide_ref[pl.ds(row, channels, stride=rows), :]
         flat_ref[:, row * width : (row + 1) * width] = slab.astype(BF16)
         left = jnp.where(lane == row, slab[:, :1], left)
         right = jnp.where(lane == row, slab[:, width - 1 :], right)
-        if row in (0, rows - 1):
-            ends.append(slab)
     left_ref[...] = left.astype(BF16)
     right_ref[...] = right.astype(BF16)
-    if len(row_refs) == 1:
-        row_refs[0][...] = jnp.where(place_ref[0] == 0, ends[-1], ends[0]).astype(BF16)
-    else:
-        row_refs[0][...] = ends[0].astype(BF16)
-        row_refs[1][...] = ends[-1].astype(BF16)
 
 
 def flatten_kernel(
@@ -446,22 +448,28 @@
         out_ref[index] = total.astype(BF16)
 
 
-def weights_kernel(span, place_ref, *refs):
-    *parts, weight_ref, bias_ref = refs
-    third = parts[0].shape[0] // 3
-    half = parts[0].shape[1]
-    for side in range(len(parts)):
-        if len(parts) == 1:
-            pick = parts[0][...]
-        else:
-            pick = jnp.where(place_ref[0] == side, parts[0][...], parts[1][...])
-        pick = pick.astype(F32)
-        lanes = slice(side * half, (side + 1) * half)
-        for index in range(3):
-            weight_ref[index * span : (index + 1) * span, lanes] = pick[
-                index * third : index * third + span
-            ]
-        bias_ref[:, lanes] = pick[span : span + 1] + pick[span + 1 : span + 2]
+def weights_kernel(span, other, place_ref, *refs):
+    *parts, weight_ref, bias_ref, block_ref, semaphore = refs
+    pick_ref = parts[1] if other else parts[0]
+    third = pick_ref.shape[0] // 3
+    half = pick_ref.shape[1]
+    for index in range(3):
+        block_ref[index * span : (index + 1) * span] = pick_ref[
+            index * third : index * third + span
+        ].astype(F32)
+    lanes = slice(None)
+    if weight_ref.shape[1] > half:
+        side = 1 - place_ref[0] if other else place_ref[0]
+        lanes = pl.ds(pl.multiple_of(side * half, half), half)
+    copy = pltpu.make_async_copy(block_ref, weight_ref.at[:, lanes], semaphore)
+    copy.start()
+    halves = weight_ref.shape[1] // half
+    for side in range(halves):
+        rows = parts[0][span:third].astype(F32)
+        if other:
+            rows = jnp.where(place_ref[0] == side, rows, parts[1][span:third].astype(F32))
+        bias_ref[:, side * half : (side + 1) * half] = rows[0:1] + rows[1:2]
+    copy.wait()
 
 
 def moved(values, lat_step, lon_step, lat_devices, lon_devices):
@@ -525,16 +533,20 @@
         return jax.ShapeDtypeStruct(shape, dtype)
 
     end_count = 1 if lat_devices == 2 else 2
-    edges = call(
+    wide, *ends = call(
         edges_kernel,
-        (shaped(channels, cells),) + (shaped(channels, width),) * (end_count + 2),
+        (shaped(channels * rows, width, dtype=F32),) + (shaped(channels, width),) * end_count,
         (place, forcing, hidden),
         scalars=1,
-        scratch=[pltpu.VMEM((channels * rows, width), F32)],
         moved=4 * channels * cells,
         fetched=2,
     )
-    flat, ends, (left, right) = edges[0], edges[1:-2], edges[-2:]
+    flat, left, right = call(
+        columns_kernel,
+        (shaped(channels, cells),) + (shaped(channels, width),) * 2,
+        (wide,),
+        moved=6 * channels * cells,
+    )
     if lat_devices == 2:
         up = down = moved(ends[0], 1, 0, lat_devices, lon_devices)
     else:
@@ -657,17 +669,27 @@
     )
     gathered = lax.all_to_all(shares, "lon", 0, 0, tiled=True).reshape(3 * third, lanes)
     gathered, finished = lax.optimization_barrier((gathered, finished))
+
+    def write(parts, other, filled=()):
+        count = len(parts)
+        return pl.pallas_call(
+            lambda *refs: weights_kernel(span, other, *refs[: 1 + count], *refs[-4:]),
+            out_shape=(shaped(3 * span, gates, dtype=F32), shaped(1, gates, dtype=F32)),
+            in_specs=[SMEM] + [VMEM] * count + [anywhere] * len(filled),
+            out_specs=(anywhere, VMEM),
+            scratch_shapes=[pltpu.VMEM((3 * span, lanes), F32), pltpu.SemaphoreType.DMA(())],
+            input_output_aliases={1 + count: 0} if filled else {},
+            compiler_params=pltpu.CompilerParams(vmem_limit_bytes=LIMIT),
+            cost_estimate=pl.CostEstimate(
+                flops=0, bytes_accessed=6 * lanes * 3 * third, transcendentals=0
+            ),
+        )(place, *parts, *filled)
+
     hidden_next, cell_grad, cell_next, hidden_grad = finished
-    gathered = (gathered,)
+    weight_grad, bias_grad = write((gathered,), False)
     if halves == 2:
-        gathered += (lax.ppermute(gathered[0], "lat", swap),)
-    weight_grad, bias_grad = call(
-        lambda *refs: weights_kernel(span, *refs),
-        (shaped(3 * span, gates, dtype=F32), shaped(1, gates, dtype=F32)),
-        (place, *gathered),
-        scalars=1,
-        moved=6 * gates * 3 * third,
-    )
+        partner = lax.ppermute(gathered, "lat", swap)
+        weight_grad, bias_grad = write((gathered, partner), True, (weight_grad,))
     return (
         hidden_next,
         cell_next,

time: 62.7 us -> 63.3 us (level)
  Pallas kernels: 17 us -> 19.3 us
  waiting for transfers between devices: 15.9 us -> 14.1 us
    pallas_call x0 -> x2, Pallas kernels: none -> 3.75 us  [write(): pl.pallas_call(lambda *refs: weights_kernel(span, other, *refs[:1 + count...]
    pallas_call x9, Pallas kernels: 16.3 us -> 14.9 us  [call(): pl.pallas_call(run, out_shape=outs, in_specs=[SMEM] * scalars + [VMEM] *...]
    ppermute x1, waiting for transfers between devices: 1.44 us -> 0.01 us  [body(): partner = lax.ppermute(gathered, 'lat', swap)]
  transfers between devices with their start and end apart: 12 -> 12, of which waited for: 6 -> 5; matrix products, arithmetic and copies ran while one was open for 1% -> 1% of each run, Pallas kernels for 13% -> 17%
where the time goes in v7:
time: 63.3 us; the launch traced here: 62.8 us
  starting transfers between devices  26.8 us (42%)
  Pallas kernels  19.3 us (30%)
  waiting for transfers between devices  14.1 us (22%)
  local copies, waits for them, and re-layouts  1.42 us (2%)
  between operations  0.83 us (1%)
    ppermute x8, starting transfers between devices, moved(): return lax.ppermute(values, ('lat', 'lon'), pairs)  15 us
    pallas_call x9, Pallas kernels, call(): pl.pallas_call(run, out_shape=outs, in_specs=[SMEM] * scalars + [VMEM] *...  14.9 us
    ppermute x8, waiting for transfers between devices, moved(): return lax.ppermute(values, ('lat', 'lon'), pairs)  7.62 us
    all_to_all x1, starting transfers between devices, body(): incoming = lax.all_to_all(outgoing, 'lon', 0, 0, tiled=True)  6.89 us
    all_to_all x1, waiting for transfers between devices, body(): lax.all_to_all(shares, 'lon', 0, 0, tiled=True).reshape(3 * third, lanes)  5.31 us
    all_to_all x1, starting transfers between devices, body(): lax.all_to_all(shares, 'lon', 0, 0, tiled=True).reshape(3 * third, lanes)  4.84 us
    pallas_call x2, Pallas kernels, write(): pl.pallas_call(lambda *refs: weights_kernel(span, other, *refs[:1 + count...  3.75 us
    unnamed x10, local copies, waits for them, and re-layouts  1.33 us
  transfers between devices with their start and end apart: 12, of which 5 were waited for; matrix products, arithmetic and copies ran while one was open for 1% of the time, Pallas kernels for 17%

profile of v7, /device:TPU:0, one launch (start us, length us, event | category | flops | bytes accessed | tf_op | source)
XLA Modules:
  0.0 62.8 jit_solution(10250624671859181814)
XLA Ops:
  0.6 0.0 copy-start.1
  0.6 0.0 copy-start.2
  0.7 0.1 pad_add_fusion.refs_0_
  0.7 1.6 %shard_map.136 = (f32[1280,128]{1,0:T(8,128)S(1)}, bf16[80,128]{1,0:T(8,128)(2,1)S(1)}) custom-call(s32[4]{0:T(128)S(1)} %pad_add_fusion.refs_0_, bf16[16,16,128]{2,1,0:T(8,128)(2,1)} %refs_1_.3, bf16[64,16,128]{2,1,0:T(8,128)(2,1)} %refs_2_.4), custom_call_target="tpu_custom_call" | custom-call | bytes 655360 | tf_op jit(solution)/shard_map/pallas_call | solution.py:46
  2.4 0.5 collective-permute-start
  2.9 0.4 shard_map.137
  3.2 0.5 collective-permute-done.refs_0_.refs_1_.refs_4_.refs_5_
  3.7 0.1 shard_map.138
  3.8 2.9 %collective-permute-start.1 = (bf16[80,128]{1,0:T(8,128)(2,1)S(1)}, bf16[80,128]{1,0:T(8,128)(2,1)S(1)}, u32[]{:S(2)}, u32[]{:S(2)}) collective-permute-start(bf16[80,128]{1,0:T(8,128)(2,1)S(1)} %get-tuple-element.50), channel_id=1, source_target_pairs={{0,1},{1,2},{2,3},{3,4},{4,5},{5,6},{6,7},{7,8},{8,9},{9,10},{10,1... | collective-permute-start | bytes 61448 | tf_op jit(solution)/shard_map/ppermute | solution.py:485
  6.7 4.1 %collective-permute-start.2 = (bf16[80,128]{1,0:T(8,128)(2,1)S(1)}, bf16[80,128]{1,0:T(8,128)(2,1)S(1)}, u32[]{:S(2)}, u32[]{:S(2)}) collective-permute-start(bf16[80,128]{1,0:T(8,128)(2,1)S(1)} %get-tuple-element.51), channel_id=1, source_target_pairs={{0,15},{1,0},{2,1},{3,2},{4,3},{5,4},{6,5},{7,6},{8,7},{9,8},{10,9... | collective-permute-start | bytes 61448 | tf_op jit(solution)/shard_map/ppermute | solution.py:485
  10.8 1.8 %shard_map.139 = (bf16[64,2048]{1,0:T(8,128)(2,1)S(1)}, bf16[64,2048]{1,0:T(8,128)(2,1)S(1)}, bf16[64,2048]{1,0:T(8,128)(2,1)S(1)}, bf16[256,768]{1,0:T(8,128)(2,1)S(1)}, f32[256,128]{1,0:T(8,128)S(1)}) custom-call(f32[1,256]{1,0:T(1,128)} %bitcast.17, bf16[720,256]{1,0:T(8,128)(2,1)} %bitcast.14, bf16[64,16,128]{2,1,0:T(8,128)(2,1)} %refs_2_.5, ...), custom_call_target="tpu_custom_call" | custom-call | bytes 1572864 | tf_op jit(solution)/shard_map/pallas_call | solution.py:46
  12.6 0.0 collective-permute-done.1.refs_6_
  12.6 0.0 collective-permute-done.2.refs_7_
  12.6 0.0 copy-done.1
  12.7 0.0 copy-done.2
  12.7 3.1 %shard_map.140 = (bf16[64,2048]{1,0:T(8,128)(2,1)S(1)}, f32[64,2048]{1,0:T(8,128)S(1)}, bf16[8,64,256]{2,1,0:T(8,128)(2,1)S(1)}, f32[768,128]{1,0:T(8,128)S(1)},...) custom-call(s32[4]{0:T(128)S(1)} %pad_add_fusion.refs_0_, s32[1,128]{1,0:T(1,128)S(1)} %copy-done.2, ...), custom_call_target="tpu_custom_call" | custom-call | flops 1509949440 | bytes 2097152 | tf_op jit(solution)/shard_map/pallas_call | solution.py:46
  15.8 0.0 copy-start.3
  15.8 0.1 collective-permute-start.3
  15.9 1.6 %shard_map.141.refs_2_ = bf16[16,176,128]{2,1,0:T(8,128)(2,1)} custom-call(s32[4]{0:T(128)S(1)} %pad_add_fusion.refs_0_, s32[1,128]{1,0:T(1,128)S(1)} %copy-done.2, s32[1,128]{1,0:T(1,128)S(1)} %copy-done.1, bf16[8,64,256]{2,1,0:T(8,128)(2,1)S(1)} %get-tuple-element.59.refs_3_), custom_call_target="tpu_custom_call" | custom-call | bytes 1048576 | tf_op jit(solution)/shard_map/pallas_call | solution.py:46
  17.5 0.1 collective-permute-done.3.refs_1_
  17.6 0.0 copy-start
  17.6 0.7 %shard_map.142 = (bf16[16,176,128]{2,1,0:T(8,128)(2,1)}, f32[8,128]{1,0:T(8,128)S(1)}) custom-call(f32[768,128]{1,0:T(8,128)S(1)} %get-tuple-element.57.refs_0_, f32[768,128]{1,0:T(8,128)S(1)} %collective-permute-done.3.refs_1_, bf16[16,176,128]{2,1,0:T(8,128)(2,1)} %shard_map.141.refs_2_), custom_call_target="tpu_custom_call", output_to_operand_aliasing={{0}: (2, {})} | custom-call | bytes 1572864 | tf_op jit(solution)/shard_map/pallas_call | solution.py:611
  18.3 0.0 copy-done.3
  18.3 6.9 %all-to-all-start = ((bf16[16,176,128]{2,1,0:T(8,128)(2,1)}), bf16[16,176,128]{2,1,0:T(8,128)(2,1)S(1)}, u32[]{:S(2)}, u32[]{:S(2)}) async-start(bf16[16,176,128]{2,1,0:T(8,128)(2,1)} %get-tuple-element.60), calls=%async_computation | async-start | bytes 1441792 | tf_op jit(solution)/shard_map/all_to_all | solution.py:626
  25.2 0.0 copy-done
  25.3 0.0 copy-start.4
  25.3 1.3 %copy-done.4 = bf16[256,2560]{1,0:T(8,128)(2,1)S(1)} copy-done((bf16[256,2560]{1,0:T(8,128)(2,1)S(1)}, bf16[256,2560]{1,0:T(8,128)(2,1)}, u32[]{:S(2)}) %copy-start.4) | copy-done | bytes 1310744
  26.6 2.6 %shard_map.143 = (f32[64,2048]{1,0:T(8,128)S(1)}, bf16[64,128]{1,0:T(8,128)(2,1)S(1)}, bf16[64,128]{1,0:T(8,128)(2,1)S(1)}, bf16[64,128]{1,0:T(8,128)(2,1)S(1)}, bf16[64,128]{1,0:T(8,128)(2,1)S(1)}) custom-call(s32[4]{0:T(128)S(1)} %pad_add_fusion.refs_0_, bf16[256,2560]{1,0:T(8,128)(2,1)S(1)} %copy-done.4, bf16[720,256]{1,0:T(8,128)(2,1)S(1)} %bitcast.15, ...), custom_call_target="tpu_custom_call" | custom-call | flops 603979776 | bytes 4194304 | tf_op jit(solution)/shard_map/pallas_call | solution.py:46
  29.2 0.1 collective-permute-start.4
  29.3 1.9 %collective-permute-start.7 = (bf16[64,128]{1,0:T(8,128)(2,1)S(1)}, bf16[64,128]{1,0:T(8,128)(2,1)S(1)}, u32[]{:S(2)}, u32[]{:S(2)}) collective-permute-start(bf16[64,128]{1,0:T(8,128)(2,1)S(1)} %get-tuple-element.65), channel_id=1, source_target_pairs={{0,1},{1,2},{2,3},{3,4},{4,5},{5,6},{6,7},{7,8},{8,9},{9,10},{10,1... | collective-permute-start | bytes 49160 | tf_op jit(solution)/shard_map/ppermute | solution.py:485
  31.2 3.7 %collective-permute-start.8 = (bf16[64,128]{1,0:T(8,128)(2,1)S(1)}, bf16[64,128]{1,0:T(8,128)(2,1)S(1)}, u32[]{:S(2)}, u32[]{:S(2)}) collective-permute-start(bf16[64,128]{1,0:T(8,128)(2,1)S(1)} %get-tuple-element.66), channel_id=1, source_target_pairs={{0,15},{1,0},{2,1},{3,2},{4,3},{5,4},{6,5},{7,6},{8,7},{9,8},{10,9... | collective-permute-start | bytes 49160 | tf_op jit(solution)/shard_map/ppermute | solution.py:485
  35.0 1.4 %collective-permute-start.6 = (bf16[64,128]{1,0:T(8,128)(2,1)S(1)}, bf16[64,128]{1,0:T(8,128)(2,1)S(1)}, u32[]{:S(2)}, u32[]{:S(2)}) collective-permute-start(bf16[64,128]{1,0:T(8,128)(2,1)S(1)} %get-tuple-element.64), channel_id=1, source_target_pairs={{0,31},{1,16},{2,17},{3,18},{4,19},{5,20},{6,21},{7,22},{8,23},{9,... | collective-permute-start | bytes 49160 | tf_op jit(solution)/shard_map/ppermute | solution.py:485
  36.4 0.3 collective-permute-start.5
  36.7 0.0 collective-permute-done.4.refs_2_.refs_3_.refs_6_.refs_7_
  36.7 7.1 %collective-permute-done.7.refs_8_.refs_12_ = bf16[64,128]{1,0:T(8,128)(2,1)S(1)} collective-permute-done((bf16[64,128]{1,0:T(8,128)(2,1)S(1)}, bf16[64,128]{1,0:T(8,128)(2,1)S(1)}, u32[]{:S(2)}, u32[]{:S(2)}) %collective-permute-start.7) | collective-permute-done | bytes 16416 | tf_op jit(solution)/shard_map/ppermute | solution.py:485
  43.8 0.0 collective-permute-done.8.refs_9_.refs_13_
  43.8 0.0 collective-permute-done.6.refs_5_.refs_7_.refs_9_.refs_11_
  43.8 0.0 collective-permute-done.5.refs_4_.refs_6_.refs_8_.refs_10_
  43.8 1.0 %all-to-all-done.refs_1_.refs_4_ = bf16[16,176,128]{2,1,0:T(8,128)(2,1)S(1)} async-done(((bf16[16,176,128]{2,1,0:T(8,128)(2,1)}), bf16[16,176,128]{2,1,0:T(8,128)(2,1)S(1)}, u32[]{:S(2)}, u32[]{:S(2)}) %all-to-all-start) | async-done | bytes 720928 | tf_op jit(solution)/shard_map/all_to_all | solution.py:626
  44.9 1.3 %shard_map.144 = (bf16[16,48,128]{2,1,0:T(8,128)(2,1)}, f32[8,128]{1,0:T(8,128)S(1)}) custom-call(s32[4]{0:T(128)S(1)} %pad_add_fusion.refs_0_, bf16[16,176,128]{2,1,0:T(8,128)(2,1)S(1)} %all-to-all-done.refs_1_.refs_4_, bf16[64,128]{1,0:T(8,128)(2,1)S(1)} %collective-permute-done.4.refs_2_.refs_3_.refs_6_.refs_7_, ...), custom_call_target="tpu_custom_call" | custom-call | bytes 393216 | tf_op jit(solution)/shard_map/pallas_call | solution.py:46
  46.2 4.8 %all-to-all-start.1 = ((bf16[16,48,128]{2,1,0:T(8,128)(2,1)}), bf16[16,48,128]{2,1,0:T(8,128)(2,1)S(1)}, u32[]{:S(2)}, u32[]{:S(2)}) async-start(bf16[16,48,128]{2,1,0:T(8,128)(2,1)} %get-tuple-element.67), calls=%async_computation.1 | async-start | bytes 393216 | tf_op jit(solution)/shard_map/all_to_all | solution.py:670
  51.0 0.1 reshape.35
  51.1 0.1 reduce_or.9
  51.2 0.1 convert_reduce_fusion
  51.3 0.1 select_reduce_fusion.refs_1_
  51.5 2.3 %shard_map.145 = (bf16[64,16,128]{2,1,0:T(8,128)(2,1)}, f32[1024,128]{1,0:T(8,128)}, f32[4,64,256]{2,1,0:T(8,128)}, f32[1024,128]{1,0:T(8,128)}) custom-call(s32[4]{0:T(128)S(1)} %pad_add_fusion.refs_0_, s32[4]{0:T(128)S(1)} %select_reduce_fusion.refs_1_, bf16[64,2048]{1,0:T(8,128)(2,1)S(1)} %get-tuple-element.68.refs_2_, ...), custom_call_target="tpu_custom_call" | custom-call | bytes 4194304 | tf_op jit(solution)/shard_map/pallas_call | solution.py:46
  53.8 5.3 %all-to-all-done.1 = bf16[16,48,128]{2,1,0:T(8,128)(2,1)S(1)} async-done(((bf16[16,48,128]{2,1,0:T(8,128)(2,1)}), bf16[16,48,128]{2,1,0:T(8,128)(2,1)S(1)}, u32[]{:S(2)}, u32[]{:S(2)}) %all-to-all-start.1) | async-done | bytes 196640 | tf_op jit(solution)/shard_map/all_to_all | solution.py:670
  59.1 0.0 collective-permute-start.9
  59.1 1.9 %shard_map.146 = (f32[720,256]{1,0:T(8,128)}, f32[1,256]{1,0:T(1,128)}) custom-call(s32[4]{0:T(128)S(1)} %pad_add_fusion.refs_0_, bf16[768,128]{1,0:T(8,128)(2,1)S(1)} %bitcast.12), custom_call_target="tpu_custom_call" | custom-call | bytes 589824 | tf_op jit(solution)/shard_map/pallas_call | solution.py:675
  61.0 0.0 collective-permute-done.9.refs_2_
  61.0 1.9 %shard_map.147 = (f32[720,256]{1,0:T(8,128)}, f32[1,256]{1,0:T(1,128)}) custom-call(s32[4]{0:T(128)S(1)} %pad_add_fusion.refs_0_, bf16[768,128]{1,0:T(8,128)(2,1)S(1)} %bitcast.13, bf16[768,128]{1,0:T(8,128)(2,1)S(1)} %collective-permute-done.9.refs_2_, f32[720,256]{1,0:T(8,128)} %get-tuple-element.81.refs_3_), custom_call_target="tpu_custom_call", output_to_operand_aliasing={{0}: (3, {})} | custom-call | bytes 589824 | tf_op jit(solution)/shard_map/pallas_call | solution.py:675
  (1 shorter events, 0.0 us)
Async XLA Ops:
  0.6 12.0 %copy-start.1 = (s32[1,128]{1,0:T(1,128)S(1)}, s32[1,128]{1,0:T(1,128)}, u32[]{:S(2)}) copy-start(s32[1,128]{1,0:T(1,128)} %refs_2_.7) | copy-start | bytes 1540
  0.6 12.0 %copy-start.2 = (s32[1,128]{1,0:T(1,128)S(1)}, s32[1,128]{1,0:T(1,128)}, u32[]{:S(2)}) copy-start(s32[1,128]{1,0:T(1,128)} %refs_1_.5) | copy-start | bytes 1540
  2.4 1.4 %collective-permute-start = (bf16[80,128]{1,0:T(8,128)(2,1)S(1)}, bf16[80,128]{1,0:T(8,128)(2,1)S(1)}, u32[]{:S(2)}, u32[]{:S(2)}) collective-permute-start(bf16[80,128]{1,0:T(8,128)(2,1)S(1)} %get-tuple-element.47), channel_id=1, source_target_pairs={{0,16},{1,17},{2,18},{3,19},{4,20},{5,21},{6,22},{7,23},{8,24},{9,... | collective-permute-start | bytes 61448 | tf_op jit(solution)/shard_map/ppermute | solution.py:485
  3.8 8.8 %collective-permute-start.1 = (bf16[80,128]{1,0:T(8,128)(2,1)S(1)}, bf16[80,128]{1,0:T(8,128)(2,1)S(1)}, u32[]{:S(2)}, u32[]{:S(2)}) collective-permute-start(bf16[80,128]{1,0:T(8,128)(2,1)S(1)} %get-tuple-element.50), channel_id=1, source_target_pairs={{0,1},{1,2},{2,3},{3,4},{4,5},{5,6},{6,7},{7,8},{8,9},{9,10},{10,1... | collective-permute-start | bytes 61448 | tf_op jit(solution)/shard_map/ppermute | solution.py:485
  6.7 5.9 %collective-permute-start.2 = (bf16[80,128]{1,0:T(8,128)(2,1)S(1)}, bf16[80,128]{1,0:T(8,128)(2,1)S(1)}, u32[]{:S(2)}, u32[]{:S(2)}) collective-permute-start(bf16[80,128]{1,0:T(8,128)(2,1)S(1)} %get-tuple-element.51), channel_id=1, source_target_pairs={{0,15},{1,0},{2,1},{3,2},{4,3},{5,4},{6,5},{7,6},{8,7},{9,8},{10,9... | collective-permute-start | bytes 61448 | tf_op jit(solution)/shard_map/ppermute | solution.py:485
  15.8 2.5 %copy-start.3 = (bf16[256,2560]{1,0:T(8,128)(2,1)}, bf16[256,2560]{1,0:T(8,128)(2,1)S(1)}, u32[]{:S(2)}) copy-start(bf16[256,2560]{1,0:T(8,128)(2,1)S(1)} %get-tuple-element.61.refs_1_) | copy-start | bytes 3932164
  15.8 1.8 %collective-permute-start.3 = (f32[768,128]{1,0:T(8,128)S(1)}, f32[768,128]{1,0:T(8,128)S(1)}, u32[]{:S(2)}, u32[]{:S(2)}) collective-permute-start(f32[768,128]{1,0:T(8,128)S(1)} %get-tuple-element.58), channel_id=1, source_target_pairs={{0,16},{16,0},{1,17},{17,1},{2,18},{18,2},{3,19},{19,3},{4,20},{20... | collective-permute-start | bytes 1179656 | tf_op jit(solution)/shard_map/ppermute | solution.py:597
  17.6 7.6 %copy-start = (bf16[256,720]{0,1:T(8,128)(2,1)S(1)}, bf16[256,720]{0,1:T(8,128)(2,1)}, u32[]{:S(2)}) copy-start(bf16[256,720]{0,1:T(8,128)(2,1)} %param.16) | copy-start | bytes 1105924
  18.3 26.5 %all-to-all-start = ((bf16[16,176,128]{2,1,0:T(8,128)(2,1)}), bf16[16,176,128]{2,1,0:T(8,128)(2,1)S(1)}, u32[]{:S(2)}, u32[]{:S(2)}) async-start(bf16[16,176,128]{2,1,0:T(8,128)(2,1)} %get-tuple-element.60), calls=%async_computation | async-start | bytes 1441792 | tf_op jit(solution)/shard_map/all_to_all | solution.py:626
  25.3 1.3 %copy-start.4 = (bf16[256,2560]{1,0:T(8,128)(2,1)S(1)}, bf16[256,2560]{1,0:T(8,128)(2,1)}, u32[]{:S(2)}) copy-start(bf16[256,2560]{1,0:T(8,128)(2,1)} %copy-done.3) | copy-start | bytes 3932164
  29.2 7.5 %collective-permute-start.4 = (bf16[64,128]{1,0:T(8,128)(2,1)S(1)}, bf16[64,128]{1,0:T(8,128)(2,1)S(1)}, u32[]{:S(2)}, u32[]{:S(2)}) collective-permute-start(bf16[64,128]{1,0:T(8,128)(2,1)S(1)} %get-tuple-element.63), channel_id=1, source_target_pairs={{0,16},{1,17},{2,18},{3,19},{4,20},{5,21},{6,22},{7,23},{8,24},{9,... | collective-permute-start | bytes 49160 | tf_op jit(solution)/shard_map/ppermute | solution.py:485
  29.3 14.5 %collective-permute-start.7 = (bf16[64,128]{1,0:T(8,128)(2,1)S(1)}, bf16[64,128]{1,0:T(8,128)(2,1)S(1)}, u32[]{:S(2)}, u32[]{:S(2)}) collective-permute-start(bf16[64,128]{1,0:T(8,128)(2,1)S(1)} %get-tuple-element.65), channel_id=1, source_target_pairs={{0,1},{1,2},{2,3},{3,4},{4,5},{5,6},{6,7},{7,8},{8,9},{9,10},{10,1... | collective-permute-start | bytes 49160 | tf_op jit(solution)/shard_map/ppermute | solution.py:485
  31.2 12.6 %collective-permute-start.8 = (bf16[64,128]{1,0:T(8,128)(2,1)S(1)}, bf16[64,128]{1,0:T(8,128)(2,1)S(1)}, u32[]{:S(2)}, u32[]{:S(2)}) collective-permute-start(bf16[64,128]{1,0:T(8,128)(2,1)S(1)} %get-tuple-element.66), channel_id=1, source_target_pairs={{0,15},{1,0},{2,1},{3,2},{4,3},{5,4},{6,5},{7,6},{8,7},{9,8},{10,9... | collective-permute-start | bytes 49160 | tf_op jit(solution)/shard_map/ppermute | solution.py:485
  35.0 8.9 %collective-permute-start.6 = (bf16[64,128]{1,0:T(8,128)(2,1)S(1)}, bf16[64,128]{1,0:T(8,128)(2,1)S(1)}, u32[]{:S(2)}, u32[]{:S(2)}) collective-permute-start(bf16[64,128]{1,0:T(8,128)(2,1)S(1)} %get-tuple-element.64), channel_id=1, source_target_pairs={{0,31},{1,16},{2,17},{3,18},{4,19},{5,20},{6,21},{7,22},{8,23},{9,... | collective-permute-start | bytes 49160 | tf_op jit(solution)/shard_map/ppermute | solution.py:485
  36.4 7.5 %collective-permute-start.5 = (bf16[64,128]{1,0:T(8,128)(2,1)S(1)}, bf16[64,128]{1,0:T(8,128)(2,1)S(1)}, u32[]{:S(2)}, u32[]{:S(2)}) collective-permute-start(bf16[64,128]{1,0:T(8,128)(2,1)S(1)} %get-tuple-element.64), channel_id=1, source_target_pairs={{0,17},{1,18},{2,19},{3,20},{4,21},{5,22},{6,23},{7,24},{8,25},{9,... | collective-permute-start | bytes 49160 | tf_op jit(solution)/shard_map/ppermute | solution.py:485
  46.2 12.9 %all-to-all-start.1 = ((bf16[16,48,128]{2,1,0:T(8,128)(2,1)}), bf16[16,48,128]{2,1,0:T(8,128)(2,1)S(1)}, u32[]{:S(2)}, u32[]{:S(2)}) async-start(bf16[16,48,128]{2,1,0:T(8,128)(2,1)} %get-tuple-element.67), calls=%async_computation.1 | async-start | bytes 393216 | tf_op jit(solution)/shard_map/all_to_all | solution.py:670
  59.1 1.9 %collective-permute-start.9 = (bf16[768,128]{1,0:T(8,128)(2,1)S(1)}, bf16[768,128]{1,0:T(8,128)(2,1)S(1)}, u32[]{:S(2)}, u32[]{:S(2)}) collective-permute-start(bf16[768,128]{1,0:T(8,128)(2,1)S(1)} %bitcast.11), channel_id=1, source_target_pairs={{0,16},{16,0},{1,17},{17,1},{2,18},{18,2},{3,19},{19,3},{4,20},{20... | collective-permute-start | bytes 589832 | tf_op jit(solution)/shard_map/ppermute | solution.py:691

commit v8 on v7

--- a/solution.py
+++ b/solution.py
@@ -214,6 +214,19 @@
     bias = jnp.concatenate([b_ref[...]] * step, 1)
     group = 128 // TILE
     states = []
+    late = (rows // step // 2) * step
+
+    def product(first, count):
+        return [
+            lax.dot_general(
+                taps_ref[:, (first + row_off) * width : (first + row_off + count) * width],
+                delta_ref[:, (first + 2) * width : (first + 2 + count) * width],
+                (((1,), (1,)), ((), ())),
+                preferred_element_type=F32,
+            )
+            for row_off in range(3)
+        ]
+
     for start in range(0, rows, step):
         pre = bias
         for row_off in range(3):
@@ -245,6 +258,8 @@
         low = (start + 2) * width
         for index, term in enumerate(terms):
             delta_ref[index * hid : (index + 1) * hid, low : low + chunk] = term.astype(BF16)
+        if start + step == rows - late:
+            products = product(0, rows - late)
         hidden_new_ref[:, lanes] = hidden_new.astype(BF16)
         cell_back_ref[:, lanes] = cell_back
         for part in range(step):
@@ -271,14 +286,8 @@
             for tile in range(tile_cols):
                 tiles_ref[tile, :, half * 128 : (half + 1) * 128] = states[tile].astype(BF16)
             states = []
-    delta = delta_ref[:, 2 * width : (rows + 2) * width]
-    for row_off in range(3):
-        part = lax.dot_general(
-            taps_ref[:, row_off * width : (row_off + rows) * width],
-            delta,
-            (((1,), (1,)), ((), ())),
-            preferred_element_type=F32,
-        )
+    products = [first + second for first, second in zip(products, product(rows - late, late))]
+    for row_off, part in enumerate(products):
         place = slice(row_off * third, (row_off + 1) * third)
         if len(weight_refs) == 1:
             weight_refs[0][place] = part
@@ -448,28 +457,32 @@
         out_ref[index] = total.astype(BF16)
 
 
-def weights_kernel(span, other, place_ref, *refs):
-    *parts, weight_ref, bias_ref, block_ref, semaphore = refs
-    pick_ref = parts[1] if other else parts[0]
-    third = pick_ref.shape[0] // 3
-    half = pick_ref.shape[1]
+def weights_kernel(span, count, place_ref, *refs):
+    parts = refs[:count]
+    weight_ref, bias_ref, block_ref, semaphores = refs[count:]
+    third = parts[0].shape[0] // 3
+    half = parts[0].shape[1]
+    copies = []
     for index in range(3):
-        block_ref[index * span : (index + 1) * span] = pick_ref[
-            index * third : index * third + span
-        ].astype(F32)
-    lanes = slice(None)
-    if weight_ref.shape[1] > half:
-        side = 1 - place_ref[0] if other else place_ref[0]
-        lanes = pl.ds(pl.multiple_of(side * half, half), half)
-    copy = pltpu.make_async_copy(block_ref, weight_ref.at[:, lanes], semaphore)
-    copy.start()
-    halves = weight_ref.shape[1] // half
-    for side in range(halves):
-        rows = parts[0][span:third].astype(F32)
-        if other:
-            rows = jnp.where(place_ref[0] == side, rows, parts[1][span:third].astype(F32))
-        bias_ref[:, side * half : (side + 1) * half] = rows[0:1] + rows[1:2]
-    copy.wait()
+        rows = slice(index * span, (index + 1) * span)
+        for side in range(count):
+            pick = parts[0][index * third : index * third + span]
+            if count == 2:
+                other = parts[1][index * third : index * third + span]
+                pick = jnp.where(place_ref[0] == side, pick.astype(F32), other.astype(F32))
+            block_ref[rows, side * half : (side + 1) * half] = pick.astype(F32)
+        copy = pltpu.make_async_copy(
+            block_ref.at[rows], weight_ref.at[rows], semaphores.at[index]
+        )
+        copy.start()
+        copies.append(copy)
+    for side in range(count):
+        pair = parts[0][span:third].astype(F32)
+        if count == 2:
+            pair = jnp.where(place_ref[0] == side, pair, parts[1][span:third].astype(F32))
+        bias_ref[:, side * half : (side + 1) * half] = pair[0:1] + pair[1:2]
+    for copy in copies:
+        copy.wait()
 
 
 def moved(values, lat_step, lon_step, lat_devices, lon_devices):
@@ -670,26 +683,21 @@
     gathered = lax.all_to_all(shares, "lon", 0, 0, tiled=True).reshape(3 * third, lanes)
     gathered, finished = lax.optimization_barrier((gathered, finished))
 
-    def write(parts, other, filled=()):
-        count = len(parts)
-        return pl.pallas_call(
-            lambda *refs: weights_kernel(span, other, *refs[: 1 + count], *refs[-4:]),
-            out_shape=(shaped(3 * span, gates, dtype=F32), shaped(1, gates, dtype=F32)),
-            in_specs=[SMEM] + [VMEM] * count + [anywhere] * len(filled),
-            out_specs=(anywhere, VMEM),
-            scratch_shapes=[pltpu.VMEM((3 * span, lanes), F32), pltpu.SemaphoreType.DMA(())],
-            input_output_aliases={1 + count: 0} if filled else {},
-            compiler_params=pltpu.CompilerParams(vmem_limit_bytes=LIMIT),
-            cost_estimate=pl.CostEstimate(
-                flops=0, bytes_accessed=6 * lanes * 3 * third, transcendentals=0
-            ),
-        )(place, *parts, *filled)
-
     hidden_next, cell_grad, cell_next, hidden_grad = finished
-    weight_grad, bias_grad = write((gathered,), False)
+    gathered = (gathered,)
     if halves == 2:
-        partner = lax.ppermute(gathered, "lat", swap)
-        weight_grad, bias_grad = write((gathered, partner), True, (weight_grad,))
+        gathered += (lax.ppermute(gathered[0], "lat", swap),)
+    weight_grad, bias_grad = pl.pallas_call(
+        lambda *refs: weights_kernel(span, count, *refs),
+        out_shape=(shaped(3 * span, gates, dtype=F32), shaped(1, gates, dtype=F32)),
+        in_specs=[SMEM] + [VMEM] * count,
+        out_specs=(anywhere, VMEM),
+        scratch_shapes=[pltpu.VMEM((3 * span, gates), F32), pltpu.SemaphoreType.DMA((3,))],
+        compiler_params=pltpu.CompilerParams(vmem_limit_bytes=LIMIT),
+        cost_estimate=pl.CostEstimate(
+            flops=0, bytes_accessed=6 * gates * 3 * third, transcendentals=0
+        ),
+    )(place, *gathered)
     return (
         hidden_next,
         cell_next,

time: 63.3 us -> 63.2 us (level)
  Pallas kernels: 19.3 us -> 17.8 us
  waiting for transfers between devices: 14.1 us -> 15.4 us
    pallas_call x2 -> x1, Pallas kernels: 3.75 us -> 2.01 us  [body(): pl.pallas_call(lambda *refs: weights_kernel(span, count, *refs), out_shap...]
    ppermute x1, waiting for transfers between devices: 0.01 us -> 1.44 us  [body(): gathered += (lax.ppermute(gathered[0], 'lat', swap),)]
  transfers between devices with their start and end apart: 12 -> 12, of which waited for: 5 -> 6; matrix products, arithmetic and copies ran while one was open for 1% -> 1% of each run, Pallas kernels for 17% -> 14%
where the time goes in v8:
time: 63.2 us; the launch traced here: 62.8 us
  starting transfers between devices  26.9 us (43%)
  Pallas kernels  17.8 us (28%)
  waiting for transfers between devices  15.4 us (24%)
  local copies, waits for them, and re-layouts  1.42 us (2%)
  between operations  0.82 us (1%)
    ppermute x8, starting transfers between devices, moved(): return lax.ppermute(values, ('lat', 'lon'), pairs)  15.1 us
    pallas_call x9, Pallas kernels, call(): pl.pallas_call(run, out_shape=outs, in_specs=[SMEM] * scalars + [VMEM] *...  15 us
    ppermute x8, waiting for transfers between devices, moved(): return lax.ppermute(values, ('lat', 'lon'), pairs)  7.6 us
    all_to_all x1, starting transfers between devices, body(): incoming = lax.all_to_all(outgoing, 'lon', 0, 0, tiled=True)  6.87 us
    all_to_all x1, waiting for transfers between devices, body(): lax.all_to_all(shares, 'lon', 0, 0, tiled=True).reshape(3 * third, lanes)  5.31 us
    all_to_all x1, starting transfers between devices, body(): lax.all_to_all(shares, 'lon', 0, 0, tiled=True).reshape(3 * third, lanes)  4.94 us
    pallas_call x1, Pallas kernels, body(): pl.pallas_call(lambda *refs: weights_kernel(span, count, *refs), out_shap...  2.01 us
    ppermute x1, waiting for transfers between devices, body(): gathered += (lax.ppermute(gathered[0], 'lat', swap),)  1.44 us
  transfers between devices with their start and end apart: 12, of which 6 were waited for; matrix products, arithmetic and copies ran while one was open for 1% of the time, Pallas kernels for 14%

profile of v8, /device:TPU:0, one launch (start us, length us, event | category | flops | bytes accessed | tf_op | source)
XLA Modules:
  0.0 62.8 jit_solution(13129633185184265927)
XLA Ops:
  0.6 0.0 copy-start.1
  0.6 0.0 copy-start.2
  0.7 0.1 pad_add_fusion.refs_0_
  0.7 1.6 %shard_map.136 = (f32[1280,128]{1,0:T(8,128)S(1)}, bf16[80,128]{1,0:T(8,128)(2,1)S(1)}) custom-call(s32[4]{0:T(128)S(1)} %pad_add_fusion.refs_0_, bf16[16,16,128]{2,1,0:T(8,128)(2,1)} %refs_1_.3, bf16[64,16,128]{2,1,0:T(8,128)(2,1)} %refs_2_.4), custom_call_target="tpu_custom_call" | custom-call | bytes 655360 | tf_op jit(solution)/shard_map/pallas_call | solution.py:46
  2.4 0.5 collective-permute-start
  2.9 0.4 shard_map.137
  3.2 0.5 collective-permute-done.refs_0_.refs_1_.refs_4_.refs_5_
  3.7 0.1 shard_map.138
  3.8 2.9 %collective-permute-start.1 = (bf16[80,128]{1,0:T(8,128)(2,1)S(1)}, bf16[80,128]{1,0:T(8,128)(2,1)S(1)}, u32[]{:S(2)}, u32[]{:S(2)}) collective-permute-start(bf16[80,128]{1,0:T(8,128)(2,1)S(1)} %get-tuple-element.49), channel_id=1, source_target_pairs={{0,1},{1,2},{2,3},{3,4},{4,5},{5,6},{6,7},{7,8},{8,9},{9,10},{10,1... | collective-permute-start | bytes 61448 | tf_op jit(solution)/shard_map/ppermute | solution.py:498
  6.7 4.1 %collective-permute-start.2 = (bf16[80,128]{1,0:T(8,128)(2,1)S(1)}, bf16[80,128]{1,0:T(8,128)(2,1)S(1)}, u32[]{:S(2)}, u32[]{:S(2)}) collective-permute-start(bf16[80,128]{1,0:T(8,128)(2,1)S(1)} %get-tuple-element.50), channel_id=1, source_target_pairs={{0,15},{1,0},{2,1},{3,2},{4,3},{5,4},{6,5},{7,6},{8,7},{9,8},{10,9... | collective-permute-start | bytes 61448 | tf_op jit(solution)/shard_map/ppermute | solution.py:498
  10.8 1.8 %shard_map.139 = (bf16[64,2048]{1,0:T(8,128)(2,1)S(1)}, bf16[64,2048]{1,0:T(8,128)(2,1)S(1)}, bf16[64,2048]{1,0:T(8,128)(2,1)S(1)}, bf16[256,768]{1,0:T(8,128)(2,1)S(1)}, f32[256,128]{1,0:T(8,128)S(1)}) custom-call(f32[1,256]{1,0:T(1,128)} %bitcast.15, bf16[720,256]{1,0:T(8,128)(2,1)} %bitcast.13, bf16[64,16,128]{2,1,0:T(8,128)(2,1)} %refs_2_.5, ...), custom_call_target="tpu_custom_call" | custom-call | bytes 1572864 | tf_op jit(solution)/shard_map/pallas_call | solution.py:46
  12.6 0.0 collective-permute-done.1.refs_6_
  12.6 0.0 collective-permute-done.2.refs_7_
  12.6 0.0 copy-done.1
  12.7 0.0 copy-done.2
  12.7 3.3 %shard_map.140 = (bf16[64,2048]{1,0:T(8,128)(2,1)S(1)}, f32[64,2048]{1,0:T(8,128)S(1)}, bf16[8,64,256]{2,1,0:T(8,128)(2,1)S(1)}, f32[768,128]{1,0:T(8,128)S(1)},...) custom-call(s32[4]{0:T(128)S(1)} %pad_add_fusion.refs_0_, s32[1,128]{1,0:T(1,128)S(1)} %copy-done.2, ...), custom_call_target="tpu_custom_call" | custom-call | flops 1509949440 | bytes 2097152 | tf_op jit(solution)/shard_map/pallas_call | solution.py:46
  16.0 0.0 copy-start.3
  16.0 0.1 collective-permute-start.3
  16.1 1.6 %shard_map.141.refs_2_ = bf16[16,176,128]{2,1,0:T(8,128)(2,1)} custom-call(s32[4]{0:T(128)S(1)} %pad_add_fusion.refs_0_, s32[1,128]{1,0:T(1,128)S(1)} %copy-done.2, s32[1,128]{1,0:T(1,128)S(1)} %copy-done.1, bf16[8,64,256]{2,1,0:T(8,128)(2,1)S(1)} %get-tuple-element.58.refs_3_), custom_call_target="tpu_custom_call" | custom-call | bytes 1048576 | tf_op jit(solution)/shard_map/pallas_call | solution.py:46
  17.7 0.1 collective-permute-done.3.refs_1_
  17.8 0.0 copy-start
  17.8 0.7 %shard_map.142 = (bf16[16,176,128]{2,1,0:T(8,128)(2,1)}, f32[8,128]{1,0:T(8,128)S(1)}) custom-call(f32[768,128]{1,0:T(8,128)S(1)} %get-tuple-element.56.refs_0_, f32[768,128]{1,0:T(8,128)S(1)} %collective-permute-done.3.refs_1_, bf16[16,176,128]{2,1,0:T(8,128)(2,1)} %shard_map.141.refs_2_), custom_call_target="tpu_custom_call", output_to_operand_aliasing={{0}: (2, {})} | custom-call | bytes 1572864 | tf_op jit(solution)/shard_map/pallas_call | solution.py:624
  18.5 0.0 copy-done.3
  18.6 6.9 %all-to-all-start = ((bf16[16,176,128]{2,1,0:T(8,128)(2,1)}), bf16[16,176,128]{2,1,0:T(8,128)(2,1)S(1)}, u32[]{:S(2)}, u32[]{:S(2)}) async-start(bf16[16,176,128]{2,1,0:T(8,128)(2,1)} %get-tuple-element.59), calls=%async_computation | async-start | bytes 1441792 | tf_op jit(solution)/shard_map/all_to_all | solution.py:639
  25.4 0.0 copy-done
  25.4 0.0 copy-start.4
  25.5 1.3 %copy-done.4 = bf16[256,2560]{1,0:T(8,128)(2,1)S(1)} copy-done((bf16[256,2560]{1,0:T(8,128)(2,1)S(1)}, bf16[256,2560]{1,0:T(8,128)(2,1)}, u32[]{:S(2)}) %copy-start.4) | copy-done | bytes 1310744
  26.8 2.6 %shard_map.143 = (f32[64,2048]{1,0:T(8,128)S(1)}, bf16[64,128]{1,0:T(8,128)(2,1)S(1)}, bf16[64,128]{1,0:T(8,128)(2,1)S(1)}, bf16[64,128]{1,0:T(8,128)(2,1)S(1)}, bf16[64,128]{1,0:T(8,128)(2,1)S(1)}) custom-call(s32[4]{0:T(128)S(1)} %pad_add_fusion.refs_0_, bf16[256,2560]{1,0:T(8,128)(2,1)S(1)} %copy-done.4, bf16[720,256]{1,0:T(8,128)(2,1)S(1)} %bitcast.14, ...), custom_call_target="tpu_custom_call" | custom-call | flops 603979776 | bytes 4194304 | tf_op jit(solution)/shard_map/pallas_call | solution.py:46
  29.4 0.2 collective-permute-start.4
  29.6 1.8 %collective-permute-start.7 = (bf16[64,128]{1,0:T(8,128)(2,1)S(1)}, bf16[64,128]{1,0:T(8,128)(2,1)S(1)}, u32[]{:S(2)}, u32[]{:S(2)}) collective-permute-start(bf16[64,128]{1,0:T(8,128)(2,1)S(1)} %get-tuple-element.64), channel_id=1, source_target_pairs={{0,1},{1,2},{2,3},{3,4},{4,5},{5,6},{6,7},{7,8},{8,9},{9,10},{10,1... | collective-permute-start | bytes 49160 | tf_op jit(solution)/shard_map/ppermute | solution.py:498
  31.4 3.8 %collective-permute-start.8 = (bf16[64,128]{1,0:T(8,128)(2,1)S(1)}, bf16[64,128]{1,0:T(8,128)(2,1)S(1)}, u32[]{:S(2)}, u32[]{:S(2)}) collective-permute-start(bf16[64,128]{1,0:T(8,128)(2,1)S(1)} %get-tuple-element.65), channel_id=1, source_target_pairs={{0,15},{1,0},{2,1},{3,2},{4,3},{5,4},{6,5},{7,6},{8,7},{9,8},{10,9... | collective-permute-start | bytes 49160 | tf_op jit(solution)/shard_map/ppermute | solution.py:498
  35.2 1.3 %collective-permute-start.6 = (bf16[64,128]{1,0:T(8,128)(2,1)S(1)}, bf16[64,128]{1,0:T(8,128)(2,1)S(1)}, u32[]{:S(2)}, u32[]{:S(2)}) collective-permute-start(bf16[64,128]{1,0:T(8,128)(2,1)S(1)} %get-tuple-element.63), channel_id=1, source_target_pairs={{0,31},{1,16},{2,17},{3,18},{4,19},{5,20},{6,21},{7,22},{8,23},{9,... | collective-permute-start | bytes 49160 | tf_op jit(solution)/shard_map/ppermute | solution.py:498
  36.6 0.4 collective-permute-start.5
  37.0 0.0 collective-permute-done.4.refs_2_.refs_3_.refs_6_.refs_7_
  37.0 7.1 %collective-permute-done.7.refs_8_.refs_12_ = bf16[64,128]{1,0:T(8,128)(2,1)S(1)} collective-permute-done((bf16[64,128]{1,0:T(8,128)(2,1)S(1)}, bf16[64,128]{1,0:T(8,128)(2,1)S(1)}, u32[]{:S(2)}, u32[]{:S(2)}) %collective-permute-start.7) | collective-permute-done | bytes 16416 | tf_op jit(solution)/shard_map/ppermute | solution.py:498
  44.1 0.0 collective-permute-done.8.refs_9_.refs_13_
  44.1 0.0 collective-permute-done.6.refs_5_.refs_7_.refs_9_.refs_11_
  44.1 0.0 collective-permute-done.5.refs_4_.refs_6_.refs_8_.refs_10_
  44.1 1.0 %all-to-all-done.refs_1_.refs_4_ = bf16[16,176,128]{2,1,0:T(8,128)(2,1)S(1)} async-done(((bf16[16,176,128]{2,1,0:T(8,128)(2,1)}), bf16[16,176,128]{2,1,0:T(8,128)(2,1)S(1)}, u32[]{:S(2)}, u32[]{:S(2)}) %all-to-all-start) | async-done | bytes 720928 | tf_op jit(solution)/shard_map/all_to_all | solution.py:639
  45.1 1.3 %shard_map.144 = (bf16[16,48,128]{2,1,0:T(8,128)(2,1)}, f32[8,128]{1,0:T(8,128)S(1)}) custom-call(s32[4]{0:T(128)S(1)} %pad_add_fusion.refs_0_, bf16[16,176,128]{2,1,0:T(8,128)(2,1)S(1)} %all-to-all-done.refs_1_.refs_4_, bf16[64,128]{1,0:T(8,128)(2,1)S(1)} %collective-permute-done.4.refs_2_.refs_3_.refs_6_.refs_7_, ...), custom_call_target="tpu_custom_call" | custom-call | bytes 393216 | tf_op jit(solution)/shard_map/pallas_call | solution.py:46
  46.3 4.9 %all-to-all-start.1 = ((bf16[16,48,128]{2,1,0:T(8,128)(2,1)}), bf16[16,48,128]{2,1,0:T(8,128)(2,1)S(1)}, u32[]{:S(2)}, u32[]{:S(2)}) async-start(bf16[16,48,128]{2,1,0:T(8,128)(2,1)} %get-tuple-element.66), calls=%async_computation.1 | async-start | bytes 393216 | tf_op jit(solution)/shard_map/all_to_all | solution.py:683
  51.3 0.1 reshape.35
  51.4 0.1 reduce_or.9
  51.5 0.1 convert_reduce_fusion
  51.6 0.1 select_reduce_fusion.refs_1_
  51.7 2.3 %shard_map.145 = (bf16[64,16,128]{2,1,0:T(8,128)(2,1)}, f32[1024,128]{1,0:T(8,128)}, f32[4,64,256]{2,1,0:T(8,128)}, f32[1024,128]{1,0:T(8,128)}) custom-call(s32[4]{0:T(128)S(1)} %pad_add_fusion.refs_0_, s32[4]{0:T(128)S(1)} %select_reduce_fusion.refs_1_, bf16[64,2048]{1,0:T(8,128)(2,1)S(1)} %get-tuple-element.67.refs_2_, ...), custom_call_target="tpu_custom_call" | custom-call | bytes 4194304 | tf_op jit(solution)/shard_map/pallas_call | solution.py:46
  54.1 5.3 %all-to-all-done.1 = bf16[16,48,128]{2,1,0:T(8,128)(2,1)S(1)} async-done(((bf16[16,48,128]{2,1,0:T(8,128)(2,1)}), bf16[16,48,128]{2,1,0:T(8,128)(2,1)S(1)}, u32[]{:S(2)}, u32[]{:S(2)}) %all-to-all-start.1) | async-done | bytes 196640 | tf_op jit(solution)/shard_map/all_to_all | solution.py:683
  59.4 0.0 collective-permute-start.9
  59.4 1.4 %collective-permute-done.9.refs_2_ = bf16[768,128]{1,0:T(8,128)(2,1)S(1)} collective-permute-done((bf16[768,128]{1,0:T(8,128)(2,1)S(1)}, bf16[768,128]{1,0:T(8,128)(2,1)S(1)}, u32[]{:S(2)}, u32[]{:S(2)}) %collective-permute-start.9) | collective-permute-done | bytes 196640 | tf_op jit(solution)/shard_map/ppermute | solution.py:689
  60.8 2.0 %shard_map.146 = (f32[720,256]{1,0:T(8,128)}, f32[1,256]{1,0:T(1,128)}) custom-call(s32[4]{0:T(128)S(1)} %pad_add_fusion.refs_0_, bf16[768,128]{1,0:T(8,128)(2,1)S(1)} %bitcast.12, bf16[768,128]{1,0:T(8,128)(2,1)S(1)} %collective-permute-done.9.refs_2_), custom_call_target="tpu_custom_call" | custom-call | bytes 1179648 | tf_op jit(solution)/shard_map/pallas_call | solution.py:690
  (1 shorter events, 0.0 us)
Async XLA Ops:
  0.6 12.0 %copy-start.1 = (s32[1,128]{1,0:T(1,128)S(1)}, s32[1,128]{1,0:T(1,128)}, u32[]{:S(2)}) copy-start(s32[1,128]{1,0:T(1,128)} %refs_2_.7) | copy-start | bytes 1540
  0.6 12.0 %copy-start.2 = (s32[1,128]{1,0:T(1,128)S(1)}, s32[1,128]{1,0:T(1,128)}, u32[]{:S(2)}) copy-start(s32[1,128]{1,0:T(1,128)} %refs_1_.5) | copy-start | bytes 1540
  2.4 1.4 %collective-permute-start = (bf16[80,128]{1,0:T(8,128)(2,1)S(1)}, bf16[80,128]{1,0:T(8,128)(2,1)S(1)}, u32[]{:S(2)}, u32[]{:S(2)}) collective-permute-start(bf16[80,128]{1,0:T(8,128)(2,1)S(1)} %get-tuple-element.46), channel_id=1, source_target_pairs={{0,16},{1,17},{2,18},{3,19},{4,20},{5,21},{6,22},{7,23},{8,24},{9,... | collective-permute-start | bytes 61448 | tf_op jit(solution)/shard_map/ppermute | solution.py:498
  3.8 8.8 %collective-permute-start.1 = (bf16[80,128]{1,0:T(8,128)(2,1)S(1)}, bf16[80,128]{1,0:T(8,128)(2,1)S(1)}, u32[]{:S(2)}, u32[]{:S(2)}) collective-permute-start(bf16[80,128]{1,0:T(8,128)(2,1)S(1)} %get-tuple-element.49), channel_id=1, source_target_pairs={{0,1},{1,2},{2,3},{3,4},{4,5},{5,6},{6,7},{7,8},{8,9},{9,10},{10,1... | collective-permute-start | bytes 61448 | tf_op jit(solution)/shard_map/ppermute | solution.py:498
  6.7 5.9 %collective-permute-start.2 = (bf16[80,128]{1,0:T(8,128)(2,1)S(1)}, bf16[80,128]{1,0:T(8,128)(2,1)S(1)}, u32[]{:S(2)}, u32[]{:S(2)}) collective-permute-start(bf16[80,128]{1,0:T(8,128)(2,1)S(1)} %get-tuple-element.50), channel_id=1, source_target_pairs={{0,15},{1,0},{2,1},{3,2},{4,3},{5,4},{6,5},{7,6},{8,7},{9,8},{10,9... | collective-permute-start | bytes 61448 | tf_op jit(solution)/shard_map/ppermute | solution.py:498
  16.0 2.5 %copy-start.3 = (bf16[256,2560]{1,0:T(8,128)(2,1)}, bf16[256,2560]{1,0:T(8,128)(2,1)S(1)}, u32[]{:S(2)}) copy-start(bf16[256,2560]{1,0:T(8,128)(2,1)S(1)} %get-tuple-element.60.refs_1_) | copy-start | bytes 3932164
  16.0 1.8 %collective-permute-start.3 = (f32[768,128]{1,0:T(8,128)S(1)}, f32[768,128]{1,0:T(8,128)S(1)}, u32[]{:S(2)}, u32[]{:S(2)}) collective-permute-start(f32[768,128]{1,0:T(8,128)S(1)} %get-tuple-element.57), channel_id=1, source_target_pairs={{0,16},{16,0},{1,17},{17,1},{2,18},{18,2},{3,19},{19,3},{4,20},{20... | collective-permute-start | bytes 1179656 | tf_op jit(solution)/shard_map/ppermute | solution.py:610
  17.8 7.6 %copy-start = (bf16[256,720]{0,1:T(8,128)(2,1)S(1)}, bf16[256,720]{0,1:T(8,128)(2,1)}, u32[]{:S(2)}) copy-start(bf16[256,720]{0,1:T(8,128)(2,1)} %param.16) | copy-start | bytes 1105924
  18.6 26.5 %all-to-all-start = ((bf16[16,176,128]{2,1,0:T(8,128)(2,1)}), bf16[16,176,128]{2,1,0:T(8,128)(2,1)S(1)}, u32[]{:S(2)}, u32[]{:S(2)}) async-start(bf16[16,176,128]{2,1,0:T(8,128)(2,1)} %get-tuple-element.59), calls=%async_computation | async-start | bytes 1441792 | tf_op jit(solution)/shard_map/all_to_all | solution.py:639
  25.4 1.3 %copy-start.4 = (bf16[256,2560]{1,0:T(8,128)(2,1)S(1)}, bf16[256,2560]{1,0:T(8,128)(2,1)}, u32[]{:S(2)}) copy-start(bf16[256,2560]{1,0:T(8,128)(2,1)} %copy-done.3) | copy-start | bytes 3932164
  29.4 7.6 %collective-permute-start.4 = (bf16[64,128]{1,0:T(8,128)(2,1)S(1)}, bf16[64,128]{1,0:T(8,128)(2,1)S(1)}, u32[]{:S(2)}, u32[]{:S(2)}) collective-permute-start(bf16[64,128]{1,0:T(8,128)(2,1)S(1)} %get-tuple-element.62), channel_id=1, source_target_pairs={{0,16},{1,17},{2,18},{3,19},{4,20},{5,21},{6,22},{7,23},{8,24},{9,... | collective-permute-start | bytes 49160 | tf_op jit(solution)/shard_map/ppermute | solution.py:498
  29.6 14.5 %collective-permute-start.7 = (bf16[64,128]{1,0:T(8,128)(2,1)S(1)}, bf16[64,128]{1,0:T(8,128)(2,1)S(1)}, u32[]{:S(2)}, u32[]{:S(2)}) collective-permute-start(bf16[64,128]{1,0:T(8,128)(2,1)S(1)} %get-tuple-element.64), channel_id=1, source_target_pairs={{0,1},{1,2},{2,3},{3,4},{4,5},{5,6},{6,7},{7,8},{8,9},{9,10},{10,1... | collective-permute-start | bytes 49160 | tf_op jit(solution)/shard_map/ppermute | solution.py:498
  31.4 12.7 %collective-permute-start.8 = (bf16[64,128]{1,0:T(8,128)(2,1)S(1)}, bf16[64,128]{1,0:T(8,128)(2,1)S(1)}, u32[]{:S(2)}, u32[]{:S(2)}) collective-permute-start(bf16[64,128]{1,0:T(8,128)(2,1)S(1)} %get-tuple-element.65), channel_id=1, source_target_pairs={{0,15},{1,0},{2,1},{3,2},{4,3},{5,4},{6,5},{7,6},{8,7},{9,8},{10,9... | collective-permute-start | bytes 49160 | tf_op jit(solution)/shard_map/ppermute | solution.py:498
  35.2 8.9 %collective-permute-start.6 = (bf16[64,128]{1,0:T(8,128)(2,1)S(1)}, bf16[64,128]{1,0:T(8,128)(2,1)S(1)}, u32[]{:S(2)}, u32[]{:S(2)}) collective-permute-start(bf16[64,128]{1,0:T(8,128)(2,1)S(1)} %get-tuple-element.63), channel_id=1, source_target_pairs={{0,31},{1,16},{2,17},{3,18},{4,19},{5,20},{6,21},{7,22},{8,23},{9,... | collective-permute-start | bytes 49160 | tf_op jit(solution)/shard_map/ppermute | solution.py:498
  36.6 7.5 %collective-permute-start.5 = (bf16[64,128]{1,0:T(8,128)(2,1)S(1)}, bf16[64,128]{1,0:T(8,128)(2,1)S(1)}, u32[]{:S(2)}, u32[]{:S(2)}) collective-permute-start(bf16[64,128]{1,0:T(8,128)(2,1)S(1)} %get-tuple-element.63), channel_id=1, source_target_pairs={{0,17},{1,18},{2,19},{3,20},{4,21},{5,22},{6,23},{7,24},{8,25},{9,... | collective-permute-start | bytes 49160 | tf_op jit(solution)/shard_map/ppermute | solution.py:498
  46.3 13.0 %all-to-all-start.1 = ((bf16[16,48,128]{2,1,0:T(8,128)(2,1)}), bf16[16,48,128]{2,1,0:T(8,128)(2,1)S(1)}, u32[]{:S(2)}, u32[]{:S(2)}) async-start(bf16[16,48,128]{2,1,0:T(8,128)(2,1)} %get-tuple-element.66), calls=%async_computation.1 | async-start | bytes 393216 | tf_op jit(solution)/shard_map/all_to_all | solution.py:683
  59.4 1.4 %collective-permute-start.9 = (bf16[768,128]{1,0:T(8,128)(2,1)S(1)}, bf16[768,128]{1,0:T(8,128)(2,1)S(1)}, u32[]{:S(2)}, u32[]{:S(2)}) collective-permute-start(bf16[768,128]{1,0:T(8,128)(2,1)S(1)} %bitcast.11), channel_id=1, source_target_pairs={{0,16},{16,0},{1,17},{17,1},{2,18},{18,2},{3,19},{19,3},{4,20},{20... | collective-permute-start | bytes 589832 | tf_op jit(solution)/shard_map/ppermute | solution.py:689

commit v9 on v5

--- a/solution.py
+++ b/solution.py
@@ -65,32 +65,34 @@
     return 0.5 * jnp.tanh(0.5 * values) + 0.5
 
 
-def edges_kernel(waits, place_ref, forcing_ref, hidden_ref, flat_ref, *rest):
-    row_refs, (left_ref, right_ref, wide_ref) = rest[:-3], rest[-3:]
+def edges_kernel(waits, place_ref, forcing_ref, hidden_ref, wide_ref, *row_refs):
     inp, rows, width = forcing_ref.shape
     channels = inp + hidden_ref.shape[0]
     for wait in waits:
         wait()
     wide_ref[: inp * rows] = forcing_ref[...].astype(F32).reshape(inp * rows, width)
     wide_ref[inp * rows :] = hidden_ref[...].astype(F32).reshape((channels - inp) * rows, width)
+    ends = [wide_ref[pl.ds(row, channels, stride=rows), :] for row in (0, rows - 1)]
+    if len(row_refs) == 1:
+        row_refs[0][...] = jnp.where(place_ref[0] == 0, ends[1], ends[0]).astype(BF16)
+    else:
+        for ref, end in zip(row_refs, ends):
+            ref[...] = end.astype(BF16)
+
+
+def columns_kernel(wide_ref, flat_ref, left_ref, right_ref):
+    channels, width = left_ref.shape
+    rows = wide_ref.shape[0] // channels
     lane = lane_index((channels, width))
     left = jnp.zeros((channels, width), F32)
     right = jnp.zeros((channels, width), F32)
-    ends = []
     for row in range(rows):
         slab = wide_ref[pl.ds(row, channels, stride=rows), :]
         flat_ref[:, row * width : (row + 1) * width] = slab.astype(BF16)
         left = jnp.where(lane == row, slab[:, :1], left)
         right = jnp.where(lane == row, slab[:, width - 1 :], right)
-        if row in (0, rows - 1):
-            ends.append(slab)
     left_ref[...] = left.astype(BF16)
     right_ref[...] = right.astype(BF16)
-    if len(row_refs) == 1:
-        row_refs[0][...] = jnp.where(place_ref[0] == 0, ends[-1], ends[0]).astype(BF16)
-    else:
-        row_refs[0][...] = ends[0].astype(BF16)
-        row_refs[1][...] = ends[-1].astype(BF16)
 
 
 def flatten_kernel(
@@ -213,14 +215,9 @@
     group = 128 // TILE
     states = []
     for start in range(0, rows, step):
-        pre = bias
-        for row_off in range(3):
-            low = (start + row_off) * width
-            pre = pre + jnp.dot(
-                w_ref[:, row_off * third : (row_off + 1) * third],
-                taps_ref[:, low : low + chunk],
-                preferred_element_type=F32,
-            )
+        lows = [(start + row_off) * width for row_off in range(3)]
+        stacked = jnp.concatenate([taps_ref[:, low : low + chunk] for low in lows], 0)
+        pre = bias + jnp.dot(w_ref[...], stacked, preferred_element_type=F32)
         gate_in = sigmoid(pre[:hid])
         gate_forget = sigmoid(pre[hid : 2 * hid])
         gate_out = sigmoid(pre[2 * hid : 3 * hid])
@@ -525,16 +522,20 @@
         return jax.ShapeDtypeStruct(shape, dtype)
 
     end_count = 1 if lat_devices == 2 else 2
-    edges = call(
+    wide, *ends = call(
         edges_kernel,
-        (shaped(channels, cells),) + (shaped(channels, width),) * (end_count + 2),
+        (shaped(channels * rows, width, dtype=F32),) + (shaped(channels, width),) * end_count,
         (place, forcing, hidden),
         scalars=1,
-        scratch=[pltpu.VMEM((channels * rows, width), F32)],
         moved=4 * channels * cells,
         fetched=2,
     )
-    flat, ends, (left, right) = edges[0], edges[1:-2], edges[-2:]
+    flat, left, right = call(
+        columns_kernel,
+        (shaped(channels, cells),) + (shaped(channels, width),) * 2,
+        (wide,),
+        moved=6 * channels * cells,
+    )
     if lat_devices == 2:
         up = down = moved(ends[0], 1, 0, lat_devices, lon_devices)
     else:

time: 62.7 us -> 62.5 us (level)
    pallas_call x9 -> x10, Pallas kernels: 16.3 us -> 16.3 us  [call(): pl.pallas_call(run, out_shape=outs, in_specs=[SMEM] * scalars + [VMEM] *...]
  transfers between devices with their start and end apart: 12 -> 12, of which waited for: 6 -> 6; matrix products, arithmetic and copies ran while one was open for 1% -> 1% of each run, Pallas kernels for 13% -> 14%
where the time goes in v9:
time: 62.5 us; the launch traced here: 62.1 us
  starting transfers between devices  26.9 us (43%)
  Pallas kernels  17.1 us (27%)
  waiting for transfers between devices  15.4 us (25%)
  local copies, waits for them, and re-layouts  1.42 us (2%)
  between operations  0.82 us (1%)
    pallas_call x10, Pallas kernels, call(): pl.pallas_call(run, out_shape=outs, in_specs=[SMEM] * scalars + [VMEM] *...  16.3 us
    ppermute x8, starting transfers between devices, moved(): return lax.ppermute(values, ('lat', 'lon'), pairs)  15.1 us
    ppermute x8, waiting for transfers between devices, moved(): return lax.ppermute(values, ('lat', 'lon'), pairs)  7.6 us
    all_to_all x1, starting transfers between devices, body(): incoming = lax.all_to_all(outgoing, 'lon', 0, 0, tiled=True)  6.86 us
    all_to_all x1, waiting for transfers between devices, body(): lax.all_to_all(shares, 'lon', 0, 0, tiled=True).reshape(3 * third, lanes)  5.31 us
    all_to_all x1, starting transfers between devices, body(): lax.all_to_all(shares, 'lon', 0, 0, tiled=True).reshape(3 * third, lanes)  4.94 us
    ppermute x1, waiting for transfers between devices, body(): gathered += (lax.ppermute(gathered[0], 'lat', swap),)  1.44 us
    unnamed x10, local copies, waits for them, and re-layouts  1.33 us
  transfers between devices with their start and end apart: 12, of which 6 were waited for; matrix products, arithmetic and copies ran while one was open for 1% of the time, Pallas kernels for 14%

profile of v9, /device:TPU:0, one launch (start us, length us, event | category | flops | bytes accessed | tf_op | source)
XLA Modules:
  0.0 62.1 jit_solution(9029397963619869271)
XLA Ops:
  0.6 0.0 copy-start.1
  0.6 0.0 copy-start.2
  0.7 0.1 pad_add_fusion.refs_0_
  0.7 1.6 %shard_map.136 = (f32[1280,128]{1,0:T(8,128)S(1)}, bf16[80,128]{1,0:T(8,128)(2,1)S(1)}) custom-call(s32[4]{0:T(128)S(1)} %pad_add_fusion.refs_0_, bf16[16,16,128]{2,1,0:T(8,128)(2,1)} %refs_1_.3, bf16[64,16,128]{2,1,0:T(8,128)(2,1)} %refs_2_.4), custom_call_target="tpu_custom_call" | custom-call | bytes 655360 | tf_op jit(solution)/shard_map/pallas_call | solution.py:46
  2.4 0.5 collective-permute-start
  2.9 0.4 shard_map.137
  3.2 0.5 collective-permute-done.refs_0_.refs_1_.refs_4_.refs_5_
  3.7 0.1 shard_map.138
  3.8 2.9 %collective-permute-start.1 = (bf16[80,128]{1,0:T(8,128)(2,1)S(1)}, bf16[80,128]{1,0:T(8,128)(2,1)S(1)}, u32[]{:S(2)}, u32[]{:S(2)}) collective-permute-start(bf16[80,128]{1,0:T(8,128)(2,1)S(1)} %get-tuple-element.49), channel_id=1, source_target_pairs={{0,1},{1,2},{2,3},{3,4},{4,5},{5,6},{6,7},{7,8},{8,9},{9,10},{10,1... | collective-permute-start | bytes 61448 | tf_op jit(solution)/shard_map/ppermute | solution.py:474
  6.7 4.1 %collective-permute-start.2 = (bf16[80,128]{1,0:T(8,128)(2,1)S(1)}, bf16[80,128]{1,0:T(8,128)(2,1)S(1)}, u32[]{:S(2)}, u32[]{:S(2)}) collective-permute-start(bf16[80,128]{1,0:T(8,128)(2,1)S(1)} %get-tuple-element.50), channel_id=1, source_target_pairs={{0,15},{1,0},{2,1},{3,2},{4,3},{5,4},{6,5},{7,6},{8,7},{9,8},{10,9... | collective-permute-start | bytes 61448 | tf_op jit(solution)/shard_map/ppermute | solution.py:474
  10.8 1.8 %shard_map.139 = (bf16[64,2048]{1,0:T(8,128)(2,1)S(1)}, bf16[64,2048]{1,0:T(8,128)(2,1)S(1)}, bf16[64,2048]{1,0:T(8,128)(2,1)S(1)}, bf16[256,768]{1,0:T(8,128)(2,1)S(1)}, f32[256,128]{1,0:T(8,128)S(1)}) custom-call(f32[1,256]{1,0:T(1,128)} %bitcast.15, bf16[720,256]{1,0:T(8,128)(2,1)} %bitcast.13, bf16[64,16,128]{2,1,0:T(8,128)(2,1)} %refs_2_.5, ...), custom_call_target="tpu_custom_call" | custom-call | bytes 1572864 | tf_op jit(solution)/shard_map/pallas_call | solution.py:46
  12.6 0.0 collective-permute-done.1.refs_6_
  12.6 0.0 collective-permute-done.2.refs_7_
  12.6 0.0 copy-done.1
  12.7 0.0 copy-done.2
  12.7 3.1 %shard_map.140 = (bf16[64,2048]{1,0:T(8,128)(2,1)S(1)}, f32[64,2048]{1,0:T(8,128)S(1)}, bf16[8,64,256]{2,1,0:T(8,128)(2,1)S(1)}, f32[768,128]{1,0:T(8,128)S(1)},...) custom-call(s32[4]{0:T(128)S(1)} %pad_add_fusion.refs_0_, s32[1,128]{1,0:T(1,128)S(1)} %copy-done.2, ...), custom_call_target="tpu_custom_call" | custom-call | flops 1509949440 | bytes 2097152 | tf_op jit(solution)/shard_map/pallas_call | solution.py:46
  15.8 0.0 copy-start.3
  15.8 0.1 collective-permute-start.3
  15.9 1.6 %shard_map.141.refs_2_ = bf16[16,176,128]{2,1,0:T(8,128)(2,1)} custom-call(s32[4]{0:T(128)S(1)} %pad_add_fusion.refs_0_, s32[1,128]{1,0:T(1,128)S(1)} %copy-done.2, s32[1,128]{1,0:T(1,128)S(1)} %copy-done.1, bf16[8,64,256]{2,1,0:T(8,128)(2,1)S(1)} %get-tuple-element.58.refs_3_), custom_call_target="tpu_custom_call" | custom-call | bytes 1048576 | tf_op jit(solution)/shard_map/pallas_call | solution.py:46
  17.5 0.1 collective-permute-done.3.refs_1_
  17.6 0.0 copy-start
  17.6 0.7 %shard_map.142 = (bf16[16,176,128]{2,1,0:T(8,128)(2,1)}, f32[8,128]{1,0:T(8,128)S(1)}) custom-call(f32[768,128]{1,0:T(8,128)S(1)} %get-tuple-element.56.refs_0_, f32[768,128]{1,0:T(8,128)S(1)} %collective-permute-done.3.refs_1_, bf16[16,176,128]{2,1,0:T(8,128)(2,1)} %shard_map.141.refs_2_), custom_call_target="tpu_custom_call", output_to_operand_aliasing={{0}: (2, {})} | custom-call | bytes 1572864 | tf_op jit(solution)/shard_map/pallas_call | solution.py:600
  18.3 0.0 copy-done.3
  18.3 6.9 %all-to-all-start = ((bf16[16,176,128]{2,1,0:T(8,128)(2,1)}), bf16[16,176,128]{2,1,0:T(8,128)(2,1)S(1)}, u32[]{:S(2)}, u32[]{:S(2)}) async-start(bf16[16,176,128]{2,1,0:T(8,128)(2,1)} %get-tuple-element.59), calls=%async_computation | async-start | bytes 1441792 | tf_op jit(solution)/shard_map/all_to_all | solution.py:615
  25.2 0.0 copy-done
  25.2 0.0 copy-start.4
  25.2 1.3 %copy-done.4 = bf16[256,2560]{1,0:T(8,128)(2,1)S(1)} copy-done((bf16[256,2560]{1,0:T(8,128)(2,1)S(1)}, bf16[256,2560]{1,0:T(8,128)(2,1)}, u32[]{:S(2)}) %copy-start.4) | copy-done | bytes 1310744
  26.5 2.6 %shard_map.143 = (f32[64,2048]{1,0:T(8,128)S(1)}, bf16[64,128]{1,0:T(8,128)(2,1)S(1)}, bf16[64,128]{1,0:T(8,128)(2,1)S(1)}, bf16[64,128]{1,0:T(8,128)(2,1)S(1)}, bf16[64,128]{1,0:T(8,128)(2,1)S(1)}) custom-call(s32[4]{0:T(128)S(1)} %pad_add_fusion.refs_0_, bf16[256,2560]{1,0:T(8,128)(2,1)S(1)} %copy-done.4, bf16[720,256]{1,0:T(8,128)(2,1)S(1)} %bitcast.14, ...), custom_call_target="tpu_custom_call" | custom-call | flops 603979776 | bytes 4194304 | tf_op jit(solution)/shard_map/pallas_call | solution.py:46
  29.2 0.2 collective-permute-start.4
  29.4 1.8 %collective-permute-start.7 = (bf16[64,128]{1,0:T(8,128)(2,1)S(1)}, bf16[64,128]{1,0:T(8,128)(2,1)S(1)}, u32[]{:S(2)}, u32[]{:S(2)}) collective-permute-start(bf16[64,128]{1,0:T(8,128)(2,1)S(1)} %get-tuple-element.64), channel_id=1, source_target_pairs={{0,1},{1,2},{2,3},{3,4},{4,5},{5,6},{6,7},{7,8},{8,9},{9,10},{10,1... | collective-permute-start | bytes 49160 | tf_op jit(solution)/shard_map/ppermute | solution.py:474
  31.2 3.8 %collective-permute-start.8 = (bf16[64,128]{1,0:T(8,128)(2,1)S(1)}, bf16[64,128]{1,0:T(8,128)(2,1)S(1)}, u32[]{:S(2)}, u32[]{:S(2)}) collective-permute-start(bf16[64,128]{1,0:T(8,128)(2,1)S(1)} %get-tuple-element.65), channel_id=1, source_target_pairs={{0,15},{1,0},{2,1},{3,2},{4,3},{5,4},{6,5},{7,6},{8,7},{9,8},{10,9... | collective-permute-start | bytes 49160 | tf_op jit(solution)/shard_map/ppermute | solution.py:474
  35.0 1.3 %collective-permute-start.6 = (bf16[64,128]{1,0:T(8,128)(2,1)S(1)}, bf16[64,128]{1,0:T(8,128)(2,1)S(1)}, u32[]{:S(2)}, u32[]{:S(2)}) collective-permute-start(bf16[64,128]{1,0:T(8,128)(2,1)S(1)} %get-tuple-element.63), channel_id=1, source_target_pairs={{0,31},{1,16},{2,17},{3,18},{4,19},{5,20},{6,21},{7,22},{8,23},{9,... | collective-permute-start | bytes 49160 | tf_op jit(solution)/shard_map/ppermute | solution.py:474
  36.3 0.4 collective-permute-start.5
  36.8 0.0 collective-permute-done.4.refs_2_.refs_3_.refs_6_.refs_7_
  36.8 7.1 %collective-permute-done.7.refs_8_.refs_12_ = bf16[64,128]{1,0:T(8,128)(2,1)S(1)} collective-permute-done((bf16[64,128]{1,0:T(8,128)(2,1)S(1)}, bf16[64,128]{1,0:T(8,128)(2,1)S(1)}, u32[]{:S(2)}, u32[]{:S(2)}) %collective-permute-start.7) | collective-permute-done | bytes 16416 | tf_op jit(solution)/shard_map/ppermute | solution.py:474
  43.9 0.0 collective-permute-done.8.refs_9_.refs_13_
  43.9 0.0 collective-permute-done.6.refs_5_.refs_7_.refs_9_.refs_11_
  43.9 0.0 collective-permute-done.5.refs_4_.refs_6_.refs_8_.refs_10_
  43.9 1.0 %all-to-all-done.refs_1_.refs_4_ = bf16[16,176,128]{2,1,0:T(8,128)(2,1)S(1)} async-done(((bf16[16,176,128]{2,1,0:T(8,128)(2,1)}), bf16[16,176,128]{2,1,0:T(8,128)(2,1)S(1)}, u32[]{:S(2)}, u32[]{:S(2)}) %all-to-all-start) | async-done | bytes 720928 | tf_op jit(solution)/shard_map/all_to_all | solution.py:615
  44.9 1.3 %shard_map.144 = (bf16[16,48,128]{2,1,0:T(8,128)(2,1)}, f32[8,128]{1,0:T(8,128)S(1)}) custom-call(s32[4]{0:T(128)S(1)} %pad_add_fusion.refs_0_, bf16[16,176,128]{2,1,0:T(8,128)(2,1)S(1)} %all-to-all-done.refs_1_.refs_4_, bf16[64,128]{1,0:T(8,128)(2,1)S(1)} %collective-permute-done.4.refs_2_.refs_3_.refs_6_.refs_7_, ...), custom_call_target="tpu_custom_call" | custom-call | bytes 393216 | tf_op jit(solution)/shard_map/pallas_call | solution.py:46
  46.1 4.9 %all-to-all-start.1 = ((bf16[16,48,128]{2,1,0:T(8,128)(2,1)}), bf16[16,48,128]{2,1,0:T(8,128)(2,1)S(1)}, u32[]{:S(2)}, u32[]{:S(2)}) async-start(bf16[16,48,128]{2,1,0:T(8,128)(2,1)} %get-tuple-element.66), calls=%async_computation.1 | async-start | bytes 393216 | tf_op jit(solution)/shard_map/all_to_all | solution.py:659
  51.1 0.1 reshape.35
  51.2 0.1 reduce_or.9
  51.3 0.1 convert_reduce_fusion
  51.4 0.1 select_reduce_fusion.refs_1_
  51.5 2.3 %shard_map.145 = (bf16[64,16,128]{2,1,0:T(8,128)(2,1)}, f32[1024,128]{1,0:T(8,128)}, f32[4,64,256]{2,1,0:T(8,128)}, f32[1024,128]{1,0:T(8,128)}) custom-call(s32[4]{0:T(128)S(1)} %pad_add_fusion.refs_0_, s32[4]{0:T(128)S(1)} %select_reduce_fusion.refs_1_, bf16[64,2048]{1,0:T(8,128)(2,1)S(1)} %get-tuple-element.67.refs_2_, ...), custom_call_target="tpu_custom_call" | custom-call | bytes 4194304 | tf_op jit(solution)/shard_map/pallas_call | solution.py:46
  53.8 5.3 %all-to-all-done.1 = bf16[16,48,128]{2,1,0:T(8,128)(2,1)S(1)} async-done(((bf16[16,48,128]{2,1,0:T(8,128)(2,1)}), bf16[16,48,128]{2,1,0:T(8,128)(2,1)S(1)}, u32[]{:S(2)}, u32[]{:S(2)}) %all-to-all-start.1) | async-done | bytes 196640 | tf_op jit(solution)/shard_map/all_to_all | solution.py:659
  59.1 0.0 collective-permute-start.9
  59.2 1.4 %collective-permute-done.9.refs_2_ = bf16[768,128]{1,0:T(8,128)(2,1)S(1)} collective-permute-done((bf16[768,128]{1,0:T(8,128)(2,1)S(1)}, bf16[768,128]{1,0:T(8,128)(2,1)S(1)}, u32[]{:S(2)}, u32[]{:S(2)}) %collective-permute-start.9) | collective-permute-done | bytes 196640 | tf_op jit(solution)/shard_map/ppermute | solution.py:664
  60.6 1.5 %shard_map.146 = (f32[720,256]{1,0:T(8,128)}, f32[1,256]{1,0:T(1,128)}) custom-call(s32[4]{0:T(128)S(1)} %pad_add_fusion.refs_0_, bf16[768,128]{1,0:T(8,128)(2,1)S(1)} %bitcast.12, bf16[768,128]{1,0:T(8,128)(2,1)S(1)} %collective-permute-done.9.refs_2_), custom_call_target="tpu_custom_call" | custom-call | bytes 1179648 | tf_op jit(solution)/shard_map/pallas_call | solution.py:46
  (1 shorter events, 0.0 us)
Async XLA Ops:
  0.6 12.0 %copy-start.1 = (s32[1,128]{1,0:T(1,128)S(1)}, s32[1,128]{1,0:T(1,128)}, u32[]{:S(2)}) copy-start(s32[1,128]{1,0:T(1,128)} %refs_2_.7) | copy-start | bytes 1540
  0.6 12.0 %copy-start.2 = (s32[1,128]{1,0:T(1,128)S(1)}, s32[1,128]{1,0:T(1,128)}, u32[]{:S(2)}) copy-start(s32[1,128]{1,0:T(1,128)} %refs_1_.5) | copy-start | bytes 1540
  2.4 1.4 %collective-permute-start = (bf16[80,128]{1,0:T(8,128)(2,1)S(1)}, bf16[80,128]{1,0:T(8,128)(2,1)S(1)}, u32[]{:S(2)}, u32[]{:S(2)}) collective-permute-start(bf16[80,128]{1,0:T(8,128)(2,1)S(1)} %get-tuple-element.46), channel_id=1, source_target_pairs={{0,16},{1,17},{2,18},{3,19},{4,20},{5,21},{6,22},{7,23},{8,24},{9,... | collective-permute-start | bytes 61448 | tf_op jit(solution)/shard_map/ppermute | solution.py:474
  3.8 8.8 %collective-permute-start.1 = (bf16[80,128]{1,0:T(8,128)(2,1)S(1)}, bf16[80,128]{1,0:T(8,128)(2,1)S(1)}, u32[]{:S(2)}, u32[]{:S(2)}) collective-permute-start(bf16[80,128]{1,0:T(8,128)(2,1)S(1)} %get-tuple-element.49), channel_id=1, source_target_pairs={{0,1},{1,2},{2,3},{3,4},{4,5},{5,6},{6,7},{7,8},{8,9},{9,10},{10,1... | collective-permute-start | bytes 61448 | tf_op jit(solution)/shard_map/ppermute | solution.py:474
  6.7 5.9 %collective-permute-start.2 = (bf16[80,128]{1,0:T(8,128)(2,1)S(1)}, bf16[80,128]{1,0:T(8,128)(2,1)S(1)}, u32[]{:S(2)}, u32[]{:S(2)}) collective-permute-start(bf16[80,128]{1,0:T(8,128)(2,1)S(1)} %get-tuple-element.50), channel_id=1, source_target_pairs={{0,15},{1,0},{2,1},{3,2},{4,3},{5,4},{6,5},{7,6},{8,7},{9,8},{10,9... | collective-permute-start | bytes 61448 | tf_op jit(solution)/shard_map/ppermute | solution.py:474
  15.8 2.5 %copy-start.3 = (bf16[256,2560]{1,0:T(8,128)(2,1)}, bf16[256,2560]{1,0:T(8,128)(2,1)S(1)}, u32[]{:S(2)}) copy-start(bf16[256,2560]{1,0:T(8,128)(2,1)S(1)} %get-tuple-element.60.refs_1_) | copy-start | bytes 3932164
  15.8 1.8 %collective-permute-start.3 = (f32[768,128]{1,0:T(8,128)S(1)}, f32[768,128]{1,0:T(8,128)S(1)}, u32[]{:S(2)}, u32[]{:S(2)}) collective-permute-start(f32[768,128]{1,0:T(8,128)S(1)} %get-tuple-element.57), channel_id=1, source_target_pairs={{0,16},{16,0},{1,17},{17,1},{2,18},{18,2},{3,19},{19,3},{4,20},{20... | collective-permute-start | bytes 1179656 | tf_op jit(solution)/shard_map/ppermute | solution.py:586
  17.6 7.6 %copy-start = (bf16[256,720]{0,1:T(8,128)(2,1)S(1)}, bf16[256,720]{0,1:T(8,128)(2,1)}, u32[]{:S(2)}) copy-start(bf16[256,720]{0,1:T(8,128)(2,1)} %param.16) | copy-start | bytes 1105924
  18.3 26.5 %all-to-all-start = ((bf16[16,176,128]{2,1,0:T(8,128)(2,1)}), bf16[16,176,128]{2,1,0:T(8,128)(2,1)S(1)}, u32[]{:S(2)}, u32[]{:S(2)}) async-start(bf16[16,176,128]{2,1,0:T(8,128)(2,1)} %get-tuple-element.59), calls=%async_computation | async-start | bytes 1441792 | tf_op jit(solution)/shard_map/all_to_all | solution.py:615
  25.2 1.3 %copy-start.4 = (bf16[256,2560]{1,0:T(8,128)(2,1)S(1)}, bf16[256,2560]{1,0:T(8,128)(2,1)}, u32[]{:S(2)}) copy-start(bf16[256,2560]{1,0:T(8,128)(2,1)} %copy-done.3) | copy-start | bytes 3932164
  29.2 7.6 %collective-permute-start.4 = (bf16[64,128]{1,0:T(8,128)(2,1)S(1)}, bf16[64,128]{1,0:T(8,128)(2,1)S(1)}, u32[]{:S(2)}, u32[]{:S(2)}) collective-permute-start(bf16[64,128]{1,0:T(8,128)(2,1)S(1)} %get-tuple-element.62), channel_id=1, source_target_pairs={{0,16},{1,17},{2,18},{3,19},{4,20},{5,21},{6,22},{7,23},{8,24},{9,... | collective-permute-start | bytes 49160 | tf_op jit(solution)/shard_map/ppermute | solution.py:474
  29.4 14.5 %collective-permute-start.7 = (bf16[64,128]{1,0:T(8,128)(2,1)S(1)}, bf16[64,128]{1,0:T(8,128)(2,1)S(1)}, u32[]{:S(2)}, u32[]{:S(2)}) collective-permute-start(bf16[64,128]{1,0:T(8,128)(2,1)S(1)} %get-tuple-element.64), channel_id=1, source_target_pairs={{0,1},{1,2},{2,3},{3,4},{4,5},{5,6},{6,7},{7,8},{8,9},{9,10},{10,1... | collective-permute-start | bytes 49160 | tf_op jit(solution)/shard_map/ppermute | solution.py:474
  31.2 12.7 %collective-permute-start.8 = (bf16[64,128]{1,0:T(8,128)(2,1)S(1)}, bf16[64,128]{1,0:T(8,128)(2,1)S(1)}, u32[]{:S(2)}, u32[]{:S(2)}) collective-permute-start(bf16[64,128]{1,0:T(8,128)(2,1)S(1)} %get-tuple-element.65), channel_id=1, source_target_pairs={{0,15},{1,0},{2,1},{3,2},{4,3},{5,4},{6,5},{7,6},{8,7},{9,8},{10,9... | collective-permute-start | bytes 49160 | tf_op jit(solution)/shard_map/ppermute | solution.py:474
  35.0 8.9 %collective-permute-start.6 = (bf16[64,128]{1,0:T(8,128)(2,1)S(1)}, bf16[64,128]{1,0:T(8,128)(2,1)S(1)}, u32[]{:S(2)}, u32[]{:S(2)}) collective-permute-start(bf16[64,128]{1,0:T(8,128)(2,1)S(1)} %get-tuple-element.63), channel_id=1, source_target_pairs={{0,31},{1,16},{2,17},{3,18},{4,19},{5,20},{6,21},{7,22},{8,23},{9,... | collective-permute-start | bytes 49160 | tf_op jit(solution)/shard_map/ppermute | solution.py:474
  36.3 7.5 %collective-permute-start.5 = (bf16[64,128]{1,0:T(8,128)(2,1)S(1)}, bf16[64,128]{1,0:T(8,128)(2,1)S(1)}, u32[]{:S(2)}, u32[]{:S(2)}) collective-permute-start(bf16[64,128]{1,0:T(8,128)(2,1)S(1)} %get-tuple-element.63), channel_id=1, source_target_pairs={{0,17},{1,18},{2,19},{3,20},{4,21},{5,22},{6,23},{7,24},{8,25},{9,... | collective-permute-start | bytes 49160 | tf_op jit(solution)/shard_map/ppermute | solution.py:474
  46.1 13.0 %all-to-all-start.1 = ((bf16[16,48,128]{2,1,0:T(8,128)(2,1)}), bf16[16,48,128]{2,1,0:T(8,128)(2,1)S(1)}, u32[]{:S(2)}, u32[]{:S(2)}) async-start(bf16[16,48,128]{2,1,0:T(8,128)(2,1)} %get-tuple-element.66), calls=%async_computation.1 | async-start | bytes 393216 | tf_op jit(solution)/shard_map/all_to_all | solution.py:659
  59.1 1.4 %collective-permute-start.9 = (bf16[768,128]{1,0:T(8,128)(2,1)S(1)}, bf16[768,128]{1,0:T(8,128)(2,1)S(1)}, u32[]{:S(2)}, u32[]{:S(2)}) collective-permute-start(bf16[768,128]{1,0:T(8,128)(2,1)S(1)} %bitcast.11), channel_id=1, source_target_pairs={{0,16},{16,0},{1,17},{17,1},{2,18},{18,2},{3,19},{19,3},{4,20},{20... | collective-permute-start | bytes 589832 | tf_op jit(solution)/shard_map/ppermute | solution.py:664

commit v10 on v9

--- a/solution.py
+++ b/solution.py
@@ -161,7 +161,7 @@
     b_ref,
     hidden_new_ref,
     cell_back_ref,
-    tiles_ref,
+    cell_new_ref,
     *rest,
 ):
     weight_refs, (delta_ref, taps_ref) = rest[:-2], rest[-2:]
@@ -212,8 +212,6 @@
     delta_ref[:, : 2 * width] = blank
     delta_ref[:, (rows + 2) * width :] = blank
     bias = jnp.concatenate([b_ref[...]] * step, 1)
-    group = 128 // TILE
-    states = []
     for start in range(0, rows, step):
         lows = [(start + row_off) * width for row_off in range(3)]
         stacked = jnp.concatenate([taps_ref[:, low : low + chunk] for low in lows], 0)
@@ -242,30 +240,7 @@
             delta_ref[index * hid : (index + 1) * hid, low : low + chunk] = term.astype(BF16)
         hidden_new_ref[:, lanes] = hidden_new.astype(BF16)
         cell_back_ref[:, lanes] = cell_back
-        for part in range(step):
-            piece = slice(part * width, (part + 1) * width)
-            states.append(cell_new[:, piece])
-        if len(states) == group:
-            block_of = lane_index((hid, width)) // TILE
-            half = (start + step) // group - 1
-            stride = group // 2
-            while stride:
-                upper = (block_of & stride) != 0
-                mixed = list(states)
-                for low_index in range(group):
-                    if low_index & stride == 0:
-                        first, second = states[low_index], states[low_index + stride]
-                        mixed[low_index] = jnp.where(
-                            upper, pltpu.roll(second, stride * TILE, 1), first
-                        )
-                        mixed[low_index + stride] = jnp.where(
-                            upper, second, pltpu.roll(first, width - stride * TILE, 1)
-                        )
-                states = mixed
-                stride //= 2
-            for tile in range(tile_cols):
-                tiles_ref[tile, :, half * 128 : (half + 1) * 128] = states[tile].astype(BF16)
-            states = []
+        cell_new_ref[:, lanes] = cell_new
     delta = delta_ref[:, 2 * width : (rows + 2) * width]
     for row_off in range(3):
         part = lax.dot_general(
@@ -396,19 +371,60 @@
     return jnp.where(index == row + 1, rest, block)
 
 
-def slots_kernel(place_ref, wet_ref, owner_ref, tiles_ref, out_ref):
+def slots_kernel(
+    place_ref, wet_ref, owner_ref, state_ref, out_ref, tiles_ref, slots_ref, semaphores
+):
     tile_cols, hid, cells = tiles_ref.shape
-    slots, _, lanes = out_ref.shape
-    out_ref[...] = jnp.zeros(out_ref.shape, BF16)
+    slots, state_rows, lanes = slots_ref.shape
+    width = tile_cols * TILE
+    rows = state_ref.shape[1] // width
+    group = 128 // TILE
+    block_of = lane_index((hid, width)) // TILE
+    slots_ref[...] = jnp.zeros(slots_ref.shape, BF16)
+    for half in range(rows // group):
+        states = [
+            state_ref[:, row * width : (row + 1) * width]
+            for row in range(half * group, (half + 1) * group)
+        ]
+        stride = group // 2
+        while stride:
+            upper = (block_of & stride) != 0
+            mixed = list(states)
+            for low in range(group):
+                if low & stride == 0:
+                    first, second = states[low], states[low + stride]
+                    mixed[low] = jnp.where(upper, pltpu.roll(second, stride * TILE, 1), first)
+                    mixed[low + stride] = jnp.where(
+                        upper, second, pltpu.roll(first, width - stride * TILE, 1)
+                    )
+            states = mixed
+            stride //= 2
+        for tile in range(tile_cols):
+            tiles_ref[tile, :, half * 128 : (half + 1) * 128] = states[tile].astype(BF16)
     for tile in range(tile_cols):
         index = place_ref[1] * tile_cols + tile
 
         @pl.when(wet_ref[0, index] > 0)
         def _():
             for piece in range(cells // lanes):
-                out_ref[owner_ref[0, index], piece * hid : (piece + 1) * hid] = tiles_ref[
+                slots_ref[owner_ref[0, index], piece * hid : (piece + 1) * hid] = tiles_ref[
                     tile, :, piece * lanes : (piece + 1) * lanes
                 ]
+
+    count = semaphores.shape[0]
+    some = slots // count
+    copies = [
+        pltpu.make_async_copy(
+            slots_ref.at[pl.ds(index * some, some)],
+            out_ref.at[pl.ds(index * some, some), pl.ds(0, state_rows)],
+            semaphores.at[index],
+        )
+        for index in range(count)
+    ]
+    for copy in copies:
+        copy.start()
+    for copy in copies:
+        copy.wait()
 
 
 def pack_kernel(span, count, *refs):
@@ -565,12 +581,12 @@
     )
     halves = 2 if lat_devices == 2 else 1
     lanes = gates // halves
-    hidden_new, cell_back, tiles, *weight_parts, delta = call(
+    hidden_new, cell_back, cell_new, *weight_parts, delta = call(
         step_kernel,
         (
             shaped(hid, cells),
             shaped(hid, cells, dtype=F32),
-            shaped(tile_cols, hid, TILE * TILE),
+            shaped(hid, cells, dtype=F32),
         )
         + (shaped(3 * third, lanes, dtype=F32),) * halves
         + (shaped(gates, (rows + 4) * width),),
@@ -588,14 +604,23 @@
         weight_parts = (lax.psum(weight_parts[0], "lat"),)
     state_rows = hid * TILE * TILE // lanes
     share = 3 * third // lon_devices
-    slots = call(
+    anywhere = pl.BlockSpec(memory_space=pl.ANY)
+    copies = 4 if lon_devices % 4 == 0 else 1
+    slots = pl.pallas_call(
         slots_kernel,
-        shaped(lon_devices, state_rows + share, lanes),
-        (place, wet_mask, tile_owner, tiles),
-        scalars=3,
-        moved=4 * lon_devices * hid * TILE * TILE,
-    )
-    anywhere = pl.BlockSpec(memory_space=pl.ANY)
+        out_shape=shaped(lon_devices, state_rows + share, lanes),
+        in_specs=[SMEM] * 3 + [VMEM],
+        out_specs=anywhere,
+        scratch_shapes=[
+            pltpu.VMEM((tile_cols, hid, TILE * TILE), BF16),
+            pltpu.VMEM((lon_devices, state_rows, lanes), BF16),
+            pltpu.SemaphoreType.DMA((copies,)),
+        ],
+        compiler_params=pltpu.CompilerParams(vmem_limit_bytes=LIMIT),
+        cost_estimate=pl.CostEstimate(
+            flops=0, bytes_accessed=4 * lon_devices * hid * TILE * TILE, transcendentals=0
+        ),
+    )(place, wet_mask, tile_owner, cell_new)
     count = len(weight_parts)
     outgoing, packed = pl.pallas_call(
         lambda *refs: pack_kernel(span, count, *refs),

time: 62.5 us -> 62.8 us (level)
    pallas_call x0 -> x1, Pallas kernels: none -> 1.9 us  [body(): pl.pallas_call(slots_kernel, out_shape=shaped(lon_devices, state_rows + s...]
    pallas_call x10 -> x9, Pallas kernels: 16.3 us -> 14.8 us  [call(): pl.pallas_call(run, out_shape=outs, in_specs=[SMEM] * scalars + [VMEM] *...]
  transfers between devices with their start and end apart: 12 -> 12, of which waited for: 6 -> 5; matrix products, arithmetic and copies ran while one was open for 1% -> 1% of each run, Pallas kernels for 14% -> 14%
where the time goes in v10:
time: 62.8 us; the launch traced here: 62.5 us
  starting transfers between devices  27.1 us (43%)
  Pallas kernels  17.4 us (28%)
  waiting for transfers between devices  15.3 us (24%)
  local copies, waits for them, and re-layouts  1.42 us (2%)
  between operations  0.84 us (1%)
    ppermute x8, starting transfers between devices, moved(): return lax.ppermute(values, ('lat', 'lon'), pairs)  15.1 us
    pallas_call x9, Pallas kernels, call(): pl.pallas_call(run, out_shape=outs, in_specs=[SMEM] * scalars + [VMEM] *...  14.8 us
    ppermute x8, waiting for transfers between devices, moved(): return lax.ppermute(values, ('lat', 'lon'), pairs)  7.76 us
    all_to_all x1, starting transfers between devices, body(): incoming = lax.all_to_all(outgoing, 'lon', 0, 0, tiled=True)  6.88 us
    all_to_all x1, waiting for transfers between devices, body(): lax.all_to_all(shares, 'lon', 0, 0, tiled=True).reshape(3 * third, lanes)  5.31 us
    all_to_all x1, starting transfers between devices, body(): lax.all_to_all(shares, 'lon', 0, 0, tiled=True).reshape(3 * third, lanes)  5.02 us
    pallas_call x1, Pallas kernels, body(): pl.pallas_call(slots_kernel, out_shape=shaped(lon_devices, state_rows + s...  1.9 us
    ppermute x1, waiting for transfers between devices, body(): gathered += (lax.ppermute(gathered[0], 'lat', swap),)  1.44 us
  transfers between devices with their start and end apart: 12, of which 5 were waited for; matrix products, arithmetic and copies ran while one was open for 1% of the time, Pallas kernels for 14%

profile of v10, /device:TPU:0, one launch (start us, length us, event | category | flops | bytes accessed | tf_op | source)
XLA Modules:
  0.0 62.5 jit_solution(2837221714022545250)
XLA Ops:
  0.6 0.0 copy-start.1
  0.6 0.0 copy-start.2
  0.7 0.1 pad_add_fusion.refs_0_.place_ref
  0.7 1.6 %shard_map.136 = (f32[1280,128]{1,0:T(8,128)S(1)}, bf16[80,128]{1,0:T(8,128)(2,1)S(1)}) custom-call(s32[4]{0:T(128)S(1)} %pad_add_fusion.refs_0_.place_ref, bf16[16,16,128]{2,1,0:T(8,128)(2,1)} %refs_1_.2, bf16[64,16,128]{2,1,0:T(8,128)(2,1)} %refs_2_.3), custom_call_target="tpu_custom_call" | custom-call | bytes 655360 | tf_op jit(solution)/shard_map/pallas_call | solution.py:46
  2.4 0.5 collective-permute-start
  2.9 0.4 shard_map.137
  3.2 0.5 collective-permute-done.refs_0_.refs_1_.refs_4_.refs_5_
  3.7 0.1 shard_map.138
  3.8 2.9 %collective-permute-start.1 = (bf16[80,128]{1,0:T(8,128)(2,1)S(1)}, bf16[80,128]{1,0:T(8,128)(2,1)S(1)}, u32[]{:S(2)}, u32[]{:S(2)}) collective-permute-start(bf16[80,128]{1,0:T(8,128)(2,1)S(1)} %get-tuple-element.49), channel_id=1, source_target_pairs={{0,1},{1,2},{2,3},{3,4},{4,5},{5,6},{6,7},{7,8},{8,9},{9,10},{10,1... | collective-permute-start | bytes 61448 | tf_op jit(solution)/shard_map/ppermute | solution.py:490
  6.7 4.1 %collective-permute-start.2 = (bf16[80,128]{1,0:T(8,128)(2,1)S(1)}, bf16[80,128]{1,0:T(8,128)(2,1)S(1)}, u32[]{:S(2)}, u32[]{:S(2)}) collective-permute-start(bf16[80,128]{1,0:T(8,128)(2,1)S(1)} %get-tuple-element.50), channel_id=1, source_target_pairs={{0,15},{1,0},{2,1},{3,2},{4,3},{5,4},{6,5},{7,6},{8,7},{9,8},{10,9... | collective-permute-start | bytes 61448 | tf_op jit(solution)/shard_map/ppermute | solution.py:490
  10.8 1.8 %shard_map.139 = (bf16[64,2048]{1,0:T(8,128)(2,1)S(1)}, bf16[64,2048]{1,0:T(8,128)(2,1)S(1)}, bf16[64,2048]{1,0:T(8,128)(2,1)S(1)}, bf16[256,768]{1,0:T(8,128)(2,1)S(1)}, f32[256,128]{1,0:T(8,128)S(1)}) custom-call(f32[1,256]{1,0:T(1,128)} %bitcast.15, bf16[720,256]{1,0:T(8,128)(2,1)} %bitcast.13, bf16[64,16,128]{2,1,0:T(8,128)(2,1)} %refs_2_.4, ...), custom_call_target="tpu_custom_call" | custom-call | bytes 1572864 | tf_op jit(solution)/shard_map/pallas_call | solution.py:46
  12.6 0.0 collective-permute-done.1.refs_6_
  12.6 0.0 collective-permute-done.2.refs_7_
  12.6 0.0 copy-done.1
  12.7 0.0 copy-done.2
  12.7 3.2 %shard_map.140 = (bf16[64,2048]{1,0:T(8,128)(2,1)S(1)}, f32[64,2048]{1,0:T(8,128)S(1)}, f32[64,2048]{1,0:T(8,128)S(1)}, f32[768,128]{1,0:T(8,128)S(1)}, f32[768,...) custom-call(s32[4]{0:T(128)S(1)} %pad_add_fusion.refs_0_.place_ref, s32[1,128]{1,0:T(1,128)S(1)} %copy-done.2, ...), custom_call_target="tpu_custom_call" | custom-call | flops 1509949440 | bytes 2097152 | tf_op jit(solution)/shard_map/pallas_call | solution.py:46
  15.9 0.0 copy-start.3
  15.9 0.1 collective-permute-start.3
  16.0 1.9 %shard_map.141.refs_2_ = bf16[16,176,128]{2,1,0:T(8,128)(2,1)} custom-call(s32[4]{0:T(128)S(1)} %pad_add_fusion.refs_0_.place_ref, s32[1,128]{1,0:T(1,128)S(1)} %copy-done.2, s32[1,128]{1,0:T(1,128)S(1)} %copy-done.1, f32[64,2048]{1,0:T(8,128)S(1)} %get-tuple-element.58.state_ref), custom_call_target="tpu_custom_call" | custom-call | bytes 1048576 | tf_op jit(solution)/shard_map/pallas_call | solution.py:609
  17.9 0.0 collective-permute-done.3.refs_1_
  17.9 0.0 copy-start
  17.9 0.7 %shard_map.142 = (bf16[16,176,128]{2,1,0:T(8,128)(2,1)}, f32[8,128]{1,0:T(8,128)S(1)}) custom-call(f32[768,128]{1,0:T(8,128)S(1)} %get-tuple-element.56.refs_0_, f32[768,128]{1,0:T(8,128)S(1)} %collective-permute-done.3.refs_1_, bf16[16,176,128]{2,1,0:T(8,128)(2,1)} %shard_map.141.refs_2_), custom_call_target="tpu_custom_call", output_to_operand_aliasing={{0}: (2, {})} | custom-call | bytes 1572864 | tf_op jit(solution)/shard_map/pallas_call | solution.py:625
  18.6 0.0 copy-done.3
  18.6 6.9 %all-to-all-start = ((bf16[16,176,128]{2,1,0:T(8,128)(2,1)}), bf16[16,176,128]{2,1,0:T(8,128)(2,1)S(1)}, u32[]{:S(2)}, u32[]{:S(2)}) async-start(bf16[16,176,128]{2,1,0:T(8,128)(2,1)} %get-tuple-element.59), calls=%async_computation | async-start | bytes 1441792 | tf_op jit(solution)/shard_map/all_to_all | solution.py:640
  25.5 0.0 copy-done
  25.5 0.0 copy-start.4
  25.5 1.3 %copy-done.4 = bf16[256,2560]{1,0:T(8,128)(2,1)S(1)} copy-done((bf16[256,2560]{1,0:T(8,128)(2,1)S(1)}, bf16[256,2560]{1,0:T(8,128)(2,1)}, u32[]{:S(2)}) %copy-start.4) | copy-done | bytes 1310744
  26.9 2.6 %shard_map.143 = (f32[64,2048]{1,0:T(8,128)S(1)}, bf16[64,128]{1,0:T(8,128)(2,1)S(1)}, bf16[64,128]{1,0:T(8,128)(2,1)S(1)}, bf16[64,128]{1,0:T(8,128)(2,1)S(1)}, bf16[64,128]{1,0:T(8,128)(2,1)S(1)}) custom-call(s32[4]{0:T(128)S(1)} %pad_add_fusion.refs_0_.place_ref, bf16[256,2560]{1,0:T(8,128)(2,1)S(1)} %copy-done.4, bf16[720,256]{1,0:T(8,128)(2,1)S(1)} %bitcast.14, ...), custom_call_target="tpu_custom_call" | custom-call | flops 603979776 | bytes 4194304 | tf_op jit(solution)/shard_map/pallas_call | solution.py:46
  29.5 0.3 collective-permute-start.4
  29.8 1.8 %collective-permute-start.7 = (bf16[64,128]{1,0:T(8,128)(2,1)S(1)}, bf16[64,128]{1,0:T(8,128)(2,1)S(1)}, u32[]{:S(2)}, u32[]{:S(2)}) collective-permute-start(bf16[64,128]{1,0:T(8,128)(2,1)S(1)} %get-tuple-element.64), channel_id=1, source_target_pairs={{0,1},{1,2},{2,3},{3,4},{4,5},{5,6},{6,7},{7,8},{8,9},{9,10},{10,1... | collective-permute-start | bytes 49160 | tf_op jit(solution)/shard_map/ppermute | solution.py:490
  31.5 3.9 %collective-permute-start.8 = (bf16[64,128]{1,0:T(8,128)(2,1)S(1)}, bf16[64,128]{1,0:T(8,128)(2,1)S(1)}, u32[]{:S(2)}, u32[]{:S(2)}) collective-permute-start(bf16[64,128]{1,0:T(8,128)(2,1)S(1)} %get-tuple-element.65), channel_id=1, source_target_pairs={{0,15},{1,0},{2,1},{3,2},{4,3},{5,4},{6,5},{7,6},{8,7},{9,8},{10,9... | collective-permute-start | bytes 49160 | tf_op jit(solution)/shard_map/ppermute | solution.py:490
  35.4 1.3 %collective-permute-start.6 = (bf16[64,128]{1,0:T(8,128)(2,1)S(1)}, bf16[64,128]{1,0:T(8,128)(2,1)S(1)}, u32[]{:S(2)}, u32[]{:S(2)}) collective-permute-start(bf16[64,128]{1,0:T(8,128)(2,1)S(1)} %get-tuple-element.63), channel_id=1, source_target_pairs={{0,31},{1,16},{2,17},{3,18},{4,19},{5,20},{6,21},{7,22},{8,23},{9,... | collective-permute-start | bytes 49160 | tf_op jit(solution)/shard_map/ppermute | solution.py:490
  36.6 0.5 collective-permute-start.5
  37.1 0.0 collective-permute-done.4.refs_2_.refs_3_.refs_6_.refs_7_
  37.1 7.3 %collective-permute-done.7.refs_8_.refs_12_ = bf16[64,128]{1,0:T(8,128)(2,1)S(1)} collective-permute-done((bf16[64,128]{1,0:T(8,128)(2,1)S(1)}, bf16[64,128]{1,0:T(8,128)(2,1)S(1)}, u32[]{:S(2)}, u32[]{:S(2)}) %collective-permute-start.7) | collective-permute-done | bytes 16416 | tf_op jit(solution)/shard_map/ppermute | solution.py:490
  44.4 0.0 collective-permute-done.8.refs_9_.refs_13_
  44.4 0.0 collective-permute-done.6.refs_5_.refs_7_.refs_9_.refs_11_
  44.4 0.0 collective-permute-done.5.refs_4_.refs_6_.refs_8_.refs_10_
  44.4 0.7 %all-to-all-done.refs_1_.refs_4_ = bf16[16,176,128]{2,1,0:T(8,128)(2,1)S(1)} async-done(((bf16[16,176,128]{2,1,0:T(8,128)(2,1)}), bf16[16,176,128]{2,1,0:T(8,128)(2,1)S(1)}, u32[]{:S(2)}, u32[]{:S(2)}) %all-to-all-start) | async-done | bytes 720928 | tf_op jit(solution)/shard_map/all_to_all | solution.py:640
  45.2 1.3 %shard_map.144 = (bf16[16,48,128]{2,1,0:T(8,128)(2,1)}, f32[8,128]{1,0:T(8,128)S(1)}) custom-call(s32[4]{0:T(128)S(1)} %pad_add_fusion.refs_0_.place_ref, bf16[16,176,128]{2,1,0:T(8,128)(2,1)S(1)} %all-to-all-done.refs_1_.refs_4_, bf16[64,128]{1,0:T(8,128)(2,1)S(1)} %collective-permute-done.4.refs_2_.refs_3_.refs_6_.refs_7_, ...), custom_call_target="tpu_custom_call" | custom-call | bytes 393216 | tf_op jit(solution)/shard_map/pallas_call | solution.py:46
  46.4 5.0 %all-to-all-start.1 = ((bf16[16,48,128]{2,1,0:T(8,128)(2,1)}), bf16[16,48,128]{2,1,0:T(8,128)(2,1)S(1)}, u32[]{:S(2)}, u32[]{:S(2)}) async-start(bf16[16,48,128]{2,1,0:T(8,128)(2,1)} %get-tuple-element.66), calls=%async_computation.1 | async-start | bytes 393216 | tf_op jit(solution)/shard_map/all_to_all | solution.py:684
  51.5 0.1 reshape.35
  51.6 0.1 reduce_or.9
  51.7 0.1 convert_reduce_fusion
  51.8 0.1 select_reduce_fusion.refs_1_
  51.9 2.3 %shard_map.145 = (bf16[64,16,128]{2,1,0:T(8,128)(2,1)}, f32[1024,128]{1,0:T(8,128)}, f32[4,64,256]{2,1,0:T(8,128)}, f32[1024,128]{1,0:T(8,128)}) custom-call(s32[4]{0:T(128)S(1)} %pad_add_fusion.refs_0_.place_ref, s32[4]{0:T(128)S(1)} %select_reduce_fusion.refs_1_, bf16[64,2048]{1,0:T(8,128)(2,1)S(1)} %get-tuple-element.67.refs_2_, ...), custom_call_target="tpu_custom_call" | custom-call | bytes 4194304 | tf_op jit(solution)/shard_map/pallas_call | solution.py:46
  54.2 5.3 %all-to-all-done.1 = bf16[16,48,128]{2,1,0:T(8,128)(2,1)S(1)} async-done(((bf16[16,48,128]{2,1,0:T(8,128)(2,1)}), bf16[16,48,128]{2,1,0:T(8,128)(2,1)S(1)}, u32[]{:S(2)}, u32[]{:S(2)}) %all-to-all-start.1) | async-done | bytes 196640 | tf_op jit(solution)/shard_map/all_to_all | solution.py:684
  59.5 0.0 collective-permute-start.9
  59.5 1.4 %collective-permute-done.9.refs_2_ = bf16[768,128]{1,0:T(8,128)(2,1)S(1)} collective-permute-done((bf16[768,128]{1,0:T(8,128)(2,1)S(1)}, bf16[768,128]{1,0:T(8,128)(2,1)S(1)}, u32[]{:S(2)}, u32[]{:S(2)}) %collective-permute-start.9) | collective-permute-done | bytes 196640 | tf_op jit(solution)/shard_map/ppermute | solution.py:689
  61.0 1.5 %shard_map.146 = (f32[720,256]{1,0:T(8,128)}, f32[1,256]{1,0:T(1,128)}) custom-call(s32[4]{0:T(128)S(1)} %pad_add_fusion.refs_0_.place_ref, bf16[768,128]{1,0:T(8,128)(2,1)S(1)} %bitcast.12, bf16[768,128]{1,0:T(8,128)(2,1)S(1)} %collective-permute-done.9.refs_2_), custom_call_target="tpu_custom_call" | custom-call | bytes 1179648 | tf_op jit(solution)/shard_map/pallas_call | solution.py:46
  (1 shorter events, 0.0 us)
Async XLA Ops:
  0.6 12.0 %copy-start.1 = (s32[1,128]{1,0:T(1,128)S(1)}, s32[1,128]{1,0:T(1,128)}, u32[]{:S(2)}) copy-start(s32[1,128]{1,0:T(1,128)} %owner_ref.1) | copy-start | bytes 1540
  0.6 12.0 %copy-start.2 = (s32[1,128]{1,0:T(1,128)S(1)}, s32[1,128]{1,0:T(1,128)}, u32[]{:S(2)}) copy-start(s32[1,128]{1,0:T(1,128)} %wet_ref.1) | copy-start | bytes 1540
  2.4 1.4 %collective-permute-start = (bf16[80,128]{1,0:T(8,128)(2,1)S(1)}, bf16[80,128]{1,0:T(8,128)(2,1)S(1)}, u32[]{:S(2)}, u32[]{:S(2)}) collective-permute-start(bf16[80,128]{1,0:T(8,128)(2,1)S(1)} %get-tuple-element.46), channel_id=1, source_target_pairs={{0,16},{1,17},{2,18},{3,19},{4,20},{5,21},{6,22},{7,23},{8,24},{9,... | collective-permute-start | bytes 61448 | tf_op jit(solution)/shard_map/ppermute | solution.py:490
  3.8 8.8 %collective-permute-start.1 = (bf16[80,128]{1,0:T(8,128)(2,1)S(1)}, bf16[80,128]{1,0:T(8,128)(2,1)S(1)}, u32[]{:S(2)}, u32[]{:S(2)}) collective-permute-start(bf16[80,128]{1,0:T(8,128)(2,1)S(1)} %get-tuple-element.49), channel_id=1, source_target_pairs={{0,1},{1,2},{2,3},{3,4},{4,5},{5,6},{6,7},{7,8},{8,9},{9,10},{10,1... | collective-permute-start | bytes 61448 | tf_op jit(solution)/shard_map/ppermute | solution.py:490
  6.7 5.9 %collective-permute-start.2 = (bf16[80,128]{1,0:T(8,128)(2,1)S(1)}, bf16[80,128]{1,0:T(8,128)(2,1)S(1)}, u32[]{:S(2)}, u32[]{:S(2)}) collective-permute-start(bf16[80,128]{1,0:T(8,128)(2,1)S(1)} %get-tuple-element.50), channel_id=1, source_target_pairs={{0,15},{1,0},{2,1},{3,2},{4,3},{5,4},{6,5},{7,6},{8,7},{9,8},{10,9... | collective-permute-start | bytes 61448 | tf_op jit(solution)/shard_map/ppermute | solution.py:490
  15.9 2.8 %copy-start.3 = (bf16[256,2560]{1,0:T(8,128)(2,1)}, bf16[256,2560]{1,0:T(8,128)(2,1)S(1)}, u32[]{:S(2)}) copy-start(bf16[256,2560]{1,0:T(8,128)(2,1)S(1)} %get-tuple-element.60.refs_1_) | copy-start | bytes 3932164
  15.9 2.0 %collective-permute-start.3 = (f32[768,128]{1,0:T(8,128)S(1)}, f32[768,128]{1,0:T(8,128)S(1)}, u32[]{:S(2)}, u32[]{:S(2)}) collective-permute-start(f32[768,128]{1,0:T(8,128)S(1)} %get-tuple-element.57), channel_id=1, source_target_pairs={{0,16},{16,0},{1,17},{17,1},{2,18},{18,2},{3,19},{19,3},{4,20},{20... | collective-permute-start | bytes 1179656 | tf_op jit(solution)/shard_map/ppermute | solution.py:602
  17.9 7.7 %copy-start = (bf16[256,720]{0,1:T(8,128)(2,1)S(1)}, bf16[256,720]{0,1:T(8,128)(2,1)}, u32[]{:S(2)}) copy-start(bf16[256,720]{0,1:T(8,128)(2,1)} %param.16) | copy-start | bytes 1105924
  18.6 26.5 %all-to-all-start = ((bf16[16,176,128]{2,1,0:T(8,128)(2,1)}), bf16[16,176,128]{2,1,0:T(8,128)(2,1)S(1)}, u32[]{:S(2)}, u32[]{:S(2)}) async-start(bf16[16,176,128]{2,1,0:T(8,128)(2,1)} %get-tuple-element.59), calls=%async_computation | async-start | bytes 1441792 | tf_op jit(solution)/shard_map/all_to_all | solution.py:640
  25.5 1.3 %copy-start.4 = (bf16[256,2560]{1,0:T(8,128)(2,1)S(1)}, bf16[256,2560]{1,0:T(8,128)(2,1)}, u32[]{:S(2)}) copy-start(bf16[256,2560]{1,0:T(8,128)(2,1)} %copy-done.3) | copy-start | bytes 3932164
  29.5 7.7 %collective-permute-start.4 = (bf16[64,128]{1,0:T(8,128)(2,1)S(1)}, bf16[64,128]{1,0:T(8,128)(2,1)S(1)}, u32[]{:S(2)}, u32[]{:S(2)}) collective-permute-start(bf16[64,128]{1,0:T(8,128)(2,1)S(1)} %get-tuple-element.62), channel_id=1, source_target_pairs={{0,16},{1,17},{2,18},{3,19},{4,20},{5,21},{6,22},{7,23},{8,24},{9,... | collective-permute-start | bytes 49160 | tf_op jit(solution)/shard_map/ppermute | solution.py:490
  29.8 14.6 %collective-permute-start.7 = (bf16[64,128]{1,0:T(8,128)(2,1)S(1)}, bf16[64,128]{1,0:T(8,128)(2,1)S(1)}, u32[]{:S(2)}, u32[]{:S(2)}) collective-permute-start(bf16[64,128]{1,0:T(8,128)(2,1)S(1)} %get-tuple-element.64), channel_id=1, source_target_pairs={{0,1},{1,2},{2,3},{3,4},{4,5},{5,6},{6,7},{7,8},{8,9},{9,10},{10,1... | collective-permute-start | bytes 49160 | tf_op jit(solution)/shard_map/ppermute | solution.py:490
  31.5 12.9 %collective-permute-start.8 = (bf16[64,128]{1,0:T(8,128)(2,1)S(1)}, bf16[64,128]{1,0:T(8,128)(2,1)S(1)}, u32[]{:S(2)}, u32[]{:S(2)}) collective-permute-start(bf16[64,128]{1,0:T(8,128)(2,1)S(1)} %get-tuple-element.65), channel_id=1, source_target_pairs={{0,15},{1,0},{2,1},{3,2},{4,3},{5,4},{6,5},{7,6},{8,7},{9,8},{10,9... | collective-permute-start | bytes 49160 | tf_op jit(solution)/shard_map/ppermute | solution.py:490
  35.4 9.0 %collective-permute-start.6 = (bf16[64,128]{1,0:T(8,128)(2,1)S(1)}, bf16[64,128]{1,0:T(8,128)(2,1)S(1)}, u32[]{:S(2)}, u32[]{:S(2)}) collective-permute-start(bf16[64,128]{1,0:T(8,128)(2,1)S(1)} %get-tuple-element.63), channel_id=1, source_target_pairs={{0,31},{1,16},{2,17},{3,18},{4,19},{5,20},{6,21},{7,22},{8,23},{9,... | collective-permute-start | bytes 49160 | tf_op jit(solution)/shard_map/ppermute | solution.py:490
  36.6 7.8 %collective-permute-start.5 = (bf16[64,128]{1,0:T(8,128)(2,1)S(1)}, bf16[64,128]{1,0:T(8,128)(2,1)S(1)}, u32[]{:S(2)}, u32[]{:S(2)}) collective-permute-start(bf16[64,128]{1,0:T(8,128)(2,1)S(1)} %get-tuple-element.63), channel_id=1, source_target_pairs={{0,17},{1,18},{2,19},{3,20},{4,21},{5,22},{6,23},{7,24},{8,25},{9,... | collective-permute-start | bytes 49160 | tf_op jit(solution)/shard_map/ppermute | solution.py:490
  46.4 13.1 %all-to-all-start.1 = ((bf16[16,48,128]{2,1,0:T(8,128)(2,1)}), bf16[16,48,128]{2,1,0:T(8,128)(2,1)S(1)}, u32[]{:S(2)}, u32[]{:S(2)}) async-start(bf16[16,48,128]{2,1,0:T(8,128)(2,1)} %get-tuple-element.66), calls=%async_computation.1 | async-start | bytes 393216 | tf_op jit(solution)/shard_map/all_to_all | solution.py:684
  59.5 1.4 %collective-permute-start.9 = (bf16[768,128]{1,0:T(8,128)(2,1)S(1)}, bf16[768,128]{1,0:T(8,128)(2,1)S(1)}, u32[]{:S(2)}, u32[]{:S(2)}) collective-permute-start(bf16[768,128]{1,0:T(8,128)(2,1)S(1)} %bitcast.11), channel_id=1, source_target_pairs={{0,16},{16,0},{1,17},{17,1},{2,18},{18,2},{3,19},{19,3},{4,20},{20... | collective-permute-start | bytes 589832 | tf_op jit(solution)/shard_map/ppermute | solution.py:689

commit v11 on v9

--- a/solution.py
+++ b/solution.py
@@ -396,19 +396,34 @@
     return jnp.where(index == row + 1, rest, block)
 
 
-def slots_kernel(place_ref, wet_ref, owner_ref, tiles_ref, out_ref):
+def slots_kernel(place_ref, wet_ref, owner_ref, tiles_ref, out_ref, slots_ref, semaphores):
     tile_cols, hid, cells = tiles_ref.shape
-    slots, _, lanes = out_ref.shape
-    out_ref[...] = jnp.zeros(out_ref.shape, BF16)
+    slots, state_rows, lanes = slots_ref.shape
+    slots_ref[...] = jnp.zeros(slots_ref.shape, BF16)
     for tile in range(tile_cols):
         index = place_ref[1] * tile_cols + tile
 
         @pl.when(wet_ref[0, index] > 0)
         def _():
             for piece in range(cells // lanes):
-                out_ref[owner_ref[0, index], piece * hid : (piece + 1) * hid] = tiles_ref[
+                slots_ref[owner_ref[0, index], piece * hid : (piece + 1) * hid] = tiles_ref[
                     tile, :, piece * lanes : (piece + 1) * lanes
                 ]
+
+    count = semaphores.shape[0]
+    some = slots // count
+    copies = [
+        pltpu.make_async_copy(
+            slots_ref.at[pl.ds(index * some, some)],
+            out_ref.at[pl.ds(index * some, some), pl.ds(0, state_rows)],
+            semaphores.at[index],
+        )
+        for index in range(count)
+    ]
+    for copy in copies:
+        copy.start()
+    for copy in copies:
+        copy.wait()
 
 
 def pack_kernel(span, count, *refs):
@@ -588,14 +603,22 @@
         weight_parts = (lax.psum(weight_parts[0], "lat"),)
     state_rows = hid * TILE * TILE // lanes
     share = 3 * third // lon_devices
-    slots = call(
+    anywhere = pl.BlockSpec(memory_space=pl.ANY)
+    copies = 4 if lon_devices % 4 == 0 else 1
+    slots = pl.pallas_call(
         slots_kernel,
-        shaped(lon_devices, state_rows + share, lanes),
-        (place, wet_mask, tile_owner, tiles),
-        scalars=3,
-        moved=4 * lon_devices * hid * TILE * TILE,
-    )
-    anywhere = pl.BlockSpec(memory_space=pl.ANY)
+        out_shape=shaped(lon_devices, state_rows + share, lanes),
+        in_specs=[SMEM] * 3 + [VMEM],
+        out_specs=anywhere,
+        scratch_shapes=[
+            pltpu.VMEM((lon_devices, state_rows, lanes), BF16),
+            pltpu.SemaphoreType.DMA((copies,)),
+        ],
+        compiler_params=pltpu.CompilerParams(vmem_limit_bytes=LIMIT),
+        cost_estimate=pl.CostEstimate(
+            flops=0, bytes_accessed=4 * lon_devices * hid * TILE * TILE, transcendentals=0
+        ),
+    )(place, wet_mask, tile_owner, tiles)
     count = len(weight_parts)
     outgoing, packed = pl.pallas_call(
         lambda *refs: pack_kernel(span, count, *refs),

time: 62.5 us -> 62.4 us (level)
    pallas_call x10 -> x9, Pallas kernels: 16.3 us -> 14.7 us  [call(): pl.pallas_call(run, out_shape=outs, in_specs=[SMEM] * scalars + [VMEM] *...]
    pallas_call x0 -> x1, Pallas kernels: none -> 1.57 us  [body(): pl.pallas_call(slots_kernel, out_shape=shaped(lon_devices, state_rows + s...]
where the time goes in v11:
time: 62.4 us; the launch traced here: 62 us
  starting transfers between devices  26.8 us (43%)
  Pallas kernels  17 us (27%)
  waiting for transfers between devices  15.5 us (25%)
  local copies, waits for them, and re-layouts  1.42 us (2%)
  between operations  0.83 us (1%)
    ppermute x8, starting transfers between devices, moved(): return lax.ppermute(values, ('lat', 'lon'), pairs)  15 us
    pallas_call x9, Pallas kernels, call(): pl.pallas_call(run, out_shape=outs, in_specs=[SMEM] * scalars + [VMEM] *...  14.7 us
    ppermute x8, waiting for transfers between devices, moved(): return lax.ppermute(values, ('lat', 'lon'), pairs)  7.62 us
    all_to_all x1, starting transfers between devices, body(): incoming = lax.all_to_all(outgoing, 'lon', 0, 0, tiled=True)  6.88 us
    all_to_all x1, waiting for transfers between devices, body(): lax.all_to_all(shares, 'lon', 0, 0, tiled=True).reshape(3 * third, lanes)  5.31 us
    all_to_all x1, starting transfers between devices, body(): lax.all_to_all(shares, 'lon', 0, 0, tiled=True).reshape(3 * third, lanes)  4.84 us
    pallas_call x1, Pallas kernels, body(): pl.pallas_call(slots_kernel, out_shape=shaped(lon_devices, state_rows + s...  1.57 us
    ppermute x1, waiting for transfers between devices, body(): gathered += (lax.ppermute(gathered[0], 'lat', swap),)  1.44 us
  transfers between devices with their start and end apart: 12, of which 6 were waited for; matrix products, arithmetic and copies ran while one was open for 1% of the time, Pallas kernels for 14%

profile of v11, /device:TPU:0, one launch (start us, length us, event | category | flops | bytes accessed | tf_op | source)
XLA Modules:
  0.0 62.0 jit_solution(2566273787770399095)
XLA Ops:
  0.6 0.0 copy-start.1
  0.6 0.0 copy-start.2
  0.7 0.1 pad_add_fusion.refs_0_.place_ref
  0.7 1.6 %shard_map.136 = (f32[1280,128]{1,0:T(8,128)S(1)}, bf16[80,128]{1,0:T(8,128)(2,1)S(1)}) custom-call(s32[4]{0:T(128)S(1)} %pad_add_fusion.refs_0_.place_ref, bf16[16,16,128]{2,1,0:T(8,128)(2,1)} %refs_1_.2, bf16[64,16,128]{2,1,0:T(8,128)(2,1)} %refs_2_.3), custom_call_target="tpu_custom_call" | custom-call | bytes 655360 | tf_op jit(solution)/shard_map/pallas_call | solution.py:46
  2.4 0.5 collective-permute-start
  2.9 0.4 shard_map.137
  3.2 0.5 collective-permute-done.refs_0_.refs_1_.refs_4_.refs_5_
  3.7 0.1 shard_map.138
  3.8 2.9 %collective-permute-start.1 = (bf16[80,128]{1,0:T(8,128)(2,1)S(1)}, bf16[80,128]{1,0:T(8,128)(2,1)S(1)}, u32[]{:S(2)}, u32[]{:S(2)}) collective-permute-start(bf16[80,128]{1,0:T(8,128)(2,1)S(1)} %get-tuple-element.49), channel_id=1, source_target_pairs={{0,1},{1,2},{2,3},{3,4},{4,5},{5,6},{6,7},{7,8},{8,9},{9,10},{10,1... | collective-permute-start | bytes 61448 | tf_op jit(solution)/shard_map/ppermute | solution.py:489
  6.7 4.1 %collective-permute-start.2 = (bf16[80,128]{1,0:T(8,128)(2,1)S(1)}, bf16[80,128]{1,0:T(8,128)(2,1)S(1)}, u32[]{:S(2)}, u32[]{:S(2)}) collective-permute-start(bf16[80,128]{1,0:T(8,128)(2,1)S(1)} %get-tuple-element.50), channel_id=1, source_target_pairs={{0,15},{1,0},{2,1},{3,2},{4,3},{5,4},{6,5},{7,6},{8,7},{9,8},{10,9... | collective-permute-start | bytes 61448 | tf_op jit(solution)/shard_map/ppermute | solution.py:489
  10.8 1.8 %shard_map.139 = (bf16[64,2048]{1,0:T(8,128)(2,1)S(1)}, bf16[64,2048]{1,0:T(8,128)(2,1)S(1)}, bf16[64,2048]{1,0:T(8,128)(2,1)S(1)}, bf16[256,768]{1,0:T(8,128)(2,1)S(1)}, f32[256,128]{1,0:T(8,128)S(1)}) custom-call(f32[1,256]{1,0:T(1,128)} %bitcast.15, bf16[720,256]{1,0:T(8,128)(2,1)} %bitcast.13, bf16[64,16,128]{2,1,0:T(8,128)(2,1)} %refs_2_.4, ...), custom_call_target="tpu_custom_call" | custom-call | bytes 1572864 | tf_op jit(solution)/shard_map/pallas_call | solution.py:46
  12.6 0.0 collective-permute-done.1.refs_6_
  12.6 0.0 collective-permute-done.2.refs_7_
  12.6 0.0 copy-done.1
  12.7 0.0 copy-done.2
  12.7 3.1 %shard_map.140 = (bf16[64,2048]{1,0:T(8,128)(2,1)S(1)}, f32[64,2048]{1,0:T(8,128)S(1)}, bf16[8,64,256]{2,1,0:T(8,128)(2,1)S(1)}, f32[768,128]{1,0:T(8,128)S(1)},...) custom-call(s32[4]{0:T(128)S(1)} %pad_add_fusion.refs_0_.place_ref, s32[1,128]{1,0:T(1,128)S(1)} %copy-done.2, ...), custom_call_target="tpu_custom_call" | custom-call | flops 1509949440 | bytes 2097152 | tf_op jit(solution)/shard_map/pallas_call | solution.py:46
  15.8 0.0 copy-start.3
  15.8 0.1 collective-permute-start.3
  15.9 1.6 %shard_map.141.refs_2_ = bf16[16,176,128]{2,1,0:T(8,128)(2,1)} custom-call(s32[4]{0:T(128)S(1)} %pad_add_fusion.refs_0_.place_ref, s32[1,128]{1,0:T(1,128)S(1)} %copy-done.2, s32[1,128]{1,0:T(1,128)S(1)} %copy-done.1, bf16[8,64,256]{2,1,0:T(8,128)(2,1)S(1)} %get-tuple-element.58.tiles_ref), custom_call_target="tpu_custom_call" | custom-call | bytes 1048576 | tf_op jit(solution)/shard_map/pallas_call | solution.py:608
  17.5 0.1 collective-permute-done.3.refs_1_
  17.6 0.0 copy-start
  17.6 0.7 %shard_map.142 = (bf16[16,176,128]{2,1,0:T(8,128)(2,1)}, f32[8,128]{1,0:T(8,128)S(1)}) custom-call(f32[768,128]{1,0:T(8,128)S(1)} %get-tuple-element.56.refs_0_, f32[768,128]{1,0:T(8,128)S(1)} %collective-permute-done.3.refs_1_, bf16[16,176,128]{2,1,0:T(8,128)(2,1)} %shard_map.141.refs_2_), custom_call_target="tpu_custom_call", output_to_operand_aliasing={{0}: (2, {})} | custom-call | bytes 1572864 | tf_op jit(solution)/shard_map/pallas_call | solution.py:623
  18.3 0.0 copy-done.3
  18.3 6.9 %all-to-all-start = ((bf16[16,176,128]{2,1,0:T(8,128)(2,1)}), bf16[16,176,128]{2,1,0:T(8,128)(2,1)S(1)}, u32[]{:S(2)}, u32[]{:S(2)}) async-start(bf16[16,176,128]{2,1,0:T(8,128)(2,1)} %get-tuple-element.59), calls=%async_computation | async-start | bytes 1441792 | tf_op jit(solution)/shard_map/all_to_all | solution.py:638
  25.2 0.0 copy-done
  25.2 0.0 copy-start.4
  25.3 1.3 %copy-done.4 = bf16[256,2560]{1,0:T(8,128)(2,1)S(1)} copy-done((bf16[256,2560]{1,0:T(8,128)(2,1)S(1)}, bf16[256,2560]{1,0:T(8,128)(2,1)}, u32[]{:S(2)}) %copy-start.4) | copy-done | bytes 1310744
  26.6 2.6 %shard_map.143 = (f32[64,2048]{1,0:T(8,128)S(1)}, bf16[64,128]{1,0:T(8,128)(2,1)S(1)}, bf16[64,128]{1,0:T(8,128)(2,1)S(1)}, bf16[64,128]{1,0:T(8,128)(2,1)S(1)}, bf16[64,128]{1,0:T(8,128)(2,1)S(1)}) custom-call(s32[4]{0:T(128)S(1)} %pad_add_fusion.refs_0_.place_ref, bf16[256,2560]{1,0:T(8,128)(2,1)S(1)} %copy-done.4, bf16[720,256]{1,0:T(8,128)(2,1)S(1)} %bitcast.14, ...), custom_call_target="tpu_custom_call" | custom-call | flops 603979776 | bytes 4194304 | tf_op jit(solution)/shard_map/pallas_call | solution.py:46
  29.2 0.1 collective-permute-start.4
  29.3 1.9 %collective-permute-start.7 = (bf16[64,128]{1,0:T(8,128)(2,1)S(1)}, bf16[64,128]{1,0:T(8,128)(2,1)S(1)}, u32[]{:S(2)}, u32[]{:S(2)}) collective-permute-start(bf16[64,128]{1,0:T(8,128)(2,1)S(1)} %get-tuple-element.64), channel_id=1, source_target_pairs={{0,1},{1,2},{2,3},{3,4},{4,5},{5,6},{6,7},{7,8},{8,9},{9,10},{10,1... | collective-permute-start | bytes 49160 | tf_op jit(solution)/shard_map/ppermute | solution.py:489
  31.2 3.7 %collective-permute-start.8 = (bf16[64,128]{1,0:T(8,128)(2,1)S(1)}, bf16[64,128]{1,0:T(8,128)(2,1)S(1)}, u32[]{:S(2)}, u32[]{:S(2)}) collective-permute-start(bf16[64,128]{1,0:T(8,128)(2,1)S(1)} %get-tuple-element.65), channel_id=1, source_target_pairs={{0,15},{1,0},{2,1},{3,2},{4,3},{5,4},{6,5},{7,6},{8,7},{9,8},{10,9... | collective-permute-start | bytes 49160 | tf_op jit(solution)/shard_map/ppermute | solution.py:489
  35.0 1.4 %collective-permute-start.6 = (bf16[64,128]{1,0:T(8,128)(2,1)S(1)}, bf16[64,128]{1,0:T(8,128)(2,1)S(1)}, u32[]{:S(2)}, u32[]{:S(2)}) collective-permute-start(bf16[64,128]{1,0:T(8,128)(2,1)S(1)} %get-tuple-element.63), channel_id=1, source_target_pairs={{0,31},{1,16},{2,17},{3,18},{4,19},{5,20},{6,21},{7,22},{8,23},{9,... | collective-permute-start | bytes 49160 | tf_op jit(solution)/shard_map/ppermute | solution.py:489
  36.4 0.3 collective-permute-start.5
  36.7 0.0 collective-permute-done.4.refs_2_.refs_3_.refs_6_.refs_7_
  36.7 7.1 %collective-permute-done.7.refs_8_.refs_12_ = bf16[64,128]{1,0:T(8,128)(2,1)S(1)} collective-permute-done((bf16[64,128]{1,0:T(8,128)(2,1)S(1)}, bf16[64,128]{1,0:T(8,128)(2,1)S(1)}, u32[]{:S(2)}, u32[]{:S(2)}) %collective-permute-start.7) | collective-permute-done | bytes 16416 | tf_op jit(solution)/shard_map/ppermute | solution.py:489
  43.8 0.0 collective-permute-done.8.refs_9_.refs_13_
  43.8 0.0 collective-permute-done.6.refs_5_.refs_7_.refs_9_.refs_11_
  43.8 0.0 collective-permute-done.5.refs_4_.refs_6_.refs_8_.refs_10_
  43.8 1.0 %all-to-all-done.refs_1_.refs_4_ = bf16[16,176,128]{2,1,0:T(8,128)(2,1)S(1)} async-done(((bf16[16,176,128]{2,1,0:T(8,128)(2,1)}), bf16[16,176,128]{2,1,0:T(8,128)(2,1)S(1)}, u32[]{:S(2)}, u32[]{:S(2)}) %all-to-all-start) | async-done | bytes 720928 | tf_op jit(solution)/shard_map/all_to_all | solution.py:638
  44.9 1.3 %shard_map.144 = (bf16[16,48,128]{2,1,0:T(8,128)(2,1)}, f32[8,128]{1,0:T(8,128)S(1)}) custom-call(s32[4]{0:T(128)S(1)} %pad_add_fusion.refs_0_.place_ref, bf16[16,176,128]{2,1,0:T(8,128)(2,1)S(1)} %all-to-all-done.refs_1_.refs_4_, bf16[64,128]{1,0:T(8,128)(2,1)S(1)} %collective-permute-done.4.refs_2_.refs_3_.refs_6_.refs_7_, ...), custom_call_target="tpu_custom_call" | custom-call | bytes 393216 | tf_op jit(solution)/shard_map/pallas_call | solution.py:46
  46.1 4.8 %all-to-all-start.1 = ((bf16[16,48,128]{2,1,0:T(8,128)(2,1)}), bf16[16,48,128]{2,1,0:T(8,128)(2,1)S(1)}, u32[]{:S(2)}, u32[]{:S(2)}) async-start(bf16[16,48,128]{2,1,0:T(8,128)(2,1)} %get-tuple-element.66), calls=%async_computation.1 | async-start | bytes 393216 | tf_op jit(solution)/shard_map/all_to_all | solution.py:682
  51.0 0.1 reshape.35
  51.1 0.1 reduce_or.9
  51.2 0.1 convert_reduce_fusion
  51.3 0.1 select_reduce_fusion.refs_1_
  51.4 2.3 %shard_map.145 = (bf16[64,16,128]{2,1,0:T(8,128)(2,1)}, f32[1024,128]{1,0:T(8,128)}, f32[4,64,256]{2,1,0:T(8,128)}, f32[1024,128]{1,0:T(8,128)}) custom-call(s32[4]{0:T(128)S(1)} %pad_add_fusion.refs_0_.place_ref, s32[4]{0:T(128)S(1)} %select_reduce_fusion.refs_1_, bf16[64,2048]{1,0:T(8,128)(2,1)S(1)} %get-tuple-element.67.refs_2_, ...), custom_call_target="tpu_custom_call" | custom-call | bytes 4194304 | tf_op jit(solution)/shard_map/pallas_call | solution.py:46
  53.8 5.3 %all-to-all-done.1 = bf16[16,48,128]{2,1,0:T(8,128)(2,1)S(1)} async-done(((bf16[16,48,128]{2,1,0:T(8,128)(2,1)}), bf16[16,48,128]{2,1,0:T(8,128)(2,1)S(1)}, u32[]{:S(2)}, u32[]{:S(2)}) %all-to-all-start.1) | async-done | bytes 196640 | tf_op jit(solution)/shard_map/all_to_all | solution.py:682
  59.1 0.0 collective-permute-start.9
  59.1 1.4 %collective-permute-done.9.refs_2_ = bf16[768,128]{1,0:T(8,128)(2,1)S(1)} collective-permute-done((bf16[768,128]{1,0:T(8,128)(2,1)S(1)}, bf16[768,128]{1,0:T(8,128)(2,1)S(1)}, u32[]{:S(2)}, u32[]{:S(2)}) %collective-permute-start.9) | collective-permute-done | bytes 196640 | tf_op jit(solution)/shard_map/ppermute | solution.py:687
  60.5 1.5 %shard_map.146 = (f32[720,256]{1,0:T(8,128)}, f32[1,256]{1,0:T(1,128)}) custom-call(s32[4]{0:T(128)S(1)} %pad_add_fusion.refs_0_.place_ref, bf16[768,128]{1,0:T(8,128)(2,1)S(1)} %bitcast.12, bf16[768,128]{1,0:T(8,128)(2,1)S(1)} %collective-permute-done.9.refs_2_), custom_call_target="tpu_custom_call" | custom-call | bytes 1179648 | tf_op jit(solution)/shard_map/pallas_call | solution.py:46
  (1 shorter events, 0.0 us)
Async XLA Ops:
  0.6 12.0 %copy-start.1 = (s32[1,128]{1,0:T(1,128)S(1)}, s32[1,128]{1,0:T(1,128)}, u32[]{:S(2)}) copy-start(s32[1,128]{1,0:T(1,128)} %owner_ref.1) | copy-start | bytes 1540
  0.6 12.0 %copy-start.2 = (s32[1,128]{1,0:T(1,128)S(1)}, s32[1,128]{1,0:T(1,128)}, u32[]{:S(2)}) copy-start(s32[1,128]{1,0:T(1,128)} %wet_ref.1) | copy-start | bytes 1540
  2.4 1.4 %collective-permute-start = (bf16[80,128]{1,0:T(8,128)(2,1)S(1)}, bf16[80,128]{1,0:T(8,128)(2,1)S(1)}, u32[]{:S(2)}, u32[]{:S(2)}) collective-permute-start(bf16[80,128]{1,0:T(8,128)(2,1)S(1)} %get-tuple-element.46), channel_id=1, source_target_pairs={{0,16},{1,17},{2,18},{3,19},{4,20},{5,21},{6,22},{7,23},{8,24},{9,... | collective-permute-start | bytes 61448 | tf_op jit(solution)/shard_map/ppermute | solution.py:489
  3.8 8.8 %collective-permute-start.1 = (bf16[80,128]{1,0:T(8,128)(2,1)S(1)}, bf16[80,128]{1,0:T(8,128)(2,1)S(1)}, u32[]{:S(2)}, u32[]{:S(2)}) collective-permute-start(bf16[80,128]{1,0:T(8,128)(2,1)S(1)} %get-tuple-element.49), channel_id=1, source_target_pairs={{0,1},{1,2},{2,3},{3,4},{4,5},{5,6},{6,7},{7,8},{8,9},{9,10},{10,1... | collective-permute-start | bytes 61448 | tf_op jit(solution)/shard_map/ppermute | solution.py:489
  6.7 5.9 %collective-permute-start.2 = (bf16[80,128]{1,0:T(8,128)(2,1)S(1)}, bf16[80,128]{1,0:T(8,128)(2,1)S(1)}, u32[]{:S(2)}, u32[]{:S(2)}) collective-permute-start(bf16[80,128]{1,0:T(8,128)(2,1)S(1)} %get-tuple-element.50), channel_id=1, source_target_pairs={{0,15},{1,0},{2,1},{3,2},{4,3},{5,4},{6,5},{7,6},{8,7},{9,8},{10,9... | collective-permute-start | bytes 61448 | tf_op jit(solution)/shard_map/ppermute | solution.py:489
  15.8 2.5 %copy-start.3 = (bf16[256,2560]{1,0:T(8,128)(2,1)}, bf16[256,2560]{1,0:T(8,128)(2,1)S(1)}, u32[]{:S(2)}) copy-start(bf16[256,2560]{1,0:T(8,128)(2,1)S(1)} %get-tuple-element.60.refs_1_) | copy-start | bytes 3932164
  15.8 1.8 %collective-permute-start.3 = (f32[768,128]{1,0:T(8,128)S(1)}, f32[768,128]{1,0:T(8,128)S(1)}, u32[]{:S(2)}, u32[]{:S(2)}) collective-permute-start(f32[768,128]{1,0:T(8,128)S(1)} %get-tuple-element.57), channel_id=1, source_target_pairs={{0,16},{16,0},{1,17},{17,1},{2,18},{18,2},{3,19},{19,3},{4,20},{20... | collective-permute-start | bytes 1179656 | tf_op jit(solution)/shard_map/ppermute | solution.py:601
  17.6 7.6 %copy-start = (bf16[256,720]{0,1:T(8,128)(2,1)S(1)}, bf16[256,720]{0,1:T(8,128)(2,1)}, u32[]{:S(2)}) copy-start(bf16[256,720]{0,1:T(8,128)(2,1)} %param.16) | copy-start | bytes 1105924
  18.3 26.5 %all-to-all-start = ((bf16[16,176,128]{2,1,0:T(8,128)(2,1)}), bf16[16,176,128]{2,1,0:T(8,128)(2,1)S(1)}, u32[]{:S(2)}, u32[]{:S(2)}) async-start(bf16[16,176,128]{2,1,0:T(8,128)(2,1)} %get-tuple-element.59), calls=%async_computation | async-start | bytes 1441792 | tf_op jit(solution)/shard_map/all_to_all | solution.py:638
  25.2 1.3 %copy-start.4 = (bf16[256,2560]{1,0:T(8,128)(2,1)S(1)}, bf16[256,2560]{1,0:T(8,128)(2,1)}, u32[]{:S(2)}) copy-start(bf16[256,2560]{1,0:T(8,128)(2,1)} %copy-done.3) | copy-start | bytes 3932164
  29.2 7.5 %collective-permute-start.4 = (bf16[64,128]{1,0:T(8,128)(2,1)S(1)}, bf16[64,128]{1,0:T(8,128)(2,1)S(1)}, u32[]{:S(2)}, u32[]{:S(2)}) collective-permute-start(bf16[64,128]{1,0:T(8,128)(2,1)S(1)} %get-tuple-element.62), channel_id=1, source_target_pairs={{0,16},{1,17},{2,18},{3,19},{4,20},{5,21},{6,22},{7,23},{8,24},{9,... | collective-permute-start | bytes 49160 | tf_op jit(solution)/shard_map/ppermute | solution.py:489
  29.3 14.5 %collective-permute-start.7 = (bf16[64,128]{1,0:T(8,128)(2,1)S(1)}, bf16[64,128]{1,0:T(8,128)(2,1)S(1)}, u32[]{:S(2)}, u32[]{:S(2)}) collective-permute-start(bf16[64,128]{1,0:T(8,128)(2,1)S(1)} %get-tuple-element.64), channel_id=1, source_target_pairs={{0,1},{1,2},{2,3},{3,4},{4,5},{5,6},{6,7},{7,8},{8,9},{9,10},{10,1... | collective-permute-start | bytes 49160 | tf_op jit(solution)/shard_map/ppermute | solution.py:489
  31.2 12.6 %collective-permute-start.8 = (bf16[64,128]{1,0:T(8,128)(2,1)S(1)}, bf16[64,128]{1,0:T(8,128)(2,1)S(1)}, u32[]{:S(2)}, u32[]{:S(2)}) collective-permute-start(bf16[64,128]{1,0:T(8,128)(2,1)S(1)} %get-tuple-element.65), channel_id=1, source_target_pairs={{0,15},{1,0},{2,1},{3,2},{4,3},{5,4},{6,5},{7,6},{8,7},{9,8},{10,9... | collective-permute-start | bytes 49160 | tf_op jit(solution)/shard_map/ppermute | solution.py:489
  35.0 8.9 %collective-permute-start.6 = (bf16[64,128]{1,0:T(8,128)(2,1)S(1)}, bf16[64,128]{1,0:T(8,128)(2,1)S(1)}, u32[]{:S(2)}, u32[]{:S(2)}) collective-permute-start(bf16[64,128]{1,0:T(8,128)(2,1)S(1)} %get-tuple-element.63), channel_id=1, source_target_pairs={{0,31},{1,16},{2,17},{3,18},{4,19},{5,20},{6,21},{7,22},{8,23},{9,... | collective-permute-start | bytes 49160 | tf_op jit(solution)/shard_map/ppermute | solution.py:489
  36.4 7.5 %collective-permute-start.5 = (bf16[64,128]{1,0:T(8,128)(2,1)S(1)}, bf16[64,128]{1,0:T(8,128)(2,1)S(1)}, u32[]{:S(2)}, u32[]{:S(2)}) collective-permute-start(bf16[64,128]{1,0:T(8,128)(2,1)S(1)} %get-tuple-element.63), channel_id=1, source_target_pairs={{0,17},{1,18},{2,19},{3,20},{4,21},{5,22},{6,23},{7,24},{8,25},{9,... | collective-permute-start | bytes 49160 | tf_op jit(solution)/shard_map/ppermute | solution.py:489
  46.1 12.9 %all-to-all-start.1 = ((bf16[16,48,128]{2,1,0:T(8,128)(2,1)}), bf16[16,48,128]{2,1,0:T(8,128)(2,1)S(1)}, u32[]{:S(2)}, u32[]{:S(2)}) async-start(bf16[16,48,128]{2,1,0:T(8,128)(2,1)} %get-tuple-element.66), calls=%async_computation.1 | async-start | bytes 393216 | tf_op jit(solution)/shard_map/all_to_all | solution.py:682
  59.1 1.4 %collective-permute-start.9 = (bf16[768,128]{1,0:T(8,128)(2,1)S(1)}, bf16[768,128]{1,0:T(8,128)(2,1)S(1)}, u32[]{:S(2)}, u32[]{:S(2)}) collective-permute-start(bf16[768,128]{1,0:T(8,128)(2,1)S(1)} %bitcast.11), channel_id=1, source_target_pairs={{0,16},{16,0},{1,17},{17,1},{2,18},{18,2},{3,19},{19,3},{4,20},{20... | collective-permute-start | bytes 589832 | tf_op jit(solution)/shard_map/ppermute | solution.py:687

commit v12 on v9

--- a/solution.py
+++ b/solution.py
@@ -10,7 +10,7 @@
 TILE = 16
 F32 = jnp.float32
 BF16 = jnp.bfloat16
-LIMIT = 48 * 1024 * 1024
+LIMIT = 24 * 1024 * 1024
 SMEM = pl.BlockSpec(memory_space=pltpu.SMEM)
 VMEM = pl.BlockSpec(memory_space=pltpu.VMEM)
 

time: 62.5 us -> 62.5 us (level)
  no operation moved by 1% of the time
where the time goes in v12:
time: 62.5 us; the launch traced here: 62.1 us
  starting transfers between devices  26.9 us (43%)
  Pallas kernels  17.1 us (27%)
  waiting for transfers between devices  15.4 us (25%)
  local copies, waits for them, and re-layouts  1.42 us (2%)
  between operations  0.82 us (1%)
    pallas_call x10, Pallas kernels, call(): pl.pallas_call(run, out_shape=outs, in_specs=[SMEM] * scalars + [VMEM] *...  16.3 us
    ppermute x8, starting transfers between devices, moved(): return lax.ppermute(values, ('lat', 'lon'), pairs)  15.1 us
    ppermute x8, waiting for transfers between devices, moved(): return lax.ppermute(values, ('lat', 'lon'), pairs)  7.6 us
    all_to_all x1, starting transfers between devices, body(): incoming = lax.all_to_all(outgoing, 'lon', 0, 0, tiled=True)  6.86 us
    all_to_all x1, waiting for transfers between devices, body(): lax.all_to_all(shares, 'lon', 0, 0, tiled=True).reshape(3 * third, lanes)  5.31 us
    all_to_all x1, starting transfers between devices, body(): lax.all_to_all(shares, 'lon', 0, 0, tiled=True).reshape(3 * third, lanes)  4.94 us
    ppermute x1, waiting for transfers between devices, body(): gathered += (lax.ppermute(gathered[0], 'lat', swap),)  1.44 us
    unnamed x10, local copies, waits for them, and re-layouts  1.33 us
  transfers between devices with their start and end apart: 12, of which 6 were waited for; matrix products, arithmetic and copies ran while one was open for 1% of the time, Pallas kernels for 14%

profile of v12, /device:TPU:0, one launch (start us, length us, event | category | flops | bytes accessed | tf_op | source)
XLA Modules:
  0.0 62.1 jit_solution(6365673083419088562)
XLA Ops:
  0.6 0.0 copy-start.1
  0.6 0.0 copy-start.2
  0.7 0.1 pad_add_fusion.refs_0_
  0.7 1.6 %shard_map.136 = (f32[1280,128]{1,0:T(8,128)S(1)}, bf16[80,128]{1,0:T(8,128)(2,1)S(1)}) custom-call(s32[4]{0:T(128)S(1)} %pad_add_fusion.refs_0_, bf16[16,16,128]{2,1,0:T(8,128)(2,1)} %refs_1_.3, bf16[64,16,128]{2,1,0:T(8,128)(2,1)} %refs_2_.4), custom_call_target="tpu_custom_call" | custom-call | bytes 655360 | tf_op jit(solution)/shard_map/pallas_call | solution.py:46
  2.4 0.5 collective-permute-start
  2.9 0.4 shard_map.137
  3.2 0.5 collective-permute-done.refs_0_.refs_1_.refs_4_.refs_5_
  3.7 0.1 shard_map.138
  3.8 2.9 %collective-permute-start.1 = (bf16[80,128]{1,0:T(8,128)(2,1)S(1)}, bf16[80,128]{1,0:T(8,128)(2,1)S(1)}, u32[]{:S(2)}, u32[]{:S(2)}) collective-permute-start(bf16[80,128]{1,0:T(8,128)(2,1)S(1)} %get-tuple-element.49), channel_id=1, source_target_pairs={{0,1},{1,2},{2,3},{3,4},{4,5},{5,6},{6,7},{7,8},{8,9},{9,10},{10,1... | collective-permute-start | bytes 61448 | tf_op jit(solution)/shard_map/ppermute | solution.py:474
  6.7 4.1 %collective-permute-start.2 = (bf16[80,128]{1,0:T(8,128)(2,1)S(1)}, bf16[80,128]{1,0:T(8,128)(2,1)S(1)}, u32[]{:S(2)}, u32[]{:S(2)}) collective-permute-start(bf16[80,128]{1,0:T(8,128)(2,1)S(1)} %get-tuple-element.50), channel_id=1, source_target_pairs={{0,15},{1,0},{2,1},{3,2},{4,3},{5,4},{6,5},{7,6},{8,7},{9,8},{10,9... | collective-permute-start | bytes 61448 | tf_op jit(solution)/shard_map/ppermute | solution.py:474
  10.8 1.8 %shard_map.139 = (bf16[64,2048]{1,0:T(8,128)(2,1)S(1)}, bf16[64,2048]{1,0:T(8,128)(2,1)S(1)}, bf16[64,2048]{1,0:T(8,128)(2,1)S(1)}, bf16[256,768]{1,0:T(8,128)(2,1)S(1)}, f32[256,128]{1,0:T(8,128)S(1)}) custom-call(f32[1,256]{1,0:T(1,128)} %bitcast.15, bf16[720,256]{1,0:T(8,128)(2,1)} %bitcast.13, bf16[64,16,128]{2,1,0:T(8,128)(2,1)} %refs_2_.5, ...), custom_call_target="tpu_custom_call" | custom-call | bytes 1572864 | tf_op jit(solution)/shard_map/pallas_call | solution.py:46
  12.6 0.0 collective-permute-done.1.refs_6_
  12.6 0.0 collective-permute-done.2.refs_7_
  12.6 0.0 copy-done.1
  12.7 0.0 copy-done.2
  12.7 3.1 %shard_map.140 = (bf16[64,2048]{1,0:T(8,128)(2,1)S(1)}, f32[64,2048]{1,0:T(8,128)S(1)}, bf16[8,64,256]{2,1,0:T(8,128)(2,1)S(1)}, f32[768,128]{1,0:T(8,128)S(1)},...) custom-call(s32[4]{0:T(128)S(1)} %pad_add_fusion.refs_0_, s32[1,128]{1,0:T(1,128)S(1)} %copy-done.2, ...), custom_call_target="tpu_custom_call" | custom-call | flops 1509949440 | bytes 2097152 | tf_op jit(solution)/shard_map/pallas_call | solution.py:46
  15.8 0.0 copy-start.3
  15.8 0.1 collective-permute-start.3
  15.9 1.6 %shard_map.141.refs_2_ = bf16[16,176,128]{2,1,0:T(8,128)(2,1)} custom-call(s32[4]{0:T(128)S(1)} %pad_add_fusion.refs_0_, s32[1,128]{1,0:T(1,128)S(1)} %copy-done.2, s32[1,128]{1,0:T(1,128)S(1)} %copy-done.1, bf16[8,64,256]{2,1,0:T(8,128)(2,1)S(1)} %get-tuple-element.58.refs_3_), custom_call_target="tpu_custom_call" | custom-call | bytes 1048576 | tf_op jit(solution)/shard_map/pallas_call | solution.py:46
  17.5 0.1 collective-permute-done.3.refs_1_
  17.6 0.0 copy-start
  17.6 0.7 %shard_map.142 = (bf16[16,176,128]{2,1,0:T(8,128)(2,1)}, f32[8,128]{1,0:T(8,128)S(1)}) custom-call(f32[768,128]{1,0:T(8,128)S(1)} %get-tuple-element.56.refs_0_, f32[768,128]{1,0:T(8,128)S(1)} %collective-permute-done.3.refs_1_, bf16[16,176,128]{2,1,0:T(8,128)(2,1)} %shard_map.141.refs_2_), custom_call_target="tpu_custom_call", output_to_operand_aliasing={{0}: (2, {})} | custom-call | bytes 1572864 | tf_op jit(solution)/shard_map/pallas_call | solution.py:600
  18.3 0.0 copy-done.3
  18.3 6.9 %all-to-all-start = ((bf16[16,176,128]{2,1,0:T(8,128)(2,1)}), bf16[16,176,128]{2,1,0:T(8,128)(2,1)S(1)}, u32[]{:S(2)}, u32[]{:S(2)}) async-start(bf16[16,176,128]{2,1,0:T(8,128)(2,1)} %get-tuple-element.59), calls=%async_computation | async-start | bytes 1441792 | tf_op jit(solution)/shard_map/all_to_all | solution.py:615
  25.2 0.0 copy-done
  25.2 0.0 copy-start.4
  25.2 1.3 %copy-done.4 = bf16[256,2560]{1,0:T(8,128)(2,1)S(1)} copy-done((bf16[256,2560]{1,0:T(8,128)(2,1)S(1)}, bf16[256,2560]{1,0:T(8,128)(2,1)}, u32[]{:S(2)}) %copy-start.4) | copy-done | bytes 1310744
  26.5 2.6 %shard_map.143 = (f32[64,2048]{1,0:T(8,128)S(1)}, bf16[64,128]{1,0:T(8,128)(2,1)S(1)}, bf16[64,128]{1,0:T(8,128)(2,1)S(1)}, bf16[64,128]{1,0:T(8,128)(2,1)S(1)}, bf16[64,128]{1,0:T(8,128)(2,1)S(1)}) custom-call(s32[4]{0:T(128)S(1)} %pad_add_fusion.refs_0_, bf16[256,2560]{1,0:T(8,128)(2,1)S(1)} %copy-done.4, bf16[720,256]{1,0:T(8,128)(2,1)S(1)} %bitcast.14, ...), custom_call_target="tpu_custom_call" | custom-call | flops 603979776 | bytes 4194304 | tf_op jit(solution)/shard_map/pallas_call | solution.py:46
  29.2 0.2 collective-permute-start.4
  29.4 1.8 %collective-permute-start.7 = (bf16[64,128]{1,0:T(8,128)(2,1)S(1)}, bf16[64,128]{1,0:T(8,128)(2,1)S(1)}, u32[]{:S(2)}, u32[]{:S(2)}) collective-permute-start(bf16[64,128]{1,0:T(8,128)(2,1)S(1)} %get-tuple-element.64), channel_id=1, source_target_pairs={{0,1},{1,2},{2,3},{3,4},{4,5},{5,6},{6,7},{7,8},{8,9},{9,10},{10,1... | collective-permute-start | bytes 49160 | tf_op jit(solution)/shard_map/ppermute | solution.py:474
  31.2 3.8 %collective-permute-start.8 = (bf16[64,128]{1,0:T(8,128)(2,1)S(1)}, bf16[64,128]{1,0:T(8,128)(2,1)S(1)}, u32[]{:S(2)}, u32[]{:S(2)}) collective-permute-start(bf16[64,128]{1,0:T(8,128)(2,1)S(1)} %get-tuple-element.65), channel_id=1, source_target_pairs={{0,15},{1,0},{2,1},{3,2},{4,3},{5,4},{6,5},{7,6},{8,7},{9,8},{10,9... | collective-permute-start | bytes 49160 | tf_op jit(solution)/shard_map/ppermute | solution.py:474
  35.0 1.3 %collective-permute-start.6 = (bf16[64,128]{1,0:T(8,128)(2,1)S(1)}, bf16[64,128]{1,0:T(8,128)(2,1)S(1)}, u32[]{:S(2)}, u32[]{:S(2)}) collective-permute-start(bf16[64,128]{1,0:T(8,128)(2,1)S(1)} %get-tuple-element.63), channel_id=1, source_target_pairs={{0,31},{1,16},{2,17},{3,18},{4,19},{5,20},{6,21},{7,22},{8,23},{9,... | collective-permute-start | bytes 49160 | tf_op jit(solution)/shard_map/ppermute | solution.py:474
  36.3 0.4 collective-permute-start.5
  36.8 0.0 collective-permute-done.4.refs_2_.refs_3_.refs_6_.refs_7_
  36.8 7.1 %collective-permute-done.7.refs_8_.refs_12_ = bf16[64,128]{1,0:T(8,128)(2,1)S(1)} collective-permute-done((bf16[64,128]{1,0:T(8,128)(2,1)S(1)}, bf16[64,128]{1,0:T(8,128)(2,1)S(1)}, u32[]{:S(2)}, u32[]{:S(2)}) %collective-permute-start.7) | collective-permute-done | bytes 16416 | tf_op jit(solution)/shard_map/ppermute | solution.py:474
  43.9 0.0 collective-permute-done.8.refs_9_.refs_13_
  43.9 0.0 collective-permute-done.6.refs_5_.refs_7_.refs_9_.refs_11_
  43.9 0.0 collective-permute-done.5.refs_4_.refs_6_.refs_8_.refs_10_
  43.9 1.0 %all-to-all-done.refs_1_.refs_4_ = bf16[16,176,128]{2,1,0:T(8,128)(2,1)S(1)} async-done(((bf16[16,176,128]{2,1,0:T(8,128)(2,1)}), bf16[16,176,128]{2,1,0:T(8,128)(2,1)S(1)}, u32[]{:S(2)}, u32[]{:S(2)}) %all-to-all-start) | async-done | bytes 720928 | tf_op jit(solution)/shard_map/all_to_all | solution.py:615
  44.9 1.3 %shard_map.144 = (bf16[16,48,128]{2,1,0:T(8,128)(2,1)}, f32[8,128]{1,0:T(8,128)S(1)}) custom-call(s32[4]{0:T(128)S(1)} %pad_add_fusion.refs_0_, bf16[16,176,128]{2,1,0:T(8,128)(2,1)S(1)} %all-to-all-done.refs_1_.refs_4_, bf16[64,128]{1,0:T(8,128)(2,1)S(1)} %collective-permute-done.4.refs_2_.refs_3_.refs_6_.refs_7_, ...), custom_call_target="tpu_custom_call" | custom-call | bytes 393216 | tf_op jit(solution)/shard_map/pallas_call | solution.py:46
  46.1 4.9 %all-to-all-start.1 = ((bf16[16,48,128]{2,1,0:T(8,128)(2,1)}), bf16[16,48,128]{2,1,0:T(8,128)(2,1)S(1)}, u32[]{:S(2)}, u32[]{:S(2)}) async-start(bf16[16,48,128]{2,1,0:T(8,128)(2,1)} %get-tuple-element.66), calls=%async_computation.1 | async-start | bytes 393216 | tf_op jit(solution)/shard_map/all_to_all | solution.py:659
  51.1 0.1 reshape.35
  51.2 0.1 reduce_or.9
  51.3 0.1 convert_reduce_fusion
  51.4 0.1 select_reduce_fusion.refs_1_
  51.5 2.3 %shard_map.145 = (bf16[64,16,128]{2,1,0:T(8,128)(2,1)}, f32[1024,128]{1,0:T(8,128)}, f32[4,64,256]{2,1,0:T(8,128)}, f32[1024,128]{1,0:T(8,128)}) custom-call(s32[4]{0:T(128)S(1)} %pad_add_fusion.refs_0_, s32[4]{0:T(128)S(1)} %select_reduce_fusion.refs_1_, bf16[64,2048]{1,0:T(8,128)(2,1)S(1)} %get-tuple-element.67.refs_2_, ...), custom_call_target="tpu_custom_call" | custom-call | bytes 4194304 | tf_op jit(solution)/shard_map/pallas_call | solution.py:46
  53.8 5.3 %all-to-all-done.1 = bf16[16,48,128]{2,1,0:T(8,128)(2,1)S(1)} async-done(((bf16[16,48,128]{2,1,0:T(8,128)(2,1)}), bf16[16,48,128]{2,1,0:T(8,128)(2,1)S(1)}, u32[]{:S(2)}, u32[]{:S(2)}) %all-to-all-start.1) | async-done | bytes 196640 | tf_op jit(solution)/shard_map/all_to_all | solution.py:659
  59.1 0.0 collective-permute-start.9
  59.2 1.4 %collective-permute-done.9.refs_2_ = bf16[768,128]{1,0:T(8,128)(2,1)S(1)} collective-permute-done((bf16[768,128]{1,0:T(8,128)(2,1)S(1)}, bf16[768,128]{1,0:T(8,128)(2,1)S(1)}, u32[]{:S(2)}, u32[]{:S(2)}) %collective-permute-start.9) | collective-permute-done | bytes 196640 | tf_op jit(solution)/shard_map/ppermute | solution.py:664
  60.6 1.5 %shard_map.146 = (f32[720,256]{1,0:T(8,128)}, f32[1,256]{1,0:T(1,128)}) custom-call(s32[4]{0:T(128)S(1)} %pad_add_fusion.refs_0_, bf16[768,128]{1,0:T(8,128)(2,1)S(1)} %bitcast.12, bf16[768,128]{1,0:T(8,128)(2,1)S(1)} %collective-permute-done.9.refs_2_), custom_call_target="tpu_custom_call" | custom-call | bytes 1179648 | tf_op jit(solution)/shard_map/pallas_call | solution.py:46
  (1 shorter events, 0.0 us)
Async XLA Ops:
  0.6 12.0 %copy-start.1 = (s32[1,128]{1,0:T(1,128)S(1)}, s32[1,128]{1,0:T(1,128)}, u32[]{:S(2)}) copy-start(s32[1,128]{1,0:T(1,128)} %refs_2_.7) | copy-start | bytes 1540
  0.6 12.0 %copy-start.2 = (s32[1,128]{1,0:T(1,128)S(1)}, s32[1,128]{1,0:T(1,128)}, u32[]{:S(2)}) copy-start(s32[1,128]{1,0:T(1,128)} %refs_1_.5) | copy-start | bytes 1540
  2.4 1.4 %collective-permute-start = (bf16[80,128]{1,0:T(8,128)(2,1)S(1)}, bf16[80,128]{1,0:T(8,128)(2,1)S(1)}, u32[]{:S(2)}, u32[]{:S(2)}) collective-permute-start(bf16[80,128]{1,0:T(8,128)(2,1)S(1)} %get-tuple-element.46), channel_id=1, source_target_pairs={{0,16},{1,17},{2,18},{3,19},{4,20},{5,21},{6,22},{7,23},{8,24},{9,... | collective-permute-start | bytes 61448 | tf_op jit(solution)/shard_map/ppermute | solution.py:474
  3.8 8.8 %collective-permute-start.1 = (bf16[80,128]{1,0:T(8,128)(2,1)S(1)}, bf16[80,128]{1,0:T(8,128)(2,1)S(1)}, u32[]{:S(2)}, u32[]{:S(2)}) collective-permute-start(bf16[80,128]{1,0:T(8,128)(2,1)S(1)} %get-tuple-element.49), channel_id=1, source_target_pairs={{0,1},{1,2},{2,3},{3,4},{4,5},{5,6},{6,7},{7,8},{8,9},{9,10},{10,1... | collective-permute-start | bytes 61448 | tf_op jit(solution)/shard_map/ppermute | solution.py:474
  6.7 5.9 %collective-permute-start.2 = (bf16[80,128]{1,0:T(8,128)(2,1)S(1)}, bf16[80,128]{1,0:T(8,128)(2,1)S(1)}, u32[]{:S(2)}, u32[]{:S(2)}) collective-permute-start(bf16[80,128]{1,0:T(8,128)(2,1)S(1)} %get-tuple-element.50), channel_id=1, source_target_pairs={{0,15},{1,0},{2,1},{3,2},{4,3},{5,4},{6,5},{7,6},{8,7},{9,8},{10,9... | collective-permute-start | bytes 61448 | tf_op jit(solution)/shard_map/ppermute | solution.py:474
  15.8 2.5 %copy-start.3 = (bf16[256,2560]{1,0:T(8,128)(2,1)}, bf16[256,2560]{1,0:T(8,128)(2,1)S(1)}, u32[]{:S(2)}) copy-start(bf16[256,2560]{1,0:T(8,128)(2,1)S(1)} %get-tuple-element.60.refs_1_) | copy-start | bytes 3932164
  15.8 1.8 %collective-permute-start.3 = (f32[768,128]{1,0:T(8,128)S(1)}, f32[768,128]{1,0:T(8,128)S(1)}, u32[]{:S(2)}, u32[]{:S(2)}) collective-permute-start(f32[768,128]{1,0:T(8,128)S(1)} %get-tuple-element.57), channel_id=1, source_target_pairs={{0,16},{16,0},{1,17},{17,1},{2,18},{18,2},{3,19},{19,3},{4,20},{20... | collective-permute-start | bytes 1179656 | tf_op jit(solution)/shard_map/ppermute | solution.py:586
  17.6 7.6 %copy-start = (bf16[256,720]{0,1:T(8,128)(2,1)S(1)}, bf16[256,720]{0,1:T(8,128)(2,1)}, u32[]{:S(2)}) copy-start(bf16[256,720]{0,1:T(8,128)(2,1)} %param.16) | copy-start | bytes 1105924
  18.3 26.5 %all-to-all-start = ((bf16[16,176,128]{2,1,0:T(8,128)(2,1)}), bf16[16,176,128]{2,1,0:T(8,128)(2,1)S(1)}, u32[]{:S(2)}, u32[]{:S(2)}) async-start(bf16[16,176,128]{2,1,0:T(8,128)(2,1)} %get-tuple-element.59), calls=%async_computation | async-start | bytes 1441792 | tf_op jit(solution)/shard_map/all_to_all | solution.py:615
  25.2 1.3 %copy-start.4 = (bf16[256,2560]{1,0:T(8,128)(2,1)S(1)}, bf16[256,2560]{1,0:T(8,128)(2,1)}, u32[]{:S(2)}) copy-start(bf16[256,2560]{1,0:T(8,128)(2,1)} %copy-done.3) | copy-start | bytes 3932164
  29.2 7.6 %collective-permute-start.4 = (bf16[64,128]{1,0:T(8,128)(2,1)S(1)}, bf16[64,128]{1,0:T(8,128)(2,1)S(1)}, u32[]{:S(2)}, u32[]{:S(2)}) collective-permute-start(bf16[64,128]{1,0:T(8,128)(2,1)S(1)} %get-tuple-element.62), channel_id=1, source_target_pairs={{0,16},{1,17},{2,18},{3,19},{4,20},{5,21},{6,22},{7,23},{8,24},{9,... | collective-permute-start | bytes 49160 | tf_op jit(solution)/shard_map/ppermute | solution.py:474
  29.4 14.5 %collective-permute-start.7 = (bf16[64,128]{1,0:T(8,128)(2,1)S(1)}, bf16[64,128]{1,0:T(8,128)(2,1)S(1)}, u32[]{:S(2)}, u32[]{:S(2)}) collective-permute-start(bf16[64,128]{1,0:T(8,128)(2,1)S(1)} %get-tuple-element.64), channel_id=1, source_target_pairs={{0,1},{1,2},{2,3},{3,4},{4,5},{5,6},{6,7},{7,8},{8,9},{9,10},{10,1... | collective-permute-start | bytes 49160 | tf_op jit(solution)/shard_map/ppermute | solution.py:474
  31.2 12.7 %collective-permute-start.8 = (bf16[64,128]{1,0:T(8,128)(2,1)S(1)}, bf16[64,128]{1,0:T(8,128)(2,1)S(1)}, u32[]{:S(2)}, u32[]{:S(2)}) collective-permute-start(bf16[64,128]{1,0:T(8,128)(2,1)S(1)} %get-tuple-element.65), channel_id=1, source_target_pairs={{0,15},{1,0},{2,1},{3,2},{4,3},{5,4},{6,5},{7,6},{8,7},{9,8},{10,9... | collective-permute-start | bytes 49160 | tf_op jit(solution)/shard_map/ppermute | solution.py:474
  35.0 8.9 %collective-permute-start.6 = (bf16[64,128]{1,0:T(8,128)(2,1)S(1)}, bf16[64,128]{1,0:T(8,128)(2,1)S(1)}, u32[]{:S(2)}, u32[]{:S(2)}) collective-permute-start(bf16[64,128]{1,0:T(8,128)(2,1)S(1)} %get-tuple-element.63), channel_id=1, source_target_pairs={{0,31},{1,16},{2,17},{3,18},{4,19},{5,20},{6,21},{7,22},{8,23},{9,... | collective-permute-start | bytes 49160 | tf_op jit(solution)/shard_map/ppermute | solution.py:474
  36.3 7.5 %collective-permute-start.5 = (bf16[64,128]{1,0:T(8,128)(2,1)S(1)}, bf16[64,128]{1,0:T(8,128)(2,1)S(1)}, u32[]{:S(2)}, u32[]{:S(2)}) collective-permute-start(bf16[64,128]{1,0:T(8,128)(2,1)S(1)} %get-tuple-element.63), channel_id=1, source_target_pairs={{0,17},{1,18},{2,19},{3,20},{4,21},{5,22},{6,23},{7,24},{8,25},{9,... | collective-permute-start | bytes 49160 | tf_op jit(solution)/shard_map/ppermute | solution.py:474
  46.1 13.0 %all-to-all-start.1 = ((bf16[16,48,128]{2,1,0:T(8,128)(2,1)}), bf16[16,48,128]{2,1,0:T(8,128)(2,1)S(1)}, u32[]{:S(2)}, u32[]{:S(2)}) async-start(bf16[16,48,128]{2,1,0:T(8,128)(2,1)} %get-tuple-element.66), calls=%async_computation.1 | async-start | bytes 393216 | tf_op jit(solution)/shard_map/all_to_all | solution.py:659
  59.1 1.4 %collective-permute-start.9 = (bf16[768,128]{1,0:T(8,128)(2,1)S(1)}, bf16[768,128]{1,0:T(8,128)(2,1)S(1)}, u32[]{:S(2)}, u32[]{:S(2)}) collective-permute-start(bf16[768,128]{1,0:T(8,128)(2,1)S(1)} %bitcast.11), channel_id=1, source_target_pairs={{0,16},{16,0},{1,17},{17,1},{2,18},{18,2},{3,19},{19,3},{4,20},{20... | collective-permute-start | bytes 589832 | tf_op jit(solution)/shard_map/ppermute | solution.py:664

commit v13 on v9

--- a/solution.py
+++ b/solution.py
@@ -634,7 +634,7 @@
         (place, incoming),
         scalars=1,
         moved=2 * gates * 3 * third,
-        after=grad_halo,
+        after=grad_halo[:-2],
     )
     owned = (wet_mask > 0) & (tile_owner == lon_index)
     arrived = jnp.any(owned.reshape(lon_devices, tile_cols), 1)

time: 62.5 us -> 65.3 us (1.045)
  starting transfers between devices: 26.9 us -> 30.6 us
  waiting for transfers between devices: 15.4 us -> 14.6 us
    all_to_all x1, waiting for transfers between devices: 5.31 us -> 0.01 us  [body(): lax.all_to_all(shares, 'lon', 0, 0, tiled=True).reshape(3 * third, lanes)]
    ppermute x8, starting transfers between devices: 15.1 us -> 18.8 us  [moved(): return lax.ppermute(values, ('lat', 'lon'), pairs)]
    ppermute x8, waiting for transfers between devices: 7.6 us -> 11.3 us  [moved(): return lax.ppermute(values, ('lat', 'lon'), pairs)]
    all_to_all x1, waiting for transfers between devices: 0.97 us -> 1.75 us  [body(): incoming = lax.all_to_all(outgoing, 'lon', 0, 0, tiled=True)]
  transfers between devices with their start and end apart: 12 -> 12, of which waited for: 6 -> 7; matrix products, arithmetic and copies ran while one was open for 1% -> 1% of each run, Pallas kernels for 14% -> 13%
where the time goes in v13:
time: 65.3 us; the launch traced here: 64.9 us
  starting transfers between devices  30.6 us (47%)
  Pallas kernels  17.1 us (26%)
  waiting for transfers between devices  14.6 us (22%)
  local copies, waits for them, and re-layouts  1.42 us (2%)
  between operations  0.82 us (1%)
    ppermute x8, starting transfers between devices, moved(): return lax.ppermute(values, ('lat', 'lon'), pairs)  18.8 us
    pallas_call x10, Pallas kernels, call(): pl.pallas_call(run, out_shape=outs, in_specs=[SMEM] * scalars + [VMEM] *...  16.4 us
    ppermute x8, waiting for transfers between devices, moved(): return lax.ppermute(values, ('lat', 'lon'), pairs)  11.3 us
    all_to_all x1, starting transfers between devices, body(): incoming = lax.all_to_all(outgoing, 'lon', 0, 0, tiled=True)  6.88 us
    all_to_all x1, starting transfers between devices, body(): lax.all_to_all(shares, 'lon', 0, 0, tiled=True).reshape(3 * third, lanes)  4.84 us
    all_to_all x1, waiting for transfers between devices, body(): incoming = lax.all_to_all(outgoing, 'lon', 0, 0, tiled=True)  1.75 us
    ppermute x1, waiting for transfers between devices, body(): gathered += (lax.ppermute(gathered[0], 'lat', swap),)  1.43 us
    unnamed x10, local copies, waits for them, and re-layouts  1.33 us
  transfers between devices with their start and end apart: 12, of which 7 were waited for; matrix products, arithmetic and copies ran while one was open for 1% of the time, Pallas kernels for 13%

profile of v13, /device:TPU:0, one launch (start us, length us, event | category | flops | bytes accessed | tf_op | source)
XLA Modules:
  0.0 64.9 jit_solution(7236857486725718824)
XLA Ops:
  0.6 0.0 copy-start.1
  0.6 0.0 copy-start.2
  0.7 0.1 pad_add_fusion.refs_0_
  0.7 1.6 %shard_map.136 = (f32[1280,128]{1,0:T(8,128)S(1)}, bf16[80,128]{1,0:T(8,128)(2,1)S(1)}) custom-call(s32[4]{0:T(128)S(1)} %pad_add_fusion.refs_0_, bf16[16,16,128]{2,1,0:T(8,128)(2,1)} %refs_1_.3, bf16[64,16,128]{2,1,0:T(8,128)(2,1)} %refs_2_.4), custom_call_target="tpu_custom_call" | custom-call | bytes 655360 | tf_op jit(solution)/shard_map/pallas_call | solution.py:46
  2.4 0.5 collective-permute-start
  2.9 0.4 shard_map.137
  3.2 0.5 collective-permute-done.refs_0_.refs_1_.refs_4_.refs_5_
  3.7 0.1 shard_map.138
  3.8 2.9 %collective-permute-start.1 = (bf16[80,128]{1,0:T(8,128)(2,1)S(1)}, bf16[80,128]{1,0:T(8,128)(2,1)S(1)}, u32[]{:S(2)}, u32[]{:S(2)}) collective-permute-start(bf16[80,128]{1,0:T(8,128)(2,1)S(1)} %get-tuple-element.49), channel_id=1, source_target_pairs={{0,1},{1,2},{2,3},{3,4},{4,5},{5,6},{6,7},{7,8},{8,9},{9,10},{10,1... | collective-permute-start | bytes 61448 | tf_op jit(solution)/shard_map/ppermute | solution.py:474
  6.7 4.1 %collective-permute-start.2 = (bf16[80,128]{1,0:T(8,128)(2,1)S(1)}, bf16[80,128]{1,0:T(8,128)(2,1)S(1)}, u32[]{:S(2)}, u32[]{:S(2)}) collective-permute-start(bf16[80,128]{1,0:T(8,128)(2,1)S(1)} %get-tuple-element.50), channel_id=1, source_target_pairs={{0,15},{1,0},{2,1},{3,2},{4,3},{5,4},{6,5},{7,6},{8,7},{9,8},{10,9... | collective-permute-start | bytes 61448 | tf_op jit(solution)/shard_map/ppermute | solution.py:474
  10.8 1.8 %shard_map.139 = (bf16[64,2048]{1,0:T(8,128)(2,1)S(1)}, bf16[64,2048]{1,0:T(8,128)(2,1)S(1)}, bf16[64,2048]{1,0:T(8,128)(2,1)S(1)}, bf16[256,768]{1,0:T(8,128)(2,1)S(1)}, f32[256,128]{1,0:T(8,128)S(1)}) custom-call(f32[1,256]{1,0:T(1,128)} %bitcast.15, bf16[720,256]{1,0:T(8,128)(2,1)} %bitcast.13, bf16[64,16,128]{2,1,0:T(8,128)(2,1)} %refs_2_.5, ...), custom_call_target="tpu_custom_call" | custom-call | bytes 1572864 | tf_op jit(solution)/shard_map/pallas_call | solution.py:46
  12.6 0.0 collective-permute-done.1.refs_6_
  12.6 0.0 collective-permute-done.2.refs_7_
  12.6 0.0 copy-done.1
  12.7 0.0 copy-done.2
  12.7 3.1 %shard_map.140 = (bf16[64,2048]{1,0:T(8,128)(2,1)S(1)}, f32[64,2048]{1,0:T(8,128)S(1)}, bf16[8,64,256]{2,1,0:T(8,128)(2,1)S(1)}, f32[768,128]{1,0:T(8,128)S(1)},...) custom-call(s32[4]{0:T(128)S(1)} %pad_add_fusion.refs_0_, s32[1,128]{1,0:T(1,128)S(1)} %copy-done.2, ...), custom_call_target="tpu_custom_call" | custom-call | flops 1509949440 | bytes 2097152 | tf_op jit(solution)/shard_map/pallas_call | solution.py:46
  15.8 0.0 copy-start.3
  15.8 0.1 collective-permute-start.3
  15.9 1.6 %shard_map.141.refs_2_ = bf16[16,176,128]{2,1,0:T(8,128)(2,1)} custom-call(s32[4]{0:T(128)S(1)} %pad_add_fusion.refs_0_, s32[1,128]{1,0:T(1,128)S(1)} %copy-done.2, s32[1,128]{1,0:T(1,128)S(1)} %copy-done.1, bf16[8,64,256]{2,1,0:T(8,128)(2,1)S(1)} %get-tuple-element.58.refs_3_), custom_call_target="tpu_custom_call" | custom-call | bytes 1048576 | tf_op jit(solution)/shard_map/pallas_call | solution.py:46
  17.5 0.1 collective-permute-done.3.refs_1_
  17.6 0.0 copy-start
  17.6 0.7 %shard_map.142 = (bf16[16,176,128]{2,1,0:T(8,128)(2,1)}, f32[8,128]{1,0:T(8,128)S(1)}) custom-call(f32[768,128]{1,0:T(8,128)S(1)} %get-tuple-element.56.refs_0_, f32[768,128]{1,0:T(8,128)S(1)} %collective-permute-done.3.refs_1_, bf16[16,176,128]{2,1,0:T(8,128)(2,1)} %shard_map.141.refs_2_), custom_call_target="tpu_custom_call", output_to_operand_aliasing={{0}: (2, {})} | custom-call | bytes 1572864 | tf_op jit(solution)/shard_map/pallas_call | solution.py:600
  18.3 0.0 copy-done.3
  18.3 6.9 %all-to-all-start = ((bf16[16,176,128]{2,1,0:T(8,128)(2,1)}), bf16[16,176,128]{2,1,0:T(8,128)(2,1)S(1)}, u32[]{:S(2)}, u32[]{:S(2)}) async-start(bf16[16,176,128]{2,1,0:T(8,128)(2,1)} %get-tuple-element.59), calls=%async_computation | async-start | bytes 1441792 | tf_op jit(solution)/shard_map/all_to_all | solution.py:615
  25.2 0.0 copy-done
  25.2 0.0 copy-start.4
  25.3 1.3 %copy-done.4 = bf16[256,2560]{1,0:T(8,128)(2,1)S(1)} copy-done((bf16[256,2560]{1,0:T(8,128)(2,1)S(1)}, bf16[256,2560]{1,0:T(8,128)(2,1)}, u32[]{:S(2)}) %copy-start.4) | copy-done | bytes 1310744
  26.6 2.6 %shard_map.143 = (f32[64,2048]{1,0:T(8,128)S(1)}, bf16[64,128]{1,0:T(8,128)(2,1)S(1)}, bf16[64,128]{1,0:T(8,128)(2,1)S(1)}, bf16[64,128]{1,0:T(8,128)(2,1)S(1)}, bf16[64,128]{1,0:T(8,128)(2,1)S(1)}) custom-call(s32[4]{0:T(128)S(1)} %pad_add_fusion.refs_0_, bf16[256,2560]{1,0:T(8,128)(2,1)S(1)} %copy-done.4, bf16[720,256]{1,0:T(8,128)(2,1)S(1)} %bitcast.14, ...), custom_call_target="tpu_custom_call" | custom-call | flops 603979776 | bytes 4194304 | tf_op jit(solution)/shard_map/pallas_call | solution.py:46
  29.2 0.1 collective-permute-start.4
  29.3 5.6 %collective-permute-start.6 = (bf16[64,128]{1,0:T(8,128)(2,1)S(1)}, bf16[64,128]{1,0:T(8,128)(2,1)S(1)}, u32[]{:S(2)}, u32[]{:S(2)}) collective-permute-start(bf16[64,128]{1,0:T(8,128)(2,1)S(1)} %get-tuple-element.63), channel_id=1, source_target_pairs={{0,31},{1,16},{2,17},{3,18},{4,19},{5,20},{6,21},{7,22},{8,23},{9,... | collective-permute-start | bytes 49160 | tf_op jit(solution)/shard_map/ppermute | solution.py:474
  34.9 0.0 collective-permute-start.5
  34.9 0.0 collective-permute-done.4.refs_2_.refs_3_.refs_6_.refs_7_
  34.9 2.9 %collective-permute-done.6.refs_5_.refs_7_.refs_9_.refs_11_ = bf16[64,128]{1,0:T(8,128)(2,1)S(1)} collective-permute-done((bf16[64,128]{1,0:T(8,128)(2,1)S(1)}, bf16[64,128]{1,0:T(8,128)(2,1)S(1)}, u32[]{:S(2)}, u32[]{:S(2)}) %collective-permute-start.6) | collective-permute-done | bytes 16416 | tf_op jit(solution)/shard_map/ppermute | solution.py:474
  37.9 4.9 %collective-permute-done.5.refs_4_.refs_6_.refs_8_.refs_10_ = bf16[64,128]{1,0:T(8,128)(2,1)S(1)} collective-permute-done((bf16[64,128]{1,0:T(8,128)(2,1)S(1)}, bf16[64,128]{1,0:T(8,128)(2,1)S(1)}, u32[]{:S(2)}, u32[]{:S(2)}) %collective-permute-start.5) | collective-permute-done | bytes 16416 | tf_op jit(solution)/shard_map/ppermute | solution.py:474
  42.8 1.8 %all-to-all-done.refs_1_.refs_4_ = bf16[16,176,128]{2,1,0:T(8,128)(2,1)S(1)} async-done(((bf16[16,176,128]{2,1,0:T(8,128)(2,1)}), bf16[16,176,128]{2,1,0:T(8,128)(2,1)S(1)}, u32[]{:S(2)}, u32[]{:S(2)}) %all-to-all-start) | async-done | bytes 720928 | tf_op jit(solution)/shard_map/all_to_all | solution.py:615
  44.5 1.3 %shard_map.144 = (bf16[16,48,128]{2,1,0:T(8,128)(2,1)}, f32[8,128]{1,0:T(8,128)S(1)}) custom-call(s32[4]{0:T(128)S(1)} %pad_add_fusion.refs_0_, bf16[16,176,128]{2,1,0:T(8,128)(2,1)S(1)} %all-to-all-done.refs_1_.refs_4_, bf16[64,128]{1,0:T(8,128)(2,1)S(1)} %collective-permute-done.4.refs_2_.refs_3_.refs_6_.refs_7_, ...), custom_call_target="tpu_custom_call" | custom-call | bytes 393216 | tf_op jit(solution)/shard_map/pallas_call | solution.py:46
  45.8 4.8 %all-to-all-start.1 = ((bf16[16,48,128]{2,1,0:T(8,128)(2,1)}), bf16[16,48,128]{2,1,0:T(8,128)(2,1)S(1)}, u32[]{:S(2)}, u32[]{:S(2)}) async-start(bf16[16,48,128]{2,1,0:T(8,128)(2,1)} %get-tuple-element.64), calls=%async_computation.1 | async-start | bytes 393216 | tf_op jit(solution)/shard_map/all_to_all | solution.py:659
  50.7 0.1 reshape.35
  50.8 0.1 reduce_or.9
  50.9 0.1 convert_reduce_fusion
  51.0 2.0 %collective-permute-start.7 = (bf16[64,128]{1,0:T(8,128)(2,1)S(1)}, bf16[64,128]{1,0:T(8,128)(2,1)S(1)}, u32[]{:S(2)}, u32[]{:S(2)}) collective-permute-start(bf16[64,128]{1,0:T(8,128)(2,1)S(1)} %get-tuple-element.68), channel_id=1, source_target_pairs={{0,1},{1,2},{2,3},{3,4},{4,5},{5,6},{6,7},{7,8},{8,9},{9,10},{10,1... | collective-permute-start | bytes 49160 | tf_op jit(solution)/shard_map/ppermute | solution.py:474
  52.9 3.7 %collective-permute-start.8 = (bf16[64,128]{1,0:T(8,128)(2,1)S(1)}, bf16[64,128]{1,0:T(8,128)(2,1)S(1)}, u32[]{:S(2)}, u32[]{:S(2)}) collective-permute-start(bf16[64,128]{1,0:T(8,128)(2,1)S(1)} %get-tuple-element.69), channel_id=1, source_target_pairs={{0,15},{1,0},{2,1},{3,2},{4,3},{5,4},{6,5},{7,6},{8,7},{9,8},{10,9... | collective-permute-start | bytes 49160 | tf_op jit(solution)/shard_map/ppermute | solution.py:474
  56.6 0.1 select_reduce_fusion.refs_1_
  56.7 2.9 %collective-permute-done.7.refs_12_ = bf16[64,128]{1,0:T(8,128)(2,1)S(1)} collective-permute-done((bf16[64,128]{1,0:T(8,128)(2,1)S(1)}, bf16[64,128]{1,0:T(8,128)(2,1)S(1)}, u32[]{:S(2)}, u32[]{:S(2)}) %collective-permute-start.7) | collective-permute-done | bytes 16416 | tf_op jit(solution)/shard_map/ppermute | solution.py:474
  59.7 0.0 collective-permute-done.8.refs_13_
  59.7 2.3 %shard_map.145 = (bf16[64,16,128]{2,1,0:T(8,128)(2,1)}, f32[1024,128]{1,0:T(8,128)}, f32[4,64,256]{2,1,0:T(8,128)}, f32[1024,128]{1,0:T(8,128)}) custom-call(s32[4]{0:T(128)S(1)} %pad_add_fusion.refs_0_, s32[4]{0:T(128)S(1)} %select_reduce_fusion.refs_1_, bf16[64,2048]{1,0:T(8,128)(2,1)S(1)} %get-tuple-element.65.refs_2_, ...), custom_call_target="tpu_custom_call" | custom-call | bytes 4194304 | tf_op jit(solution)/shard_map/pallas_call | solution.py:46
  62.0 0.0 all-to-all-done.1
  62.0 0.0 collective-permute-start.9
  62.0 1.4 %collective-permute-done.9.refs_2_ = bf16[768,128]{1,0:T(8,128)(2,1)S(1)} collective-permute-done((bf16[768,128]{1,0:T(8,128)(2,1)S(1)}, bf16[768,128]{1,0:T(8,128)(2,1)S(1)}, u32[]{:S(2)}, u32[]{:S(2)}) %collective-permute-start.9) | collective-permute-done | bytes 196640 | tf_op jit(solution)/shard_map/ppermute | solution.py:664
  63.4 1.5 %shard_map.146 = (f32[720,256]{1,0:T(8,128)}, f32[1,256]{1,0:T(1,128)}) custom-call(s32[4]{0:T(128)S(1)} %pad_add_fusion.refs_0_, bf16[768,128]{1,0:T(8,128)(2,1)S(1)} %bitcast.12, bf16[768,128]{1,0:T(8,128)(2,1)S(1)} %collective-permute-done.9.refs_2_), custom_call_target="tpu_custom_call" | custom-call | bytes 1179648 | tf_op jit(solution)/shard_map/pallas_call | solution.py:46
  (1 shorter events, 0.0 us)
Async XLA Ops:
  0.6 12.0 %copy-start.1 = (s32[1,128]{1,0:T(1,128)S(1)}, s32[1,128]{1,0:T(1,128)}, u32[]{:S(2)}) copy-start(s32[1,128]{1,0:T(1,128)} %refs_2_.7) | copy-start | bytes 1540
  0.6 12.0 %copy-start.2 = (s32[1,128]{1,0:T(1,128)S(1)}, s32[1,128]{1,0:T(1,128)}, u32[]{:S(2)}) copy-start(s32[1,128]{1,0:T(1,128)} %refs_1_.5) | copy-start | bytes 1540
  2.4 1.4 %collective-permute-start = (bf16[80,128]{1,0:T(8,128)(2,1)S(1)}, bf16[80,128]{1,0:T(8,128)(2,1)S(1)}, u32[]{:S(2)}, u32[]{:S(2)}) collective-permute-start(bf16[80,128]{1,0:T(8,128)(2,1)S(1)} %get-tuple-element.46), channel_id=1, source_target_pairs={{0,16},{1,17},{2,18},{3,19},{4,20},{5,21},{6,22},{7,23},{8,24},{9,... | collective-permute-start | bytes 61448 | tf_op jit(solution)/shard_map/ppermute | solution.py:474
  3.8 8.8 %collective-permute-start.1 = (bf16[80,128]{1,0:T(8,128)(2,1)S(1)}, bf16[80,128]{1,0:T(8,128)(2,1)S(1)}, u32[]{:S(2)}, u32[]{:S(2)}) collective-permute-start(bf16[80,128]{1,0:T(8,128)(2,1)S(1)} %get-tuple-element.49), channel_id=1, source_target_pairs={{0,1},{1,2},{2,3},{3,4},{4,5},{5,6},{6,7},{7,8},{8,9},{9,10},{10,1... | collective-permute-start | bytes 61448 | tf_op jit(solution)/shard_map/ppermute | solution.py:474
  6.7 5.9 %collective-permute-start.2 = (bf16[80,128]{1,0:T(8,128)(2,1)S(1)}, bf16[80,128]{1,0:T(8,128)(2,1)S(1)}, u32[]{:S(2)}, u32[]{:S(2)}) collective-permute-start(bf16[80,128]{1,0:T(8,128)(2,1)S(1)} %get-tuple-element.50), channel_id=1, source_target_pairs={{0,15},{1,0},{2,1},{3,2},{4,3},{5,4},{6,5},{7,6},{8,7},{9,8},{10,9... | collective-permute-start | bytes 61448 | tf_op jit(solution)/shard_map/ppermute | solution.py:474
  15.8 2.5 %copy-start.3 = (bf16[256,2560]{1,0:T(8,128)(2,1)}, bf16[256,2560]{1,0:T(8,128)(2,1)S(1)}, u32[]{:S(2)}) copy-start(bf16[256,2560]{1,0:T(8,128)(2,1)S(1)} %get-tuple-element.60.refs_1_) | copy-start | bytes 3932164
  15.8 1.8 %collective-permute-start.3 = (f32[768,128]{1,0:T(8,128)S(1)}, f32[768,128]{1,0:T(8,128)S(1)}, u32[]{:S(2)}, u32[]{:S(2)}) collective-permute-start(f32[768,128]{1,0:T(8,128)S(1)} %get-tuple-element.57), channel_id=1, source_target_pairs={{0,16},{16,0},{1,17},{17,1},{2,18},{18,2},{3,19},{19,3},{4,20},{20... | collective-permute-start | bytes 1179656 | tf_op jit(solution)/shard_map/ppermute | solution.py:586
  17.6 7.6 %copy-start = (bf16[256,720]{0,1:T(8,128)(2,1)S(1)}, bf16[256,720]{0,1:T(8,128)(2,1)}, u32[]{:S(2)}) copy-start(bf16[256,720]{0,1:T(8,128)(2,1)} %param.16) | copy-start | bytes 1105924
  18.3 26.2 %all-to-all-start = ((bf16[16,176,128]{2,1,0:T(8,128)(2,1)}), bf16[16,176,128]{2,1,0:T(8,128)(2,1)S(1)}, u32[]{:S(2)}, u32[]{:S(2)}) async-start(bf16[16,176,128]{2,1,0:T(8,128)(2,1)} %get-tuple-element.59), calls=%async_computation | async-start | bytes 1441792 | tf_op jit(solution)/shard_map/all_to_all | solution.py:615
  25.2 1.3 %copy-start.4 = (bf16[256,2560]{1,0:T(8,128)(2,1)S(1)}, bf16[256,2560]{1,0:T(8,128)(2,1)}, u32[]{:S(2)}) copy-start(bf16[256,2560]{1,0:T(8,128)(2,1)} %copy-done.3) | copy-start | bytes 3932164
  29.2 5.7 %collective-permute-start.4 = (bf16[64,128]{1,0:T(8,128)(2,1)S(1)}, bf16[64,128]{1,0:T(8,128)(2,1)S(1)}, u32[]{:S(2)}, u32[]{:S(2)}) collective-permute-start(bf16[64,128]{1,0:T(8,128)(2,1)S(1)} %get-tuple-element.62), channel_id=1, source_target_pairs={{0,16},{1,17},{2,18},{3,19},{4,20},{5,21},{6,22},{7,23},{8,24},{9,... | collective-permute-start | bytes 49160 | tf_op jit(solution)/shard_map/ppermute | solution.py:474
  29.3 8.5 %collective-permute-start.6 = (bf16[64,128]{1,0:T(8,128)(2,1)S(1)}, bf16[64,128]{1,0:T(8,128)(2,1)S(1)}, u32[]{:S(2)}, u32[]{:S(2)}) collective-permute-start(bf16[64,128]{1,0:T(8,128)(2,1)S(1)} %get-tuple-element.63), channel_id=1, source_target_pairs={{0,31},{1,16},{2,17},{3,18},{4,19},{5,20},{6,21},{7,22},{8,23},{9,... | collective-permute-start | bytes 49160 | tf_op jit(solution)/shard_map/ppermute | solution.py:474
  34.9 7.9 %collective-permute-start.5 = (bf16[64,128]{1,0:T(8,128)(2,1)S(1)}, bf16[64,128]{1,0:T(8,128)(2,1)S(1)}, u32[]{:S(2)}, u32[]{:S(2)}) collective-permute-start(bf16[64,128]{1,0:T(8,128)(2,1)S(1)} %get-tuple-element.63), channel_id=1, source_target_pairs={{0,17},{1,18},{2,19},{3,20},{4,21},{5,22},{6,23},{7,24},{8,25},{9,... | collective-permute-start | bytes 49160 | tf_op jit(solution)/shard_map/ppermute | solution.py:474
  45.8 16.2 %all-to-all-start.1 = ((bf16[16,48,128]{2,1,0:T(8,128)(2,1)}), bf16[16,48,128]{2,1,0:T(8,128)(2,1)S(1)}, u32[]{:S(2)}, u32[]{:S(2)}) async-start(bf16[16,48,128]{2,1,0:T(8,128)(2,1)} %get-tuple-element.64), calls=%async_computation.1 | async-start | bytes 393216 | tf_op jit(solution)/shard_map/all_to_all | solution.py:659
  51.0 8.7 %collective-permute-start.7 = (bf16[64,128]{1,0:T(8,128)(2,1)S(1)}, bf16[64,128]{1,0:T(8,128)(2,1)S(1)}, u32[]{:S(2)}, u32[]{:S(2)}) collective-permute-start(bf16[64,128]{1,0:T(8,128)(2,1)S(1)} %get-tuple-element.68), channel_id=1, source_target_pairs={{0,1},{1,2},{2,3},{3,4},{4,5},{5,6},{6,7},{7,8},{8,9},{9,10},{10,1... | collective-permute-start | bytes 49160 | tf_op jit(solution)/shard_map/ppermute | solution.py:474
  52.9 6.7 %collective-permute-start.8 = (bf16[64,128]{1,0:T(8,128)(2,1)S(1)}, bf16[64,128]{1,0:T(8,128)(2,1)S(1)}, u32[]{:S(2)}, u32[]{:S(2)}) collective-permute-start(bf16[64,128]{1,0:T(8,128)(2,1)S(1)} %get-tuple-element.69), channel_id=1, source_target_pairs={{0,15},{1,0},{2,1},{3,2},{4,3},{5,4},{6,5},{7,6},{8,7},{9,8},{10,9... | collective-permute-start | bytes 49160 | tf_op jit(solution)/shard_map/ppermute | solution.py:474
  62.0 1.4 %collective-permute-start.9 = (bf16[768,128]{1,0:T(8,128)(2,1)S(1)}, bf16[768,128]{1,0:T(8,128)(2,1)S(1)}, u32[]{:S(2)}, u32[]{:S(2)}) collective-permute-start(bf16[768,128]{1,0:T(8,128)(2,1)S(1)} %bitcast.11), channel_id=1, source_target_pairs={{0,16},{16,0},{1,17},{17,1},{2,18},{18,2},{3,19},{19,3},{4,20},{20... | collective-permute-start | bytes 589832 | tf_op jit(solution)/shard_map/ppermute | solution.py:664
